TPU v7x, 256 devices: a whole 4x4x8 slice. The times are simulated.
256 devices in a mesh: dom: 32 (over y, x, core), chan: 8 (over z).
Axes of the slice: x: 4, y: 4, z: 8, core: 2. Of those that a mesh axis runs over, the one named last changes fastest.
Arguments:
- feats: bfloat16 [131072, 512], P('dom', 'chan'), may hold values from -6 to 6
- block_vals: bfloat16 [1024, 8, 128, 128], P('dom'), may hold values from 0.019897461 to 1
- block_cols: int32 [1024, 8], P('dom'), may hold values from 0 to 159
- block_counts: int32 [1024], P('dom'), may hold values from 4 to 8
- send_list: int32 [32, 32, 4], P('dom'), may hold values from 0 to 31
- w_self: bfloat16 [512, 256], replicated, may hold values from -0.25 to 0.25
- w_neigh: bfloat16 [512, 256], replicated, may hold values from -6 to 6
- bias: float32 [256], replicated, may hold values from -4 to 4
- cotangent: bfloat16 [131072, 256], P(('dom', 'chan')), may hold values from -6 to 6
Outputs:
- out_h: bfloat16 [131072, 256], P(('dom', 'chan'))
- grad_feats: bfloat16 [131072, 512], P('dom', 'chan')
- grad_w_self: float32 [512, 256], P('chan')
- grad_w_neigh: float32 [512, 256], P('chan')
All inputs are finite; a program needn't handle non-finite values.
Results may differ from a plain program's by a relative error of at most 0.02.
Values may be sent and summed in bfloat16 or wider, within the bound.
No kernel may reach another device: no remote copies, remote signals or barrier semaphores. Data moves between devices by JAX's collectives and lax.ppermute only.
A program may use at most 128 MiB of HBM per device.

v0:
```python
import jax
import jax.numpy as jnp
from jax import lax
from jax.sharding import PartitionSpec as P


def layer_head(preact, cotangent):
    logistic = jax.nn.sigmoid(preact)
    activated = preact * logistic
    slope_value = logistic * (1.0 + preact * (1.0 - logistic))
    rms_value = jnp.sqrt(jnp.mean(activated * activated, axis=-1, keepdims=True) + 1e-06)
    unit_rows = activated / rms_value
    cot_value = cotangent.astype(jnp.float32)
    grad_act = (
        cot_value - unit_rows * jnp.mean(cot_value * unit_rows, axis=-1, keepdims=True)
    ) / rms_value
    return (unit_rows.astype(jnp.bfloat16), (grad_act * slope_value).astype(jnp.bfloat16))


def contract_rows(left, right):
    return lax.dot_general(
        left, right, (((0,), (0,)), ((), ())), preferred_element_type=jnp.float32
    )


def contract_cols(left, right):
    return lax.dot_general(
        left, right, (((1,), (1,)), ((), ())), preferred_element_type=jnp.float32
    )


def per_device(
    feats, block_vals, block_cols, block_counts, send_list, w_self, w_neigh, bias, cotangent
):
    row_count, chan_width = feats.shape
    block_rows, block_depth, block_size, _ = block_vals.shape
    partitions = lax.axis_size("dom")
    slot_count = send_list.shape[2]
    feat_blocks = feats.reshape(block_rows, block_size, chan_width)
    outgoing = jnp.take(feat_blocks, send_list[0].reshape(-1), axis=0).reshape(
        partitions, slot_count, block_size, chan_width
    )
    incoming = lax.all_to_all(outgoing, "dom", split_axis=0, concat_axis=0, tiled=True)
    lookup_table = jnp.concatenate(
        [feat_blocks, incoming.reshape(partitions * slot_count, block_size, chan_width)], axis=0
    )
    live_mask = jnp.arange(block_depth, dtype=jnp.int32)[None, :] < block_counts[:, None]
    picked = jnp.take(lookup_table, block_cols.reshape(-1), axis=0).reshape(
        block_rows, block_depth, block_size, chan_width
    )
    picked = jnp.where(live_mask[:, :, None, None], picked, jnp.zeros((), jnp.bfloat16))
    summed = jnp.einsum("rkij,rkjc->ric", block_vals, picked, preferred_element_type=jnp.float32)
    rowsums = jnp.einsum(
        "rkij,j->rki",
        block_vals,
        jnp.ones((block_size,), jnp.bfloat16),
        preferred_element_type=jnp.float32,
    )
    degree = jnp.sum(rowsums * live_mask[:, :, None].astype(jnp.float32), axis=1).reshape(
        row_count, 1
    )
    neighbor_mean = (summed.reshape(row_count, chan_width) / degree).astype(jnp.bfloat16)
    grad_scale = float(row_count * partitions) ** (-0.5)
    column = lax.axis_index("chan") * chan_width
    self_part = lax.dynamic_slice_in_dim(w_self, column, chan_width, 0)
    neigh_part = lax.dynamic_slice_in_dim(w_neigh, column, chan_width, 0)
    preact = (
        lax.psum_scatter(
            jnp.dot(feats, self_part, preferred_element_type=jnp.float32)
            + jnp.dot(neighbor_mean, neigh_part, preferred_element_type=jnp.float32),
            "chan",
            scatter_dimension=0,
            tiled=True,
        )
        + bias
    )
    out_h, grad_pre = layer_head(preact, cotangent)
    grad_all = lax.all_gather(grad_pre, "chan", axis=0, tiled=True)
    own_self = contract_rows(feats, grad_all)
    own_neigh = contract_rows(neighbor_mean, grad_all)
    grad_self = contract_cols(grad_all, self_part).astype(jnp.bfloat16)
    grad_mean = contract_cols(grad_all, neigh_part).astype(jnp.bfloat16)
    grad_w_self, grad_w_neigh = (
        lax.psum(own_self.astype(jnp.bfloat16), "dom").astype(jnp.float32),
        lax.psum(own_neigh.astype(jnp.bfloat16), "dom").astype(jnp.float32),
    )
    grad_w_self = grad_w_self * grad_scale
    grad_w_neigh = grad_w_neigh * grad_scale
    grad_scaled = (
        (grad_mean.astype(jnp.float32) / degree)
        .astype(jnp.bfloat16)
        .reshape(block_rows, block_size, chan_width)
    )
    contrib = jnp.einsum(
        "rkij,ric->rkjc", block_vals, grad_scaled, preferred_element_type=jnp.float32
    )
    table_count = block_rows + partitions * slot_count
    block_width = block_size * chan_width
    target_index = jnp.where(live_mask.reshape(-1), block_cols.reshape(-1), table_count)
    table_grad = (
        jnp.zeros((table_count, block_width), jnp.float32)
        .at[target_index]
        .add(contrib.reshape(block_rows * block_depth, block_width), mode="drop")
    )
    returned = lax.all_to_all(
        table_grad[block_rows:].reshape(partitions, slot_count, block_width).astype(jnp.bfloat16),
        "dom",
        split_axis=0,
        concat_axis=0,
        tiled=True,
    ).astype(jnp.float32)
    returned_sum = (
        jnp.zeros((block_rows, block_width), jnp.float32)
        .at[send_list[0].reshape(-1)]
        .add(returned.reshape(partitions * slot_count, block_width))
    )
    grad_feats = (
        grad_self.astype(jnp.float32)
        + (table_grad[:block_rows] + returned_sum).reshape(row_count, chan_width)
    ).astype(jnp.bfloat16)
    return (out_h, grad_feats, grad_w_self, grad_w_neigh)


def solution(mesh):
    return jax.shard_map(
        per_device,
        mesh=mesh,
        in_specs=(
            P("dom", "chan"),
            P("dom", None, None, None),
            P("dom", None),
            P("dom"),
            P("dom", None, None),
            P(),
            P(),
            P(),
            P(("dom", "chan"), None),
        ),
        out_specs=(P(("dom", "chan"), None), P("dom", "chan"), P("chan", None), P("chan", None)),
        check_vma=False,
    )
```

profile of v0, /device:TPU:2, one launch (start us, length us, event | category | flops | bytes accessed | tf_op | source)
XLA Modules:
  0.0 376.1 jit_solution(8492703900616834798)
XLA Ops:
  7.2 0.7 compare_and_fusion.1
  7.9 0.8 copy.46
  8.7 0.1 copy.45
  8.8 0.1 reshape_squeeze.7
  8.9 0.1 copy_bitcast_fusion
  9.1 1.0 gather_fusion
  10.1 1.6 broadcast_select_fusion
  11.6 7.6 %all-to-all-start = ((bf16[32,4,128,64]{2,3,1,0:T(8,128)(2,1)}), bf16[32,4,128,64]{2,3,1,0:T(8,128)(2,1)S(1)}, u32[]{:S(2)}, u32[]{:S(2)}) async-start(bf16[32,4,128,64]{2,3,1,0:T(8,128)(2,1)} %broadcast_select_fusion), calls=%async_computation | async-start | bytes 4194304 | tf_op jit(solution)/shard_map/all_to_all | solution.py:43
  19.3 0.1 copy.49
  19.4 0.1 copy.44
  19.5 0.1 reshape.212
  19.6 0.1 fusion.41
  19.7 0.1 lt.105
  19.8 5.6 %fusion.36 = f32[1,32,8,128]{3,0,2,1:T(1,128)S(1)} fusion(bf16[32,8,128,128]{3,2,1,0:T(8,128)(2,1)} %param.10), kind=kOutput, calls=%fused_computation.70 | convolution fusion | flops 8388608 | bytes 8519680 | tf_op jit(solution)/shard_map/rkij,j->rki/dot_general | solution.py:53
  25.4 0.1 multiply_reduce_fusion.1
  25.6 3.4 convolution_bitcast_fusion
  29.0 18.1 %all-to-all-done = bf16[32,4,128,64]{2,3,1,0:T(8,128)(2,1)S(1)} async-done(((bf16[32,4,128,64]{2,3,1,0:T(8,128)(2,1)}), bf16[32,4,128,64]{2,3,1,0:T(8,128)(2,1)S(1)}, u32[]{:S(2)}, u32[]{:S(2)}) %all-to-all-start) | async-done | bytes 2097184 | tf_op jit(solution)/shard_map/all_to_all | solution.py:43
  47.1 1.8 pad_maximum_fusion
  49.0 4.8 %gather_fusion.1 = bf16[256,128,64]{1,2,0:T(8,128)(2,1)} fusion(bf16[160,128,64]{1,2,0:T(8,128)(2,1)} %pad_maximum_fusion, s32[1024]{0:T(1024)S(1)} %pad_clamp_fusion), kind=kCustom, calls=%fused_computation.1 | custom fusion | bytes 8389632 | tf_op jit(solution)/shard_map/jit(_take)/gather | solution.py:48
  53.8 6.4 %fusion.15 = f32[32,8,8,128]{3,2,1,0:T(8,128)S(1)} fusion(bf16[32,8,128,128]{3,2,1,0:T(8,128)(2,1)} %param.10, bf16[32,8,128,64]{2,3,1,0:T(8,128)(2,1)} %bitcast.57, pred[32,8]{1,0:T(8,128)(4,1)S(1)} %copy.44, pred[32,8]{1,0:T(8,128)(4,1)S(1)} %get-tuple-element.27), kind=kOutput, calls=%fused_computation.27 | convolution fusion | flops 541065216 | bytes 13632000 | tf_op jit(solution)/shard_map/rkij,rkjc->ric/dot_general | solution.py:52
  60.2 1.0 copy-done.4
  61.1 3.5 convolution_add_fusion
  64.7 0.9 copy-done.5
  65.6 0.1 copy.52
  65.7 54.9 %reduce-scatter.2.cloned.1.call-done = f32[512,256]{0,1:T(8,128)} async-done(((f32[4096,256]{0,1:T(8,128)}), f32[512,256]{0,1:T(8,128)}) %reduce-scatter.2.cloned.1.call-update) | async-done | bytes 524304 | tf_op jit(solution)/shard_map/reduce_scatter | solution.py:68
  120.6 1.3 multiply_reduce_fusion
  121.9 1.3 fusion.21
  123.2 2.1 fusion.24
  125.4 39.9 %all-gather.2.cloned.1.call-done = bf16[4096,256]{0,1:T(8,128)(2,1)} async-done(((bf16[512,256]{0,1:T(8,128)(2,1)}), bf16[4096,256]{0,1:T(8,128)(2,1)}) %all-gather.2.cloned.1.call-update) | async-done | bytes 2097168 | tf_op jit(solution)/shard_map/all_gather | solution.py:78
  165.3 2.1 fusion.18
  167.4 0.1 copy.66
  167.5 8.0 %convolution_bitcast_fusion.1 = f32[32,8,128,64]{2,3,1,0:T(8,128)} fusion(bf16[32,8,128,128]{3,2,1,0:T(8,128)(2,1)} %param.10, bf16[32,128,64,1]{1,0,2,3:T(8,128)(2,1)S(1)} %bitcast.59), kind=kOutput, calls=%fused_computation.20 | convolution fusion | flops 536870912 | bytes 17301504 | tf_op jit(solution)/shard_map/rkij,ric->rkjc/dot_general | solution.py:94
  175.5 12.2 %copy.54 = f32[32,8,128,64]{3,2,1,0:T(8,128)} copy(f32[32,8,128,64]{2,3,1,0:T(8,128)} %convolution_bitcast_fusion.1) | data formatting | bytes 16777216 | tf_op jit(solution)/shard_map/rkij,ric->rkjc/dot_general | solution.py:94
  187.7 14.8 %reshape.241 = f32[256,8192]{1,0:T(8,128)} reshape(f32[32,8,128,64]{3,2,1,0:T(8,128)} %copy.54) | data formatting | bytes 16777216 | tf_op jit(solution)/shard_map/reshape | solution.py:103
  202.4 15.6 %scatter_custom_fusion = f32[160,8192]{1,0:T(8,128)} fusion(s32[256]{0:T(256)S(1)} %bitcast.65, f32[256,8192]{1,0:T(8,128)} %reshape.241, f32[]{:T(128)} %constant.32.clone.1), kind=kCustom, calls=%fused_computation.22 | custom fusion | flops 2097152 | bytes 5243392 | tf_op jit(solution)/shard_map/scatter-add | solution.py:103
  218.0 3.8 %slice.16 = bf16[128,8192]{1,0:T(8,128)(2,1)} slice(f32[160,8192]{1,0:T(8,128)} %scatter_custom_fusion), slice={[32:160], [0:8192]} | slice | bytes 4194304 | tf_op jit(solution)/shard_map/slice | solution.py:106
  221.9 4.3 %convert_element_type.68 = bf16[32,4,8192]{2,1,0:T(4,128)(2,1)} reshape(bf16[128,8192]{1,0:T(8,128)(2,1)} %slice.16) | data formatting | bytes 4194304 | tf_op jit(solution)/shard_map/convert_element_type | solution.py:106
  226.2 7.5 %all-to-all-start.1 = ((bf16[32,4,8192]{2,1,0:T(4,128)(2,1)}), bf16[32,4,8192]{2,1,0:T(4,128)(2,1)}, u32[]{:S(2)}, u32[]{:S(2)}) async-start(bf16[32,4,8192]{2,1,0:T(4,128)(2,1)} %convert_element_type.68), calls=%async_computation.2 | async-start | bytes 4194304 | tf_op jit(solution)/shard_map/all_to_all | solution.py:105
  233.7 1.4 fusion.19
  235.1 2.6 convolution_convert_fusion.2
  237.7 0.8 copy.56
  238.5 109.8 %all-reduce.3.cloned.1.call-done = (bf16[64,256]{1,0:T(8,128)(2,1)}, bf16[64,256]{1,0:T(8,128)(2,1)}) async-done(((bf16[64,256]{1,0:T(8,128)(2,1)}, bf16[64,256]{1,0:T(8,128)(2,1)}), (bf16[64,256]{1,0:T(8,128)(2,1)}, bf16[64,256]{1,0:T(8,128)(2,1)})) %all-reduce.3.cloned.1.call-update) | async-done | bytes 65552 | tf_op jit(solution)/shard_map/psum | solution.py:84
  348.3 1.4 convert_multiply_fusion.1
  349.8 4.3 %reshape.249 = f32[128,8192]{1,0:T(8,128)} reshape(bf16[32,4,8192]{2,1,0:T(4,128)(2,1)} %all-to-all-done.1) | data formatting | bytes 6291456 | tf_op jit(solution)/shard_map/reshape | solution.py:115
  354.1 7.4 %scatter_fusion = f32[32,8192]{1,0:T(8,128)S(1)} fusion(f32[32,8192]{1,0:T(8,128)S(1)} %slice-done, s32[128]{0:T(128)S(1)} %fusion.31, f32[128,8192]{1,0:T(8,128)} %reshape.249), kind=kCustom, calls=%fused_computation.3 | custom fusion | flops 1048576 | bytes 12583424 | tf_op jit(solution)/shard_map/scatter-add | solution.py:115
  361.5 2.2 reshape.218
  363.7 3.3 copy.55
  367.0 2.5 fusion.5
  (32 shorter events, 0.3 us)
Async XLA Ops:
  7.2 1.8 copy-start
  10.0 9.3 %copy-start.6 = (s32[32,8]{0,1:T(8,128)S(1)}, s32[32,8]{0,1:T(8,128)}, u32[]{:S(2)}) copy-start(s32[32,8]{0,1:T(8,128)} %param.11) | copy-start | bytes 3076
  10.0 9.6 %copy-start.8 = (s32[32]{0:T(128)S(1)}, s32[32]{0:T(128)}, u32[]{:S(2)}) copy-start(s32[32]{0:T(128)} %param.12) | copy-start | bytes 388
  11.6 35.5 %all-to-all-start = ((bf16[32,4,128,64]{2,3,1,0:T(8,128)(2,1)}), bf16[32,4,128,64]{2,3,1,0:T(8,128)(2,1)S(1)}, u32[]{:S(2)}, u32[]{:S(2)}) async-start(bf16[32,4,128,64]{2,3,1,0:T(8,128)(2,1)} %broadcast_select_fusion), calls=%async_computation | async-start | bytes 4194304 | tf_op jit(solution)/shard_map/all_to_all | solution.py:43
  19.3 101.3 %reduce-scatter.2.cloned.1.call-start = ((), (), s32[]{:S(2)}) async-start(), calls=%async_computation.3 | async-start | bytes 4718592 | tf_op jit(solution)/shard_map/reduce_scatter | solution.py:68
  53.8 7.4 %copy-start.1 = (f32[4096,256]{0,1:T(8,128)S(1)}, f32[4096,256]{0,1:T(8,128)}, u32[]{:S(2)}) copy-start(f32[4096,256]{0,1:T(8,128)} %convolution_bitcast_fusion) | copy-start | bytes 12582916
  60.2 1.0 copy-start.4
  64.6 0.9 copy-start.5
  64.6 56.0 %copy-start.7 = (f32[256]{0:T(256)S(1)}, f32[256]{0:T(256)}, u32[]{:S(2)}) copy-start(f32[256]{0:T(256)} %param.16) | copy-start | bytes 3076
  64.6 100.6 %all-gather.2.cloned.1.call-start = ((), (), s32[]{:S(2)}) async-start(), calls=%async_computation.4 | async-start | bytes 2359296 | tf_op jit(solution)/shard_map/all_gather | solution.py:78
  221.9 11.8 %copy-start.2 = (bf16[4096,256]{0,1:T(8,128)(2,1)S(1)}, bf16[4096,256]{0,1:T(8,128)(2,1)}, u32[]{:S(2)}) copy-start(bf16[4096,256]{0,1:T(8,128)(2,1)} %all-gather.2.cloned.1.call-done) | copy-start | bytes 6291460
  226.2 123.6 %all-to-all-start.1 = ((bf16[32,4,8192]{2,1,0:T(4,128)(2,1)}), bf16[32,4,8192]{2,1,0:T(4,128)(2,1)}, u32[]{:S(2)}, u32[]{:S(2)}) async-start(bf16[32,4,8192]{2,1,0:T(4,128)(2,1)} %convert_element_type.68), calls=%async_computation.2 | async-start | bytes 4194304 | tf_op jit(solution)/shard_map/all_to_all | solution.py:105
  233.6 114.7 %all-reduce.3.cloned.1.call-start = ((), (), s32[]{:S(2)}) async-start(), calls=%async_computation.5 | async-start | bytes 131072 | tf_op jit(solution)/shard_map/psum | solution.py:84
  238.5 115.6 %slice-start = ((f32[160,8192]{1,0:T(8,128)}), f32[32,8192]{1,0:T(8,128)S(1)}, s32[]{:S(2)}) async-start(f32[160,8192]{1,0:T(8,128)} %scatter_custom_fusion), calls=%async_computation.6 | async-start | bytes 2097152 | tf_op jit(solution)/shard_map/slice | solution.py:119
  363.7 3.3 copy-start.3
Sparse Core Ops, SparseCore 0:
  64.8 55.7 reduce-scatter.1
  125.5 39.7 all-gather.1
  238.4 109.8 all-reduce.2
where the time goes:
time: 380 us; the launch traced here: 376 us
  waiting for transfers between devices  223 us (59%)
  local copies, waits for them, and re-layouts  55 us (14%)
  matrix products  35.5 us (9%)
  other arithmetic  33.6 us (9%)
  starting transfers between devices  15.2 us (4%)
  between operations  14 us (4%)
    psum x1, waiting for transfers between devices, per_device(): lax.psum(own_self.astype(jnp.bfloat16), 'dom').astype(jnp.float32)  110 us
    reduce_scatter x1, waiting for transfers between devices, per_device(): lax.psum_scatter(jnp.dot(feats, self_part, preferred_element_type=jnp.flo...  54.9 us
    all_gather x1, waiting for transfers between devices, per_device(): grad_all = lax.all_gather(grad_pre, 'chan', axis=0, tiled=True)  39.9 us
    all_to_all x1, waiting for transfers between devices, per_device(): lax.all_to_all(outgoing, 'dom', split_axis=0, concat_axis=0, tiled=True)  18.1 us
    scatter-add x1, other arithmetic, per_device(): table_grad = jnp.zeros((table_count, block_width), jnp.float32).at[target...  15.6 us
    reshape x1, local copies, waits for them, and re-layouts, per_device(): contrib.reshape(block_rows * block_depth, block_width)  14.8 us
    dot_general x1, local copies, waits for them, and re-layouts, per_device(): jnp.einsum('rkij,ric->rkjc', block_vals, grad_scaled, preferred_element_t...  12.2 us
    dot_general x1, matrix products, per_device(): jnp.einsum('rkij,ric->rkjc', block_vals, grad_scaled, preferred_element_t...  8.01 us
  transfers between devices with their start and end apart: 5, of which 4 were waited for; matrix products, arithmetic and copies ran while one was open for 4% of the time, Pallas kernels for 0%

commit v1 on v0

v1 whole, which is shorter than its diff:
```python
import functools

import jax
import jax.numpy as jnp
from jax import lax
from jax.experimental import pallas as pl
from jax.experimental.pallas import tpu as pltpu
from jax.sharding import PartitionSpec as P

BF = jnp.bfloat16
F32 = jnp.float32
MIB = 1 << 20


def vmem():
    return pl.BlockSpec(memory_space=pltpu.VMEM)


def smem():
    return pl.BlockSpec(memory_space=pltpu.SMEM)


def params(mib):
    return pltpu.CompilerParams(vmem_limit_bytes=mib * MIB)


def cost(flops, nbytes):
    return pl.CostEstimate(flops=flops, bytes_accessed=nbytes, transcendentals=0)


def nt_dot(left, right):
    return lax.dot_general(left, right, (((1,), (1,)), ((), ())), preferred_element_type=F32)


def nn_dot(left, right):
    return lax.dot_general(left, right, (((1,), (0,)), ((), ())), preferred_element_type=F32)


def pack_kernel(send_ref, feats_ref, out_ref):
    dests, slots, _, size = out_ref.shape

    def one(dest, carry):
        for slot in range(slots):
            lane = pl.multiple_of(send_ref[dest, slot] * size, size)
            out_ref[dest, slot] = feats_ref[:, pl.ds(lane, size)]
        return carry

    lax.fori_loop(0, dests, one, 0, unroll=4)


def split_kernel(me_ref, feats_ref, *out_refs):
    chans = len(out_refs)
    width = out_refs[0].shape[1]
    for shift, out_ref in enumerate(out_refs):
        lane = pl.multiple_of(lax.rem(me_ref[0] + shift, chans) * width, width)
        out_ref[...] = feats_ref[:, pl.ds(lane, width)]


def degree_kernel(counts_ref, vals_ref, out_ref):
    rows, depth, size, _ = vals_ref.shape
    ones = jnp.ones((16, size), BF)
    step = pl.program_id(0)
    for row in range(rows):
        count = counts_ref[step * rows + row]
        left = jnp.concatenate([jnp.where(k < count, ones, jnp.zeros_like(ones)) for k in range(depth)], axis=1)
        right = jnp.concatenate([vals_ref[row, k] for k in range(depth)], axis=1)
        total = nt_dot(left, right)
        out_ref[0, :, row * size : (row + 1) * size] = total[:8]


def gather_kernel(me_ref, cols_ref, counts_ref, feats_ref, recv_ref, degree_ref, vals_ref, *out_refs):
    rows, depth, size, _ = vals_ref.shape
    chans = len(out_refs)
    own = feats_ref.shape[1] // size
    step = pl.program_id(0)
    group = lax.rem(me_ref[0] + step, chans)
    parts = []
    for row in range(rows):
        index = group * rows + row
        count = counts_ref[index]
        picked = []
        for k in range(depth):
            col = cols_ref[index, k]
            lane = pl.multiple_of(jnp.minimum(col, own - 1) * size, size)
            near = feats_ref[:, pl.ds(lane, size)]
            far = recv_ref[jnp.maximum(col - own, 0)]
            block = jnp.where(col < own, near, far)
            picked.append(jnp.where(k < count, block, jnp.zeros_like(block)))
        left = jnp.concatenate(picked, axis=1)
        right = jnp.concatenate([vals_ref[row, k] for k in range(depth)], axis=1)
        total = nt_dot(left, right)
        scale = degree_ref[group, 0:1, row * size : (row + 1) * size]
        parts.append((total / scale).astype(BF))
    for shift, out_ref in enumerate(out_refs):

        @pl.when(step == shift)
        def _():
            for row in range(rows):
                out_ref[:, row * size : (row + 1) * size] = parts[row]


def assemble(me_ref, chunk_refs, full_ref):
    chans = len(chunk_refs)
    height = chunk_refs[0].shape[0]
    for shift, chunk_ref in enumerate(chunk_refs):
        start = pl.multiple_of(lax.rem(me_ref[0] + (chans - shift), chans) * height, height)
        full_ref[pl.ds(start, height), :] = chunk_ref[...]


def self_kernel(chans, me_ref, weight_ref, bias_ref, *refs):
    chunk_refs = refs[:chans]
    full_ref, pre_ref = refs[chans:]
    assemble(me_ref, chunk_refs, full_ref)
    pre_ref[...] = nn_dot(weight_ref[...], full_ref[...]) + bias_ref[...]


def head_kernel(chans, me_ref, degree_ref, pre_ref, turned_ref, weight_ref, cot_ref, *refs):
    chunk_refs = refs[:chans]
    mean_ref, out_ref, grad_ref = refs[chans : chans + 3]
    scaled_refs = refs[chans + 3 : 2 * chans + 3]
    (hold_ref,) = refs[2 * chans + 3 :]
    assemble(me_ref, chunk_refs, mean_ref)
    preact = pre_ref[...] + nn_dot(turned_ref[...], mean_ref[...])
    logistic = jax.nn.sigmoid(preact)
    activated = preact * logistic
    slope = logistic * (1.0 + preact * (1.0 - logistic))
    inverse = 1.0 / jnp.sqrt(jnp.mean(activated * activated, axis=0, keepdims=True) + 1e-06)
    unit = activated * inverse
    cot = cot_ref[...].astype(F32)
    grad_act = (cot - unit * jnp.mean(cot * unit, axis=0, keepdims=True)) * inverse
    grad = (grad_act * slope).astype(BF)
    out_ref[...] = unit.astype(BF)
    grad_ref[...] = grad
    mean_grad = nn_dot(weight_ref[...], grad).astype(BF).astype(F32)
    degree = degree_ref[me_ref[0], 0:1, :]
    hold_ref[...] = (mean_grad / degree).astype(BF)
    height = scaled_refs[0].shape[0]
    for shift, scaled_ref in enumerate(scaled_refs):
        start = pl.multiple_of(lax.rem(me_ref[0] + shift, chans) * height, height)
        scaled_ref[...] = hold_ref[pl.ds(start, height), :]


def side_kernel(chans, me_ref, weight_ref, feats_ref, mean_ref, out_ref, grad_ref, *refs):
    turned_ref = refs[0]
    packed_refs = refs[1 : chans + 1]
    (hold_ref,) = refs[chans + 1 :]
    turned_ref[...] = out_ref[...].T
    grad = grad_ref[...]
    nodes = grad.shape[1]
    feature = grad.shape[0]
    hold_ref[:, :nodes] = nn_dot(weight_ref[...], grad).astype(BF)
    hold_ref[:, nodes : nodes + feature] = nt_dot(feats_ref[...], grad).astype(BF)
    hold_ref[:, nodes + feature :] = nt_dot(mean_ref[...], grad).astype(BF)
    height = packed_refs[0].shape[0]
    for shift, packed_ref in enumerate(packed_refs):
        start = pl.multiple_of(lax.rem(me_ref[0] + shift, chans) * height, height)
        packed_ref[...] = hold_ref[pl.ds(start, height), :]


def scatter_kernel(chans, me_ref, cols_ref, counts_ref, vals_ref, *refs):
    chunk_refs = refs[:chans]
    own_ref, far_ref, hold_ref = refs[chans:]
    rows, depth, size, _ = vals_ref.shape
    own = own_ref.shape[0]
    step = pl.program_id(0)
    group = lax.rem(me_ref[0] + (chans - step), chans)

    @pl.when(step == 0)
    def _():
        hold_ref[...] = jnp.zeros_like(hold_ref)

    for shift, chunk_ref in enumerate(chunk_refs):

        @pl.when(step == shift)
        def _():
            for row in range(rows):
                index = group * rows + row
                count = counts_ref[index]
                left = chunk_ref[:, row * size : (row + 1) * size]
                right = jnp.concatenate([vals_ref[row, k] for k in range(depth)], axis=1)
                total = nn_dot(left, right)
                for k in range(depth):
                    col = cols_ref[index, k]
                    part = total[:, k * size : (k + 1) * size]
                    hold_ref[col] += jnp.where(k < count, part, jnp.zeros_like(part))

    @pl.when(step == chans - 1)
    def _():
        own_ref[...] = hold_ref[:own]
        far_ref[...] = hold_ref[own:].astype(BF)


def weight_kernel(*refs):
    packed_refs = refs[:-1]
    out_ref = refs[-1]
    width = out_ref.shape[1]
    total = packed_refs[0][:, width:].astype(F32)
    for packed_ref in packed_refs[1:]:
        total = total + packed_ref[:, width:].astype(F32)
    out_ref[...] = total.astype(BF)


def final_kernel(chans, me_ref, send_ref, own_ref, back_ref, *refs):
    packed_refs = refs[:chans]
    out_ref, hold_ref = refs[chans:]
    dests, slots = send_ref.shape
    blocks, _, size = hold_ref.shape
    rows = blocks // chans
    hold_ref[...] = own_ref[...]

    def one(dest, carry):
        for slot in range(slots):
            hold_ref[send_ref[dest, slot]] += back_ref[dest, slot].astype(F32)
        return carry

    lax.fori_loop(0, dests, one, 0, unroll=4)
    for shift, packed_ref in enumerate(packed_refs):
        group = lax.rem(me_ref[0] + (chans - shift), chans)
        for row in range(rows):
            index = group * rows + row
            total = hold_ref[index] + packed_ref[:, row * size : (row + 1) * size].astype(F32)
            out_ref[:, pl.ds(pl.multiple_of(index * size, size), size)] = total.astype(BF)


def exchange(chunks):
    count = len(chunks)
    return [chunks[0]] + [
        lax.ppermute(chunks[shift], "chan", [(i, (i + shift) % count) for i in range(count)])
        for shift in range(1, count)
    ]


def sds(shape, dtype):
    return jax.ShapeDtypeStruct(shape, dtype)


def per_device(feats, block_vals, block_cols, block_counts, send_list, w_self, w_neigh, bias, cotangent):
    node_count, chan_width = feats.shape
    block_rows, depth, size, _ = block_vals.shape
    parts = lax.axis_size("dom")
    chans = lax.axis_size("chan")
    slots = send_list.shape[2]
    f_in, f_out = w_self.shape
    nodes = node_count // chans
    rows = block_rows // chans
    table = block_rows + parts * slots
    me = lax.axis_index("chan").astype(jnp.int32).reshape(1)
    send = send_list[0]
    feats_t = feats.T
    val_bytes = block_vals.size * 2
    block_flops = 2 * block_rows * depth * size * size * chan_width

    outgoing = pl.pallas_call(
        pack_kernel,
        out_shape=sds((parts, slots, chan_width, size), BF),
        in_specs=[smem(), vmem()],
        out_specs=vmem(),
        compiler_params=params(16),
        cost_estimate=cost(0, 5 * MIB),
        name="pack_outgoing",
    )(send, feats_t)
    incoming = lax.all_to_all(outgoing, "dom", split_axis=0, concat_axis=0, tiled=True)

    feat_chunks = pl.pallas_call(
        split_kernel,
        out_shape=[sds((chan_width, nodes), BF)] * chans,
        in_specs=[smem(), vmem()],
        out_specs=[vmem()] * chans,
        compiler_params=params(16),
        cost_estimate=cost(0, MIB),
        name="split_feats",
    )(me, feats_t)
    feat_chunks = exchange(feat_chunks)
    degree = pl.pallas_call(
        degree_kernel,
        grid_spec=pltpu.PrefetchScalarGridSpec(
            num_scalar_prefetch=1,
            grid=(chans,),
            in_specs=[pl.BlockSpec((rows, depth, size, size), lambda i, *_: (i, 0, 0, 0))],
            out_specs=pl.BlockSpec((1, 8, nodes), lambda i, *_: (i, 0, 0)),
        ),
        out_shape=sds((chans, 8, nodes), F32),
        compiler_params=params(16),
        cost_estimate=cost(block_flops // 4, val_bytes),
        name="degree",
    )(block_counts, block_vals)
    feats_own, pre_self = pl.pallas_call(
        functools.partial(self_kernel, chans),
        out_shape=[sds((f_in, nodes), BF), sds((f_out, nodes), F32)],
        in_specs=[smem(), vmem(), vmem()] + [vmem()] * chans,
        out_specs=[vmem()] * 2,
        compiler_params=params(16),
        cost_estimate=cost(2 * f_in * f_out * nodes, 2 * MIB),
        name="self_part",
    )(me, w_self.T, bias.reshape(f_out, 1), *feat_chunks)

    mean_chunks = pl.pallas_call(
        gather_kernel,
        grid_spec=pltpu.PrefetchScalarGridSpec(
            num_scalar_prefetch=3,
            grid=(chans,),
            in_specs=[
                vmem(),
                vmem(),
                vmem(),
                pl.BlockSpec((rows, depth, size, size), lambda i, me, *_: (lax.rem(me[0] + i, chans), 0, 0, 0)),
            ],
            out_specs=[vmem()] * chans,
        ),
        out_shape=[sds((chan_width, nodes), BF)] * chans,
        compiler_params=params(24),
        cost_estimate=cost(block_flops, val_bytes + 3 * MIB),
        name="neighbour_mean",
    )(me, block_cols, block_counts, feats_t, incoming.reshape(parts * slots, chan_width, size), degree, block_vals)
    mean_chunks = exchange(mean_chunks)

    head = pl.pallas_call(
        functools.partial(head_kernel, chans),
        out_shape=[sds((f_in, nodes), BF), sds((f_out, nodes), BF), sds((f_out, nodes), BF)]
        + [sds((chan_width, nodes), BF)] * chans,
        in_specs=[smem()] + [vmem()] * (5 + chans),
        out_specs=[vmem()] * (3 + chans),
        scratch_shapes=[pltpu.VMEM((f_in, nodes), BF)],
        compiler_params=params(32),
        cost_estimate=cost(4 * f_in * f_out * nodes, 4 * MIB),
        name="layer_head",
    )(me, degree, pre_self, w_neigh.T, w_neigh, cotangent.T, *mean_chunks)
    mean_own, out_t, grad_t = head[:3]
    scaled_chunks = exchange(head[3:])

    side = pl.pallas_call(
        functools.partial(side_kernel, chans),
        out_shape=[sds((nodes, f_out), BF)] + [sds((chan_width, nodes + 2 * f_out), BF)] * chans,
        in_specs=[smem()] + [vmem()] * 5,
        out_specs=[vmem()] * (1 + chans),
        scratch_shapes=[pltpu.VMEM((f_in, nodes + 2 * f_out), BF)],
        compiler_params=params(32),
        cost_estimate=cost(6 * f_in * f_out * nodes, 4 * MIB),
        name="side_grads",
    )(me, w_self, feats_own, mean_own, out_t, grad_t)
    out_h = side[0]

    own_grad, far_grad = pl.pallas_call(
        functools.partial(scatter_kernel, chans),
        grid_spec=pltpu.PrefetchScalarGridSpec(
            num_scalar_prefetch=3,
            grid=(chans,),
            in_specs=[
                pl.BlockSpec(
                    (rows, depth, size, size), lambda i, me, *_: (lax.rem(me[0] + (chans - i), chans), 0, 0, 0)
                ),
            ]
            + [vmem()] * chans,
            out_specs=[vmem()] * 2,
            scratch_shapes=[pltpu.VMEM((table, chan_width, size), F32)],
        ),
        out_shape=[sds((block_rows, chan_width, size), F32), sds((parts * slots, chan_width, size), BF)],
        compiler_params=params(32),
        cost_estimate=cost(block_flops, val_bytes + 4 * MIB),
        name="table_grad",
    )(me, block_cols, block_counts, block_vals, *scaled_chunks)
    back = lax.all_to_all(
        far_grad.reshape(parts, slots, chan_width, size), "dom", split_axis=0, concat_axis=0, tiled=True
    )

    packed = exchange(side[1:])
    weight_sum = pl.pallas_call(
        weight_kernel,
        out_shape=sds((chan_width, 2 * f_out), BF),
        in_specs=[vmem()] * chans,
        out_specs=vmem(),
        compiler_params=params(16),
        cost_estimate=cost(0, MIB),
        name="weight_sum",
    )(*packed)
    flip = 1
    while flip < parts:
        other = lax.ppermute(weight_sum, "dom", [(i, i ^ flip) for i in range(parts)])
        total = weight_sum.astype(F32) + other.astype(F32)
        flip *= 2
        if flip < parts:
            weight_sum = total.astype(BF)
    total = total * (float(node_count * parts) ** (-0.5))
    grad_w_self = total[:, :f_out]
    grad_w_neigh = total[:, f_out:]

    grad_feats = pl.pallas_call(
        functools.partial(final_kernel, chans),
        out_shape=sds((chan_width, node_count), BF),
        in_specs=[smem(), smem()] + [vmem()] * (2 + chans),
        out_specs=vmem(),
        scratch_shapes=[pltpu.VMEM((block_rows, chan_width, size), F32)],
        compiler_params=params(24),
        cost_estimate=cost(0, 6 * MIB),
        name="sum_returned",
    )(me, send, own_grad, back, *packed)
    return (out_h, grad_feats.T, grad_w_self, grad_w_neigh)


def solution(mesh):
    return jax.shard_map(
        per_device,
        mesh=mesh,
        in_specs=(
            P("dom", "chan"),
            P("dom", None, None, None),
            P("dom", None),
            P("dom"),
            P("dom", None, None),
            P(),
            P(),
            P(),
            P(("dom", "chan"), None),
        ),
        out_specs=(P(("dom", "chan"), None), P("dom", "chan"), P("chan", None), P("chan", None)),
        check_vma=False,
    )
```

time: 380 us -> 185 us (0.49)
  waiting for transfers between devices: 223 us -> 42.7 us
  starting transfers between devices: 15.2 us -> 84.5 us
  matrix products: 35.5 us -> 0 us
  other arithmetic: 33.6 us -> 0.1 us
  Pallas kernels: 0 us -> 23.8 us
  local copies, waits for them, and re-layouts: 55 us -> 32.2 us
  between operations: 14 us -> 0.95 us
    psum x1 -> x0, waiting for transfers between devices: 110 us -> none  [per_device(): lax.psum(own_self.astype(jnp.bfloat16), 'dom').astype(jnp.float32)]
    ppermute x0 -> x33, starting transfers between devices: none -> 71 us  [the longest x28 63.7 us: exchange(): lax.ppermute(chunks[shift], 'chan', [(i, (i + shift) % count) for i in ra...]
    reduce_scatter x1 -> x0, waiting for transfers between devices: 54.9 us -> none  [per_device(): lax.psum_scatter(jnp.dot(feats, self_part, preferred_element_type=jnp.flo...]
    all_gather x1 -> x0, waiting for transfers between devices: 39.9 us -> none  [per_device(): grad_all = lax.all_gather(grad_pre, 'chan', axis=0, tiled=True)]
    ppermute x0 -> x33, waiting for transfers between devices: none -> 39.3 us  [the longest x28 24.8 us: exchange(): lax.ppermute(chunks[shift], 'chan', [(i, (i + shift) % count) for i in ra...]
    dot_general x9 -> x0, matrix products: 35.5 us -> none  [the longest x1 8.01 us: per_device(): jnp.einsum('rkij,ric->rkjc', block_vals, grad_scaled, preferred_element_t...]
    unnamed x23 -> x86, local copies, waits for them, and re-layouts: 3.78 us -> 30.7 us
    reshape x6 -> x1, local copies, waits for them, and re-layouts: 24.8 us -> 0.13 us  [per_device(): bias.reshape(f_out, 1)]
  transfers between devices with their start and end apart: 5 -> 35, of which waited for: 4 -> 17; matrix products, arithmetic and copies ran while one was open for 4% -> 1% of each run, Pallas kernels for 0% -> 7%
where the time goes in v1:
time: 185 us; the launch traced here: 184 us
  starting transfers between devices  84.5 us (46%)
  waiting for transfers between devices  42.7 us (23%)
  local copies, waits for them, and re-layouts  32.2 us (17%)
  Pallas kernels  23.8 us (13%)
    ppermute x28, starting transfers between devices, exchange(): lax.ppermute(chunks[shift], 'chan', [(i, (i + shift) % count) for i in ra...  63.7 us
    unnamed x86, local copies, waits for them, and re-layouts  30.7 us
    ppermute x28, waiting for transfers between devices, exchange(): lax.ppermute(chunks[shift], 'chan', [(i, (i + shift) % count) for i in ra...  24.8 us
    ppermute x5, waiting for transfers between devices, per_device(): lax.ppermute(weight_sum, 'dom', [(i, i ^ flip) for i in range(parts)])  14.4 us
    all_to_all x1, starting transfers between devices, per_device(): lax.all_to_all(outgoing, 'dom', split_axis=0, concat_axis=0, tiled=True)  7.75 us
    ppermute x5, starting transfers between devices, per_device(): lax.ppermute(weight_sum, 'dom', [(i, i ^ flip) for i in range(parts)])  7.31 us
    pallas_call x1, Pallas kernels, per_device(): pl.pallas_call(gather_kernel, grid_spec=pltpu.PrefetchScalarGridSpec(num_...  6.08 us
    all_to_all x1, starting transfers between devices, per_device(): lax.all_to_all(far_grad.reshape(parts, slots, chan_width, size), 'dom', s...  5.83 us
  transfers between devices with their start and end apart: 35, of which 17 were waited for; matrix products, arithmetic and copies ran while one was open for 1% of the time, Pallas kernels for 7%

profile of v1, /device:TPU:2, one launch (start us, length us, event | category | flops | bytes accessed | tf_op | source)
XLA Modules:
  0.0 184.4 jit_solution(10126676928923590510)
XLA Ops:
  2.4 2.7 %pack_outgoing.1 = bf16[32,4,64,128]{3,2,1,0:T(8,128)(2,1)} custom-call(s32[32,4]{1,0:T(8,128)S(1)} %copy.24.send_ref, bf16[64,4096]{1,0:T(8,128)(2,1)S(1)} %bitcast.11), custom_call_target="tpu_custom_call" | custom-call | bytes 5242880 | tf_op jit(solution)/shard_map/pack_outgoing/pallas_call | solution.py:253
  5.1 7.7 %all-to-all-start = ((bf16[32,4,64,128]{3,2,1,0:T(8,128)(2,1)}), bf16[32,4,64,128]{3,2,1,0:T(8,128)(2,1)S(1)}, u32[]{:S(2)}, u32[]{:S(2)}) async-start(bf16[32,4,64,128]{3,2,1,0:T(8,128)(2,1)} %pack_outgoing.1), calls=%async_computation | async-start | bytes 4194304 | tf_op jit(solution)/shard_map/all_to_all | solution.py:262
  15.5 1.9 %collective-permute-start = (bf16[64,512]{1,0:T(8,128)(2,1)}, bf16[64,512]{1,0:T(8,128)(2,1)S(1)}, u32[]{:S(2)}, u32[]{:S(2)}) collective-permute-start(bf16[64,512]{1,0:T(8,128)(2,1)} %get-tuple-element.45), channel_id=1, source_target_pairs={{0,1},{1,2},{2,3},{3,4},{4,5},{5,6},{6,7},{7,0},{8,9},{9,10},{10,1... | collective-permute-start | bytes 196616 | tf_op jit(solution)/shard_map/ppermute | solution.py:228
  17.4 3.3 %collective-permute-start.1 = (bf16[64,512]{1,0:T(8,128)(2,1)}, bf16[64,512]{1,0:T(8,128)(2,1)S(1)}, u32[]{:S(2)}, u32[]{:S(2)}) collective-permute-start(bf16[64,512]{1,0:T(8,128)(2,1)} %get-tuple-element.46), channel_id=1, source_target_pairs={{0,2},{1,3},{2,4},{3,5},{4,6},{5,7},{6,0},{7,1},{8,10},{9,11},{10,... | collective-permute-start | bytes 196616 | tf_op jit(solution)/shard_map/ppermute | solution.py:228
  20.7 4.0 %collective-permute-start.2 = (bf16[64,512]{1,0:T(8,128)(2,1)}, bf16[64,512]{1,0:T(8,128)(2,1)}, u32[]{:S(2)}, u32[]{:S(2)}) collective-permute-start(bf16[64,512]{1,0:T(8,128)(2,1)} %get-tuple-element.47), channel_id=1, source_target_pairs={{0,3},{1,4},{2,5},{3,6},{4,7},{5,0},{6,1},{7,2},{8,11},{9,12},{10,... | collective-permute-start | bytes 196616 | tf_op jit(solution)/shard_map/ppermute | solution.py:228
  25.3 4.9 %collective-permute-start.4 = (bf16[64,512]{1,0:T(8,128)(2,1)}, bf16[64,512]{1,0:T(8,128)(2,1)}, u32[]{:S(2)}, u32[]{:S(2)}) collective-permute-start(bf16[64,512]{1,0:T(8,128)(2,1)} %get-tuple-element.49), channel_id=1, source_target_pairs={{0,5},{1,6},{2,7},{3,0},{4,1},{5,2},{6,3},{7,4},{8,13},{9,14},{10,... | collective-permute-start | bytes 196616 | tf_op jit(solution)/shard_map/ppermute | solution.py:228
  30.3 3.4 %copy-done = bf16[32,8,128,128]{3,2,1,0:T(8,128)(2,1)S(1)} copy-done((bf16[32,8,128,128]{3,2,1,0:T(8,128)(2,1)S(1)}, bf16[32,8,128,128]{3,2,1,0:T(8,128)(2,1)}, u32[]{:S(2)}) %copy-start) | copy-done | bytes 8388632
  33.7 3.6 %degree.1.degree_ref = f32[8,8,512]{2,1,0:T(8,128)S(1)} custom-call(s32[32]{0:T(128)S(1)} %copy-done.34, bf16[32,8,128,128]{3,2,1,0:T(8,128)(2,1)S(1)} %copy-done), custom_call_target="tpu_custom_call" | custom-call | flops 134217728 | bytes 8388608 | tf_op jit(solution)/shard_map/degree/pallas_call | solution.py:274
  37.3 3.4 %all-to-all-done = bf16[32,4,64,128]{3,2,1,0:T(8,128)(2,1)S(1)} async-done(((bf16[32,4,64,128]{3,2,1,0:T(8,128)(2,1)}), bf16[32,4,64,128]{3,2,1,0:T(8,128)(2,1)S(1)}, u32[]{:S(2)}, u32[]{:S(2)}) %all-to-all-start) | async-done | bytes 2097184 | tf_op jit(solution)/shard_map/all_to_all | solution.py:262
  40.8 3.4 %copy-done.1 = bf16[32,8,128,128]{3,2,1,0:T(8,128)(2,1)S(1)} copy-done((bf16[32,8,128,128]{3,2,1,0:T(8,128)(2,1)S(1)}, bf16[32,8,128,128]{3,2,1,0:T(8,128)(2,1)}, u32[]{:S(2)}) %copy-start.1) | copy-done | bytes 8388632
  44.2 6.1 %neighbour_mean.1 = (bf16[64,512]{1,0:T(8,128)(2,1)S(1)}, bf16[64,512]{1,0:T(8,128)(2,1)S(1)}, bf16[64,512]{1,0:T(8,128)(2,1)S(1)}, bf16[64,512]{1,0:T(8,128)(2,...) custom-call(s32[1]{0:T(128)} %bitcast.me_ref, ...), custom_call_target="tpu_custom_call" | custom-call | flops 536870912 | bytes 11534336 | tf_op jit(solution)/shard_map/neighbour_mean/pallas_call | solution.py:297
  50.3 6.4 %collective-permute-start.5 = (bf16[64,512]{1,0:T(8,128)(2,1)S(1)}, bf16[64,512]{1,0:T(8,128)(2,1)S(1)}, u32[]{:S(2)}, u32[]{:S(2)}) collective-permute-start(bf16[64,512]{1,0:T(8,128)(2,1)S(1)} %copy-done.38), channel_id=1, source_target_pairs={{0,6},{1,7},{2,0},{3,1},{4,2},{5,3},{6,4},{7,5},{8,14},{9,15},{10,... | collective-permute-start | bytes 196616 | tf_op jit(solution)/shard_map/ppermute | solution.py:228
  59.3 1.9 %collective-permute-start.9 = (bf16[64,512]{1,0:T(8,128)(2,1)}, bf16[64,512]{1,0:T(8,128)(2,1)S(1)}, u32[]{:S(2)}, u32[]{:S(2)}) collective-permute-start(bf16[64,512]{1,0:T(8,128)(2,1)} %get-tuple-element.57), channel_id=1, source_target_pairs={{0,3},{1,4},{2,5},{3,6},{4,7},{5,0},{6,1},{7,2},{8,11},{9,12},{10,... | collective-permute-start | bytes 196616 | tf_op jit(solution)/shard_map/ppermute | solution.py:228
  61.2 4.5 %collective-permute-start.10 = (bf16[64,512]{1,0:T(8,128)(2,1)}, bf16[64,512]{1,0:T(8,128)(2,1)S(1)}, u32[]{:S(2)}, u32[]{:S(2)}) collective-permute-start(bf16[64,512]{1,0:T(8,128)(2,1)} %get-tuple-element.58), channel_id=1, source_target_pairs={{0,4},{1,5},{2,6},{3,7},{4,0},{5,1},{6,2},{7,3},{8,12},{9,13},{10,... | collective-permute-start | bytes 196616 | tf_op jit(solution)/shard_map/ppermute | solution.py:228
  65.7 1.9 %collective-permute-start.11 = (bf16[64,512]{1,0:T(8,128)(2,1)}, bf16[64,512]{1,0:T(8,128)(2,1)S(1)}, u32[]{:S(2)}, u32[]{:S(2)}) collective-permute-start(bf16[64,512]{1,0:T(8,128)(2,1)} %get-tuple-element.59), channel_id=1, source_target_pairs={{0,5},{1,6},{2,7},{3,0},{4,1},{5,2},{6,3},{7,4},{8,13},{9,14},{10,... | collective-permute-start | bytes 196616 | tf_op jit(solution)/shard_map/ppermute | solution.py:228
  67.6 1.3 collective-permute-start.12
  68.9 1.9 %collective-permute-start.13 = (bf16[64,512]{1,0:T(8,128)(2,1)}, bf16[64,512]{1,0:T(8,128)(2,1)S(1)}, u32[]{:S(2)}, u32[]{:S(2)}) collective-permute-start(bf16[64,512]{1,0:T(8,128)(2,1)} %get-tuple-element.61), channel_id=1, source_target_pairs={{0,7},{1,0},{2,1},{3,2},{4,3},{5,4},{6,5},{7,6},{8,15},{9,8},{10,9... | collective-permute-start | bytes 196616 | tf_op jit(solution)/shard_map/ppermute | solution.py:228
  82.6 2.6 %collective-permute-start.15 = (bf16[64,512]{1,0:T(8,128)(2,1)S(1)}, bf16[64,512]{1,0:T(8,128)(2,1)S(1)}, u32[]{:S(2)}, u32[]{:S(2)}) collective-permute-start(bf16[64,512]{1,0:T(8,128)(2,1)S(1)} %get-tuple-element.68), channel_id=1, source_target_pairs={{0,2},{1,3},{2,4},{3,5},{4,6},{5,7},{6,0},{7,1},{8,10},{9,11},{10,... | collective-permute-start | bytes 196616 | tf_op jit(solution)/shard_map/ppermute | solution.py:228
  85.2 1.4 collective-permute-start.16
  86.5 3.7 %collective-permute-start.17 = (bf16[64,512]{1,0:T(8,128)(2,1)S(1)}, bf16[64,512]{1,0:T(8,128)(2,1)S(1)}, u32[]{:S(2)}, u32[]{:S(2)}) collective-permute-start(bf16[64,512]{1,0:T(8,128)(2,1)S(1)} %get-tuple-element.70), channel_id=1, source_target_pairs={{0,4},{1,5},{2,6},{3,7},{4,0},{5,1},{6,2},{7,3},{8,12},{9,13},{10,... | collective-permute-start | bytes 196616 | tf_op jit(solution)/shard_map/ppermute | solution.py:228
  90.2 2.1 %collective-permute-start.18 = (bf16[64,512]{1,0:T(8,128)(2,1)S(1)}, bf16[64,512]{1,0:T(8,128)(2,1)S(1)}, u32[]{:S(2)}, u32[]{:S(2)}) collective-permute-start(bf16[64,512]{1,0:T(8,128)(2,1)S(1)} %get-tuple-element.71), channel_id=1, source_target_pairs={{0,5},{1,6},{2,7},{3,0},{4,1},{5,2},{6,3},{7,4},{8,13},{9,14},{10,... | collective-permute-start | bytes 196616 | tf_op jit(solution)/shard_map/ppermute | solution.py:228
  92.3 3.1 %collective-permute-start.19 = (bf16[64,512]{1,0:T(8,128)(2,1)S(1)}, bf16[64,512]{1,0:T(8,128)(2,1)S(1)}, u32[]{:S(2)}, u32[]{:S(2)}) collective-permute-start(bf16[64,512]{1,0:T(8,128)(2,1)S(1)} %get-tuple-element.72), channel_id=1, source_target_pairs={{0,6},{1,7},{2,0},{3,1},{4,2},{5,3},{6,4},{7,5},{8,14},{9,15},{10,... | collective-permute-start | bytes 196616 | tf_op jit(solution)/shard_map/ppermute | solution.py:228
  96.4 2.8 %collective-permute-done.18.refs_5_ = bf16[64,512]{1,0:T(8,128)(2,1)S(1)} collective-permute-done((bf16[64,512]{1,0:T(8,128)(2,1)S(1)}, bf16[64,512]{1,0:T(8,128)(2,1)S(1)}, u32[]{:S(2)}, u32[]{:S(2)}) %collective-permute-start.18) | collective-permute-done | bytes 65568 | tf_op jit(solution)/shard_map/ppermute | solution.py:228
  99.2 2.7 %collective-permute-done.19.refs_6_ = bf16[64,512]{1,0:T(8,128)(2,1)S(1)} collective-permute-done((bf16[64,512]{1,0:T(8,128)(2,1)S(1)}, bf16[64,512]{1,0:T(8,128)(2,1)S(1)}, u32[]{:S(2)}, u32[]{:S(2)}) %collective-permute-start.19) | collective-permute-done | bytes 65568 | tf_op jit(solution)/shard_map/ppermute | solution.py:228
  102.4 3.4 %copy-done.2 = bf16[32,8,128,128]{3,2,1,0:T(8,128)(2,1)S(1)} copy-done((bf16[32,8,128,128]{3,2,1,0:T(8,128)(2,1)S(1)}, bf16[32,8,128,128]{3,2,1,0:T(8,128)(2,1)}, u32[]{:S(2)}) %copy-start.2) | copy-done | bytes 8388632
  105.8 4.6 %table_grad.1 = (f32[32,64,128]{2,1,0:T(8,128)S(1)}, bf16[128,64,128]{2,1,0:T(8,128)(2,1)S(1)}) custom-call(s32[1]{0:T(128)} %bitcast.me_ref, s32[32,8]{1,0:T(8,128)S(1)} %copy.25.cols_ref, s32[32]{0:T(128)S(1)} %copy-done.34, bf16[32,8,128,128]{3,2,1,0:T(8,128)(2,1)S(1)} %copy-done.2, bf16[64,512]{1,0:T(8,128)(2,1)S(1)} %get-tuple-element.66.refs_0_, ...), custom_call_target="tpu_custom_call" | custom-call | flops 536870912 | bytes 12582912 | tf_op jit(solution)/shard_map/table_grad/pallas_call | solution.py:343
  110.5 1.3 copy-done.5
  111.8 5.8 %all-to-all-start.1 = ((bf16[32,4,64,128]{3,2,1,0:T(8,128)(2,1)}), bf16[32,4,64,128]{3,2,1,0:T(8,128)(2,1)S(1)}, u32[]{:S(2)}, u32[]{:S(2)}) async-start(bf16[32,4,64,128]{3,2,1,0:T(8,128)(2,1)} %bitcast.14), calls=%async_computation.1 | async-start | bytes 4194304 | tf_op jit(solution)/shard_map/all_to_all | solution.py:362
  122.8 1.7 collective-permute-start.21
  124.5 1.3 collective-permute-start.22
  125.9 2.2 %collective-permute-start.23 = (bf16[64,1024]{1,0:T(8,128)(2,1)S(1)}, bf16[64,1024]{1,0:T(8,128)(2,1)S(1)}, u32[]{:S(2)}, u32[]{:S(2)}) collective-permute-start(bf16[64,1024]{1,0:T(8,128)(2,1)S(1)} %get-tuple-element.79), channel_id=1, source_target_pairs={{0,3},{1,4},{2,5},{3,6},{4,7},{5,0},{6,1},{7,2},{8,11},{9,12},{10,... | collective-permute-start | bytes 393224 | tf_op jit(solution)/shard_map/ppermute | solution.py:228
  128.0 3.0 %collective-permute-start.24 = (bf16[64,1024]{1,0:T(8,128)(2,1)S(1)}, bf16[64,1024]{1,0:T(8,128)(2,1)S(1)}, u32[]{:S(2)}, u32[]{:S(2)}) collective-permute-start(bf16[64,1024]{1,0:T(8,128)(2,1)S(1)} %get-tuple-element.80), channel_id=1, source_target_pairs={{0,4},{1,5},{2,6},{3,7},{4,0},{5,1},{6,2},{7,3},{8,12},{9,13},{10,... | collective-permute-start | bytes 393224 | tf_op jit(solution)/shard_map/ppermute | solution.py:228
  131.0 3.1 %collective-permute-start.25 = (bf16[64,1024]{1,0:T(8,128)(2,1)S(1)}, bf16[64,1024]{1,0:T(8,128)(2,1)S(1)}, u32[]{:S(2)}, u32[]{:S(2)}) collective-permute-start(bf16[64,1024]{1,0:T(8,128)(2,1)S(1)} %get-tuple-element.81), channel_id=1, source_target_pairs={{0,5},{1,6},{2,7},{3,0},{4,1},{5,2},{6,3},{7,4},{8,13},{9,14},{10,... | collective-permute-start | bytes 393224 | tf_op jit(solution)/shard_map/ppermute | solution.py:228
  134.2 2.2 %collective-permute-start.26 = (bf16[64,1024]{1,0:T(8,128)(2,1)S(1)}, bf16[64,1024]{1,0:T(8,128)(2,1)S(1)}, u32[]{:S(2)}, u32[]{:S(2)}) collective-permute-start(bf16[64,1024]{1,0:T(8,128)(2,1)S(1)} %get-tuple-element.82), channel_id=1, source_target_pairs={{0,6},{1,7},{2,0},{3,1},{4,2},{5,3},{6,4},{7,5},{8,14},{9,15},{10,... | collective-permute-start | bytes 393224 | tf_op jit(solution)/shard_map/ppermute | solution.py:228
  136.3 4.2 %collective-permute-done.22.refs_2_ = bf16[64,1024]{1,0:T(8,128)(2,1)S(1)} collective-permute-done((bf16[64,1024]{1,0:T(8,128)(2,1)S(1)}, bf16[64,1024]{1,0:T(8,128)(2,1)S(1)}, u32[]{:S(2)}, u32[]{:S(2)}) %collective-permute-start.22) | collective-permute-done | bytes 131104 | tf_op jit(solution)/shard_map/ppermute | solution.py:228
  140.5 3.0 %collective-permute-done.23.refs_3_ = bf16[64,1024]{1,0:T(8,128)(2,1)S(1)} collective-permute-done((bf16[64,1024]{1,0:T(8,128)(2,1)S(1)}, bf16[64,1024]{1,0:T(8,128)(2,1)S(1)}, u32[]{:S(2)}, u32[]{:S(2)}) %collective-permute-start.23) | collective-permute-done | bytes 131104 | tf_op jit(solution)/shard_map/ppermute | solution.py:228
  143.5 4.1 %collective-permute-done.24.refs_4_ = bf16[64,1024]{1,0:T(8,128)(2,1)S(1)} collective-permute-done((bf16[64,1024]{1,0:T(8,128)(2,1)S(1)}, bf16[64,1024]{1,0:T(8,128)(2,1)S(1)}, u32[]{:S(2)}, u32[]{:S(2)}) %collective-permute-start.24) | collective-permute-done | bytes 131104 | tf_op jit(solution)/shard_map/ppermute | solution.py:228
  148.3 4.8 %collective-permute-done.26.refs_6_ = bf16[64,1024]{1,0:T(8,128)(2,1)S(1)} collective-permute-done((bf16[64,1024]{1,0:T(8,128)(2,1)S(1)}, bf16[64,1024]{1,0:T(8,128)(2,1)S(1)}, u32[]{:S(2)}, u32[]{:S(2)}) %collective-permute-start.26) | collective-permute-done | bytes 131104 | tf_op jit(solution)/shard_map/ppermute | solution.py:228
  153.1 1.6 collective-permute-done.27.refs_7_
  154.9 1.2 collective-permute-done.28
  156.6 3.9 %collective-permute-done.29 = bf16[64,512]{1,0:T(8,128)(2,1)S(1)} collective-permute-done((bf16[64,512]{1,0:T(8,128)(2,1)S(1)}, bf16[64,512]{1,0:T(8,128)(2,1)S(1)}, u32[]{:S(2)}, u32[]{:S(2)}) %collective-permute-start.29) | collective-permute-done | bytes 65568 | tf_op jit(solution)/shard_map/ppermute | solution.py:378
  160.5 2.2 %collective-permute-start.30 = (bf16[64,512]{1,0:T(8,128)(2,1)S(1)}, bf16[64,512]{1,0:T(8,128)(2,1)S(1)}, u32[]{:S(2)}, u32[]{:S(2)}) collective-permute-start(bf16[64,512]{1,0:T(8,128)(2,1)S(1)} %add_convert_fusion.2), channel_id=1, source_target_pairs={{0,32},{8,40},{16,48},{24,56},{32,0},{40,8},{48,16},{56,24},{64,96... | collective-permute-start | bytes 196616 | tf_op jit(solution)/shard_map/ppermute | solution.py:378
  162.7 3.7 %collective-permute-done.30 = bf16[64,512]{1,0:T(8,128)(2,1)S(1)} collective-permute-done((bf16[64,512]{1,0:T(8,128)(2,1)S(1)}, bf16[64,512]{1,0:T(8,128)(2,1)S(1)}, u32[]{:S(2)}, u32[]{:S(2)}) %collective-permute-start.30) | collective-permute-done | bytes 65568 | tf_op jit(solution)/shard_map/ppermute | solution.py:378
  166.4 1.6 collective-permute-start.31
  168.0 2.8 %collective-permute-done.31 = bf16[64,512]{1,0:T(8,128)(2,1)S(1)} collective-permute-done((bf16[64,512]{1,0:T(8,128)(2,1)S(1)}, bf16[64,512]{1,0:T(8,128)(2,1)S(1)}, u32[]{:S(2)}, u32[]{:S(2)}) %collective-permute-start.31) | collective-permute-done | bytes 65568 | tf_op jit(solution)/shard_map/ppermute | solution.py:378
  170.8 3.1 %collective-permute-start.32 = (bf16[64,512]{1,0:T(8,128)(2,1)S(1)}, bf16[64,512]{1,0:T(8,128)(2,1)S(1)}, u32[]{:S(2)}, u32[]{:S(2)}) collective-permute-start(bf16[64,512]{1,0:T(8,128)(2,1)S(1)} %add_convert_fusion), channel_id=1, source_target_pairs={{0,128},{8,136},{16,144},{24,152},{32,160},{40,168},{48,176},{56,1... | collective-permute-start | bytes 196616 | tf_op jit(solution)/shard_map/ppermute | solution.py:378
  173.8 2.8 %collective-permute-done.32 = bf16[64,512]{1,0:T(8,128)(2,1)S(1)} collective-permute-done((bf16[64,512]{1,0:T(8,128)(2,1)S(1)}, bf16[64,512]{1,0:T(8,128)(2,1)S(1)}, u32[]{:S(2)}, u32[]{:S(2)}) %collective-permute-start.32) | collective-permute-done | bytes 65568 | tf_op jit(solution)/shard_map/ppermute | solution.py:378
  181.9 2.5 %sum_returned.1 = bf16[64,4096]{1,0:T(8,128)(2,1)} custom-call(s32[1]{0:T(128)} %bitcast.me_ref, s32[32,4]{1,0:T(8,128)S(1)} %copy.24.send_ref, f32[32,64,128]{2,1,0:T(8,128)S(1)} %get-tuple-element.74.own_ref, bf16[32,4,64,128]{3,2,1,0:T(8,128)(2,1)S(1)} %all-to-all-done.1.back_ref, bf16[64,1024]{1,0:T(8,128)(2,1)S(1)} %get-tuple-element.76.refs_0_, ...), custom_call_target="tpu_custom_call" | custom-call | bytes 6291456 | tf_op jit(solution)/shard_map/sum_returned/pallas_call | solution.py:387
  (126 shorter events, 32.6 us)
Async XLA Ops:
  5.1 25.1 %copy-start.39 = (s32[32,8]{0,1:T(8,128)S(1)}, s32[32,8]{0,1:T(8,128)}, u32[]{:S(2)}) copy-start(s32[32,8]{0,1:T(8,128)} %param.11) | copy-start | bytes 3076
  5.1 25.2 %copy-start.34 = (s32[32]{0:T(128)S(1)}, s32[32]{0:T(128)}, u32[]{:S(2)}) copy-start(s32[32]{0:T(128)} %counts_ref.5) | copy-start | bytes 388
  5.1 35.6 %all-to-all-start = ((bf16[32,4,64,128]{3,2,1,0:T(8,128)(2,1)}), bf16[32,4,64,128]{3,2,1,0:T(8,128)(2,1)S(1)}, u32[]{:S(2)}, u32[]{:S(2)}) async-start(bf16[32,4,64,128]{3,2,1,0:T(8,128)(2,1)} %pack_outgoing.1), calls=%async_computation | async-start | bytes 4194304 | tf_op jit(solution)/shard_map/all_to_all | solution.py:262
  15.5 34.7 %collective-permute-start = (bf16[64,512]{1,0:T(8,128)(2,1)}, bf16[64,512]{1,0:T(8,128)(2,1)S(1)}, u32[]{:S(2)}, u32[]{:S(2)}) collective-permute-start(bf16[64,512]{1,0:T(8,128)(2,1)} %get-tuple-element.45), channel_id=1, source_target_pairs={{0,1},{1,2},{2,3},{3,4},{4,5},{5,6},{6,7},{7,0},{8,9},{9,10},{10,1... | collective-permute-start | bytes 196616 | tf_op jit(solution)/shard_map/ppermute | solution.py:228
  17.4 39.2 %collective-permute-start.1 = (bf16[64,512]{1,0:T(8,128)(2,1)}, bf16[64,512]{1,0:T(8,128)(2,1)S(1)}, u32[]{:S(2)}, u32[]{:S(2)}) collective-permute-start(bf16[64,512]{1,0:T(8,128)(2,1)} %get-tuple-element.46), channel_id=1, source_target_pairs={{0,2},{1,3},{2,4},{3,5},{4,6},{5,7},{6,0},{7,1},{8,10},{9,11},{10,... | collective-permute-start | bytes 196616 | tf_op jit(solution)/shard_map/ppermute | solution.py:228
  20.7 37.0 %collective-permute-start.2 = (bf16[64,512]{1,0:T(8,128)(2,1)}, bf16[64,512]{1,0:T(8,128)(2,1)}, u32[]{:S(2)}, u32[]{:S(2)}) collective-permute-start(bf16[64,512]{1,0:T(8,128)(2,1)} %get-tuple-element.47), channel_id=1, source_target_pairs={{0,3},{1,4},{2,5},{3,6},{4,7},{5,0},{6,1},{7,2},{8,11},{9,12},{10,... | collective-permute-start | bytes 196616 | tf_op jit(solution)/shard_map/ppermute | solution.py:228
  24.8 34.0 %collective-permute-start.3 = (bf16[64,512]{1,0:T(8,128)(2,1)}, bf16[64,512]{1,0:T(8,128)(2,1)}, u32[]{:S(2)}, u32[]{:S(2)}) collective-permute-start(bf16[64,512]{1,0:T(8,128)(2,1)} %get-tuple-element.48), channel_id=1, source_target_pairs={{0,4},{1,5},{2,6},{3,7},{4,0},{5,1},{6,2},{7,3},{8,12},{9,13},{10,... | collective-permute-start | bytes 196616 | tf_op jit(solution)/shard_map/ppermute | solution.py:228
  25.3 34.0 %collective-permute-start.4 = (bf16[64,512]{1,0:T(8,128)(2,1)}, bf16[64,512]{1,0:T(8,128)(2,1)}, u32[]{:S(2)}, u32[]{:S(2)}) collective-permute-start(bf16[64,512]{1,0:T(8,128)(2,1)} %get-tuple-element.49), channel_id=1, source_target_pairs={{0,5},{1,6},{2,7},{3,0},{4,1},{5,2},{6,3},{7,4},{8,13},{9,14},{10,... | collective-permute-start | bytes 196616 | tf_op jit(solution)/shard_map/ppermute | solution.py:228
  44.2 26.7 %copy-start.7 = (bf16[512,256]{1,0:T(8,128)(2,1)S(1)}, bf16[512,256]{1,0:T(8,128)(2,1)}, u32[]{:S(2)}) copy-start(bf16[512,256]{1,0:T(8,128)(2,1)} %weight_ref.3) | copy-start | bytes 786436
  44.2 26.8 %copy-start.40 = (f32[256]{0:T(256)S(1)}, f32[256]{0:T(256)}, u32[]{:S(2)}) copy-start(f32[256]{0:T(256)} %param.16) | copy-start | bytes 3076
  44.2 27.0 %copy-start.6 = (bf16[512,256]{1,0:T(8,128)(2,1)S(1)}, bf16[512,256]{1,0:T(8,128)(2,1)}, u32[]{:S(2)}) copy-start(bf16[512,256]{1,0:T(8,128)(2,1)} %weight_ref.2) | copy-start | bytes 786436
  50.3 27.1 %copy-start.26 = (bf16[64,512]{1,0:T(8,128)(2,1)}, bf16[64,512]{1,0:T(8,128)(2,1)S(1)}, u32[]{:S(2)}) copy-start(bf16[64,512]{1,0:T(8,128)(2,1)S(1)} %get-tuple-element.54.refs_0_) | copy-start | bytes 196612
  50.3 20.7 %copy-start.30 = (bf16[64,512]{1,0:T(8,128)(2,1)}, bf16[64,512]{1,0:T(8,128)(2,1)S(1)}, u32[]{:S(2)}) copy-start(bf16[64,512]{1,0:T(8,128)(2,1)S(1)} %collective-permute-done.refs_1_) | copy-start | bytes 196612
  50.3 11.0 %collective-permute-start.5 = (bf16[64,512]{1,0:T(8,128)(2,1)S(1)}, bf16[64,512]{1,0:T(8,128)(2,1)S(1)}, u32[]{:S(2)}, u32[]{:S(2)}) collective-permute-start(bf16[64,512]{1,0:T(8,128)(2,1)S(1)} %copy-done.38), channel_id=1, source_target_pairs={{0,6},{1,7},{2,0},{3,1},{4,2},{5,3},{6,4},{7,5},{8,14},{9,15},{10,... | collective-permute-start | bytes 196616 | tf_op jit(solution)/shard_map/ppermute | solution.py:228
  56.7 14.3 %copy-start.32 = (bf16[64,512]{1,0:T(8,128)(2,1)}, bf16[64,512]{1,0:T(8,128)(2,1)S(1)}, u32[]{:S(2)}) copy-start(bf16[64,512]{1,0:T(8,128)(2,1)S(1)} %collective-permute-done.1.refs_2_) | copy-start | bytes 196612
  56.7 9.1 %collective-permute-start.6 = (bf16[64,512]{1,0:T(8,128)(2,1)S(1)}, bf16[64,512]{1,0:T(8,128)(2,1)S(1)}, u32[]{:S(2)}, u32[]{:S(2)}) collective-permute-start(bf16[64,512]{1,0:T(8,128)(2,1)S(1)} %copy-done.36), channel_id=1, source_target_pairs={{0,7},{1,0},{2,1},{3,2},{4,3},{5,4},{6,5},{7,6},{8,15},{9,8},{10,9... | collective-permute-start | bytes 196616 | tf_op jit(solution)/shard_map/ppermute | solution.py:228
  57.7 9.9 %collective-permute-start.7 = (bf16[64,512]{1,0:T(8,128)(2,1)S(1)}, bf16[64,512]{1,0:T(8,128)(2,1)S(1)}, u32[]{:S(2)}, u32[]{:S(2)}) collective-permute-start(bf16[64,512]{1,0:T(8,128)(2,1)S(1)} %get-tuple-element.55), channel_id=1, source_target_pairs={{0,1},{1,2},{2,3},{3,4},{4,5},{5,6},{6,7},{7,0},{8,9},{9,10},{10,1... | collective-permute-start | bytes 196616 | tf_op jit(solution)/shard_map/ppermute | solution.py:228
  58.8 10.1 %collective-permute-start.8 = (bf16[64,512]{1,0:T(8,128)(2,1)S(1)}, bf16[64,512]{1,0:T(8,128)(2,1)S(1)}, u32[]{:S(2)}, u32[]{:S(2)}) collective-permute-start(bf16[64,512]{1,0:T(8,128)(2,1)S(1)} %get-tuple-element.56), channel_id=1, source_target_pairs={{0,2},{1,3},{2,4},{3,5},{4,6},{5,7},{6,0},{7,1},{8,10},{9,11},{10,... | collective-permute-start | bytes 196616 | tf_op jit(solution)/shard_map/ppermute | solution.py:228
  59.3 17.7 %collective-permute-start.9 = (bf16[64,512]{1,0:T(8,128)(2,1)}, bf16[64,512]{1,0:T(8,128)(2,1)S(1)}, u32[]{:S(2)}, u32[]{:S(2)}) collective-permute-start(bf16[64,512]{1,0:T(8,128)(2,1)} %get-tuple-element.57), channel_id=1, source_target_pairs={{0,3},{1,4},{2,5},{3,6},{4,7},{5,0},{6,1},{7,2},{8,11},{9,12},{10,... | collective-permute-start | bytes 196616 | tf_op jit(solution)/shard_map/ppermute | solution.py:228
  61.2 15.7 %collective-permute-start.10 = (bf16[64,512]{1,0:T(8,128)(2,1)}, bf16[64,512]{1,0:T(8,128)(2,1)S(1)}, u32[]{:S(2)}, u32[]{:S(2)}) collective-permute-start(bf16[64,512]{1,0:T(8,128)(2,1)} %get-tuple-element.58), channel_id=1, source_target_pairs={{0,4},{1,5},{2,6},{3,7},{4,0},{5,1},{6,2},{7,3},{8,12},{9,13},{10,... | collective-permute-start | bytes 196616 | tf_op jit(solution)/shard_map/ppermute | solution.py:228
  65.7 11.2 %collective-permute-start.11 = (bf16[64,512]{1,0:T(8,128)(2,1)}, bf16[64,512]{1,0:T(8,128)(2,1)S(1)}, u32[]{:S(2)}, u32[]{:S(2)}) collective-permute-start(bf16[64,512]{1,0:T(8,128)(2,1)} %get-tuple-element.59), channel_id=1, source_target_pairs={{0,5},{1,6},{2,7},{3,0},{4,1},{5,2},{6,3},{7,4},{8,13},{9,14},{10,... | collective-permute-start | bytes 196616 | tf_op jit(solution)/shard_map/ppermute | solution.py:228
  67.6 9.6 %collective-permute-start.12 = (bf16[64,512]{1,0:T(8,128)(2,1)}, bf16[64,512]{1,0:T(8,128)(2,1)S(1)}, u32[]{:S(2)}, u32[]{:S(2)}) collective-permute-start(bf16[64,512]{1,0:T(8,128)(2,1)} %get-tuple-element.60), channel_id=1, source_target_pairs={{0,6},{1,7},{2,0},{3,1},{4,2},{5,3},{6,4},{7,5},{8,14},{9,15},{10,... | collective-permute-start | bytes 196616 | tf_op jit(solution)/shard_map/ppermute | solution.py:228
  68.9 8.5 %collective-permute-start.13 = (bf16[64,512]{1,0:T(8,128)(2,1)}, bf16[64,512]{1,0:T(8,128)(2,1)S(1)}, u32[]{:S(2)}, u32[]{:S(2)}) collective-permute-start(bf16[64,512]{1,0:T(8,128)(2,1)} %get-tuple-element.61), channel_id=1, source_target_pairs={{0,7},{1,0},{2,1},{3,2},{4,3},{5,4},{6,5},{7,6},{8,15},{9,8},{10,9... | collective-permute-start | bytes 196616 | tf_op jit(solution)/shard_map/ppermute | solution.py:228
  81.5 10.8 %collective-permute-start.14 = (bf16[64,512]{1,0:T(8,128)(2,1)S(1)}, bf16[64,512]{1,0:T(8,128)(2,1)S(1)}, u32[]{:S(2)}, u32[]{:S(2)}) collective-permute-start(bf16[64,512]{1,0:T(8,128)(2,1)S(1)} %get-tuple-element.67), channel_id=1, source_target_pairs={{0,1},{1,2},{2,3},{3,4},{4,5},{5,6},{6,7},{7,0},{8,9},{9,10},{10,1... | collective-permute-start | bytes 196616 | tf_op jit(solution)/shard_map/ppermute | solution.py:228
  82.6 12.8 %collective-permute-start.15 = (bf16[64,512]{1,0:T(8,128)(2,1)S(1)}, bf16[64,512]{1,0:T(8,128)(2,1)S(1)}, u32[]{:S(2)}, u32[]{:S(2)}) collective-permute-start(bf16[64,512]{1,0:T(8,128)(2,1)S(1)} %get-tuple-element.68), channel_id=1, source_target_pairs={{0,2},{1,3},{2,4},{3,5},{4,6},{5,7},{6,0},{7,1},{8,10},{9,11},{10,... | collective-permute-start | bytes 196616 | tf_op jit(solution)/shard_map/ppermute | solution.py:228
  85.2 11.2 %collective-permute-start.16 = (bf16[64,512]{1,0:T(8,128)(2,1)S(1)}, bf16[64,512]{1,0:T(8,128)(2,1)S(1)}, u32[]{:S(2)}, u32[]{:S(2)}) collective-permute-start(bf16[64,512]{1,0:T(8,128)(2,1)S(1)} %get-tuple-element.69), channel_id=1, source_target_pairs={{0,3},{1,4},{2,5},{3,6},{4,7},{5,0},{6,1},{7,2},{8,11},{9,12},{10,... | collective-permute-start | bytes 196616 | tf_op jit(solution)/shard_map/ppermute | solution.py:228
  86.5 9.8 %collective-permute-start.17 = (bf16[64,512]{1,0:T(8,128)(2,1)S(1)}, bf16[64,512]{1,0:T(8,128)(2,1)S(1)}, u32[]{:S(2)}, u32[]{:S(2)}) collective-permute-start(bf16[64,512]{1,0:T(8,128)(2,1)S(1)} %get-tuple-element.70), channel_id=1, source_target_pairs={{0,4},{1,5},{2,6},{3,7},{4,0},{5,1},{6,2},{7,3},{8,12},{9,13},{10,... | collective-permute-start | bytes 196616 | tf_op jit(solution)/shard_map/ppermute | solution.py:228
  90.2 9.0 %collective-permute-start.18 = (bf16[64,512]{1,0:T(8,128)(2,1)S(1)}, bf16[64,512]{1,0:T(8,128)(2,1)S(1)}, u32[]{:S(2)}, u32[]{:S(2)}) collective-permute-start(bf16[64,512]{1,0:T(8,128)(2,1)S(1)} %get-tuple-element.71), channel_id=1, source_target_pairs={{0,5},{1,6},{2,7},{3,0},{4,1},{5,2},{6,3},{7,4},{8,13},{9,14},{10,... | collective-permute-start | bytes 196616 | tf_op jit(solution)/shard_map/ppermute | solution.py:228
  92.3 9.6 %collective-permute-start.19 = (bf16[64,512]{1,0:T(8,128)(2,1)S(1)}, bf16[64,512]{1,0:T(8,128)(2,1)S(1)}, u32[]{:S(2)}, u32[]{:S(2)}) collective-permute-start(bf16[64,512]{1,0:T(8,128)(2,1)S(1)} %get-tuple-element.72), channel_id=1, source_target_pairs={{0,6},{1,7},{2,0},{3,1},{4,2},{5,3},{6,4},{7,5},{8,14},{9,15},{10,... | collective-permute-start | bytes 196616 | tf_op jit(solution)/shard_map/ppermute | solution.py:228
  95.4 7.1 %collective-permute-start.20 = (bf16[64,512]{1,0:T(8,128)(2,1)S(1)}, bf16[64,512]{1,0:T(8,128)(2,1)S(1)}, u32[]{:S(2)}, u32[]{:S(2)}) collective-permute-start(bf16[64,512]{1,0:T(8,128)(2,1)S(1)} %get-tuple-element.73), channel_id=1, source_target_pairs={{0,7},{1,0},{2,1},{3,2},{4,3},{5,4},{6,5},{7,6},{8,15},{9,8},{10,9... | collective-permute-start | bytes 196616 | tf_op jit(solution)/shard_map/ppermute | solution.py:228
  111.8 65.6 %all-to-all-start.1 = ((bf16[32,4,64,128]{3,2,1,0:T(8,128)(2,1)}), bf16[32,4,64,128]{3,2,1,0:T(8,128)(2,1)S(1)}, u32[]{:S(2)}, u32[]{:S(2)}) async-start(bf16[32,4,64,128]{3,2,1,0:T(8,128)(2,1)} %bitcast.14), calls=%async_computation.1 | async-start | bytes 4194304 | tf_op jit(solution)/shard_map/all_to_all | solution.py:362
  122.8 11.3 %collective-permute-start.21 = (bf16[64,1024]{1,0:T(8,128)(2,1)S(1)}, bf16[64,1024]{1,0:T(8,128)(2,1)S(1)}, u32[]{:S(2)}, u32[]{:S(2)}) collective-permute-start(bf16[64,1024]{1,0:T(8,128)(2,1)S(1)} %get-tuple-element.77), channel_id=1, source_target_pairs={{0,1},{1,2},{2,3},{3,4},{4,5},{5,6},{6,7},{7,0},{8,9},{9,10},{10,1... | collective-permute-start | bytes 393224 | tf_op jit(solution)/shard_map/ppermute | solution.py:228
  124.5 16.0 %collective-permute-start.22 = (bf16[64,1024]{1,0:T(8,128)(2,1)S(1)}, bf16[64,1024]{1,0:T(8,128)(2,1)S(1)}, u32[]{:S(2)}, u32[]{:S(2)}) collective-permute-start(bf16[64,1024]{1,0:T(8,128)(2,1)S(1)} %get-tuple-element.78), channel_id=1, source_target_pairs={{0,2},{1,3},{2,4},{3,5},{4,6},{5,7},{6,0},{7,1},{8,10},{9,11},{10,... | collective-permute-start | bytes 393224 | tf_op jit(solution)/shard_map/ppermute | solution.py:228
  125.9 17.7 %collective-permute-start.23 = (bf16[64,1024]{1,0:T(8,128)(2,1)S(1)}, bf16[64,1024]{1,0:T(8,128)(2,1)S(1)}, u32[]{:S(2)}, u32[]{:S(2)}) collective-permute-start(bf16[64,1024]{1,0:T(8,128)(2,1)S(1)} %get-tuple-element.79), channel_id=1, source_target_pairs={{0,3},{1,4},{2,5},{3,6},{4,7},{5,0},{6,1},{7,2},{8,11},{9,12},{10,... | collective-permute-start | bytes 393224 | tf_op jit(solution)/shard_map/ppermute | solution.py:228
  128.0 19.6 %collective-permute-start.24 = (bf16[64,1024]{1,0:T(8,128)(2,1)S(1)}, bf16[64,1024]{1,0:T(8,128)(2,1)S(1)}, u32[]{:S(2)}, u32[]{:S(2)}) collective-permute-start(bf16[64,1024]{1,0:T(8,128)(2,1)S(1)} %get-tuple-element.80), channel_id=1, source_target_pairs={{0,4},{1,5},{2,6},{3,7},{4,0},{5,1},{6,2},{7,3},{8,12},{9,13},{10,... | collective-permute-start | bytes 393224 | tf_op jit(solution)/shard_map/ppermute | solution.py:228
  131.0 17.2 %collective-permute-start.25 = (bf16[64,1024]{1,0:T(8,128)(2,1)S(1)}, bf16[64,1024]{1,0:T(8,128)(2,1)S(1)}, u32[]{:S(2)}, u32[]{:S(2)}) collective-permute-start(bf16[64,1024]{1,0:T(8,128)(2,1)S(1)} %get-tuple-element.81), channel_id=1, source_target_pairs={{0,5},{1,6},{2,7},{3,0},{4,1},{5,2},{6,3},{7,4},{8,13},{9,14},{10,... | collective-permute-start | bytes 393224 | tf_op jit(solution)/shard_map/ppermute | solution.py:228
  134.2 18.9 %collective-permute-start.26 = (bf16[64,1024]{1,0:T(8,128)(2,1)S(1)}, bf16[64,1024]{1,0:T(8,128)(2,1)S(1)}, u32[]{:S(2)}, u32[]{:S(2)}) collective-permute-start(bf16[64,1024]{1,0:T(8,128)(2,1)S(1)} %get-tuple-element.82), channel_id=1, source_target_pairs={{0,6},{1,7},{2,0},{3,1},{4,2},{5,3},{6,4},{7,5},{8,14},{9,15},{10,... | collective-permute-start | bytes 393224 | tf_op jit(solution)/shard_map/ppermute | solution.py:228
  140.5 14.2 %collective-permute-start.27 = (bf16[64,1024]{1,0:T(8,128)(2,1)S(1)}, bf16[64,1024]{1,0:T(8,128)(2,1)S(1)}, u32[]{:S(2)}, u32[]{:S(2)}) collective-permute-start(bf16[64,1024]{1,0:T(8,128)(2,1)S(1)} %get-tuple-element.83), channel_id=1, source_target_pairs={{0,7},{1,0},{2,1},{3,2},{4,3},{5,4},{6,5},{7,6},{8,15},{9,8},{10,9... | collective-permute-start | bytes 393224 | tf_op jit(solution)/shard_map/ppermute | solution.py:228
  143.5 33.1 %copy-start.8 = (bf16[64,1024]{1,0:T(8,128)(2,1)}, bf16[64,1024]{1,0:T(8,128)(2,1)S(1)}, u32[]{:S(2)}) copy-start(bf16[64,1024]{1,0:T(8,128)(2,1)S(1)} %collective-permute-done.23.refs_3_) | copy-start | bytes 393220
  147.7 29.0 %copy-start.10 = (bf16[64,1024]{1,0:T(8,128)(2,1)}, bf16[64,1024]{1,0:T(8,128)(2,1)S(1)}, u32[]{:S(2)}) copy-start(bf16[64,1024]{1,0:T(8,128)(2,1)S(1)} %collective-permute-done.24.refs_4_) | copy-start | bytes 393220
  148.2 28.4 %copy-start.12 = (bf16[64,1024]{1,0:T(8,128)(2,1)}, bf16[64,1024]{1,0:T(8,128)(2,1)S(1)}, u32[]{:S(2)}) copy-start(bf16[64,1024]{1,0:T(8,128)(2,1)S(1)} %collective-permute-done.25.refs_5_) | copy-start | bytes 393220
  153.1 23.6 %copy-start.14 = (bf16[64,1024]{1,0:T(8,128)(2,1)}, bf16[64,1024]{1,0:T(8,128)(2,1)S(1)}, u32[]{:S(2)}) copy-start(bf16[64,1024]{1,0:T(8,128)(2,1)S(1)} %collective-permute-done.26.refs_6_) | copy-start | bytes 393220
  154.7 22.0 %copy-start.16 = (bf16[64,1024]{1,0:T(8,128)(2,1)}, bf16[64,1024]{1,0:T(8,128)(2,1)S(1)}, u32[]{:S(2)}) copy-start(bf16[64,1024]{1,0:T(8,128)(2,1)S(1)} %collective-permute-done.27.refs_7_) | copy-start | bytes 393220
  154.8 1.3 collective-permute-start.28
  156.1 4.4 %collective-permute-start.29 = (bf16[64,512]{1,0:T(8,128)(2,1)S(1)}, bf16[64,512]{1,0:T(8,128)(2,1)S(1)}, u32[]{:S(2)}, u32[]{:S(2)}) collective-permute-start(bf16[64,512]{1,0:T(8,128)(2,1)S(1)} %add_convert_fusion.3), channel_id=1, source_target_pairs={{0,16},{8,24},{16,0},{24,8},{32,48},{40,56},{48,32},{56,40},{64,80... | collective-permute-start | bytes 196616 | tf_op jit(solution)/shard_map/ppermute | solution.py:378
  160.5 5.9 %collective-permute-start.30 = (bf16[64,512]{1,0:T(8,128)(2,1)S(1)}, bf16[64,512]{1,0:T(8,128)(2,1)S(1)}, u32[]{:S(2)}, u32[]{:S(2)}) collective-permute-start(bf16[64,512]{1,0:T(8,128)(2,1)S(1)} %add_convert_fusion.2), channel_id=1, source_target_pairs={{0,32},{8,40},{16,48},{24,56},{32,0},{40,8},{48,16},{56,24},{64,96... | collective-permute-start | bytes 196616 | tf_op jit(solution)/shard_map/ppermute | solution.py:378
  166.4 4.4 %collective-permute-start.31 = (bf16[64,512]{1,0:T(8,128)(2,1)S(1)}, bf16[64,512]{1,0:T(8,128)(2,1)S(1)}, u32[]{:S(2)}, u32[]{:S(2)}) collective-permute-start(bf16[64,512]{1,0:T(8,128)(2,1)S(1)} %add_convert_fusion.1), channel_id=1, source_target_pairs={{0,64},{8,72},{16,80},{24,88},{32,96},{40,104},{48,112},{56,120},{... | collective-permute-start | bytes 196616 | tf_op jit(solution)/shard_map/ppermute | solution.py:378
  170.8 5.9 %collective-permute-start.32 = (bf16[64,512]{1,0:T(8,128)(2,1)S(1)}, bf16[64,512]{1,0:T(8,128)(2,1)S(1)}, u32[]{:S(2)}, u32[]{:S(2)}) collective-permute-start(bf16[64,512]{1,0:T(8,128)(2,1)S(1)} %add_convert_fusion), channel_id=1, source_target_pairs={{0,128},{8,136},{16,144},{24,152},{32,160},{40,168},{48,176},{56,1... | collective-permute-start | bytes 196616 | tf_op jit(solution)/shard_map/ppermute | solution.py:378
  (28 other events, 55.6 us)

commit v2 on v0

v2 whole, which is shorter than its diff:
```python
import functools

import jax
import jax.numpy as jnp
from jax import lax
from jax.experimental import pallas as pl
from jax.experimental.pallas import tpu as pltpu
from jax.sharding import PartitionSpec as P

BF = jnp.bfloat16
F32 = jnp.float32
MIB = 1 << 20
BIG = 8


def vmem():
    return pl.BlockSpec(memory_space=pltpu.VMEM)


def hbm():
    return pl.BlockSpec(memory_space=pltpu.HBM)


def smem():
    return pl.BlockSpec(memory_space=pltpu.SMEM)


def params(mib):
    return pltpu.CompilerParams(vmem_limit_bytes=mib * MIB)


def cost(flops, nbytes):
    return pl.CostEstimate(flops=flops, bytes_accessed=nbytes, transcendentals=0)


def nt_dot(left, right):
    return lax.dot_general(left, right, (((1,), (1,)), ((), ())), preferred_element_type=F32)


def nn_dot(left, right):
    return lax.dot_general(left, right, (((1,), (0,)), ((), ())), preferred_element_type=F32)


def pack_kernel(send_ref, feats_ref, out_ref, hold_ref, sems):
    dests, slots, _, size = hold_ref.shape
    copies = sems.shape[0]
    span = dests // copies
    for copy in range(copies):
        for dest in range(copy * span, (copy + 1) * span):
            for slot in range(slots):
                lane = pl.multiple_of(send_ref[slot, dest] * size, size)
                hold_ref[dest, slot] = feats_ref[:, pl.ds(lane, size)]
        place = pl.ds(copy * span, span)
        pltpu.make_async_copy(hold_ref.at[place], out_ref.at[place], sems.at[copy]).start()
    for copy in range(copies):
        place = pl.ds(copy * span, span)
        pltpu.make_async_copy(hold_ref.at[place], out_ref.at[place], sems.at[copy]).wait()


def split_kernel(me_ref, feats_ref, *out_refs):
    chans = len(out_refs)
    width = out_refs[0].shape[1]
    for shift, out_ref in enumerate(out_refs):
        lane = pl.multiple_of(lax.rem(me_ref[0] + shift, chans) * width, width)
        out_ref[...] = feats_ref[:, pl.ds(lane, width)]


def join_slots(vals_ref, row):
    return jnp.concatenate([vals_ref[row, k] for k in range(vals_ref.shape[1])], axis=1)


def stream_rows(vals_ref, held_ref, sems, body):
    copies = sems.shape[0]
    span = held_ref.shape[0] // copies

    def copy(place):
        rows = pl.ds(place * span, span)
        return pltpu.make_async_copy(vals_ref.at[rows], held_ref.at[rows], sems.at[place])

    for place in range(copies):
        copy(place).start()

    def one(place, carry):
        copy(place).wait()
        for row in range(span):
            body(place * span + row)
        return carry

    lax.fori_loop(0, copies, one, 0)


def gather_kernel(cols_ref, counts_ref, feats_ref, recv_ref, vals_ref, out_ref, degree_ref, held_ref, sems):
    _, depth, size, _ = vals_ref.shape
    width = feats_ref.shape[0]
    rows = out_ref.shape[2] // size
    own = feats_ref.shape[1] // size
    ones = jnp.ones((16, size), BF)

    def body(index):
        count = counts_ref[index]
        picked = []
        for k in range(depth):
            col = cols_ref[k, index]
            lane = pl.multiple_of(jnp.minimum(col, own - 1) * size, size)
            near = feats_ref[:, pl.ds(lane, size)]
            far = recv_ref[jnp.maximum(col - own, 0)]
            block = jnp.concatenate([jnp.where(col < own, near, far), ones], axis=0)
            picked.append(jnp.where(k < count, block, jnp.zeros_like(block)))
        total = nt_dot(join_slots(held_ref, index), jnp.concatenate(picked, axis=1)).T
        group = index // rows
        place = pl.ds(pl.multiple_of(lax.rem(index, rows) * size, size), size)
        degree_ref[group, :, place] = total[width : width + 8]
        out_ref[group, :, place] = (total[:width] / total[width : width + 1]).astype(BF)

    stream_rows(vals_ref, held_ref, sems, body)


def self_kernel(chans, me_ref, weight_ref, bias_ref, neigh_ref, cot_ref, *refs):
    chunk_refs = refs[:chans]
    full_ref, pre_ref, neigh_turned_ref, cot_turned_ref = refs[chans:]
    neigh_turned_ref[...] = neigh_ref[...].T
    cot_turned_ref[...] = cot_ref[...].T
    height = chunk_refs[0].shape[0]
    for shift, chunk_ref in enumerate(chunk_refs):
        start = pl.multiple_of(lax.rem(me_ref[0] + (chans - shift), chans) * height, height)
        full_ref[pl.ds(start, height), :] = chunk_ref[...]
    pre_ref[...] = nn_dot(weight_ref[...].T, full_ref[...]) + bias_ref[...]


def head_kernel(me_ref, degree_ref, pre_ref, turned_ref, weight_ref, cot_ref, mean_ref, out_ref, grad_ref, scaled_ref):
    preact = pre_ref[...] + nn_dot(turned_ref[...], mean_ref[...])
    logistic = jax.nn.sigmoid(preact)
    activated = preact * logistic
    slope = logistic * (1.0 + preact * (1.0 - logistic))
    inverse = 1.0 / jnp.sqrt(jnp.mean(activated * activated, axis=0, keepdims=True) + 1e-06)
    unit = activated * inverse
    cot = cot_ref[...].astype(F32)
    grad_act = (cot - unit * jnp.mean(cot * unit, axis=0, keepdims=True)) * inverse
    grad = (grad_act * slope).astype(BF)
    out_ref[...] = unit.astype(BF)
    grad_ref[...] = grad
    mean_grad = nn_dot(weight_ref[...], grad).astype(BF).astype(F32)
    degree = degree_ref[me_ref[0], 0:1, :]
    scaled_ref[...] = (mean_grad / degree).astype(BF)


def weight_partial_kernel(me_ref, feats_ref, mean_ref, grad_ref, keep_ref, give_ref, hold_ref):
    parts, chans, unit, lanes = hold_ref.shape
    grad = grad_ref[...]
    totals = [nt_dot(feats_ref[...], grad), nt_dot(mean_ref[...], grad)]
    width = totals[0].shape[0] // chans
    halves = totals[0].shape[1] // lanes
    count = width // unit
    for which, total in enumerate(totals):
        for half in range(halves):
            place = (which * halves + half) * count
            for chan in range(chans):
                piece = total[chan * width : (chan + 1) * width, half * lanes : (half + 1) * lanes]
                hold_ref[place : place + count, chan] = piece.reshape(count, unit, lanes)
    half = parts // 2
    bit = me_ref[0]
    keep_ref[...] = hold_ref[pl.ds(bit * half, half)]
    give_ref[...] = hold_ref[pl.ds((1 - bit) * half, half)].astype(BF)


def halve_kernel(me_ref, held_ref, recv_ref, keep_ref, give_ref, hold_ref):
    half = keep_ref.shape[0]
    bit = me_ref[0]
    hold_ref[...] = held_ref[...] + recv_ref[...].astype(F32)
    keep_ref[...] = hold_ref[pl.ds(bit * half, half)]
    give_ref[...] = hold_ref[pl.ds((1 - bit) * half, half)].astype(BF)


def add_round_kernel(held_ref, recv_ref, out_ref):
    out_ref[...] = (held_ref[...] + recv_ref[...].astype(F32)).astype(BF)


def add_pair_kernel(held_ref, recv_ref, out_ref):
    out_ref[...] = (held_ref[...].astype(F32) + recv_ref[...].astype(F32)).astype(BF)


def turn_kernel(out_ref, turned_ref):
    turned_ref[...] = out_ref[...].T


def message_kernel(chans, me_ref, unit_ref, *packed_refs):
    units, _, unit, lanes = unit_ref.shape
    for shift, packed_ref in enumerate(packed_refs):
        dest = lax.rem(me_ref[0] + shift, chans)
        piece = unit_ref[:, dest].astype(F32).reshape(units * unit, lanes)
        packed_ref[...] = piece.astype(BF)


def scatter_kernel(
    cols_ref, counts_ref, vals_ref, scaled_ref, own_ref, far_ref, held_ref, hold_ref, send_ref, val_sems, sems, own_sem
):
    _, depth, size, _ = vals_ref.shape
    rows = scaled_ref.shape[2] // size
    own = own_ref.shape[0]
    hold_ref[...] = jnp.zeros_like(hold_ref)

    def body(index):
        count = counts_ref[index]
        place = pl.ds(pl.multiple_of(lax.rem(index, rows) * size, size), size)
        total = nn_dot(scaled_ref[index // rows, :, place], join_slots(held_ref, index))
        for k in range(depth):
            part = total[:, k * size : (k + 1) * size]
            hold_ref[cols_ref[k, index]] += jnp.where(k < count, part, jnp.zeros_like(part))

    stream_rows(vals_ref, held_ref, val_sems, body)
    copies = sems.shape[0]
    span = far_ref.shape[0] // copies
    for copy in range(copies):
        send_ref[copy * span : (copy + 1) * span] = hold_ref[own + copy * span : own + (copy + 1) * span].astype(BF)
        place = pl.ds(copy * span, span)
        pltpu.make_async_copy(send_ref.at[place], far_ref.at[place], sems.at[copy]).start()
    pltpu.make_async_copy(hold_ref.at[pl.ds(0, own)], own_ref, own_sem).start()
    for copy in range(copies):
        place = pl.ds(copy * span, span)
        pltpu.make_async_copy(send_ref.at[place], far_ref.at[place], sems.at[copy]).wait()
    pltpu.make_async_copy(hold_ref.at[pl.ds(0, own)], own_ref, own_sem).wait()


def unit_kernel(*refs):
    packed_refs = refs[:-1]
    out_ref = refs[-1]
    total = packed_refs[0][...].astype(F32)
    for packed_ref in packed_refs[1:]:
        total = total + packed_ref[...].astype(F32)
    out_ref[...] = total.astype(BF)


def spread_kernel(scale, me_ref, held_ref, self_ref, neigh_ref):
    pieces, rows, lanes = held_ref.shape
    half = pieces // 2
    unit_rows = self_ref.shape[0]
    per = unit_rows // rows
    for place in range(pieces):
        value = held_ref[lax.bitwise_xor(me_ref[0], place)].astype(F32) * scale
        target = self_ref if place < half else neigh_ref
        inside = place % half
        column, row = inside // per, inside % per
        target[row * rows : (row + 1) * rows, column * lanes : (column + 1) * lanes] = value


def near_kernel(me_ref, weight_ref, grad_ref, own_ref, out_ref):
    blocks, width, size = out_ref.shape
    chans, _, nodes = grad_ref.shape
    rows = nodes // size
    weight = weight_ref[pl.ds(pl.multiple_of(me_ref[0] * width, width), width), :]
    for group in range(chans):
        total = nn_dot(weight, grad_ref[group]).astype(BF).astype(F32)
        for row in range(rows):
            index = group * rows + row
            out_ref[index] = own_ref[index] + total[:, row * size : (row + 1) * size]


def final_kernel(send_ref, near_ref, back_ref, out_ref, hold_ref):
    slots, dests = send_ref.shape
    blocks, _, size = hold_ref.shape
    hold_ref[...] = near_ref[...]

    def one(dest, carry):
        for slot in range(slots):
            hold_ref[send_ref[slot, dest]] += back_ref[dest, slot].astype(F32)
        return carry

    lax.fori_loop(0, dests, one, 0, unroll=8)
    for block in range(blocks):
        out_ref[:, block * size : (block + 1) * size] = hold_ref[block].astype(BF)


def exchange(chunks):
    count = len(chunks)
    return [chunks[0]] + [
        lax.ppermute(chunks[shift], "chan", [(i, (i + shift) % count) for i in range(count)])
        for shift in range(1, count)
    ]


def sds(shape, dtype):
    return jax.ShapeDtypeStruct(shape, dtype)


def halving_order(parts):
    count = parts.bit_length() - 1
    return [bit for bit in (0, 1, 3, 2, 4) if bit < count] + list(range(5, count))


def add_round(kernel, left, right):
    return pl.pallas_call(
        kernel,
        out_shape=sds(left.shape, BF),
        in_specs=[vmem()] * 2,
        out_specs=vmem(),
        compiler_params=params(BIG),
        cost_estimate=cost(0, MIB),
        name="weight_add",
    )(left, right)


def per_device(feats, block_vals, block_cols, block_counts, send_list, w_self, w_neigh, bias, cotangent):
    node_count, chan_width = feats.shape
    block_rows, depth, size, _ = block_vals.shape
    parts = lax.axis_size("dom")
    chans = lax.axis_size("chan")
    slots = send_list.shape[2]
    f_in, f_out = w_self.shape
    nodes = node_count // chans
    rows = block_rows // chans
    table = block_rows + parts * slots
    chan = lax.axis_index("chan").astype(jnp.int32)
    part = lax.axis_index("dom").astype(jnp.int32)
    me = chan.reshape(1)
    send = send_list[0].T
    cols = block_cols.T
    feats_t = feats.T
    val_bytes = block_vals.size * 2
    vals = pltpu.with_memory_space_constraint(block_vals, pltpu.HBM)
    block_flops = 2 * block_rows * depth * size * size * chan_width
    layer_flops = 2 * f_in * f_out * nodes
    unit, lanes = 8, 128
    copies, streams = 8, 4

    outgoing = pl.pallas_call(
        pack_kernel,
        out_shape=pltpu.HBM((parts, slots, chan_width, size), BF),
        in_specs=[smem(), vmem()],
        out_specs=hbm(),
        scratch_shapes=[pltpu.VMEM((parts, slots, chan_width, size), BF), pltpu.SemaphoreType.DMA((copies,))],
        compiler_params=params(8),
        cost_estimate=cost(0, 5 * MIB),
        name="pack_outgoing",
    )(send, feats_t)
    incoming = lax.all_to_all(outgoing, "dom", split_axis=0, concat_axis=0, tiled=True)

    feat_chunks = pl.pallas_call(
        split_kernel,
        out_shape=[sds((chan_width, nodes), BF)] * chans,
        in_specs=[smem(), vmem()],
        out_specs=[vmem()] * chans,
        compiler_params=params(BIG),
        cost_estimate=cost(0, MIB),
        name="split_feats",
    )(me, feats_t)
    feat_chunks = exchange(feat_chunks)
    feats_own, pre_self, neigh_turned, cot_turned = pl.pallas_call(
        functools.partial(self_kernel, chans),
        out_shape=[sds((f_in, nodes), BF), sds((f_out, nodes), F32), sds((f_out, f_in), BF), sds((f_out, nodes), BF)],
        in_specs=[smem()] + [vmem()] * (4 + chans),
        out_specs=[vmem()] * 4,
        compiler_params=params(BIG),
        cost_estimate=cost(layer_flops, 2 * MIB),
        name="self_part",
    )(me, w_self, bias.reshape(f_out, 1), w_neigh, cotangent, *feat_chunks)

    incoming, pre_self, feats_own, neigh_turned, cot_turned = lax.optimization_barrier(
        (incoming, pre_self, feats_own, neigh_turned, cot_turned)
    )
    mean, degree = pl.pallas_call(
        gather_kernel,
        out_shape=[sds((chans, chan_width, nodes), BF), sds((chans, 8, nodes), F32)],
        in_specs=[smem(), smem()] + [vmem()] * 2 + [hbm()],
        out_specs=[vmem()] * 2,
        scratch_shapes=[pltpu.VMEM(block_vals.shape, BF), pltpu.SemaphoreType.DMA((streams,))],
        compiler_params=params(16),
        cost_estimate=cost(block_flops, val_bytes + 3 * MIB),
        name="neighbour_mean",
    )(cols, block_counts, feats_t, incoming.reshape(parts * slots, chan_width, size), vals)
    mean = lax.all_to_all(mean, "chan", split_axis=0, concat_axis=0, tiled=True).reshape(f_in, nodes)

    out_t, grad_t, scaled = pl.pallas_call(
        head_kernel,
        out_shape=[sds((f_out, nodes), BF), sds((f_out, nodes), BF), sds((f_in, nodes), BF)],
        in_specs=[smem()] + [vmem()] * 6,
        out_specs=[vmem()] * 3,
        compiler_params=params(BIG),
        cost_estimate=cost(2 * layer_flops, 4 * MIB),
        name="layer_head",
    )(me, degree, pre_self, neigh_turned, w_neigh, cot_turned, mean)
    scaled = lax.all_to_all(
        scaled.reshape(chans, chan_width, nodes), "chan", split_axis=0, concat_axis=0, tiled=True
    )

    order = halving_order(parts)
    halves, wholes = order[:3], order[3:]
    flips = [[(i, i ^ (1 << bit)) for i in range(parts)] for bit in order]
    bits = [((part >> bit) & 1).reshape(1) for bit in order]
    pieces = parts
    keep, give = pl.pallas_call(
        weight_partial_kernel,
        out_shape=[sds((pieces // 2, chans, unit, lanes), F32), sds((pieces // 2, chans, unit, lanes), BF)],
        in_specs=[smem()] + [vmem()] * 3,
        out_specs=[vmem()] * 2,
        scratch_shapes=[pltpu.VMEM((pieces, chans, unit, lanes), F32)],
        compiler_params=params(BIG),
        cost_estimate=cost(2 * layer_flops, 3 * MIB),
        name="weight_partial",
    )(bits[0], feats_own, mean, grad_t)
    pieces //= 2
    for level in range(1, len(halves)):
        got = lax.ppermute(give, "dom", flips[level - 1])
        keep, give = pl.pallas_call(
            halve_kernel,
            out_shape=[sds((pieces // 2, chans, unit, lanes), F32), sds((pieces // 2, chans, unit, lanes), BF)],
            in_specs=[smem()] + [vmem()] * 2,
            out_specs=[vmem()] * 2,
            scratch_shapes=[pltpu.VMEM((pieces, chans, unit, lanes), F32)],
            compiler_params=params(BIG),
            cost_estimate=cost(0, MIB),
            name="weight_halve",
        )(bits[level], keep, got)
        pieces //= 2
    got = lax.ppermute(give, "dom", flips[len(halves) - 1])
    total = add_round(add_round_kernel, keep, got)

    out_h = pl.pallas_call(
        turn_kernel,
        out_shape=sds((nodes, f_out), BF),
        in_specs=[vmem()],
        out_specs=vmem(),
        compiler_params=params(BIG),
        cost_estimate=cost(0, MIB),
        name="turn_out",
    )(out_t)
    grad_all = lax.all_gather(grad_t, "chan", axis=0, tiled=False)

    for level in range(len(halves), len(order) - 1):
        got = lax.ppermute(total, "dom", flips[level])
        total = add_round(add_pair_kernel, total, got)
    scaled, total, out_h = lax.optimization_barrier((scaled, total, out_h))
    got = lax.ppermute(total, "dom", flips[-1])
    own_grad, far_grad = pl.pallas_call(
        scatter_kernel,
        out_shape=[
            pltpu.HBM((block_rows, chan_width, size), F32),
            pltpu.HBM((parts * slots, chan_width, size), BF),
        ],
        in_specs=[smem(), smem(), hbm(), vmem()],
        out_specs=[hbm(), hbm()],
        scratch_shapes=[
            pltpu.VMEM(block_vals.shape, BF),
            pltpu.VMEM((table, chan_width, size), F32),
            pltpu.VMEM((parts * slots, chan_width, size), BF),
            pltpu.SemaphoreType.DMA((streams,)),
            pltpu.SemaphoreType.DMA((copies,)),
            pltpu.SemaphoreType.DMA,
        ],
        compiler_params=params(24),
        cost_estimate=cost(block_flops, val_bytes + 4 * MIB),
        name="table_grad",
    )(cols, block_counts, vals, scaled)
    far_grad, got = lax.optimization_barrier((far_grad, got))
    total = add_round(add_pair_kernel, total, got)
    back = lax.all_to_all(
        far_grad.reshape(parts, slots, chan_width, size), "dom", split_axis=0, concat_axis=0, tiled=True
    )

    packed = pl.pallas_call(
        functools.partial(message_kernel, chans),
        out_shape=[sds((pieces * unit, lanes), BF)] * chans,
        in_specs=[smem(), vmem()],
        out_specs=[vmem()] * chans,
        compiler_params=params(BIG),
        cost_estimate=cost(0, MIB),
        name="pack_messages",
    )(me, total)
    packed = exchange(packed)
    held = pl.pallas_call(
        unit_kernel,
        out_shape=sds((pieces * unit, lanes), BF),
        in_specs=[vmem()] * chans,
        out_specs=vmem(),
        compiler_params=params(BIG),
        cost_estimate=cost(0, MIB),
        name="weight_sum",
    )(*packed).reshape(1, pieces * unit, lanes)
    near = pl.pallas_call(
        near_kernel,
        out_shape=sds((block_rows, chan_width, size), F32),
        in_specs=[smem()] + [vmem()] * 3,
        out_specs=vmem(),
        compiler_params=params(BIG),
        cost_estimate=cost(0, 3 * MIB),
        name="sum_near",
    )(me, w_self, grad_all, own_grad)
    held, near = lax.optimization_barrier((held, near))
    for level in reversed(range(len(halves))):
        held = jnp.concatenate([held, lax.ppermute(held, "dom", flips[level])], axis=0)
    address = jnp.int32(0)
    for level in range(len(halves)):
        address = address * 2 + bits[level][0]
    grad_w_self, grad_w_neigh = pl.pallas_call(
        functools.partial(spread_kernel, float(node_count * parts) ** (-0.5)),
        out_shape=[sds((chan_width, f_out), F32)] * 2,
        in_specs=[smem(), vmem()],
        out_specs=[vmem()] * 2,
        compiler_params=params(BIG),
        cost_estimate=cost(0, MIB),
        name="weight_spread",
    )(address.reshape(1), held)

    grad_feats = pl.pallas_call(
        final_kernel,
        out_shape=sds((chan_width, node_count), BF),
        in_specs=[smem()] + [vmem()] * 2,
        out_specs=vmem(),
        scratch_shapes=[pltpu.VMEM((block_rows, chan_width, size), F32)],
        compiler_params=params(BIG),
        cost_estimate=cost(0, 4 * MIB),
        name="sum_returned",
    )(send, near, back)
    return (out_h, grad_feats.T, grad_w_self, grad_w_neigh)


def solution(mesh):
    return jax.shard_map(
        per_device,
        mesh=mesh,
        in_specs=(
            P("dom", "chan"),
            P("dom", None, None, None),
            P("dom", None),
            P("dom"),
            P("dom", None, None),
            P(),
            P(),
            P(),
            P(("dom", "chan"), None),
        ),
        out_specs=(P(("dom", "chan"), None), P("dom", "chan"), P("chan", None), P("chan", None)),
        check_vma=False,
    )
```

time: 380 us -> 162 us (0.43)
  waiting for transfers between devices: 223 us -> 30 us
  local copies, waits for them, and re-layouts: 55 us -> 8.69 us
  starting transfers between devices: 15.2 us -> 60.7 us
  matrix products: 35.5 us -> 0 us
  other arithmetic: 33.6 us -> 0.02 us
  Pallas kernels: 0 us -> 23.8 us
  blocking collectives: 0 us -> 22.5 us
    psum x1 -> x0, waiting for transfers between devices: 110 us -> none  [per_device(): lax.psum(own_self.astype(jnp.bfloat16), 'dom').astype(jnp.float32)]
    reduce_scatter x1 -> x0, waiting for transfers between devices: 54.9 us -> none  [per_device(): lax.psum_scatter(jnp.dot(feats, self_part, preferred_element_type=jnp.flo...]
    ppermute x0 -> x22, starting transfers between devices: none -> 40.4 us  [the longest x14 31.5 us: exchange(): lax.ppermute(chunks[shift], 'chan', [(i, (i + shift) % count) for i in ra...]
    all_gather x1, waiting for transfers between devices: 39.9 us -> 0.02 us  [per_device(): grad_all = lax.all_gather(grad_t, 'chan', axis=0, tiled=False)]
    dot_general x9 -> x0, matrix products: 35.5 us -> none  [the longest x1 8.01 us: per_device(): jnp.einsum('rkij,ric->rkjc', block_vals, grad_scaled, preferred_element_t...]
    ppermute x0 -> x22, waiting for transfers between devices: none -> 28.8 us  [the longest x3 8.53 us: per_device(): lax.ppermute(held, 'dom', flips[level])]
    reshape x6 -> x1, local copies, waits for them, and re-layouts: 24.8 us -> 0.13 us  [per_device(): bias.reshape(f_out, 1)]
    pallas_call x0 -> x18, Pallas kernels: none -> 23.8 us  [the longest x1 6.5 us: per_device(): pl.pallas_call(scatter_kernel, out_shape=[pltpu.HBM((block_rows, chan_wid...]
  transfers between devices with their start and end apart: 5 -> 26, of which waited for: 4 -> 11; matrix products, arithmetic and copies ran while one was open for 4% -> 0% of each run, Pallas kernels for 0% -> 9%
where the time goes in v2:
time: 162 us; the launch traced here: 160 us
  starting transfers between devices  60.7 us (37%)
  waiting for transfers between devices  30 us (19%)
  Pallas kernels  23.8 us (15%)
  blocking collectives  22.5 us (14%)
  between operations  14.4 us (9%)
  local copies, waits for them, and re-layouts  8.69 us (5%)
    ppermute x14, starting transfers between devices, exchange(): lax.ppermute(chunks[shift], 'chan', [(i, (i + shift) % count) for i in ra...  31.5 us
    all_to_all x1, blocking collectives, per_device(): lax.all_to_all(mean, 'chan', split_axis=0, concat_axis=0, tiled=True)  22.5 us
    all_to_all x1, starting transfers between devices, per_device(): lax.all_to_all(far_grad.reshape(parts, slots, chan_width, size), 'dom', s...  9.05 us
    unnamed x40, local copies, waits for them, and re-layouts  8.56 us
    ppermute x3, waiting for transfers between devices, per_device(): lax.ppermute(held, 'dom', flips[level])  8.53 us
    ppermute x14, waiting for transfers between devices, exchange(): lax.ppermute(chunks[shift], 'chan', [(i, (i + shift) % count) for i in ra...  8.36 us
    all_to_all x1, starting transfers between devices, per_device(): lax.all_to_all(outgoing, 'dom', split_axis=0, concat_axis=0, tiled=True)  7.76 us
    pallas_call x1, Pallas kernels, per_device(): pl.pallas_call(scatter_kernel, out_shape=[pltpu.HBM((block_rows, chan_wid...  6.5 us
  transfers between devices with their start and end apart: 26, of which 11 were waited for; matrix products, arithmetic and copies ran while one was open for 0% of the time, Pallas kernels for 9%

profile of v2, /device:TPU:2, one launch (start us, length us, event | category | flops | bytes accessed | tf_op | source)
XLA Modules:
  0.0 160.1 jit_solution(9432787093266221785)
XLA Ops:
  7.2 1.0 copy-done
  8.2 0.7 copy-done.16
  8.9 2.1 %pack_outgoing.1 = bf16[32,4,64,128]{3,2,1,0:T(8,128)(2,1)} custom-call(s32[4,32]{1,0:T(4,128)S(1)} %bitcast.31, bf16[64,4096]{1,0:T(8,128)(2,1)S(1)} %bitcast.21), custom_call_target="tpu_custom_call" | custom-call | bytes 5242880 | tf_op jit(solution)/shard_map/pack_outgoing/pallas_call | solution.py:325
  11.0 7.8 %all-to-all-start = ((bf16[32,4,64,128]{3,2,1,0:T(8,128)(2,1)}), bf16[32,4,64,128]{3,2,1,0:T(8,128)(2,1)S(1)}, u32[]{:S(2)}, u32[]{:S(2)}) async-start(bf16[32,4,64,128]{3,2,1,0:T(8,128)(2,1)} %pack_outgoing.1), calls=%async_computation | async-start | bytes 4194304 | tf_op jit(solution)/shard_map/all_to_all | solution.py:335
  18.9 0.7 split_feats.1
  19.6 1.9 %collective-permute-start = (bf16[64,512]{1,0:T(8,128)(2,1)S(1)}, bf16[64,512]{1,0:T(8,128)(2,1)S(1)}, u32[]{:S(2)}, u32[]{:S(2)}) collective-permute-start(bf16[64,512]{1,0:T(8,128)(2,1)S(1)} %get-tuple-element.52), channel_id=1, source_target_pairs={{0,1},{1,2},{2,3},{3,4},{4,5},{5,6},{6,7},{7,0},{8,9},{9,10},{10,1... | collective-permute-start | bytes 196616 | tf_op jit(solution)/shard_map/ppermute | solution.py:276
  21.5 3.3 %collective-permute-start.1 = (bf16[64,512]{1,0:T(8,128)(2,1)S(1)}, bf16[64,512]{1,0:T(8,128)(2,1)S(1)}, u32[]{:S(2)}, u32[]{:S(2)}) collective-permute-start(bf16[64,512]{1,0:T(8,128)(2,1)S(1)} %get-tuple-element.53), channel_id=1, source_target_pairs={{0,2},{1,3},{2,4},{3,5},{4,6},{5,7},{6,0},{7,1},{8,10},{9,11},{10,... | collective-permute-start | bytes 196616 | tf_op jit(solution)/shard_map/ppermute | solution.py:276
  24.8 4.0 %collective-permute-start.2 = (bf16[64,512]{1,0:T(8,128)(2,1)}, bf16[64,512]{1,0:T(8,128)(2,1)S(1)}, u32[]{:S(2)}, u32[]{:S(2)}) collective-permute-start(bf16[64,512]{1,0:T(8,128)(2,1)} %get-tuple-element.54), channel_id=1, source_target_pairs={{0,3},{1,4},{2,5},{3,6},{4,7},{5,0},{6,1},{7,2},{8,11},{9,12},{10,... | collective-permute-start | bytes 196616 | tf_op jit(solution)/shard_map/ppermute | solution.py:276
  29.4 4.9 %collective-permute-start.4 = (bf16[64,512]{1,0:T(8,128)(2,1)}, bf16[64,512]{1,0:T(8,128)(2,1)}, u32[]{:S(2)}, u32[]{:S(2)}) collective-permute-start(bf16[64,512]{1,0:T(8,128)(2,1)} %get-tuple-element.56), channel_id=1, source_target_pairs={{0,5},{1,6},{2,7},{3,0},{4,1},{5,2},{6,3},{7,4},{8,13},{9,14},{10,... | collective-permute-start | bytes 196616 | tf_op jit(solution)/shard_map/ppermute | solution.py:276
  34.3 2.7 %collective-permute-start.5 = (bf16[64,512]{1,0:T(8,128)(2,1)}, bf16[64,512]{1,0:T(8,128)(2,1)}, u32[]{:S(2)}, u32[]{:S(2)}) collective-permute-start(bf16[64,512]{1,0:T(8,128)(2,1)} %get-tuple-element.57), channel_id=1, source_target_pairs={{0,6},{1,7},{2,0},{3,1},{4,2},{5,3},{6,4},{7,5},{8,14},{9,15},{10,... | collective-permute-start | bytes 196616 | tf_op jit(solution)/shard_map/ppermute | solution.py:276
  37.0 1.0 collective-permute-start.6
  38.2 5.7 %collective-permute-done.4.refs_5_ = bf16[64,512]{1,0:T(8,128)(2,1)} collective-permute-done((bf16[64,512]{1,0:T(8,128)(2,1)}, bf16[64,512]{1,0:T(8,128)(2,1)}, u32[]{:S(2)}, u32[]{:S(2)}) %collective-permute-start.4) | collective-permute-done | bytes 65568 | tf_op jit(solution)/shard_map/ppermute | solution.py:276
  44.4 0.9 copy-done.14
  45.3 1.3 self_part.1
  46.6 0.8 copy-done.6
  47.4 0.8 copy-done.8
  48.2 0.7 copy-done.10
  48.9 0.7 copy-done.12
  49.7 5.5 %neighbour_mean.1 = (bf16[8,64,512]{2,1,0:T(8,128)(2,1)S(1)}, f32[8,8,512]{2,1,0:T(8,128)S(1)}) custom-call(s32[8,32]{1,0:T(8,128)S(1)} %bitcast.29, s32[32]{0:T(128)S(1)} %copy-done.18, bf16[64,4096]{1,0:T(8,128)(2,1)S(1)} %bitcast.23, bf16[128,64,128]{2,1,0:T(8,128)(2,1)S(1)} %bitcast.18, bf16[32,8,128,128]{3,2,1,0:T(8,128)(2,1)} %vals_ref.3), custom_call_target="tpu_custom_call" | custom-call | flops 536870912 | bytes 11534336 | tf_op jit(solution)/shard_map/neighbour_mean/pallas_call | solution.py:360
  55.2 22.5 %all_to_all.20 = bf16[8,64,512]{2,1,0:T(8,128)(2,1)S(1)} all-to-all(bf16[8,64,512]{2,1,0:T(8,128)(2,1)S(1)} %get-tuple-element.68), channel_id=1, replica_groups=mesh['dom'=32,'chan'=8] {'chan'}, dimensions={0} | all-to-all | bytes 1048576 | tf_op jit(solution)/shard_map/all_to_all | solution.py:370
  77.7 1.8 %layer_head.1 = (bf16[256,512]{1,0:T(8,128)(2,1)S(1)}, bf16[256,512]{1,0:T(8,128)(2,1)}, bf16[512,512]{1,0:T(8,128)(2,1)}) custom-call(s32[1]{0:T(128)} %bitcast.me_ref, f32[8,8,512]{2,1,0:T(8,128)S(1)} %get-tuple-element.64.degree_ref, f32[256,512]{1,0:T(8,128)S(1)} %copy-done.9, bf16[256,512]{1,0:T(8,128)(2,1)S(1)} %copy-done.11, ...), custom_call_target="tpu_custom_call" | custom-call | flops 268435456 | bytes 4194304 | tf_op jit(solution)/shard_map/layer_head/pallas_call | solution.py:372
  79.5 3.5 %all-to-all-start.2 = ((bf16[8,64,512]{2,1,0:T(8,128)(2,1)}), bf16[8,64,512]{2,1,0:T(8,128)(2,1)S(1)}, u32[]{:S(2)}, u32[]{:S(2)}) async-start(bf16[8,64,512]{2,1,0:T(8,128)(2,1)} %bitcast.8), calls=%async_computation.2 | async-start | bytes 1048576 | tf_op jit(solution)/shard_map/all_to_all | solution.py:381
  83.0 1.5 weight_partial.1
  84.6 1.5 collective-permute-done.7.recv_ref
  86.2 1.1 collective-permute-start.8
  87.4 4.5 %collective-permute-done.8.recv_ref = bf16[8,8,8,128]{3,2,1,0:T(8,128)(2,1)S(1)} collective-permute-done((bf16[8,8,8,128]{3,2,1,0:T(8,128)(2,1)S(1)}, bf16[8,8,8,128]{3,2,1,0:T(8,128)(2,1)S(1)}, u32[]{:S(2)}, u32[]{:S(2)}) %collective-permute-start.8) | collective-permute-done | bytes 131104 | tf_op jit(solution)/shard_map/ppermute | solution.py:402
  91.9 1.2 collective-permute-start.9
  93.1 3.2 %collective-permute-done.9.recv_ref = bf16[4,8,8,128]{3,2,1,0:T(8,128)(2,1)S(1)} collective-permute-done((bf16[4,8,8,128]{3,2,1,0:T(8,128)(2,1)S(1)}, bf16[4,8,8,128]{3,2,1,0:T(8,128)(2,1)S(1)}, u32[]{:S(2)}, u32[]{:S(2)}) %collective-permute-start.9) | collective-permute-done | bytes 65568 | tf_op jit(solution)/shard_map/ppermute | solution.py:414
  96.3 2.3 %collective-permute-start.10 = (bf16[4,8,8,128]{3,2,1,0:T(8,128)(2,1)S(1)}, bf16[4,8,8,128]{3,2,1,0:T(8,128)(2,1)S(1)}, u32[]{:S(2)}, u32[]{:S(2)}) collective-permute-start(bf16[4,8,8,128]{3,2,1,0:T(8,128)(2,1)S(1)} %weight_add.3.held_ref), channel_id=1, source_target_pairs={{0,32},{8,40},{16,48},{24,56},{32,0},{40,8},{48,16},{56,24},{64,96... | collective-permute-start | bytes 196616 | tf_op jit(solution)/shard_map/ppermute | solution.py:429
  98.6 0.8 turn_out.1
  99.5 2.7 %collective-permute-done.10.recv_ref = bf16[4,8,8,128]{3,2,1,0:T(8,128)(2,1)S(1)} collective-permute-done((bf16[4,8,8,128]{3,2,1,0:T(8,128)(2,1)S(1)}, bf16[4,8,8,128]{3,2,1,0:T(8,128)(2,1)S(1)}, u32[]{:S(2)}, u32[]{:S(2)}) %collective-permute-start.10) | collective-permute-done | bytes 65568 | tf_op jit(solution)/shard_map/ppermute | solution.py:429
  102.2 1.2 all-to-all-done.2.scaled_ref
  103.4 2.2 %collective-permute-start.11 = (bf16[4,8,8,128]{3,2,1,0:T(8,128)(2,1)S(1)}, bf16[4,8,8,128]{3,2,1,0:T(8,128)(2,1)S(1)}, u32[]{:S(2)}, u32[]{:S(2)}) collective-permute-start(bf16[4,8,8,128]{3,2,1,0:T(8,128)(2,1)S(1)} %weight_add.4.held_ref), channel_id=1, source_target_pairs={{0,128},{8,136},{16,144},{24,152},{32,160},{40,168},{48,176},{56,1... | collective-permute-start | bytes 196616 | tf_op jit(solution)/shard_map/ppermute | solution.py:432
  105.6 6.5 %table_grad.1 = (f32[32,64,128]{2,1,0:T(8,128)}, bf16[128,64,128]{2,1,0:T(8,128)(2,1)}) custom-call(s32[8,32]{1,0:T(8,128)S(1)} %bitcast.30, s32[32]{0:T(128)S(1)} %copy-done.18, bf16[32,8,128,128]{3,2,1,0:T(8,128)(2,1)} %vals_ref.3, bf16[8,64,512]{2,1,0:T(8,128)(2,1)S(1)} %all-to-all-done.2.scaled_ref), custom_call_target="tpu_custom_call" | custom-call | flops 536870912 | bytes 12582912 | tf_op jit(solution)/shard_map/table_grad/pallas_call | solution.py:433
  112.1 9.0 %all-to-all-start.3 = ((bf16[32,4,64,128]{3,2,1,0:T(8,128)(2,1)}), bf16[32,4,64,128]{3,2,1,0:T(8,128)(2,1)S(1)}, u32[]{:S(2)}, u32[]{:S(2)}) async-start(bf16[32,4,64,128]{3,2,1,0:T(8,128)(2,1)} %bitcast.33), calls=%async_computation.3 | async-start | bytes 4194304 | tf_op jit(solution)/shard_map/all_to_all | solution.py:455
  121.6 2.7 %collective-permute-start.14 = (bf16[32,128]{1,0:T(8,128)(2,1)S(1)}, bf16[32,128]{1,0:T(8,128)(2,1)S(1)}, u32[]{:S(2)}, u32[]{:S(2)}) collective-permute-start(bf16[32,128]{1,0:T(8,128)(2,1)S(1)} %get-tuple-element.87), channel_id=1, source_target_pairs={{0,3},{1,4},{2,5},{3,6},{4,7},{5,0},{6,1},{7,2},{8,11},{9,12},{10,... | collective-permute-start | bytes 24584 | tf_op jit(solution)/shard_map/ppermute | solution.py:276
  124.3 3.5 %collective-permute-start.15 = (bf16[32,128]{1,0:T(8,128)(2,1)S(1)}, bf16[32,128]{1,0:T(8,128)(2,1)S(1)}, u32[]{:S(2)}, u32[]{:S(2)}) collective-permute-start(bf16[32,128]{1,0:T(8,128)(2,1)S(1)} %get-tuple-element.88), channel_id=1, source_target_pairs={{0,4},{1,5},{2,6},{3,7},{4,0},{5,1},{6,2},{7,3},{8,12},{9,13},{10,... | collective-permute-start | bytes 24584 | tf_op jit(solution)/shard_map/ppermute | solution.py:276
  127.8 1.5 collective-permute-start.16
  129.3 3.5 %collective-permute-start.17 = (bf16[32,128]{1,0:T(8,128)(2,1)S(1)}, bf16[32,128]{1,0:T(8,128)(2,1)S(1)}, u32[]{:S(2)}, u32[]{:S(2)}) collective-permute-start(bf16[32,128]{1,0:T(8,128)(2,1)S(1)} %get-tuple-element.90), channel_id=1, source_target_pairs={{0,6},{1,7},{2,0},{3,1},{4,2},{5,3},{6,4},{7,5},{8,14},{9,15},{10,... | collective-permute-start | bytes 24584 | tf_op jit(solution)/shard_map/ppermute | solution.py:276
  132.9 1.5 collective-permute-start.18
  134.7 1.8 %collective-permute-done.18.refs_7_ = bf16[32,128]{1,0:T(8,128)(2,1)S(1)} collective-permute-done((bf16[32,128]{1,0:T(8,128)(2,1)S(1)}, bf16[32,128]{1,0:T(8,128)(2,1)S(1)}, u32[]{:S(2)}, u32[]{:S(2)}) %collective-permute-start.18) | collective-permute-done | bytes 8224 | tf_op jit(solution)/shard_map/ppermute | solution.py:276
  136.6 1.6 copy-done.2
  138.2 1.2 copy-done.3
  139.9 1.6 collective-permute-start.19
  141.4 5.2 %collective-permute-done.19 = bf16[1,32,128]{2,1,0:T(8,128)(2,1)S(1)} collective-permute-done((bf16[1,32,128]{2,1,0:T(8,128)(2,1)S(1)}, bf16[1,32,128]{2,1,0:T(8,128)(2,1)S(1)}, u32[]{:S(2)}, u32[]{:S(2)}) %collective-permute-start.19) | collective-permute-done | bytes 8224 | tf_op jit(solution)/shard_map/ppermute | solution.py:489
  147.0 3.4 %collective-permute-done.20 = bf16[2,32,128]{2,1,0:T(8,128)(2,1)S(1)} collective-permute-done((bf16[2,32,128]{2,1,0:T(8,128)(2,1)S(1)}, bf16[2,32,128]{2,1,0:T(8,128)(2,1)S(1)}, u32[]{:S(2)}, u32[]{:S(2)}) %collective-permute-start.20) | collective-permute-done | bytes 16416 | tf_op jit(solution)/shard_map/ppermute | solution.py:489
  150.4 2.2 %sum_returned.1 = bf16[64,4096]{1,0:T(8,128)(2,1)} custom-call(s32[4,32]{1,0:T(4,128)S(1)} %bitcast.32, f32[32,64,128]{2,1,0:T(8,128)S(1)} %sum_near.1.near_ref, bf16[32,4,64,128]{3,2,1,0:T(8,128)(2,1)S(1)} %all-to-all-done.3.back_ref), custom_call_target="tpu_custom_call" | custom-call | bytes 4194304 | tf_op jit(solution)/shard_map/sum_returned/pallas_call | solution.py:503
  152.6 0.7 weight_spread.1
  (68 shorter events, 3.2 us)
Async XLA Ops:
  7.2 1.0 copy-start
  8.2 0.7 copy-start.16
  11.0 7.9 %copy-start.1 = (bf16[4096,64]{0,1:T(8,128)(2,1)S(1)}, bf16[4096,64]{0,1:T(8,128)(2,1)}, u32[]{:S(2)}) copy-start(bf16[4096,64]{0,1:T(8,128)(2,1)} %param.9) | copy-start | bytes 1572868
  11.0 27.0 %copy-start.19 = (f32[256]{0:T(256)S(1)}, f32[256]{0:T(256)}, u32[]{:S(2)}) copy-start(f32[256]{0:T(256)} %param.16) | copy-start | bytes 3076
  11.0 33.4 %copy-start.4 = (bf16[512,256]{1,0:T(8,128)(2,1)S(1)}, bf16[512,256]{1,0:T(8,128)(2,1)}, u32[]{:S(2)}) copy-start(bf16[512,256]{1,0:T(8,128)(2,1)} %weight_ref.4) | copy-start | bytes 786436
  11.0 33.4 %copy-start.5 = (bf16[512,256]{1,0:T(8,128)(2,1)S(1)}, bf16[512,256]{1,0:T(8,128)(2,1)}, u32[]{:S(2)}) copy-start(bf16[512,256]{1,0:T(8,128)(2,1)} %weight_ref.5) | copy-start | bytes 786436
  11.0 38.6 %all-to-all-start = ((bf16[32,4,64,128]{3,2,1,0:T(8,128)(2,1)}), bf16[32,4,64,128]{3,2,1,0:T(8,128)(2,1)S(1)}, u32[]{:S(2)}, u32[]{:S(2)}) async-start(bf16[32,4,64,128]{3,2,1,0:T(8,128)(2,1)} %pack_outgoing.1), calls=%async_computation | async-start | bytes 4194304 | tf_op jit(solution)/shard_map/all_to_all | solution.py:335
  18.8 30.9 %copy-start.15 = (s32[32,8]{0,1:T(8,128)S(1)}, s32[32,8]{0,1:T(8,128)}, u32[]{:S(2)}) copy-start(s32[32,8]{0,1:T(8,128)} %param.11) | copy-start | bytes 3076
  18.8 30.9 %copy-start.18 = (s32[32]{0:T(128)S(1)}, s32[32]{0:T(128)}, u32[]{:S(2)}) copy-start(s32[32]{0:T(128)} %counts_ref.3) | copy-start | bytes 388
  18.8 117.8 %all-gather.3.cloned.1.call-start = ((), (), s32[]{:S(2)}) async-start(), calls=%async_computation.4 | async-start | bytes 2359296 | tf_op jit(solution)/shard_map/all_gather | solution.py:426
  19.6 14.7 %collective-permute-start = (bf16[64,512]{1,0:T(8,128)(2,1)S(1)}, bf16[64,512]{1,0:T(8,128)(2,1)S(1)}, u32[]{:S(2)}, u32[]{:S(2)}) collective-permute-start(bf16[64,512]{1,0:T(8,128)(2,1)S(1)} %get-tuple-element.52), channel_id=1, source_target_pairs={{0,1},{1,2},{2,3},{3,4},{4,5},{5,6},{6,7},{7,0},{8,9},{9,10},{10,1... | collective-permute-start | bytes 196616 | tf_op jit(solution)/shard_map/ppermute | solution.py:276
  21.5 15.5 %collective-permute-start.1 = (bf16[64,512]{1,0:T(8,128)(2,1)S(1)}, bf16[64,512]{1,0:T(8,128)(2,1)S(1)}, u32[]{:S(2)}, u32[]{:S(2)}) collective-permute-start(bf16[64,512]{1,0:T(8,128)(2,1)S(1)} %get-tuple-element.53), channel_id=1, source_target_pairs={{0,2},{1,3},{2,4},{3,5},{4,6},{5,7},{6,0},{7,1},{8,10},{9,11},{10,... | collective-permute-start | bytes 196616 | tf_op jit(solution)/shard_map/ppermute | solution.py:276
  24.8 13.4 %collective-permute-start.2 = (bf16[64,512]{1,0:T(8,128)(2,1)}, bf16[64,512]{1,0:T(8,128)(2,1)S(1)}, u32[]{:S(2)}, u32[]{:S(2)}) collective-permute-start(bf16[64,512]{1,0:T(8,128)(2,1)} %get-tuple-element.54), channel_id=1, source_target_pairs={{0,3},{1,4},{2,5},{3,6},{4,7},{5,0},{6,1},{7,2},{8,11},{9,12},{10,... | collective-permute-start | bytes 196616 | tf_op jit(solution)/shard_map/ppermute | solution.py:276
  28.8 9.3 %collective-permute-start.3 = (bf16[64,512]{1,0:T(8,128)(2,1)}, bf16[64,512]{1,0:T(8,128)(2,1)}, u32[]{:S(2)}, u32[]{:S(2)}) collective-permute-start(bf16[64,512]{1,0:T(8,128)(2,1)} %get-tuple-element.55), channel_id=1, source_target_pairs={{0,4},{1,5},{2,6},{3,7},{4,0},{5,1},{6,2},{7,3},{8,12},{9,13},{10,... | collective-permute-start | bytes 196616 | tf_op jit(solution)/shard_map/ppermute | solution.py:276
  29.4 14.5 %collective-permute-start.4 = (bf16[64,512]{1,0:T(8,128)(2,1)}, bf16[64,512]{1,0:T(8,128)(2,1)}, u32[]{:S(2)}, u32[]{:S(2)}) collective-permute-start(bf16[64,512]{1,0:T(8,128)(2,1)} %get-tuple-element.56), channel_id=1, source_target_pairs={{0,5},{1,6},{2,7},{3,0},{4,1},{5,2},{6,3},{7,4},{8,13},{9,14},{10,... | collective-permute-start | bytes 196616 | tf_op jit(solution)/shard_map/ppermute | solution.py:276
  34.3 9.5 %collective-permute-start.5 = (bf16[64,512]{1,0:T(8,128)(2,1)}, bf16[64,512]{1,0:T(8,128)(2,1)}, u32[]{:S(2)}, u32[]{:S(2)}) collective-permute-start(bf16[64,512]{1,0:T(8,128)(2,1)} %get-tuple-element.57), channel_id=1, source_target_pairs={{0,6},{1,7},{2,0},{3,1},{4,2},{5,3},{6,4},{7,5},{8,14},{9,15},{10,... | collective-permute-start | bytes 196616 | tf_op jit(solution)/shard_map/ppermute | solution.py:276
  37.0 7.3 %collective-permute-start.6 = (bf16[64,512]{1,0:T(8,128)(2,1)}, bf16[64,512]{1,0:T(8,128)(2,1)}, u32[]{:S(2)}, u32[]{:S(2)}) collective-permute-start(bf16[64,512]{1,0:T(8,128)(2,1)} %get-tuple-element.58), channel_id=1, source_target_pairs={{0,7},{1,0},{2,1},{3,2},{4,3},{5,4},{6,5},{7,6},{8,15},{9,8},{10,9... | collective-permute-start | bytes 196616 | tf_op jit(solution)/shard_map/ppermute | solution.py:276
  44.3 1.0 copy-start.14
  46.6 0.8 copy-start.6
  47.4 0.8 copy-start.8
  48.2 0.7 copy-start.10
  48.9 0.7 copy-start.12
  49.6 28.0 %copy-start.9 = (f32[256,512]{1,0:T(8,128)S(1)}, f32[256,512]{1,0:T(8,128)}, u32[]{:S(2)}) copy-start(f32[256,512]{1,0:T(8,128)} %copy-done.8) | copy-start | bytes 1572868
  49.7 28.0 %copy-start.11 = (bf16[256,512]{1,0:T(8,128)(2,1)S(1)}, bf16[256,512]{1,0:T(8,128)(2,1)}, u32[]{:S(2)}) copy-start(bf16[256,512]{1,0:T(8,128)(2,1)} %copy-done.10) | copy-start | bytes 786436
  49.7 28.0 %copy-start.13 = (bf16[256,512]{1,0:T(8,128)(2,1)S(1)}, bf16[256,512]{1,0:T(8,128)(2,1)}, u32[]{:S(2)}) copy-start(bf16[256,512]{1,0:T(8,128)(2,1)} %copy-done.12) | copy-start | bytes 786436
  55.2 27.8 %copy-start.7 = (bf16[512,512]{1,0:T(8,128)(2,1)S(1)}, bf16[512,512]{1,0:T(8,128)(2,1)}, u32[]{:S(2)}) copy-start(bf16[512,512]{1,0:T(8,128)(2,1)} %copy-done.6) | copy-start | bytes 1572868
  79.5 23.9 %all-to-all-start.2 = ((bf16[8,64,512]{2,1,0:T(8,128)(2,1)}), bf16[8,64,512]{2,1,0:T(8,128)(2,1)S(1)}, u32[]{:S(2)}, u32[]{:S(2)}) async-start(bf16[8,64,512]{2,1,0:T(8,128)(2,1)} %bitcast.8), calls=%async_computation.2 | async-start | bytes 1048576 | tf_op jit(solution)/shard_map/all_to_all | solution.py:381
  84.5 1.6 %collective-permute-start.7 = (bf16[16,8,8,128]{3,2,1,0:T(8,128)(2,1)S(1)}, bf16[16,8,8,128]{3,2,1,0:T(8,128)(2,1)S(1)}, u32[]{:S(2)}, u32[]{:S(2)}) collective-permute-start(bf16[16,8,8,128]{3,2,1,0:T(8,128)(2,1)S(1)} %get-tuple-element.73), channel_id=1, source_target_pairs={{0,8},{8,0},{16,24},{24,16},{32,40},{40,32},{48,56},{56,48},{64,72... | collective-permute-start | bytes 786440 | tf_op jit(solution)/shard_map/ppermute | solution.py:402
  86.2 5.6 %collective-permute-start.8 = (bf16[8,8,8,128]{3,2,1,0:T(8,128)(2,1)S(1)}, bf16[8,8,8,128]{3,2,1,0:T(8,128)(2,1)S(1)}, u32[]{:S(2)}, u32[]{:S(2)}) collective-permute-start(bf16[8,8,8,128]{3,2,1,0:T(8,128)(2,1)S(1)} %get-tuple-element.75), channel_id=1, source_target_pairs={{0,16},{8,24},{16,0},{24,8},{32,48},{40,56},{48,32},{56,40},{64,80... | collective-permute-start | bytes 393224 | tf_op jit(solution)/shard_map/ppermute | solution.py:402
  91.9 4.4 %collective-permute-start.9 = (bf16[4,8,8,128]{3,2,1,0:T(8,128)(2,1)S(1)}, bf16[4,8,8,128]{3,2,1,0:T(8,128)(2,1)S(1)}, u32[]{:S(2)}, u32[]{:S(2)}) collective-permute-start(bf16[4,8,8,128]{3,2,1,0:T(8,128)(2,1)S(1)} %get-tuple-element.77), channel_id=1, source_target_pairs={{0,64},{8,72},{16,80},{24,88},{32,96},{40,104},{48,112},{56,120},{... | collective-permute-start | bytes 196616 | tf_op jit(solution)/shard_map/ppermute | solution.py:414
  96.3 5.9 %collective-permute-start.10 = (bf16[4,8,8,128]{3,2,1,0:T(8,128)(2,1)S(1)}, bf16[4,8,8,128]{3,2,1,0:T(8,128)(2,1)S(1)}, u32[]{:S(2)}, u32[]{:S(2)}) collective-permute-start(bf16[4,8,8,128]{3,2,1,0:T(8,128)(2,1)S(1)} %weight_add.3.held_ref), channel_id=1, source_target_pairs={{0,32},{8,40},{16,48},{24,56},{32,0},{40,8},{48,16},{56,24},{64,96... | collective-permute-start | bytes 196616 | tf_op jit(solution)/shard_map/ppermute | solution.py:429
  103.4 8.7 %collective-permute-start.11 = (bf16[4,8,8,128]{3,2,1,0:T(8,128)(2,1)S(1)}, bf16[4,8,8,128]{3,2,1,0:T(8,128)(2,1)S(1)}, u32[]{:S(2)}, u32[]{:S(2)}) collective-permute-start(bf16[4,8,8,128]{3,2,1,0:T(8,128)(2,1)S(1)} %weight_add.4.held_ref), channel_id=1, source_target_pairs={{0,128},{8,136},{16,144},{24,152},{32,160},{40,168},{48,176},{56,1... | collective-permute-start | bytes 196616 | tf_op jit(solution)/shard_map/ppermute | solution.py:432
  112.1 38.3 %all-to-all-start.3 = ((bf16[32,4,64,128]{3,2,1,0:T(8,128)(2,1)}), bf16[32,4,64,128]{3,2,1,0:T(8,128)(2,1)S(1)}, u32[]{:S(2)}, u32[]{:S(2)}) async-start(bf16[32,4,64,128]{3,2,1,0:T(8,128)(2,1)} %bitcast.33), calls=%async_computation.3 | async-start | bytes 4194304 | tf_op jit(solution)/shard_map/all_to_all | solution.py:455
  121.2 8.1 %collective-permute-start.12 = (bf16[32,128]{1,0:T(8,128)(2,1)S(1)}, bf16[32,128]{1,0:T(8,128)(2,1)S(1)}, u32[]{:S(2)}, u32[]{:S(2)}) collective-permute-start(bf16[32,128]{1,0:T(8,128)(2,1)S(1)} %get-tuple-element.85), channel_id=1, source_target_pairs={{0,1},{1,2},{2,3},{3,4},{4,5},{5,6},{6,7},{7,0},{8,9},{9,10},{10,1... | collective-permute-start | bytes 24584 | tf_op jit(solution)/shard_map/ppermute | solution.py:276
  121.3 11.5 %collective-permute-start.13 = (bf16[32,128]{1,0:T(8,128)(2,1)S(1)}, bf16[32,128]{1,0:T(8,128)(2,1)S(1)}, u32[]{:S(2)}, u32[]{:S(2)}) collective-permute-start(bf16[32,128]{1,0:T(8,128)(2,1)S(1)} %get-tuple-element.86), channel_id=1, source_target_pairs={{0,2},{1,3},{2,4},{3,5},{4,6},{5,7},{6,0},{7,1},{8,10},{9,11},{10,... | collective-permute-start | bytes 24584 | tf_op jit(solution)/shard_map/ppermute | solution.py:276
  121.6 12.8 %collective-permute-start.14 = (bf16[32,128]{1,0:T(8,128)(2,1)S(1)}, bf16[32,128]{1,0:T(8,128)(2,1)S(1)}, u32[]{:S(2)}, u32[]{:S(2)}) collective-permute-start(bf16[32,128]{1,0:T(8,128)(2,1)S(1)} %get-tuple-element.87), channel_id=1, source_target_pairs={{0,3},{1,4},{2,5},{3,6},{4,7},{5,0},{6,1},{7,2},{8,11},{9,12},{10,... | collective-permute-start | bytes 24584 | tf_op jit(solution)/shard_map/ppermute | solution.py:276
  124.3 10.1 %collective-permute-start.15 = (bf16[32,128]{1,0:T(8,128)(2,1)S(1)}, bf16[32,128]{1,0:T(8,128)(2,1)S(1)}, u32[]{:S(2)}, u32[]{:S(2)}) collective-permute-start(bf16[32,128]{1,0:T(8,128)(2,1)S(1)} %get-tuple-element.88), channel_id=1, source_target_pairs={{0,4},{1,5},{2,6},{3,7},{4,0},{5,1},{6,2},{7,3},{8,12},{9,13},{10,... | collective-permute-start | bytes 24584 | tf_op jit(solution)/shard_map/ppermute | solution.py:276
  127.8 6.5 %collective-permute-start.16 = (bf16[32,128]{1,0:T(8,128)(2,1)S(1)}, bf16[32,128]{1,0:T(8,128)(2,1)S(1)}, u32[]{:S(2)}, u32[]{:S(2)}) collective-permute-start(bf16[32,128]{1,0:T(8,128)(2,1)S(1)} %get-tuple-element.89), channel_id=1, source_target_pairs={{0,5},{1,6},{2,7},{3,0},{4,1},{5,2},{6,3},{7,4},{8,13},{9,14},{10,... | collective-permute-start | bytes 24584 | tf_op jit(solution)/shard_map/ppermute | solution.py:276
  129.3 5.4 %collective-permute-start.17 = (bf16[32,128]{1,0:T(8,128)(2,1)S(1)}, bf16[32,128]{1,0:T(8,128)(2,1)S(1)}, u32[]{:S(2)}, u32[]{:S(2)}) collective-permute-start(bf16[32,128]{1,0:T(8,128)(2,1)S(1)} %get-tuple-element.90), channel_id=1, source_target_pairs={{0,6},{1,7},{2,0},{3,1},{4,2},{5,3},{6,4},{7,5},{8,14},{9,15},{10,... | collective-permute-start | bytes 24584 | tf_op jit(solution)/shard_map/ppermute | solution.py:276
  132.9 3.7 %collective-permute-start.18 = (bf16[32,128]{1,0:T(8,128)(2,1)S(1)}, bf16[32,128]{1,0:T(8,128)(2,1)S(1)}, u32[]{:S(2)}, u32[]{:S(2)}) collective-permute-start(bf16[32,128]{1,0:T(8,128)(2,1)S(1)} %get-tuple-element.91), channel_id=1, source_target_pairs={{0,7},{1,0},{2,1},{3,2},{4,3},{5,4},{6,5},{7,6},{8,15},{9,8},{10,9... | collective-permute-start | bytes 24584 | tf_op jit(solution)/shard_map/ppermute | solution.py:276
  136.6 1.6 copy-start.2
  138.2 1.2 copy-start.3
  139.4 11.0 %copy-start.17 = (s32[1,32,4]{1,2,0:T(4,128)S(1)}, s32[1,32,4]{1,2,0:T(4,128)}, u32[]{:S(2)}) copy-start(s32[1,32,4]{1,2,0:T(4,128)} %param.13) | copy-start | bytes 1540
  139.9 6.7 %collective-permute-start.19 = (bf16[1,32,128]{2,1,0:T(8,128)(2,1)S(1)}, bf16[1,32,128]{2,1,0:T(8,128)(2,1)S(1)}, u32[]{:S(2)}, u32[]{:S(2)}) collective-permute-start(bf16[1,32,128]{2,1,0:T(8,128)(2,1)S(1)} %bitcast.25), channel_id=1, source_target_pairs={{0,64},{8,72},{16,80},{24,88},{32,96},{40,104},{48,112},{56,120},{... | collective-permute-start | bytes 24584 | tf_op jit(solution)/shard_map/ppermute | solution.py:489
  146.6 3.7 %collective-permute-start.20 = (bf16[2,32,128]{2,1,0:T(8,128)(2,1)S(1)}, bf16[2,32,128]{2,1,0:T(8,128)(2,1)S(1)}, u32[]{:S(2)}, u32[]{:S(2)}) collective-permute-start(bf16[2,32,128]{2,1,0:T(8,128)(2,1)S(1)} %pad_maximum_fusion.2), channel_id=1, source_target_pairs={{0,16},{8,24},{16,0},{24,8},{32,48},{40,56},{48,32},{56,40},{64,80... | collective-permute-start | bytes 49160 | tf_op jit(solution)/shard_map/ppermute | solution.py:489
  150.3 2.2 %collective-permute-start.21 = (bf16[4,32,128]{2,1,0:T(8,128)(2,1)S(1)}, bf16[4,32,128]{2,1,0:T(8,128)(2,1)S(1)}, u32[]{:S(2)}, u32[]{:S(2)}) collective-permute-start(bf16[4,32,128]{2,1,0:T(8,128)(2,1)S(1)} %pad_maximum_fusion.1), channel_id=1, source_target_pairs={{0,8},{8,0},{16,24},{24,16},{32,40},{40,32},{48,56},{56,48},{64,72... | collective-permute-start | bytes 98312 | tf_op jit(solution)/shard_map/ppermute | solution.py:489
Sparse Core Ops, SparseCore 0:
  79.6 41.8 all-gather.2

commit v3 on v2

--- a/solution.py
+++ b/solution.py
@@ -69,7 +69,7 @@
     return jnp.concatenate([vals_ref[row, k] for k in range(vals_ref.shape[1])], axis=1)
 
 
-def stream_rows(vals_ref, held_ref, sems, body):
+def stream_rows(vals_ref, held_ref, sems, body, before=None):
     copies = sems.shape[0]
     span = held_ref.shape[0] // copies
 
@@ -79,6 +79,8 @@
 
     for place in range(copies):
         copy(place).start()
+    if before is not None:
+        before()
 
     def one(place, carry):
         copy(place).wait()
@@ -179,16 +181,28 @@
     out_ref[...] = (held_ref[...].astype(F32) + recv_ref[...].astype(F32)).astype(BF)
 
 
-def turn_kernel(out_ref, turned_ref):
+def side_kernel(chans, me_ref, weight_ref, out_ref, grad_ref, turned_ref, *refs):
+    self_refs = refs[:chans]
+    (hold_ref,) = refs[chans:]
     turned_ref[...] = out_ref[...].T
-
-
-def message_kernel(chans, me_ref, unit_ref, *packed_refs):
+    hold_ref[...] = nn_dot(weight_ref[...], grad_ref[...]).astype(BF)
+    height = self_refs[0].shape[0]
+    for shift, self_ref in enumerate(self_refs):
+        start = pl.multiple_of(lax.rem(me_ref[0] + shift, chans) * height, height)
+        self_ref[...] = hold_ref[pl.ds(start, height), :]
+
+
+def message_kernel(chans, me_ref, unit_ref, *refs):
+    self_refs = refs[:chans]
+    packed_refs = refs[chans:]
+    nodes = self_refs[0].shape[1]
     units, _, unit, lanes = unit_ref.shape
     for shift, packed_ref in enumerate(packed_refs):
         dest = lax.rem(me_ref[0] + shift, chans)
         piece = unit_ref[:, dest].astype(F32).reshape(units * unit, lanes)
-        packed_ref[...] = piece.astype(BF)
+        packed_ref[:, :nodes] = self_refs[shift][...]
+        packed_ref[: units * unit, nodes:] = piece.astype(BF)
+        packed_ref[units * unit :, nodes:] = jnp.zeros_like(packed_ref[units * unit :, nodes:])
 
 
 def scatter_kernel(
@@ -197,7 +211,9 @@
     _, depth, size, _ = vals_ref.shape
     rows = scaled_ref.shape[2] // size
     own = own_ref.shape[0]
-    hold_ref[...] = jnp.zeros_like(hold_ref)
+
+    def clear():
+        hold_ref[...] = jnp.zeros_like(hold_ref)
 
     def body(index):
         count = counts_ref[index]
@@ -207,7 +223,7 @@
             part = total[:, k * size : (k + 1) * size]
             hold_ref[cols_ref[k, index]] += jnp.where(k < count, part, jnp.zeros_like(part))
 
-    stream_rows(vals_ref, held_ref, val_sems, body)
+    stream_rows(vals_ref, held_ref, val_sems, body, clear)
     copies = sems.shape[0]
     span = far_ref.shape[0] // copies
     for copy in range(copies):
@@ -224,9 +240,10 @@
 def unit_kernel(*refs):
     packed_refs = refs[:-1]
     out_ref = refs[-1]
-    total = packed_refs[0][...].astype(F32)
+    rows, lanes = out_ref.shape
+    total = packed_refs[0][:rows, -lanes:].astype(F32)
     for packed_ref in packed_refs[1:]:
-        total = total + packed_ref[...].astype(F32)
+        total = total + packed_ref[:rows, -lanes:].astype(F32)
     out_ref[...] = total.astype(BF)
 
 
@@ -243,16 +260,16 @@
         target[row * rows : (row + 1) * rows, column * lanes : (column + 1) * lanes] = value
 
 
-def near_kernel(me_ref, weight_ref, grad_ref, own_ref, out_ref):
-    blocks, width, size = out_ref.shape
-    chans, _, nodes = grad_ref.shape
-    rows = nodes // size
-    weight = weight_ref[pl.ds(pl.multiple_of(me_ref[0] * width, width), width), :]
-    for group in range(chans):
-        total = nn_dot(weight, grad_ref[group]).astype(BF).astype(F32)
+def near_kernel(chans, me_ref, own_ref, *refs):
+    packed_refs = refs[:chans]
+    (out_ref,) = refs[chans:]
+    blocks, _, size = out_ref.shape
+    rows = blocks // chans
+    for shift, packed_ref in enumerate(packed_refs):
+        group = lax.rem(me_ref[0] + (chans - shift), chans)
         for row in range(rows):
             index = group * rows + row
-            out_ref[index] = own_ref[index] + total[:, row * size : (row + 1) * size]
+            out_ref[index] = own_ref[index] + packed_ref[:, row * size : (row + 1) * size].astype(F32)
 
 
 def final_kernel(send_ref, near_ref, back_ref, out_ref, hold_ref):
@@ -331,7 +348,10 @@
         compiler_params=params(8),
         cost_estimate=cost(0, 5 * MIB),
         name="pack_outgoing",
-    )(send, feats_t)
+    )(
+        pltpu.with_memory_space_constraint(send, pltpu.HBM),
+        pltpu.with_memory_space_constraint(feats_t, pltpu.HBM),
+    )
     incoming = lax.all_to_all(outgoing, "dom", split_axis=0, concat_axis=0, tiled=True)
 
     feat_chunks = pl.pallas_call(
@@ -414,21 +434,21 @@
     got = lax.ppermute(give, "dom", flips[len(halves) - 1])
     total = add_round(add_round_kernel, keep, got)
 
-    out_h = pl.pallas_call(
-        turn_kernel,
-        out_shape=sds((nodes, f_out), BF),
-        in_specs=[vmem()],
-        out_specs=vmem(),
-        compiler_params=params(BIG),
-        cost_estimate=cost(0, MIB),
-        name="turn_out",
-    )(out_t)
-    grad_all = lax.all_gather(grad_t, "chan", axis=0, tiled=False)
-
+    side = pl.pallas_call(
+        functools.partial(side_kernel, chans),
+        out_shape=[sds((nodes, f_out), BF)] + [sds((chan_width, nodes), BF)] * chans,
+        in_specs=[smem()] + [vmem()] * 3,
+        out_specs=[vmem()] * (1 + chans),
+        scratch_shapes=[pltpu.VMEM((f_in, nodes), BF)],
+        compiler_params=params(BIG),
+        cost_estimate=cost(layer_flops, 3 * MIB),
+        name="side_grads",
+    )(me, w_self, out_t, grad_t)
     for level in range(len(halves), len(order) - 1):
         got = lax.ppermute(total, "dom", flips[level])
         total = add_round(add_pair_kernel, total, got)
-    scaled, total, out_h = lax.optimization_barrier((scaled, total, out_h))
+    scaled, total, side = lax.optimization_barrier((scaled, total, side))
+    out_h = side[0]
     got = lax.ppermute(total, "dom", flips[-1])
     own_grad, far_grad = pl.pallas_call(
         scatter_kernel,
@@ -458,13 +478,13 @@
 
     packed = pl.pallas_call(
         functools.partial(message_kernel, chans),
-        out_shape=[sds((pieces * unit, lanes), BF)] * chans,
-        in_specs=[smem(), vmem()],
+        out_shape=[sds((chan_width, nodes + lanes), BF)] * chans,
+        in_specs=[smem()] + [vmem()] * (1 + chans),
         out_specs=[vmem()] * chans,
         compiler_params=params(BIG),
         cost_estimate=cost(0, MIB),
         name="pack_messages",
-    )(me, total)
+    )(me, total, *side[1:])
     packed = exchange(packed)
     held = pl.pallas_call(
         unit_kernel,
@@ -476,17 +496,19 @@
         name="weight_sum",
     )(*packed).reshape(1, pieces * unit, lanes)
     near = pl.pallas_call(
-        near_kernel,
+        functools.partial(near_kernel, chans),
         out_shape=sds((block_rows, chan_width, size), F32),
-        in_specs=[smem()] + [vmem()] * 3,
+        in_specs=[smem()] + [vmem()] * (1 + chans),
         out_specs=vmem(),
         compiler_params=params(BIG),
         cost_estimate=cost(0, 3 * MIB),
         name="sum_near",
-    )(me, w_self, grad_all, own_grad)
+    )(me, own_grad, *packed)
     held, near = lax.optimization_barrier((held, near))
     for level in reversed(range(len(halves))):
         held = jnp.concatenate([held, lax.ppermute(held, "dom", flips[level])], axis=0)
+        if level == len(halves) - 1:
+            held, back = lax.optimization_barrier((held, back))
     address = jnp.int32(0)
     for level in range(len(halves)):
         address = address * 2 + bits[level][0]

time: 162 us -> 152 us (0.938)
  between operations: 14.4 us -> 0.99 us
  local copies, waits for them, and re-layouts: 8.69 us -> 13.7 us
    unnamed x40 -> x58, local copies, waits for them, and re-layouts: 8.56 us -> 13.5 us
    ppermute x14, starting transfers between devices: 31.5 us -> 35.5 us  [exchange(): lax.ppermute(chunks[shift], 'chan', [(i, (i + shift) % count) for i in ra...]
    ppermute x3, waiting for transfers between devices: 8.53 us -> 4.96 us  [per_device(): lax.ppermute(held, 'dom', flips[level])]
    all_to_all x1, starting transfers between devices: 9.05 us -> 5.57 us  [per_device(): lax.all_to_all(far_grad.reshape(parts, slots, chan_width, size), 'dom', s...]
    ppermute x14, waiting for transfers between devices: 8.36 us -> 11.2 us  [exchange(): lax.ppermute(chunks[shift], 'chan', [(i, (i + shift) % count) for i in ra...]
  transfers between devices with their start and end apart: 26 -> 25, of which waited for: 11 -> 11; matrix products, arithmetic and copies ran while one was open for 0% -> 0% of each run, Pallas kernels for 9% -> 8%
where the time goes in v3:
time: 152 us; the launch traced here: 149 us
  starting transfers between devices  62.3 us (41%)
  waiting for transfers between devices  28.4 us (19%)
  Pallas kernels  22.9 us (15%)
  blocking collectives  21.1 us (14%)
  local copies, waits for them, and re-layouts  13.7 us (9%)
    ppermute x14, starting transfers between devices, exchange(): lax.ppermute(chunks[shift], 'chan', [(i, (i + shift) % count) for i in ra...  35.5 us
    all_to_all x1, blocking collectives, per_device(): lax.all_to_all(mean, 'chan', split_axis=0, concat_axis=0, tiled=True)  21.1 us
    unnamed x58, local copies, waits for them, and re-layouts  13.5 us
    ppermute x14, waiting for transfers between devices, exchange(): lax.ppermute(chunks[shift], 'chan', [(i, (i + shift) % count) for i in ra...  11.2 us
    all_to_all x1, starting transfers between devices, per_device(): lax.all_to_all(outgoing, 'dom', split_axis=0, concat_axis=0, tiled=True)  7.76 us
    ppermute x2, waiting for transfers between devices, per_device(): got = lax.ppermute(give, 'dom', flips[level - 1])  6.71 us
    pallas_call x1, Pallas kernels, per_device(): pl.pallas_call(scatter_kernel, out_shape=[pltpu.HBM((block_rows, chan_wid...  6.42 us
    all_to_all x1, starting transfers between devices, per_device(): lax.all_to_all(far_grad.reshape(parts, slots, chan_width, size), 'dom', s...  5.57 us
  transfers between devices with their start and end apart: 25, of which 11 were waited for; matrix products, arithmetic and copies ran while one was open for 0% of the time, Pallas kernels for 8%

profile of v3, /device:TPU:2, one launch (start us, length us, event | category | flops | bytes accessed | tf_op | source)
XLA Modules:
  0.0 149.3 jit_solution(6823403872055559663)
XLA Ops:
  0.6 2.5 %pack_outgoing.1 = bf16[32,4,64,128]{3,2,1,0:T(8,128)(2,1)} custom-call(s32[4,32]{1,0:T(4,128)} %bitcast.27, bf16[64,4096]{1,0:T(8,128)(2,1)} %bitcast.20), custom_call_target="tpu_custom_call" | custom-call | bytes 5242880 | tf_op jit(solution)/shard_map/pack_outgoing/pallas_call | solution.py:342
  3.2 7.8 %all-to-all-start = ((bf16[32,4,64,128]{3,2,1,0:T(8,128)(2,1)}), bf16[32,4,64,128]{3,2,1,0:T(8,128)(2,1)S(1)}, u32[]{:S(2)}, u32[]{:S(2)}) async-start(bf16[32,4,64,128]{3,2,1,0:T(8,128)(2,1)} %pack_outgoing.1), calls=%async_computation | async-start | bytes 4194304 | tf_op jit(solution)/shard_map/all_to_all | solution.py:355
  12.4 1.9 %collective-permute-start = (bf16[64,512]{1,0:T(8,128)(2,1)S(1)}, bf16[64,512]{1,0:T(8,128)(2,1)S(1)}, u32[]{:S(2)}, u32[]{:S(2)}) collective-permute-start(bf16[64,512]{1,0:T(8,128)(2,1)S(1)} %get-tuple-element.71), channel_id=1, source_target_pairs={{0,1},{1,2},{2,3},{3,4},{4,5},{5,6},{6,7},{7,0},{8,9},{9,10},{10,1... | collective-permute-start | bytes 196616 | tf_op jit(solution)/shard_map/ppermute | solution.py:293
  14.3 3.3 %collective-permute-start.1 = (bf16[64,512]{1,0:T(8,128)(2,1)S(1)}, bf16[64,512]{1,0:T(8,128)(2,1)S(1)}, u32[]{:S(2)}, u32[]{:S(2)}) collective-permute-start(bf16[64,512]{1,0:T(8,128)(2,1)S(1)} %get-tuple-element.72), channel_id=1, source_target_pairs={{0,2},{1,3},{2,4},{3,5},{4,6},{5,7},{6,0},{7,1},{8,10},{9,11},{10,... | collective-permute-start | bytes 196616 | tf_op jit(solution)/shard_map/ppermute | solution.py:293
  17.6 4.0 %collective-permute-start.2 = (bf16[64,512]{1,0:T(8,128)(2,1)}, bf16[64,512]{1,0:T(8,128)(2,1)S(1)}, u32[]{:S(2)}, u32[]{:S(2)}) collective-permute-start(bf16[64,512]{1,0:T(8,128)(2,1)} %get-tuple-element.73), channel_id=1, source_target_pairs={{0,3},{1,4},{2,5},{3,6},{4,7},{5,0},{6,1},{7,2},{8,11},{9,12},{10,... | collective-permute-start | bytes 196616 | tf_op jit(solution)/shard_map/ppermute | solution.py:293
  22.2 4.9 %collective-permute-start.4 = (bf16[64,512]{1,0:T(8,128)(2,1)}, bf16[64,512]{1,0:T(8,128)(2,1)S(1)}, u32[]{:S(2)}, u32[]{:S(2)}) collective-permute-start(bf16[64,512]{1,0:T(8,128)(2,1)} %get-tuple-element.75), channel_id=1, source_target_pairs={{0,5},{1,6},{2,7},{3,0},{4,1},{5,2},{6,3},{7,4},{8,13},{9,14},{10,... | collective-permute-start | bytes 196616 | tf_op jit(solution)/shard_map/ppermute | solution.py:293
  27.7 2.7 %collective-permute-start.5 = (bf16[64,512]{1,0:T(8,128)(2,1)}, bf16[64,512]{1,0:T(8,128)(2,1)S(1)}, u32[]{:S(2)}, u32[]{:S(2)}) collective-permute-start(bf16[64,512]{1,0:T(8,128)(2,1)} %get-tuple-element.76), channel_id=1, source_target_pairs={{0,6},{1,7},{2,0},{3,1},{4,2},{5,3},{6,4},{7,5},{8,14},{9,15},{10,... | collective-permute-start | bytes 196616 | tf_op jit(solution)/shard_map/ppermute | solution.py:293
  31.0 1.0 collective-permute-start.6
  33.4 3.0 %collective-permute-done.4.refs_5_ = bf16[64,512]{1,0:T(8,128)(2,1)S(1)} collective-permute-done((bf16[64,512]{1,0:T(8,128)(2,1)}, bf16[64,512]{1,0:T(8,128)(2,1)S(1)}, u32[]{:S(2)}, u32[]{:S(2)}) %collective-permute-start.4) | collective-permute-done | bytes 65568 | tf_op jit(solution)/shard_map/ppermute | solution.py:293
  37.7 0.9 copy-done.10
  38.7 0.8 copy-done.12
  39.5 0.8 copy-done.14
  40.3 0.8 copy-done.16
  41.2 0.8 copy-done.18
  42.0 0.8 copy-done.20
  42.9 0.8 copy-done.22
  43.7 0.8 copy-done.24
  44.5 1.2 self_part.1
  46.5 0.8 copy-done.6
  48.1 5.5 %neighbour_mean.1 = (bf16[8,64,512]{2,1,0:T(8,128)(2,1)S(1)}, f32[8,8,512]{2,1,0:T(8,128)S(1)}) custom-call(s32[8,32]{1,0:T(8,128)S(1)} %bitcast.25, s32[32]{0:T(128)S(1)} %copy-done.27, bf16[64,4096]{1,0:T(8,128)(2,1)S(1)} %bitcast.22, bf16[128,64,128]{2,1,0:T(8,128)(2,1)S(1)} %bitcast.17, bf16[32,8,128,128]{3,2,1,0:T(8,128)(2,1)} %vals_ref.3), custom_call_target="tpu_custom_call" | custom-call | flops 536870912 | bytes 11534336 | tf_op jit(solution)/shard_map/neighbour_mean/pallas_call | solution.py:380
  53.6 21.1 %all_to_all.20 = bf16[8,64,512]{2,1,0:T(8,128)(2,1)S(1)} all-to-all(bf16[8,64,512]{2,1,0:T(8,128)(2,1)S(1)} %get-tuple-element.87), channel_id=1, replica_groups=mesh['dom'=32,'chan'=8] {'chan'}, dimensions={0} | all-to-all | bytes 1048576 | tf_op jit(solution)/shard_map/all_to_all | solution.py:390
  74.7 1.8 %layer_head.1 = (bf16[256,512]{1,0:T(8,128)(2,1)S(1)}, bf16[256,512]{1,0:T(8,128)(2,1)S(1)}, bf16[512,512]{1,0:T(8,128)(2,1)}) custom-call(s32[1]{0:T(128)} %bitcast.me_ref, f32[8,8,512]{2,1,0:T(8,128)S(1)} %get-tuple-element.83.degree_ref, f32[256,512]{1,0:T(8,128)S(1)} %copy-done.7, bf16[256,512]{1,0:T(8,128)(2,1)S(1)} %get-tuple-element.85.turned_ref, ...), custom_call_target="tpu_custom_call" | custom-call | flops 268435456 | bytes 4194304 | tf_op jit(solution)/shard_map/layer_head/pallas_call | solution.py:392
  76.5 3.5 %all-to-all-start.2 = ((bf16[8,64,512]{2,1,0:T(8,128)(2,1)}), bf16[8,64,512]{2,1,0:T(8,128)(2,1)S(1)}, u32[]{:S(2)}, u32[]{:S(2)}) async-start(bf16[8,64,512]{2,1,0:T(8,128)(2,1)} %bitcast.8), calls=%async_computation.2 | async-start | bytes 1048576 | tf_op jit(solution)/shard_map/all_to_all | solution.py:401
  80.6 1.5 %collective-permute-done.7.recv_ref = bf16[16,8,8,128]{3,2,1,0:T(8,128)(2,1)S(1)} collective-permute-done((bf16[16,8,8,128]{3,2,1,0:T(8,128)(2,1)S(1)}, bf16[16,8,8,128]{3,2,1,0:T(8,128)(2,1)S(1)}, u32[]{:S(2)}, u32[]{:S(2)}) %collective-permute-start.7) | collective-permute-done | bytes 262176 | tf_op jit(solution)/shard_map/ppermute | solution.py:422
  82.7 5.2 %collective-permute-done.8.recv_ref = bf16[8,8,8,128]{3,2,1,0:T(8,128)(2,1)S(1)} collective-permute-done((bf16[8,8,8,128]{3,2,1,0:T(8,128)(2,1)S(1)}, bf16[8,8,8,128]{3,2,1,0:T(8,128)(2,1)S(1)}, u32[]{:S(2)}, u32[]{:S(2)}) %collective-permute-start.8) | collective-permute-done | bytes 131104 | tf_op jit(solution)/shard_map/ppermute | solution.py:422
  87.9 1.6 %collective-permute-start.9 = (bf16[4,8,8,128]{3,2,1,0:T(8,128)(2,1)S(1)}, bf16[4,8,8,128]{3,2,1,0:T(8,128)(2,1)S(1)}, u32[]{:S(2)}, u32[]{:S(2)}) collective-permute-start(bf16[4,8,8,128]{3,2,1,0:T(8,128)(2,1)S(1)} %get-tuple-element.96), channel_id=1, source_target_pairs={{0,64},{8,72},{16,80},{24,88},{32,96},{40,104},{48,112},{56,120},{... | collective-permute-start | bytes 196616 | tf_op jit(solution)/shard_map/ppermute | solution.py:434
  89.5 2.8 %collective-permute-done.9.recv_ref = bf16[4,8,8,128]{3,2,1,0:T(8,128)(2,1)S(1)} collective-permute-done((bf16[4,8,8,128]{3,2,1,0:T(8,128)(2,1)S(1)}, bf16[4,8,8,128]{3,2,1,0:T(8,128)(2,1)S(1)}, u32[]{:S(2)}, u32[]{:S(2)}) %collective-permute-start.9) | collective-permute-done | bytes 65568 | tf_op jit(solution)/shard_map/ppermute | solution.py:434
  92.3 2.2 %collective-permute-start.10 = (bf16[4,8,8,128]{3,2,1,0:T(8,128)(2,1)S(1)}, bf16[4,8,8,128]{3,2,1,0:T(8,128)(2,1)S(1)}, u32[]{:S(2)}, u32[]{:S(2)}) collective-permute-start(bf16[4,8,8,128]{3,2,1,0:T(8,128)(2,1)S(1)} %weight_add.3.held_ref), channel_id=1, source_target_pairs={{0,32},{8,40},{16,48},{24,56},{32,0},{40,8},{48,16},{56,24},{64,96... | collective-permute-start | bytes 196616 | tf_op jit(solution)/shard_map/ppermute | solution.py:448
  94.4 0.9 side_grads.1
  95.4 2.8 %collective-permute-done.10.recv_ref = bf16[4,8,8,128]{3,2,1,0:T(8,128)(2,1)S(1)} collective-permute-done((bf16[4,8,8,128]{3,2,1,0:T(8,128)(2,1)S(1)}, bf16[4,8,8,128]{3,2,1,0:T(8,128)(2,1)S(1)}, u32[]{:S(2)}, u32[]{:S(2)}) %collective-permute-start.10) | collective-permute-done | bytes 65568 | tf_op jit(solution)/shard_map/ppermute | solution.py:448
  98.2 3.2 %collective-permute-start.11 = (bf16[4,8,8,128]{3,2,1,0:T(8,128)(2,1)S(1)}, bf16[4,8,8,128]{3,2,1,0:T(8,128)(2,1)S(1)}, u32[]{:S(2)}, u32[]{:S(2)}) collective-permute-start(bf16[4,8,8,128]{3,2,1,0:T(8,128)(2,1)S(1)} %weight_add.4.held_ref), channel_id=1, source_target_pairs={{0,128},{8,136},{16,144},{24,152},{32,160},{40,168},{48,176},{56,1... | collective-permute-start | bytes 196616 | tf_op jit(solution)/shard_map/ppermute | solution.py:452
  101.4 6.4 %table_grad.1 = (f32[32,64,128]{2,1,0:T(8,128)}, bf16[128,64,128]{2,1,0:T(8,128)(2,1)}) custom-call(s32[8,32]{1,0:T(8,128)S(1)} %bitcast.26, s32[32]{0:T(128)S(1)} %copy-done.27, bf16[32,8,128,128]{3,2,1,0:T(8,128)(2,1)} %vals_ref.3, bf16[8,64,512]{2,1,0:T(8,128)(2,1)S(1)} %all-to-all-done.2.scaled_ref), custom_call_target="tpu_custom_call" | custom-call | flops 536870912 | bytes 12582912 | tf_op jit(solution)/shard_map/table_grad/pallas_call | solution.py:453
  107.9 5.6 %all-to-all-start.3 = ((bf16[32,4,64,128]{3,2,1,0:T(8,128)(2,1)}), bf16[32,4,64,128]{3,2,1,0:T(8,128)(2,1)S(1)}, u32[]{:S(2)}, u32[]{:S(2)}) async-start(bf16[32,4,64,128]{3,2,1,0:T(8,128)(2,1)} %bitcast.29), calls=%async_computation.3 | async-start | bytes 4194304 | tf_op jit(solution)/shard_map/all_to_all | solution.py:475
  113.5 2.0 %collective-permute-start.12 = (bf16[64,640]{1,0:T(8,128)(2,1)S(1)}, bf16[64,640]{1,0:T(8,128)(2,1)S(1)}, u32[]{:S(2)}, u32[]{:S(2)}) collective-permute-start(bf16[64,640]{1,0:T(8,128)(2,1)S(1)} %get-tuple-element.121), channel_id=1, source_target_pairs={{0,1},{1,2},{2,3},{3,4},{4,5},{5,6},{6,7},{7,0},{8,9},{9,10},{10,1... | collective-permute-start | bytes 245768 | tf_op jit(solution)/shard_map/ppermute | solution.py:293
  115.5 2.4 %collective-permute-start.13 = (bf16[64,640]{1,0:T(8,128)(2,1)S(1)}, bf16[64,640]{1,0:T(8,128)(2,1)S(1)}, u32[]{:S(2)}, u32[]{:S(2)}) collective-permute-start(bf16[64,640]{1,0:T(8,128)(2,1)S(1)} %get-tuple-element.122), channel_id=1, source_target_pairs={{0,2},{1,3},{2,4},{3,5},{4,6},{5,7},{6,0},{7,1},{8,10},{9,11},{10,... | collective-permute-start | bytes 245768 | tf_op jit(solution)/shard_map/ppermute | solution.py:293
  117.9 2.7 %collective-permute-start.14 = (bf16[64,640]{1,0:T(8,128)(2,1)S(1)}, bf16[64,640]{1,0:T(8,128)(2,1)S(1)}, u32[]{:S(2)}, u32[]{:S(2)}) collective-permute-start(bf16[64,640]{1,0:T(8,128)(2,1)S(1)} %get-tuple-element.123), channel_id=1, source_target_pairs={{0,3},{1,4},{2,5},{3,6},{4,7},{5,0},{6,1},{7,2},{8,11},{9,12},{10,... | collective-permute-start | bytes 245768 | tf_op jit(solution)/shard_map/ppermute | solution.py:293
  120.6 2.3 %collective-permute-start.15 = (bf16[64,640]{1,0:T(8,128)(2,1)S(1)}, bf16[64,640]{1,0:T(8,128)(2,1)S(1)}, u32[]{:S(2)}, u32[]{:S(2)}) collective-permute-start(bf16[64,640]{1,0:T(8,128)(2,1)S(1)} %get-tuple-element.124), channel_id=1, source_target_pairs={{0,4},{1,5},{2,6},{3,7},{4,0},{5,1},{6,2},{7,3},{8,12},{9,13},{10,... | collective-permute-start | bytes 245768 | tf_op jit(solution)/shard_map/ppermute | solution.py:293
  122.9 2.7 %collective-permute-start.16 = (bf16[64,640]{1,0:T(8,128)(2,1)S(1)}, bf16[64,640]{1,0:T(8,128)(2,1)S(1)}, u32[]{:S(2)}, u32[]{:S(2)}) collective-permute-start(bf16[64,640]{1,0:T(8,128)(2,1)S(1)} %get-tuple-element.125), channel_id=1, source_target_pairs={{0,5},{1,6},{2,7},{3,0},{4,1},{5,2},{6,3},{7,4},{8,13},{9,14},{10,... | collective-permute-start | bytes 245768 | tf_op jit(solution)/shard_map/ppermute | solution.py:293
  125.6 3.6 %collective-permute-start.17 = (bf16[64,640]{1,0:T(8,128)(2,1)S(1)}, bf16[64,640]{1,0:T(8,128)(2,1)S(1)}, u32[]{:S(2)}, u32[]{:S(2)}) collective-permute-start(bf16[64,640]{1,0:T(8,128)(2,1)S(1)} %get-tuple-element.126), channel_id=1, source_target_pairs={{0,6},{1,7},{2,0},{3,1},{4,2},{5,3},{6,4},{7,5},{8,14},{9,15},{10,... | collective-permute-start | bytes 245768 | tf_op jit(solution)/shard_map/ppermute | solution.py:293
  129.2 1.4 collective-permute-start.18
  130.7 1.7 %collective-permute-done.15.refs_4_ = bf16[64,640]{1,0:T(8,128)(2,1)S(1)} collective-permute-done((bf16[64,640]{1,0:T(8,128)(2,1)S(1)}, bf16[64,640]{1,0:T(8,128)(2,1)S(1)}, u32[]{:S(2)}, u32[]{:S(2)}) %collective-permute-start.15) | collective-permute-done | bytes 81952 | tf_op jit(solution)/shard_map/ppermute | solution.py:293
  132.3 4.8 %collective-permute-done.16.refs_5_ = bf16[64,640]{1,0:T(8,128)(2,1)S(1)} collective-permute-done((bf16[64,640]{1,0:T(8,128)(2,1)S(1)}, bf16[64,640]{1,0:T(8,128)(2,1)S(1)}, u32[]{:S(2)}, u32[]{:S(2)}) %collective-permute-start.16) | collective-permute-done | bytes 81952 | tf_op jit(solution)/shard_map/ppermute | solution.py:293
  137.2 1.2 collective-permute-done.17.refs_6_
  138.9 1.6 %collective-permute-start.19 = (bf16[1,32,128]{2,1,0:T(8,128)(2,1)S(1)}, bf16[1,32,128]{2,1,0:T(8,128)(2,1)S(1)}, u32[]{:S(2)}, u32[]{:S(2)}) collective-permute-start(bf16[1,32,128]{2,1,0:T(8,128)(2,1)S(1)} %bitcast.23), channel_id=1, source_target_pairs={{0,64},{8,72},{16,80},{24,88},{32,96},{40,104},{48,112},{56,120},{... | collective-permute-start | bytes 24584 | tf_op jit(solution)/shard_map/ppermute | solution.py:509
  140.5 2.2 %collective-permute-done.19 = bf16[1,32,128]{2,1,0:T(8,128)(2,1)S(1)} collective-permute-done((bf16[1,32,128]{2,1,0:T(8,128)(2,1)S(1)}, bf16[1,32,128]{2,1,0:T(8,128)(2,1)S(1)}, u32[]{:S(2)}, u32[]{:S(2)}) %collective-permute-start.19) | collective-permute-done | bytes 8224 | tf_op jit(solution)/shard_map/ppermute | solution.py:509
  142.7 1.0 collective-permute-start.20
  143.7 2.8 %collective-permute-done.20 = bf16[2,32,128]{2,1,0:T(8,128)(2,1)S(1)} collective-permute-done((bf16[2,32,128]{2,1,0:T(8,128)(2,1)S(1)}, bf16[2,32,128]{2,1,0:T(8,128)(2,1)S(1)}, u32[]{:S(2)}, u32[]{:S(2)}) %collective-permute-start.20) | collective-permute-done | bytes 16416 | tf_op jit(solution)/shard_map/ppermute | solution.py:509
  146.5 2.2 %sum_returned.1 = bf16[64,4096]{1,0:T(8,128)(2,1)} custom-call(s32[4,32]{1,0:T(4,128)S(1)} %bitcast.28, f32[32,64,128]{2,1,0:T(8,128)S(1)} %sum_near.1.near_ref, bf16[32,4,64,128]{3,2,1,0:T(8,128)(2,1)S(1)} %all-to-all-done.3.back_ref), custom_call_target="tpu_custom_call" | custom-call | bytes 4194304 | tf_op jit(solution)/shard_map/sum_returned/pallas_call | solution.py:525
  (83 shorter events, 9.9 us)
Async XLA Ops:
  3.2 7.9 %copy-start = (bf16[4096,64]{0,1:T(8,128)(2,1)S(1)}, bf16[4096,64]{0,1:T(8,128)(2,1)}, u32[]{:S(2)}) copy-start(bf16[4096,64]{0,1:T(8,128)(2,1)} %param.9) | copy-start | bytes 1572868
  3.2 28.8 %copy-start.28 = (f32[256]{0:T(256)S(1)}, f32[256]{0:T(256)}, u32[]{:S(2)}) copy-start(f32[256]{0:T(256)} %param.16) | copy-start | bytes 3076
  3.2 34.5 %copy-start.2 = (bf16[512,256]{1,0:T(8,128)(2,1)S(1)}, bf16[512,256]{1,0:T(8,128)(2,1)}, u32[]{:S(2)}) copy-start(bf16[512,256]{1,0:T(8,128)(2,1)} %weight_ref.4) | copy-start | bytes 786436
  3.2 34.5 %copy-start.3 = (bf16[512,256]{1,0:T(8,128)(2,1)S(1)}, bf16[512,256]{1,0:T(8,128)(2,1)}, u32[]{:S(2)}) copy-start(bf16[512,256]{1,0:T(8,128)(2,1)} %weight_ref.5) | copy-start | bytes 786436
  3.2 44.8 %all-to-all-start = ((bf16[32,4,64,128]{3,2,1,0:T(8,128)(2,1)}), bf16[32,4,64,128]{3,2,1,0:T(8,128)(2,1)S(1)}, u32[]{:S(2)}, u32[]{:S(2)}) async-start(bf16[32,4,64,128]{3,2,1,0:T(8,128)(2,1)} %pack_outgoing.1), calls=%async_computation | async-start | bytes 4194304 | tf_op jit(solution)/shard_map/all_to_all | solution.py:355
  11.0 37.0 %copy-start.25 = (s32[32,8]{0,1:T(8,128)S(1)}, s32[32,8]{0,1:T(8,128)}, u32[]{:S(2)}) copy-start(s32[32,8]{0,1:T(8,128)} %param.11) | copy-start | bytes 3076
  11.0 37.0 %copy-start.27 = (s32[32]{0:T(128)S(1)}, s32[32]{0:T(128)}, u32[]{:S(2)}) copy-start(s32[32]{0:T(128)} %counts_ref.3) | copy-start | bytes 388
  12.4 14.7 %collective-permute-start = (bf16[64,512]{1,0:T(8,128)(2,1)S(1)}, bf16[64,512]{1,0:T(8,128)(2,1)S(1)}, u32[]{:S(2)}, u32[]{:S(2)}) collective-permute-start(bf16[64,512]{1,0:T(8,128)(2,1)S(1)} %get-tuple-element.71), channel_id=1, source_target_pairs={{0,1},{1,2},{2,3},{3,4},{4,5},{5,6},{6,7},{7,0},{8,9},{9,10},{10,1... | collective-permute-start | bytes 196616 | tf_op jit(solution)/shard_map/ppermute | solution.py:293
  14.3 16.1 %collective-permute-start.1 = (bf16[64,512]{1,0:T(8,128)(2,1)S(1)}, bf16[64,512]{1,0:T(8,128)(2,1)S(1)}, u32[]{:S(2)}, u32[]{:S(2)}) collective-permute-start(bf16[64,512]{1,0:T(8,128)(2,1)S(1)} %get-tuple-element.72), channel_id=1, source_target_pairs={{0,2},{1,3},{2,4},{3,5},{4,6},{5,7},{6,0},{7,1},{8,10},{9,11},{10,... | collective-permute-start | bytes 196616 | tf_op jit(solution)/shard_map/ppermute | solution.py:293
  17.6 14.6 %collective-permute-start.2 = (bf16[64,512]{1,0:T(8,128)(2,1)}, bf16[64,512]{1,0:T(8,128)(2,1)S(1)}, u32[]{:S(2)}, u32[]{:S(2)}) collective-permute-start(bf16[64,512]{1,0:T(8,128)(2,1)} %get-tuple-element.73), channel_id=1, source_target_pairs={{0,3},{1,4},{2,5},{3,6},{4,7},{5,0},{6,1},{7,2},{8,11},{9,12},{10,... | collective-permute-start | bytes 196616 | tf_op jit(solution)/shard_map/ppermute | solution.py:293
  21.6 11.2 %collective-permute-start.3 = (bf16[64,512]{1,0:T(8,128)(2,1)}, bf16[64,512]{1,0:T(8,128)(2,1)S(1)}, u32[]{:S(2)}, u32[]{:S(2)}) collective-permute-start(bf16[64,512]{1,0:T(8,128)(2,1)} %get-tuple-element.74), channel_id=1, source_target_pairs={{0,4},{1,5},{2,6},{3,7},{4,0},{5,1},{6,2},{7,3},{8,12},{9,13},{10,... | collective-permute-start | bytes 196616 | tf_op jit(solution)/shard_map/ppermute | solution.py:293
  22.2 14.3 %collective-permute-start.4 = (bf16[64,512]{1,0:T(8,128)(2,1)}, bf16[64,512]{1,0:T(8,128)(2,1)S(1)}, u32[]{:S(2)}, u32[]{:S(2)}) collective-permute-start(bf16[64,512]{1,0:T(8,128)(2,1)} %get-tuple-element.75), channel_id=1, source_target_pairs={{0,5},{1,6},{2,7},{3,0},{4,1},{5,2},{6,3},{7,4},{8,13},{9,14},{10,... | collective-permute-start | bytes 196616 | tf_op jit(solution)/shard_map/ppermute | solution.py:293
  27.7 9.3 %collective-permute-start.5 = (bf16[64,512]{1,0:T(8,128)(2,1)}, bf16[64,512]{1,0:T(8,128)(2,1)S(1)}, u32[]{:S(2)}, u32[]{:S(2)}) collective-permute-start(bf16[64,512]{1,0:T(8,128)(2,1)} %get-tuple-element.76), channel_id=1, source_target_pairs={{0,6},{1,7},{2,0},{3,1},{4,2},{5,3},{6,4},{7,5},{8,14},{9,15},{10,... | collective-permute-start | bytes 196616 | tf_op jit(solution)/shard_map/ppermute | solution.py:293
  31.0 6.7 %collective-permute-start.6 = (bf16[64,512]{1,0:T(8,128)(2,1)}, bf16[64,512]{1,0:T(8,128)(2,1)}, u32[]{:S(2)}, u32[]{:S(2)}) collective-permute-start(bf16[64,512]{1,0:T(8,128)(2,1)} %get-tuple-element.77), channel_id=1, source_target_pairs={{0,7},{1,0},{2,1},{3,2},{4,3},{5,4},{6,5},{7,6},{8,15},{9,8},{10,9... | collective-permute-start | bytes 196616 | tf_op jit(solution)/shard_map/ppermute | solution.py:293
  32.2 0.6 copy-start.17
  37.7 1.0 copy-start.10
  38.7 0.8 copy-start.12
  39.5 0.8 copy-start.14
  40.3 0.8 copy-start.16
  41.2 0.8 copy-start.18
  42.0 0.8 copy-start.20
  42.9 0.8 copy-start.22
  43.7 0.8 copy-start.24
  45.7 0.8 copy-start.4
  46.5 0.8 copy-start.6
  47.3 0.7 copy-start.8
  48.0 26.6 %copy-start.7 = (f32[256,512]{1,0:T(8,128)S(1)}, f32[256,512]{1,0:T(8,128)}, u32[]{:S(2)}) copy-start(f32[256,512]{1,0:T(8,128)} %copy-done.6) | copy-start | bytes 1572868
  48.0 26.6 %copy-start.9 = (bf16[256,512]{1,0:T(8,128)(2,1)S(1)}, bf16[256,512]{1,0:T(8,128)(2,1)}, u32[]{:S(2)}) copy-start(bf16[256,512]{1,0:T(8,128)(2,1)} %copy-done.8) | copy-start | bytes 786436
  53.6 26.4 %copy-start.5 = (bf16[512,512]{1,0:T(8,128)(2,1)S(1)}, bf16[512,512]{1,0:T(8,128)(2,1)}, u32[]{:S(2)}) copy-start(bf16[512,512]{1,0:T(8,128)(2,1)} %copy-done.4) | copy-start | bytes 1572868
  76.5 21.7 %all-to-all-start.2 = ((bf16[8,64,512]{2,1,0:T(8,128)(2,1)}), bf16[8,64,512]{2,1,0:T(8,128)(2,1)S(1)}, u32[]{:S(2)}, u32[]{:S(2)}) async-start(bf16[8,64,512]{2,1,0:T(8,128)(2,1)} %bitcast.8), calls=%async_computation.2 | async-start | bytes 1048576 | tf_op jit(solution)/shard_map/all_to_all | solution.py:401
  80.5 1.6 %collective-permute-start.7 = (bf16[16,8,8,128]{3,2,1,0:T(8,128)(2,1)S(1)}, bf16[16,8,8,128]{3,2,1,0:T(8,128)(2,1)S(1)}, u32[]{:S(2)}, u32[]{:S(2)}) collective-permute-start(bf16[16,8,8,128]{3,2,1,0:T(8,128)(2,1)S(1)} %get-tuple-element.92), channel_id=1, source_target_pairs={{0,8},{8,0},{16,24},{24,16},{32,40},{40,32},{48,56},{56,48},{64,72... | collective-permute-start | bytes 786440 | tf_op jit(solution)/shard_map/ppermute | solution.py:422
  82.2 5.6 %collective-permute-start.8 = (bf16[8,8,8,128]{3,2,1,0:T(8,128)(2,1)S(1)}, bf16[8,8,8,128]{3,2,1,0:T(8,128)(2,1)S(1)}, u32[]{:S(2)}, u32[]{:S(2)}) collective-permute-start(bf16[8,8,8,128]{3,2,1,0:T(8,128)(2,1)S(1)} %get-tuple-element.94), channel_id=1, source_target_pairs={{0,16},{8,24},{16,0},{24,8},{32,48},{40,56},{48,32},{56,40},{64,80... | collective-permute-start | bytes 393224 | tf_op jit(solution)/shard_map/ppermute | solution.py:422
  87.9 4.4 %collective-permute-start.9 = (bf16[4,8,8,128]{3,2,1,0:T(8,128)(2,1)S(1)}, bf16[4,8,8,128]{3,2,1,0:T(8,128)(2,1)S(1)}, u32[]{:S(2)}, u32[]{:S(2)}) collective-permute-start(bf16[4,8,8,128]{3,2,1,0:T(8,128)(2,1)S(1)} %get-tuple-element.96), channel_id=1, source_target_pairs={{0,64},{8,72},{16,80},{24,88},{32,96},{40,104},{48,112},{56,120},{... | collective-permute-start | bytes 196616 | tf_op jit(solution)/shard_map/ppermute | solution.py:434
  92.3 5.9 %collective-permute-start.10 = (bf16[4,8,8,128]{3,2,1,0:T(8,128)(2,1)S(1)}, bf16[4,8,8,128]{3,2,1,0:T(8,128)(2,1)S(1)}, u32[]{:S(2)}, u32[]{:S(2)}) collective-permute-start(bf16[4,8,8,128]{3,2,1,0:T(8,128)(2,1)S(1)} %weight_add.3.held_ref), channel_id=1, source_target_pairs={{0,32},{8,40},{16,48},{24,56},{32,0},{40,8},{48,16},{56,24},{64,96... | collective-permute-start | bytes 196616 | tf_op jit(solution)/shard_map/ppermute | solution.py:448
  98.2 9.7 %collective-permute-start.11 = (bf16[4,8,8,128]{3,2,1,0:T(8,128)(2,1)S(1)}, bf16[4,8,8,128]{3,2,1,0:T(8,128)(2,1)S(1)}, u32[]{:S(2)}, u32[]{:S(2)}) collective-permute-start(bf16[4,8,8,128]{3,2,1,0:T(8,128)(2,1)S(1)} %weight_add.4.held_ref), channel_id=1, source_target_pairs={{0,128},{8,136},{16,144},{24,152},{32,160},{40,168},{48,176},{56,1... | collective-permute-start | bytes 196616 | tf_op jit(solution)/shard_map/ppermute | solution.py:452
  107.9 34.8 %all-to-all-start.3 = ((bf16[32,4,64,128]{3,2,1,0:T(8,128)(2,1)}), bf16[32,4,64,128]{3,2,1,0:T(8,128)(2,1)S(1)}, u32[]{:S(2)}, u32[]{:S(2)}) async-start(bf16[32,4,64,128]{3,2,1,0:T(8,128)(2,1)} %bitcast.29), calls=%async_computation.3 | async-start | bytes 4194304 | tf_op jit(solution)/shard_map/all_to_all | solution.py:475
  113.4 25.4 %copy-start.1 = (f32[32,64,128]{2,1,0:T(8,128)S(1)}, f32[32,64,128]{2,1,0:T(8,128)}, u32[]{:S(2)}) copy-start(f32[32,64,128]{2,1,0:T(8,128)} %get-tuple-element.128.own_ref) | copy-start | bytes 3145732
  113.5 33.0 %copy-start.26 = (s32[1,32,4]{1,2,0:T(4,128)S(1)}, s32[1,32,4]{1,2,0:T(4,128)}, u32[]{:S(2)}) copy-start(s32[1,32,4]{1,2,0:T(4,128)} %param.13) | copy-start | bytes 1540
  113.5 12.1 %collective-permute-start.12 = (bf16[64,640]{1,0:T(8,128)(2,1)S(1)}, bf16[64,640]{1,0:T(8,128)(2,1)S(1)}, u32[]{:S(2)}, u32[]{:S(2)}) collective-permute-start(bf16[64,640]{1,0:T(8,128)(2,1)S(1)} %get-tuple-element.121), channel_id=1, source_target_pairs={{0,1},{1,2},{2,3},{3,4},{4,5},{5,6},{6,7},{7,0},{8,9},{9,10},{10,1... | collective-permute-start | bytes 245768 | tf_op jit(solution)/shard_map/ppermute | solution.py:293
  115.5 13.7 %collective-permute-start.13 = (bf16[64,640]{1,0:T(8,128)(2,1)S(1)}, bf16[64,640]{1,0:T(8,128)(2,1)S(1)}, u32[]{:S(2)}, u32[]{:S(2)}) collective-permute-start(bf16[64,640]{1,0:T(8,128)(2,1)S(1)} %get-tuple-element.122), channel_id=1, source_target_pairs={{0,2},{1,3},{2,4},{3,5},{4,6},{5,7},{6,0},{7,1},{8,10},{9,11},{10,... | collective-permute-start | bytes 245768 | tf_op jit(solution)/shard_map/ppermute | solution.py:293
  117.9 12.8 %collective-permute-start.14 = (bf16[64,640]{1,0:T(8,128)(2,1)S(1)}, bf16[64,640]{1,0:T(8,128)(2,1)S(1)}, u32[]{:S(2)}, u32[]{:S(2)}) collective-permute-start(bf16[64,640]{1,0:T(8,128)(2,1)S(1)} %get-tuple-element.123), channel_id=1, source_target_pairs={{0,3},{1,4},{2,5},{3,6},{4,7},{5,0},{6,1},{7,2},{8,11},{9,12},{10,... | collective-permute-start | bytes 245768 | tf_op jit(solution)/shard_map/ppermute | solution.py:293
  120.6 11.7 %collective-permute-start.15 = (bf16[64,640]{1,0:T(8,128)(2,1)S(1)}, bf16[64,640]{1,0:T(8,128)(2,1)S(1)}, u32[]{:S(2)}, u32[]{:S(2)}) collective-permute-start(bf16[64,640]{1,0:T(8,128)(2,1)S(1)} %get-tuple-element.124), channel_id=1, source_target_pairs={{0,4},{1,5},{2,6},{3,7},{4,0},{5,1},{6,2},{7,3},{8,12},{9,13},{10,... | collective-permute-start | bytes 245768 | tf_op jit(solution)/shard_map/ppermute | solution.py:293
  122.9 14.2 %collective-permute-start.16 = (bf16[64,640]{1,0:T(8,128)(2,1)S(1)}, bf16[64,640]{1,0:T(8,128)(2,1)S(1)}, u32[]{:S(2)}, u32[]{:S(2)}) collective-permute-start(bf16[64,640]{1,0:T(8,128)(2,1)S(1)} %get-tuple-element.125), channel_id=1, source_target_pairs={{0,5},{1,6},{2,7},{3,0},{4,1},{5,2},{6,3},{7,4},{8,13},{9,14},{10,... | collective-permute-start | bytes 245768 | tf_op jit(solution)/shard_map/ppermute | solution.py:293
  125.6 12.7 %collective-permute-start.17 = (bf16[64,640]{1,0:T(8,128)(2,1)S(1)}, bf16[64,640]{1,0:T(8,128)(2,1)S(1)}, u32[]{:S(2)}, u32[]{:S(2)}) collective-permute-start(bf16[64,640]{1,0:T(8,128)(2,1)S(1)} %get-tuple-element.126), channel_id=1, source_target_pairs={{0,6},{1,7},{2,0},{3,1},{4,2},{5,3},{6,4},{7,5},{8,14},{9,15},{10,... | collective-permute-start | bytes 245768 | tf_op jit(solution)/shard_map/ppermute | solution.py:293
  129.2 9.6 %collective-permute-start.18 = (bf16[64,640]{1,0:T(8,128)(2,1)S(1)}, bf16[64,640]{1,0:T(8,128)(2,1)S(1)}, u32[]{:S(2)}, u32[]{:S(2)}) collective-permute-start(bf16[64,640]{1,0:T(8,128)(2,1)S(1)} %get-tuple-element.127), channel_id=1, source_target_pairs={{0,7},{1,0},{2,1},{3,2},{4,3},{5,4},{6,5},{7,6},{8,15},{9,8},{10,9... | collective-permute-start | bytes 245768 | tf_op jit(solution)/shard_map/ppermute | solution.py:293
  138.9 3.7 %collective-permute-start.19 = (bf16[1,32,128]{2,1,0:T(8,128)(2,1)S(1)}, bf16[1,32,128]{2,1,0:T(8,128)(2,1)S(1)}, u32[]{:S(2)}, u32[]{:S(2)}) collective-permute-start(bf16[1,32,128]{2,1,0:T(8,128)(2,1)S(1)} %bitcast.23), channel_id=1, source_target_pairs={{0,64},{8,72},{16,80},{24,88},{32,96},{40,104},{48,112},{56,120},{... | collective-permute-start | bytes 24584 | tf_op jit(solution)/shard_map/ppermute | solution.py:509
  142.7 3.7 %collective-permute-start.20 = (bf16[2,32,128]{2,1,0:T(8,128)(2,1)S(1)}, bf16[2,32,128]{2,1,0:T(8,128)(2,1)S(1)}, u32[]{:S(2)}, u32[]{:S(2)}) collective-permute-start(bf16[2,32,128]{2,1,0:T(8,128)(2,1)S(1)} %pad_maximum_fusion.2), channel_id=1, source_target_pairs={{0,16},{8,24},{16,0},{24,8},{32,48},{40,56},{48,32},{56,40},{64,80... | collective-permute-start | bytes 49160 | tf_op jit(solution)/shard_map/ppermute | solution.py:509
  146.4 2.2 %collective-permute-start.21 = (bf16[4,32,128]{2,1,0:T(8,128)(2,1)S(1)}, bf16[4,32,128]{2,1,0:T(8,128)(2,1)S(1)}, u32[]{:S(2)}, u32[]{:S(2)}) collective-permute-start(bf16[4,32,128]{2,1,0:T(8,128)(2,1)S(1)} %pad_maximum_fusion.1), channel_id=1, source_target_pairs={{0,8},{8,0},{16,24},{24,16},{32,40},{40,32},{48,56},{56,48},{64,72... | collective-permute-start | bytes 98312 | tf_op jit(solution)/shard_map/ppermute | solution.py:509
  (6 other events, 3.7 us)

commit v4 on v3

--- a/solution.py
+++ b/solution.py
@@ -57,19 +57,26 @@
         pltpu.make_async_copy(hold_ref.at[place], out_ref.at[place], sems.at[copy]).wait()
 
 
-def split_kernel(me_ref, feats_ref, *out_refs):
+def split_kernel(me_ref, feats_ref, *refs):
+    out_refs, sems = refs[:-1], refs[-1]
     chans = len(out_refs)
     width = out_refs[0].shape[1]
-    for shift, out_ref in enumerate(out_refs):
+
+    def copy(shift):
         lane = pl.multiple_of(lax.rem(me_ref[0] + shift, chans) * width, width)
-        out_ref[...] = feats_ref[:, pl.ds(lane, width)]
+        return pltpu.make_async_copy(feats_ref.at[:, pl.ds(lane, width)], out_refs[shift], sems.at[shift])
+
+    for shift in range(chans):
+        copy(shift).start()
+    for shift in range(chans):
+        copy(shift).wait()
 
 
 def join_slots(vals_ref, row):
     return jnp.concatenate([vals_ref[row, k] for k in range(vals_ref.shape[1])], axis=1)
 
 
-def stream_rows(vals_ref, held_ref, sems, body, before=None):
+def stream_rows(vals_ref, held_ref, sems, body, before=None, after=None):
     copies = sems.shape[0]
     span = held_ref.shape[0] // copies
 
@@ -86,12 +93,16 @@
         copy(place).wait()
         for row in range(span):
             body(place * span + row)
+        if after is not None:
+            after(place)
         return carry
 
     lax.fori_loop(0, copies, one, 0)
 
 
-def gather_kernel(cols_ref, counts_ref, feats_ref, recv_ref, vals_ref, out_ref, degree_ref, held_ref, sems):
+def gather_kernel(
+    cols_ref, counts_ref, feats_ref, recv_ref, vals_ref, out_ref, degree_ref, held_ref, mean_ref, sems, out_sems
+):
     _, depth, size, _ = vals_ref.shape
     width = feats_ref.shape[0]
     rows = out_ref.shape[2] // size
@@ -112,9 +123,18 @@
         group = index // rows
         place = pl.ds(pl.multiple_of(lax.rem(index, rows) * size, size), size)
         degree_ref[group, :, place] = total[width : width + 8]
-        out_ref[group, :, place] = (total[:width] / total[width : width + 1]).astype(BF)
-
-    stream_rows(vals_ref, held_ref, sems, body)
+        mean_ref[group, :, place] = (total[:width] / total[width : width + 1]).astype(BF)
+
+    copies = out_sems.shape[0]
+    span = mean_ref.shape[0] // copies
+
+    def copy(place):
+        groups = pl.ds(place * span, span)
+        return pltpu.make_async_copy(mean_ref.at[groups], out_ref.at[groups], out_sems.at[place])
+
+    stream_rows(vals_ref, held_ref, sems, body, after=lambda place: copy(place).start())
+    for place in range(copies):
+        copy(place).wait()
 
 
 def self_kernel(chans, me_ref, weight_ref, bias_ref, neigh_ref, cot_ref, *refs):
@@ -356,14 +376,16 @@
 
     feat_chunks = pl.pallas_call(
         split_kernel,
-        out_shape=[sds((chan_width, nodes), BF)] * chans,
+        out_shape=[pltpu.HBM((chan_width, nodes), BF)] * chans,
         in_specs=[smem(), vmem()],
-        out_specs=[vmem()] * chans,
+        out_specs=[hbm()] * chans,
+        scratch_shapes=[pltpu.SemaphoreType.DMA((chans,))],
         compiler_params=params(BIG),
         cost_estimate=cost(0, MIB),
         name="split_feats",
     )(me, feats_t)
-    feat_chunks = exchange(feat_chunks)
+    incoming, feat_chunks = lax.optimization_barrier((incoming, exchange(feat_chunks)))
+    feat_chunks = [pltpu.with_memory_space_constraint(chunk, pltpu.HBM) for chunk in feat_chunks]
     feats_own, pre_self, neigh_turned, cot_turned = pl.pallas_call(
         functools.partial(self_kernel, chans),
         out_shape=[sds((f_in, nodes), BF), sds((f_out, nodes), F32), sds((f_out, f_in), BF), sds((f_out, nodes), BF)],
@@ -374,15 +396,17 @@
         name="self_part",
     )(me, w_self, bias.reshape(f_out, 1), w_neigh, cotangent, *feat_chunks)
 
-    incoming, pre_self, feats_own, neigh_turned, cot_turned = lax.optimization_barrier(
-        (incoming, pre_self, feats_own, neigh_turned, cot_turned)
-    )
     mean, degree = pl.pallas_call(
         gather_kernel,
-        out_shape=[sds((chans, chan_width, nodes), BF), sds((chans, 8, nodes), F32)],
+        out_shape=[pltpu.HBM((chans, chan_width, nodes), BF), sds((chans, 8, nodes), F32)],
         in_specs=[smem(), smem()] + [vmem()] * 2 + [hbm()],
-        out_specs=[vmem()] * 2,
-        scratch_shapes=[pltpu.VMEM(block_vals.shape, BF), pltpu.SemaphoreType.DMA((streams,))],
+        out_specs=[hbm(), vmem()],
+        scratch_shapes=[
+            pltpu.VMEM(block_vals.shape, BF),
+            pltpu.VMEM((chans, chan_width, nodes), BF),
+            pltpu.SemaphoreType.DMA((streams,)),
+            pltpu.SemaphoreType.DMA((streams,)),
+        ],
         compiler_params=params(16),
         cost_estimate=cost(block_flops, val_bytes + 3 * MIB),
         name="neighbour_mean",
@@ -449,7 +473,6 @@
         total = add_round(add_pair_kernel, total, got)
     scaled, total, side = lax.optimization_barrier((scaled, total, side))
     out_h = side[0]
-    got = lax.ppermute(total, "dom", flips[-1])
     own_grad, far_grad = pl.pallas_call(
         scatter_kernel,
         out_shape=[
@@ -470,8 +493,7 @@
         cost_estimate=cost(block_flops, val_bytes + 4 * MIB),
         name="table_grad",
     )(cols, block_counts, vals, scaled)
-    far_grad, got = lax.optimization_barrier((far_grad, got))
-    total = add_round(add_pair_kernel, total, got)
+    total, far_grad = lax.optimization_barrier((total, far_grad))
     back = lax.all_to_all(
         far_grad.reshape(parts, slots, chan_width, size), "dom", split_axis=0, concat_axis=0, tiled=True
     )
@@ -505,10 +527,16 @@
         name="sum_near",
     )(me, own_grad, *packed)
     held, near = lax.optimization_barrier((held, near))
-    for level in reversed(range(len(halves))):
+    whole, half = 1 << order[-1], 1 << halves[-1]
+    across, beside, both = (
+        lax.ppermute(held, "dom", [(i, i ^ flip) for i in range(parts)]) for flip in (whole, half, whole | half)
+    )
+    mine = held.astype(F32) + across.astype(F32)
+    other = beside.astype(F32) + both.astype(F32)
+    held = jnp.concatenate([mine, other], axis=0).astype(BF)
+    held, back = lax.optimization_barrier((held, back))
+    for level in reversed(range(len(halves) - 1)):
         held = jnp.concatenate([held, lax.ppermute(held, "dom", flips[level])], axis=0)
-        if level == len(halves) - 1:
-            held, back = lax.optimization_barrier((held, back))
     address = jnp.int32(0)
     for level in range(len(halves)):
         address = address * 2 + bits[level][0]

time: 152 us -> 150 us (0.987)
  waiting for transfers between devices: 28.4 us -> 50.4 us
  blocking collectives: 21.1 us -> 0 us
  local copies, waits for them, and re-layouts: 13.7 us -> 2.63 us
  starting transfers between devices: 62.3 us -> 70.4 us
    all_to_all x1 -> x0, blocking collectives: 21.1 us -> none  [per_device(): lax.all_to_all(mean, 'chan', split_axis=0, concat_axis=0, tiled=True)]
    all_to_all x0 -> x1, waiting for transfers between devices: none -> 15.5 us  [per_device(): lax.all_to_all(mean, 'chan', split_axis=0, concat_axis=0, tiled=True)]
    unnamed x58 -> x30, local copies, waits for them, and re-layouts: 13.5 us -> 2.49 us
    all_to_all x0 -> x1, starting transfers between devices: none -> 8.48 us  [per_device(): lax.all_to_all(mean, 'chan', split_axis=0, concat_axis=0, tiled=True)]
    ppermute x1 -> x3, waiting for transfers between devices: 0.01 us -> 3.69 us  [per_device(): lax.ppermute(held, 'dom', [(i, i ^ flip) for i in range(parts)])]
    ppermute x14, waiting for transfers between devices: 11.2 us -> 13.9 us  [exchange(): lax.ppermute(chunks[shift], 'chan', [(i, (i + shift) % count) for i in ra...]
    ppermute x3 -> x2, starting transfers between devices: 2.52 us -> 0.65 us  [per_device(): lax.ppermute(held, 'dom', flips[level])]
    ppermute x3 -> x2, waiting for transfers between devices: 4.96 us -> 3.18 us  [per_device(): lax.ppermute(held, 'dom', flips[level])]
  transfers between devices with their start and end apart: 25 -> 27, of which waited for: 11 -> 14; matrix products, arithmetic and copies ran while one was open for 0% -> 0% of each run, Pallas kernels for 8% -> 4%
where the time goes in v4:
time: 150 us; the launch traced here: 148 us
  starting transfers between devices  70.4 us (47%)
  waiting for transfers between devices  50.4 us (34%)
  Pallas kernels  23.9 us (16%)
  local copies, waits for them, and re-layouts  2.63 us (2%)
    ppermute x14, starting transfers between devices, exchange(): lax.ppermute(chunks[shift], 'chan', [(i, (i + shift) % count) for i in ra...  35.6 us
    all_to_all x1, waiting for transfers between devices, per_device(): lax.all_to_all(mean, 'chan', split_axis=0, concat_axis=0, tiled=True)  15.5 us
    ppermute x14, waiting for transfers between devices, exchange(): lax.ppermute(chunks[shift], 'chan', [(i, (i + shift) % count) for i in ra...  13.9 us
    all_to_all x1, starting transfers between devices, per_device(): lax.all_to_all(mean, 'chan', split_axis=0, concat_axis=0, tiled=True)  8.48 us
    all_to_all x1, starting transfers between devices, per_device(): lax.all_to_all(outgoing, 'dom', split_axis=0, concat_axis=0, tiled=True)  7.76 us
    pallas_call x1, Pallas kernels, per_device(): pl.pallas_call(scatter_kernel, out_shape=[pltpu.HBM((block_rows, chan_wid...  6.44 us
    pallas_call x1, Pallas kernels, per_device(): pl.pallas_call(gather_kernel, out_shape=[pltpu.HBM((chans, chan_width, no...  6.18 us
    all_to_all x1, starting transfers between devices, per_device(): lax.all_to_all(far_grad.reshape(parts, slots, chan_width, size), 'dom', s...  6.14 us
  transfers between devices with their start and end apart: 27, of which 14 were waited for; matrix products, arithmetic and copies ran while one was open for 0% of the time, Pallas kernels for 4%

profile of v4, /device:TPU:2, one launch (start us, length us, event | category | flops | bytes accessed | tf_op | source)
XLA Modules:
  0.0 148.3 jit_solution(3042487322727593849)
XLA Ops:
  0.6 2.5 %pack_outgoing.1 = bf16[32,4,64,128]{3,2,1,0:T(8,128)(2,1)} custom-call(s32[4,32]{1,0:T(4,128)} %bitcast.29, bf16[64,4096]{1,0:T(8,128)(2,1)} %bitcast.20), custom_call_target="tpu_custom_call" | custom-call | bytes 5242880 | tf_op jit(solution)/shard_map/pack_outgoing/pallas_call | solution.py:362
  3.2 7.8 %all-to-all-start = ((bf16[32,4,64,128]{3,2,1,0:T(8,128)(2,1)}), bf16[32,4,64,128]{3,2,1,0:T(8,128)(2,1)S(1)}, u32[]{:S(2)}, u32[]{:S(2)}) async-start(bf16[32,4,64,128]{3,2,1,0:T(8,128)(2,1)} %pack_outgoing.1), calls=%async_computation | async-start | bytes 4194304 | tf_op jit(solution)/shard_map/all_to_all | solution.py:375
  11.0 0.9 split_feats.1
  11.9 2.0 %collective-permute-start = (bf16[64,512]{1,0:T(8,128)(2,1)}, bf16[64,512]{1,0:T(8,128)(2,1)S(1)}, u32[]{:S(2)}, u32[]{:S(2)}) collective-permute-start(bf16[64,512]{1,0:T(8,128)(2,1)} %get-tuple-element.75), channel_id=1, source_target_pairs={{0,1},{1,2},{2,3},{3,4},{4,5},{5,6},{6,7},{7,0},{8,9},{9,10},{10,1... | collective-permute-start | bytes 196616 | tf_op jit(solution)/shard_map/ppermute | solution.py:313
  13.9 3.3 %collective-permute-start.1 = (bf16[64,512]{1,0:T(8,128)(2,1)}, bf16[64,512]{1,0:T(8,128)(2,1)S(1)}, u32[]{:S(2)}, u32[]{:S(2)}) collective-permute-start(bf16[64,512]{1,0:T(8,128)(2,1)} %get-tuple-element.76), channel_id=1, source_target_pairs={{0,2},{1,3},{2,4},{3,5},{4,6},{5,7},{6,0},{7,1},{8,10},{9,11},{10,... | collective-permute-start | bytes 196616 | tf_op jit(solution)/shard_map/ppermute | solution.py:313
  17.1 4.0 %collective-permute-start.2 = (bf16[64,512]{1,0:T(8,128)(2,1)}, bf16[64,512]{1,0:T(8,128)(2,1)S(1)}, u32[]{:S(2)}, u32[]{:S(2)}) collective-permute-start(bf16[64,512]{1,0:T(8,128)(2,1)} %get-tuple-element.77), channel_id=1, source_target_pairs={{0,3},{1,4},{2,5},{3,6},{4,7},{5,0},{6,1},{7,2},{8,11},{9,12},{10,... | collective-permute-start | bytes 196616 | tf_op jit(solution)/shard_map/ppermute | solution.py:313
  21.7 4.9 %collective-permute-start.4 = (bf16[64,512]{1,0:T(8,128)(2,1)}, bf16[64,512]{1,0:T(8,128)(2,1)S(1)}, u32[]{:S(2)}, u32[]{:S(2)}) collective-permute-start(bf16[64,512]{1,0:T(8,128)(2,1)} %get-tuple-element.79), channel_id=1, source_target_pairs={{0,5},{1,6},{2,7},{3,0},{4,1},{5,2},{6,3},{7,4},{8,13},{9,14},{10,... | collective-permute-start | bytes 196616 | tf_op jit(solution)/shard_map/ppermute | solution.py:313
  26.7 2.7 %collective-permute-start.5 = (bf16[64,512]{1,0:T(8,128)(2,1)}, bf16[64,512]{1,0:T(8,128)(2,1)S(1)}, u32[]{:S(2)}, u32[]{:S(2)}) collective-permute-start(bf16[64,512]{1,0:T(8,128)(2,1)} %get-tuple-element.80), channel_id=1, source_target_pairs={{0,6},{1,7},{2,0},{3,1},{4,2},{5,3},{6,4},{7,5},{8,14},{9,15},{10,... | collective-permute-start | bytes 196616 | tf_op jit(solution)/shard_map/ppermute | solution.py:313
  29.3 1.0 collective-permute-start.6
  30.4 5.7 %collective-permute-done.4.refs_5_ = bf16[64,512]{1,0:T(8,128)(2,1)S(1)} collective-permute-done((bf16[64,512]{1,0:T(8,128)(2,1)}, bf16[64,512]{1,0:T(8,128)(2,1)S(1)}, u32[]{:S(2)}, u32[]{:S(2)}) %collective-permute-start.4) | collective-permute-done | bytes 65568 | tf_op jit(solution)/shard_map/ppermute | solution.py:313
  36.1 0.6 copy-done.12
  36.7 0.6 copy-done.13
  37.4 1.5 %all-to-all-done = bf16[32,4,64,128]{3,2,1,0:T(8,128)(2,1)S(1)} async-done(((bf16[32,4,64,128]{3,2,1,0:T(8,128)(2,1)}), bf16[32,4,64,128]{3,2,1,0:T(8,128)(2,1)S(1)}, u32[]{:S(2)}, u32[]{:S(2)}) %all-to-all-start) | async-done | bytes 2097184 | tf_op jit(solution)/shard_map/all_to_all | solution.py:375
  38.9 6.2 %neighbour_mean.1 = (bf16[8,64,512]{2,1,0:T(8,128)(2,1)}, f32[8,8,512]{2,1,0:T(8,128)S(1)}) custom-call(s32[8,32]{1,0:T(8,128)S(1)} %bitcast.27, s32[32]{0:T(128)S(1)} %copy-done.7, bf16[64,4096]{1,0:T(8,128)(2,1)S(1)} %bitcast.22, bf16[128,64,128]{2,1,0:T(8,128)(2,1)S(1)} %bitcast.17, bf16[32,8,128,128]{3,2,1,0:T(8,128)(2,1)} %vals_ref.3), custom_call_target="tpu_custom_call" | custom-call | flops 536870912 | bytes 11534336 | tf_op jit(solution)/shard_map/neighbour_mean/pallas_call | solution.py:399
  45.1 8.5 %all-to-all-start.1 = ((bf16[8,64,512]{2,1,0:T(8,128)(2,1)}), bf16[8,64,512]{2,1,0:T(8,128)(2,1)S(1)}, u32[]{:S(2)}, u32[]{:S(2)}) async-start(bf16[8,64,512]{2,1,0:T(8,128)(2,1)} %get-tuple-element.95), calls=%async_computation.1 | async-start | bytes 1048576 | tf_op jit(solution)/shard_map/all_to_all | solution.py:414
  53.7 1.4 self_part.1
  55.2 15.5 %all-to-all-done.1 = bf16[8,64,512]{2,1,0:T(8,128)(2,1)S(1)} async-done(((bf16[8,64,512]{2,1,0:T(8,128)(2,1)}), bf16[8,64,512]{2,1,0:T(8,128)(2,1)S(1)}, u32[]{:S(2)}, u32[]{:S(2)}) %all-to-all-start.1) | async-done | bytes 524320 | tf_op jit(solution)/shard_map/all_to_all | solution.py:414
  70.7 1.8 %layer_head.1 = (bf16[256,512]{1,0:T(8,128)(2,1)S(1)}, bf16[256,512]{1,0:T(8,128)(2,1)S(1)}, bf16[512,512]{1,0:T(8,128)(2,1)}) custom-call(s32[1]{0:T(128)} %bitcast.me_ref, f32[8,8,512]{2,1,0:T(8,128)S(1)} %get-tuple-element.83.degree_ref, f32[256,512]{1,0:T(8,128)S(1)} %get-tuple-element.92.pre_ref, bf16[256,512]{1,0:T(8,128)(2,1)S(1)} %get-tuple-element.93.turned_ref, ...), custom_call_target="tpu_custom_call" | custom-call | flops 268435456 | bytes 4194304 | tf_op jit(solution)/shard_map/layer_head/pallas_call | solution.py:416
  72.5 3.5 %all-to-all-start.2 = ((bf16[8,64,512]{2,1,0:T(8,128)(2,1)}), bf16[8,64,512]{2,1,0:T(8,128)(2,1)S(1)}, u32[]{:S(2)}, u32[]{:S(2)}) async-start(bf16[8,64,512]{2,1,0:T(8,128)(2,1)} %bitcast.8), calls=%async_computation.2 | async-start | bytes 1048576 | tf_op jit(solution)/shard_map/all_to_all | solution.py:425
  76.6 1.5 %collective-permute-done.7.recv_ref = bf16[16,8,8,128]{3,2,1,0:T(8,128)(2,1)S(1)} collective-permute-done((bf16[16,8,8,128]{3,2,1,0:T(8,128)(2,1)S(1)}, bf16[16,8,8,128]{3,2,1,0:T(8,128)(2,1)S(1)}, u32[]{:S(2)}, u32[]{:S(2)}) %collective-permute-start.7) | collective-permute-done | bytes 262176 | tf_op jit(solution)/shard_map/ppermute | solution.py:446
  78.2 1.1 collective-permute-start.8
  79.3 4.5 %collective-permute-done.8.recv_ref = bf16[8,8,8,128]{3,2,1,0:T(8,128)(2,1)S(1)} collective-permute-done((bf16[8,8,8,128]{3,2,1,0:T(8,128)(2,1)S(1)}, bf16[8,8,8,128]{3,2,1,0:T(8,128)(2,1)S(1)}, u32[]{:S(2)}, u32[]{:S(2)}) %collective-permute-start.8) | collective-permute-done | bytes 131104 | tf_op jit(solution)/shard_map/ppermute | solution.py:446
  83.9 1.1 collective-permute-start.9
  85.0 3.3 %collective-permute-done.9.recv_ref = bf16[4,8,8,128]{3,2,1,0:T(8,128)(2,1)S(1)} collective-permute-done((bf16[4,8,8,128]{3,2,1,0:T(8,128)(2,1)S(1)}, bf16[4,8,8,128]{3,2,1,0:T(8,128)(2,1)S(1)}, u32[]{:S(2)}, u32[]{:S(2)}) %collective-permute-start.9) | collective-permute-done | bytes 65568 | tf_op jit(solution)/shard_map/ppermute | solution.py:458
  88.3 1.8 %collective-permute-start.10 = (bf16[4,8,8,128]{3,2,1,0:T(8,128)(2,1)S(1)}, bf16[4,8,8,128]{3,2,1,0:T(8,128)(2,1)S(1)}, u32[]{:S(2)}, u32[]{:S(2)}) collective-permute-start(bf16[4,8,8,128]{3,2,1,0:T(8,128)(2,1)S(1)} %weight_add.2.held_ref), channel_id=1, source_target_pairs={{0,32},{8,40},{16,48},{24,56},{32,0},{40,8},{48,16},{56,24},{64,96... | collective-permute-start | bytes 196616 | tf_op jit(solution)/shard_map/ppermute | solution.py:472
  90.0 0.9 side_grads.1
  91.0 3.3 %collective-permute-done.10.recv_ref = bf16[4,8,8,128]{3,2,1,0:T(8,128)(2,1)S(1)} collective-permute-done((bf16[4,8,8,128]{3,2,1,0:T(8,128)(2,1)S(1)}, bf16[4,8,8,128]{3,2,1,0:T(8,128)(2,1)S(1)}, u32[]{:S(2)}, u32[]{:S(2)}) %collective-permute-start.10) | collective-permute-done | bytes 65568 | tf_op jit(solution)/shard_map/ppermute | solution.py:472
  94.3 6.4 %table_grad.1 = (f32[32,64,128]{2,1,0:T(8,128)}, bf16[128,64,128]{2,1,0:T(8,128)(2,1)}) custom-call(s32[8,32]{1,0:T(8,128)S(1)} %bitcast.28, s32[32]{0:T(128)S(1)} %copy-done.7, bf16[32,8,128,128]{3,2,1,0:T(8,128)(2,1)} %vals_ref.3, bf16[8,64,512]{2,1,0:T(8,128)(2,1)S(1)} %all-to-all-done.2.scaled_ref), custom_call_target="tpu_custom_call" | custom-call | flops 536870912 | bytes 12582912 | tf_op jit(solution)/shard_map/table_grad/pallas_call | solution.py:476
  100.8 6.1 %all-to-all-start.3 = ((bf16[32,4,64,128]{3,2,1,0:T(8,128)(2,1)}), bf16[32,4,64,128]{3,2,1,0:T(8,128)(2,1)S(1)}, u32[]{:S(2)}, u32[]{:S(2)}) async-start(bf16[32,4,64,128]{3,2,1,0:T(8,128)(2,1)} %bitcast.31), calls=%async_computation.3 | async-start | bytes 4194304 | tf_op jit(solution)/shard_map/all_to_all | solution.py:497
  107.0 2.0 %collective-permute-start.11 = (bf16[64,640]{1,0:T(8,128)(2,1)S(1)}, bf16[64,640]{1,0:T(8,128)(2,1)S(1)}, u32[]{:S(2)}, u32[]{:S(2)}) collective-permute-start(bf16[64,640]{1,0:T(8,128)(2,1)S(1)} %get-tuple-element.129), channel_id=1, source_target_pairs={{0,1},{1,2},{2,3},{3,4},{4,5},{5,6},{6,7},{7,0},{8,9},{9,10},{10,1... | collective-permute-start | bytes 245768 | tf_op jit(solution)/shard_map/ppermute | solution.py:313
  109.0 2.4 %collective-permute-start.12 = (bf16[64,640]{1,0:T(8,128)(2,1)S(1)}, bf16[64,640]{1,0:T(8,128)(2,1)S(1)}, u32[]{:S(2)}, u32[]{:S(2)}) collective-permute-start(bf16[64,640]{1,0:T(8,128)(2,1)S(1)} %get-tuple-element.130), channel_id=1, source_target_pairs={{0,2},{1,3},{2,4},{3,5},{4,6},{5,7},{6,0},{7,1},{8,10},{9,11},{10,... | collective-permute-start | bytes 245768 | tf_op jit(solution)/shard_map/ppermute | solution.py:313
  111.4 2.7 %collective-permute-start.13 = (bf16[64,640]{1,0:T(8,128)(2,1)S(1)}, bf16[64,640]{1,0:T(8,128)(2,1)S(1)}, u32[]{:S(2)}, u32[]{:S(2)}) collective-permute-start(bf16[64,640]{1,0:T(8,128)(2,1)S(1)} %get-tuple-element.131), channel_id=1, source_target_pairs={{0,3},{1,4},{2,5},{3,6},{4,7},{5,0},{6,1},{7,2},{8,11},{9,12},{10,... | collective-permute-start | bytes 245768 | tf_op jit(solution)/shard_map/ppermute | solution.py:313
  114.1 2.3 %collective-permute-start.14 = (bf16[64,640]{1,0:T(8,128)(2,1)S(1)}, bf16[64,640]{1,0:T(8,128)(2,1)S(1)}, u32[]{:S(2)}, u32[]{:S(2)}) collective-permute-start(bf16[64,640]{1,0:T(8,128)(2,1)S(1)} %get-tuple-element.132), channel_id=1, source_target_pairs={{0,4},{1,5},{2,6},{3,7},{4,0},{5,1},{6,2},{7,3},{8,12},{9,13},{10,... | collective-permute-start | bytes 245768 | tf_op jit(solution)/shard_map/ppermute | solution.py:313
  116.4 2.7 %collective-permute-start.15 = (bf16[64,640]{1,0:T(8,128)(2,1)S(1)}, bf16[64,640]{1,0:T(8,128)(2,1)S(1)}, u32[]{:S(2)}, u32[]{:S(2)}) collective-permute-start(bf16[64,640]{1,0:T(8,128)(2,1)S(1)} %get-tuple-element.133), channel_id=1, source_target_pairs={{0,5},{1,6},{2,7},{3,0},{4,1},{5,2},{6,3},{7,4},{8,13},{9,14},{10,... | collective-permute-start | bytes 245768 | tf_op jit(solution)/shard_map/ppermute | solution.py:313
  119.1 3.6 %collective-permute-start.16 = (bf16[64,640]{1,0:T(8,128)(2,1)S(1)}, bf16[64,640]{1,0:T(8,128)(2,1)S(1)}, u32[]{:S(2)}, u32[]{:S(2)}) collective-permute-start(bf16[64,640]{1,0:T(8,128)(2,1)S(1)} %get-tuple-element.134), channel_id=1, source_target_pairs={{0,6},{1,7},{2,0},{3,1},{4,2},{5,3},{6,4},{7,5},{8,14},{9,15},{10,... | collective-permute-start | bytes 245768 | tf_op jit(solution)/shard_map/ppermute | solution.py:313
  122.7 1.5 collective-permute-start.17
  124.2 1.6 %collective-permute-done.14.refs_4_ = bf16[64,640]{1,0:T(8,128)(2,1)S(1)} collective-permute-done((bf16[64,640]{1,0:T(8,128)(2,1)S(1)}, bf16[64,640]{1,0:T(8,128)(2,1)S(1)}, u32[]{:S(2)}, u32[]{:S(2)}) %collective-permute-start.14) | collective-permute-done | bytes 81952 | tf_op jit(solution)/shard_map/ppermute | solution.py:313
  125.8 4.8 %collective-permute-done.15.refs_5_ = bf16[64,640]{1,0:T(8,128)(2,1)S(1)} collective-permute-done((bf16[64,640]{1,0:T(8,128)(2,1)S(1)}, bf16[64,640]{1,0:T(8,128)(2,1)S(1)}, u32[]{:S(2)}, u32[]{:S(2)}) %collective-permute-start.15) | collective-permute-done | bytes 81952 | tf_op jit(solution)/shard_map/ppermute | solution.py:313
  130.6 1.2 collective-permute-done.16.refs_6_
  132.3 1.2 copy-done.1
  133.6 3.1 %collective-permute-start.18 = (bf16[1,32,128]{2,1,0:T(8,128)(2,1)S(1)}, bf16[1,32,128]{2,1,0:T(8,128)(2,1)S(1)}, u32[]{:S(2)}, u32[]{:S(2)}) collective-permute-start(bf16[1,32,128]{2,1,0:T(8,128)(2,1)S(1)} %bitcast.23), channel_id=1, source_target_pairs={{0,128},{8,136},{16,144},{24,152},{32,160},{40,168},{48,176},{56,1... | collective-permute-start | bytes 24584 | tf_op jit(solution)/shard_map/ppermute | solution.py:532
  136.7 1.2 collective-permute-start.20
  137.9 1.0 collective-permute-done.18
  138.9 2.7 %collective-permute-done.20 = bf16[1,32,128]{2,1,0:T(8,128)(2,1)S(1)} collective-permute-done((bf16[1,32,128]{2,1,0:T(8,128)(2,1)S(1)}, bf16[1,32,128]{2,1,0:T(8,128)(2,1)S(1)}, u32[]{:S(2)}, u32[]{:S(2)}) %collective-permute-start.20) | collective-permute-done | bytes 8224 | tf_op jit(solution)/shard_map/ppermute | solution.py:532
  141.6 0.6 collective-permute-start.21
  142.2 3.2 %collective-permute-done.21 = bf16[2,32,128]{2,1,0:T(8,128)(2,1)S(1)} collective-permute-done((bf16[2,32,128]{2,1,0:T(8,128)(2,1)S(1)}, bf16[2,32,128]{2,1,0:T(8,128)(2,1)S(1)}, u32[]{:S(2)}, u32[]{:S(2)}) %collective-permute-start.21) | collective-permute-done | bytes 16416 | tf_op jit(solution)/shard_map/ppermute | solution.py:539
  145.5 2.2 %sum_returned.1 = bf16[64,4096]{1,0:T(8,128)(2,1)} custom-call(s32[4,32]{1,0:T(4,128)S(1)} %bitcast.30, f32[32,64,128]{2,1,0:T(8,128)S(1)} %sum_near.1.near_ref, bf16[32,4,64,128]{3,2,1,0:T(8,128)(2,1)S(1)} %all-to-all-done.3.back_ref), custom_call_target="tpu_custom_call" | custom-call | bytes 4194304 | tf_op jit(solution)/shard_map/sum_returned/pallas_call | solution.py:553
  147.7 0.7 weight_spread.1
  (59 shorter events, 2.2 us)
Async XLA Ops:
  3.2 7.8 %copy-start = (bf16[4096,64]{0,1:T(8,128)(2,1)S(1)}, bf16[4096,64]{0,1:T(8,128)(2,1)}, u32[]{:S(2)}) copy-start(bf16[4096,64]{0,1:T(8,128)(2,1)} %param.9) | copy-start | bytes 1572868
  3.2 35.7 %copy-start.5 = (s32[32,8]{0,1:T(8,128)S(1)}, s32[32,8]{0,1:T(8,128)}, u32[]{:S(2)}) copy-start(s32[32,8]{0,1:T(8,128)} %param.11) | copy-start | bytes 3076
  3.2 35.7 %copy-start.7 = (s32[32]{0:T(128)S(1)}, s32[32]{0:T(128)}, u32[]{:S(2)}) copy-start(s32[32]{0:T(128)} %counts_ref.3) | copy-start | bytes 388
  3.2 35.6 %all-to-all-start = ((bf16[32,4,64,128]{3,2,1,0:T(8,128)(2,1)}), bf16[32,4,64,128]{3,2,1,0:T(8,128)(2,1)S(1)}, u32[]{:S(2)}, u32[]{:S(2)}) async-start(bf16[32,4,64,128]{3,2,1,0:T(8,128)(2,1)} %pack_outgoing.1), calls=%async_computation | async-start | bytes 4194304 | tf_op jit(solution)/shard_map/all_to_all | solution.py:375
  11.9 14.8 %collective-permute-start = (bf16[64,512]{1,0:T(8,128)(2,1)}, bf16[64,512]{1,0:T(8,128)(2,1)S(1)}, u32[]{:S(2)}, u32[]{:S(2)}) collective-permute-start(bf16[64,512]{1,0:T(8,128)(2,1)} %get-tuple-element.75), channel_id=1, source_target_pairs={{0,1},{1,2},{2,3},{3,4},{4,5},{5,6},{6,7},{7,0},{8,9},{9,10},{10,1... | collective-permute-start | bytes 196616 | tf_op jit(solution)/shard_map/ppermute | solution.py:313
  13.9 15.5 %collective-permute-start.1 = (bf16[64,512]{1,0:T(8,128)(2,1)}, bf16[64,512]{1,0:T(8,128)(2,1)S(1)}, u32[]{:S(2)}, u32[]{:S(2)}) collective-permute-start(bf16[64,512]{1,0:T(8,128)(2,1)} %get-tuple-element.76), channel_id=1, source_target_pairs={{0,2},{1,3},{2,4},{3,5},{4,6},{5,7},{6,0},{7,1},{8,10},{9,11},{10,... | collective-permute-start | bytes 196616 | tf_op jit(solution)/shard_map/ppermute | solution.py:313
  17.1 13.2 %collective-permute-start.2 = (bf16[64,512]{1,0:T(8,128)(2,1)}, bf16[64,512]{1,0:T(8,128)(2,1)S(1)}, u32[]{:S(2)}, u32[]{:S(2)}) collective-permute-start(bf16[64,512]{1,0:T(8,128)(2,1)} %get-tuple-element.77), channel_id=1, source_target_pairs={{0,3},{1,4},{2,5},{3,6},{4,7},{5,0},{6,1},{7,2},{8,11},{9,12},{10,... | collective-permute-start | bytes 196616 | tf_op jit(solution)/shard_map/ppermute | solution.py:313
  21.2 9.2 %collective-permute-start.3 = (bf16[64,512]{1,0:T(8,128)(2,1)}, bf16[64,512]{1,0:T(8,128)(2,1)S(1)}, u32[]{:S(2)}, u32[]{:S(2)}) collective-permute-start(bf16[64,512]{1,0:T(8,128)(2,1)} %get-tuple-element.78), channel_id=1, source_target_pairs={{0,4},{1,5},{2,6},{3,7},{4,0},{5,1},{6,2},{7,3},{8,12},{9,13},{10,... | collective-permute-start | bytes 196616 | tf_op jit(solution)/shard_map/ppermute | solution.py:313
  21.7 14.4 %collective-permute-start.4 = (bf16[64,512]{1,0:T(8,128)(2,1)}, bf16[64,512]{1,0:T(8,128)(2,1)S(1)}, u32[]{:S(2)}, u32[]{:S(2)}) collective-permute-start(bf16[64,512]{1,0:T(8,128)(2,1)} %get-tuple-element.79), channel_id=1, source_target_pairs={{0,5},{1,6},{2,7},{3,0},{4,1},{5,2},{6,3},{7,4},{8,13},{9,14},{10,... | collective-permute-start | bytes 196616 | tf_op jit(solution)/shard_map/ppermute | solution.py:313
  26.7 9.4 %copy-start.8 = (bf16[64,512]{1,0:T(8,128)(2,1)}, bf16[64,512]{1,0:T(8,128)(2,1)S(1)}, u32[]{:S(2)}) copy-start(bf16[64,512]{1,0:T(8,128)(2,1)S(1)} %collective-permute-done.refs_1_) | copy-start | bytes 196612
  26.7 9.4 %collective-permute-start.5 = (bf16[64,512]{1,0:T(8,128)(2,1)}, bf16[64,512]{1,0:T(8,128)(2,1)S(1)}, u32[]{:S(2)}, u32[]{:S(2)}) collective-permute-start(bf16[64,512]{1,0:T(8,128)(2,1)} %get-tuple-element.80), channel_id=1, source_target_pairs={{0,6},{1,7},{2,0},{3,1},{4,2},{5,3},{6,4},{7,5},{8,14},{9,15},{10,... | collective-permute-start | bytes 196616 | tf_op jit(solution)/shard_map/ppermute | solution.py:313
  29.3 6.8 %copy-start.9 = (bf16[64,512]{1,0:T(8,128)(2,1)}, bf16[64,512]{1,0:T(8,128)(2,1)S(1)}, u32[]{:S(2)}) copy-start(bf16[64,512]{1,0:T(8,128)(2,1)S(1)} %collective-permute-done.1.refs_2_) | copy-start | bytes 196612
  29.3 8.0 %collective-permute-start.6 = (bf16[64,512]{1,0:T(8,128)(2,1)}, bf16[64,512]{1,0:T(8,128)(2,1)}, u32[]{:S(2)}, u32[]{:S(2)}) collective-permute-start(bf16[64,512]{1,0:T(8,128)(2,1)} %get-tuple-element.81), channel_id=1, source_target_pairs={{0,7},{1,0},{2,1},{3,2},{4,3},{5,4},{6,5},{7,6},{8,15},{9,8},{10,9... | collective-permute-start | bytes 196616 | tf_op jit(solution)/shard_map/ppermute | solution.py:313
  30.3 5.8 %copy-start.10 = (bf16[64,512]{1,0:T(8,128)(2,1)}, bf16[64,512]{1,0:T(8,128)(2,1)S(1)}, u32[]{:S(2)}) copy-start(bf16[64,512]{1,0:T(8,128)(2,1)S(1)} %collective-permute-done.2.refs_3_) | copy-start | bytes 196612
  30.4 5.8 %copy-start.11 = (bf16[64,512]{1,0:T(8,128)(2,1)}, bf16[64,512]{1,0:T(8,128)(2,1)S(1)}, u32[]{:S(2)}) copy-start(bf16[64,512]{1,0:T(8,128)(2,1)S(1)} %collective-permute-done.3.refs_4_) | copy-start | bytes 196612
  36.1 0.6 copy-start.12
  36.7 0.6 copy-start.13
  38.9 14.7 %copy-start.14 = (f32[256]{0:T(256)S(1)}, f32[256]{0:T(256)}, u32[]{:S(2)}) copy-start(f32[256]{0:T(256)} %param.16) | copy-start | bytes 3076
  38.9 14.8 %copy-start.2 = (bf16[512,256]{1,0:T(8,128)(2,1)S(1)}, bf16[512,256]{1,0:T(8,128)(2,1)}, u32[]{:S(2)}) copy-start(bf16[512,256]{1,0:T(8,128)(2,1)} %weight_ref.4) | copy-start | bytes 786436
  38.9 14.8 %copy-start.3 = (bf16[512,256]{1,0:T(8,128)(2,1)S(1)}, bf16[512,256]{1,0:T(8,128)(2,1)}, u32[]{:S(2)}) copy-start(bf16[512,256]{1,0:T(8,128)(2,1)} %weight_ref.5) | copy-start | bytes 786436
  38.9 14.8 %copy-start.4 = (bf16[512,256]{1,0:T(8,128)(2,1)S(1)}, bf16[512,256]{1,0:T(8,128)(2,1)}, u32[]{:S(2)}) copy-start(bf16[512,256]{1,0:T(8,128)(2,1)} %cot_ref.1) | copy-start | bytes 786436
  45.1 25.6 %all-to-all-start.1 = ((bf16[8,64,512]{2,1,0:T(8,128)(2,1)}), bf16[8,64,512]{2,1,0:T(8,128)(2,1)S(1)}, u32[]{:S(2)}, u32[]{:S(2)}) async-start(bf16[8,64,512]{2,1,0:T(8,128)(2,1)} %get-tuple-element.95), calls=%async_computation.1 | async-start | bytes 1048576 | tf_op jit(solution)/shard_map/all_to_all | solution.py:414
  72.5 21.9 %all-to-all-start.2 = ((bf16[8,64,512]{2,1,0:T(8,128)(2,1)}), bf16[8,64,512]{2,1,0:T(8,128)(2,1)S(1)}, u32[]{:S(2)}, u32[]{:S(2)}) async-start(bf16[8,64,512]{2,1,0:T(8,128)(2,1)} %bitcast.8), calls=%async_computation.2 | async-start | bytes 1048576 | tf_op jit(solution)/shard_map/all_to_all | solution.py:425
  76.5 1.6 %collective-permute-start.7 = (bf16[16,8,8,128]{3,2,1,0:T(8,128)(2,1)S(1)}, bf16[16,8,8,128]{3,2,1,0:T(8,128)(2,1)S(1)}, u32[]{:S(2)}, u32[]{:S(2)}) collective-permute-start(bf16[16,8,8,128]{3,2,1,0:T(8,128)(2,1)S(1)} %get-tuple-element.100), channel_id=1, source_target_pairs={{0,8},{8,0},{16,24},{24,16},{32,40},{40,32},{48,56},{56,48},{64,72... | collective-permute-start | bytes 786440 | tf_op jit(solution)/shard_map/ppermute | solution.py:446
  78.2 5.6 %collective-permute-start.8 = (bf16[8,8,8,128]{3,2,1,0:T(8,128)(2,1)S(1)}, bf16[8,8,8,128]{3,2,1,0:T(8,128)(2,1)S(1)}, u32[]{:S(2)}, u32[]{:S(2)}) collective-permute-start(bf16[8,8,8,128]{3,2,1,0:T(8,128)(2,1)S(1)} %get-tuple-element.102), channel_id=1, source_target_pairs={{0,16},{8,24},{16,0},{24,8},{32,48},{40,56},{48,32},{56,40},{64,80... | collective-permute-start | bytes 393224 | tf_op jit(solution)/shard_map/ppermute | solution.py:446
  83.9 4.4 %collective-permute-start.9 = (bf16[4,8,8,128]{3,2,1,0:T(8,128)(2,1)S(1)}, bf16[4,8,8,128]{3,2,1,0:T(8,128)(2,1)S(1)}, u32[]{:S(2)}, u32[]{:S(2)}) collective-permute-start(bf16[4,8,8,128]{3,2,1,0:T(8,128)(2,1)S(1)} %get-tuple-element.104), channel_id=1, source_target_pairs={{0,64},{8,72},{16,80},{24,88},{32,96},{40,104},{48,112},{56,120},{... | collective-permute-start | bytes 196616 | tf_op jit(solution)/shard_map/ppermute | solution.py:458
  88.3 6.0 %collective-permute-start.10 = (bf16[4,8,8,128]{3,2,1,0:T(8,128)(2,1)S(1)}, bf16[4,8,8,128]{3,2,1,0:T(8,128)(2,1)S(1)}, u32[]{:S(2)}, u32[]{:S(2)}) collective-permute-start(bf16[4,8,8,128]{3,2,1,0:T(8,128)(2,1)S(1)} %weight_add.2.held_ref), channel_id=1, source_target_pairs={{0,32},{8,40},{16,48},{24,56},{32,0},{40,8},{48,16},{56,24},{64,96... | collective-permute-start | bytes 196616 | tf_op jit(solution)/shard_map/ppermute | solution.py:472
  100.8 40.8 %all-to-all-start.3 = ((bf16[32,4,64,128]{3,2,1,0:T(8,128)(2,1)}), bf16[32,4,64,128]{3,2,1,0:T(8,128)(2,1)S(1)}, u32[]{:S(2)}, u32[]{:S(2)}) async-start(bf16[32,4,64,128]{3,2,1,0:T(8,128)(2,1)} %bitcast.31), calls=%async_computation.3 | async-start | bytes 4194304 | tf_op jit(solution)/shard_map/all_to_all | solution.py:497
  106.9 38.5 %copy-start.6 = (s32[1,32,4]{1,2,0:T(4,128)S(1)}, s32[1,32,4]{1,2,0:T(4,128)}, u32[]{:S(2)}) copy-start(s32[1,32,4]{1,2,0:T(4,128)} %param.13) | copy-start | bytes 1540
  107.0 12.1 %collective-permute-start.11 = (bf16[64,640]{1,0:T(8,128)(2,1)S(1)}, bf16[64,640]{1,0:T(8,128)(2,1)S(1)}, u32[]{:S(2)}, u32[]{:S(2)}) collective-permute-start(bf16[64,640]{1,0:T(8,128)(2,1)S(1)} %get-tuple-element.129), channel_id=1, source_target_pairs={{0,1},{1,2},{2,3},{3,4},{4,5},{5,6},{6,7},{7,0},{8,9},{9,10},{10,1... | collective-permute-start | bytes 245768 | tf_op jit(solution)/shard_map/ppermute | solution.py:313
  109.0 13.7 %collective-permute-start.12 = (bf16[64,640]{1,0:T(8,128)(2,1)S(1)}, bf16[64,640]{1,0:T(8,128)(2,1)S(1)}, u32[]{:S(2)}, u32[]{:S(2)}) collective-permute-start(bf16[64,640]{1,0:T(8,128)(2,1)S(1)} %get-tuple-element.130), channel_id=1, source_target_pairs={{0,2},{1,3},{2,4},{3,5},{4,6},{5,7},{6,0},{7,1},{8,10},{9,11},{10,... | collective-permute-start | bytes 245768 | tf_op jit(solution)/shard_map/ppermute | solution.py:313
  111.4 12.8 %collective-permute-start.13 = (bf16[64,640]{1,0:T(8,128)(2,1)S(1)}, bf16[64,640]{1,0:T(8,128)(2,1)S(1)}, u32[]{:S(2)}, u32[]{:S(2)}) collective-permute-start(bf16[64,640]{1,0:T(8,128)(2,1)S(1)} %get-tuple-element.131), channel_id=1, source_target_pairs={{0,3},{1,4},{2,5},{3,6},{4,7},{5,0},{6,1},{7,2},{8,11},{9,12},{10,... | collective-permute-start | bytes 245768 | tf_op jit(solution)/shard_map/ppermute | solution.py:313
  114.1 11.7 %collective-permute-start.14 = (bf16[64,640]{1,0:T(8,128)(2,1)S(1)}, bf16[64,640]{1,0:T(8,128)(2,1)S(1)}, u32[]{:S(2)}, u32[]{:S(2)}) collective-permute-start(bf16[64,640]{1,0:T(8,128)(2,1)S(1)} %get-tuple-element.132), channel_id=1, source_target_pairs={{0,4},{1,5},{2,6},{3,7},{4,0},{5,1},{6,2},{7,3},{8,12},{9,13},{10,... | collective-permute-start | bytes 245768 | tf_op jit(solution)/shard_map/ppermute | solution.py:313
  116.4 14.2 %collective-permute-start.15 = (bf16[64,640]{1,0:T(8,128)(2,1)S(1)}, bf16[64,640]{1,0:T(8,128)(2,1)S(1)}, u32[]{:S(2)}, u32[]{:S(2)}) collective-permute-start(bf16[64,640]{1,0:T(8,128)(2,1)S(1)} %get-tuple-element.133), channel_id=1, source_target_pairs={{0,5},{1,6},{2,7},{3,0},{4,1},{5,2},{6,3},{7,4},{8,13},{9,14},{10,... | collective-permute-start | bytes 245768 | tf_op jit(solution)/shard_map/ppermute | solution.py:313
  119.1 12.7 %collective-permute-start.16 = (bf16[64,640]{1,0:T(8,128)(2,1)S(1)}, bf16[64,640]{1,0:T(8,128)(2,1)S(1)}, u32[]{:S(2)}, u32[]{:S(2)}) collective-permute-start(bf16[64,640]{1,0:T(8,128)(2,1)S(1)} %get-tuple-element.134), channel_id=1, source_target_pairs={{0,6},{1,7},{2,0},{3,1},{4,2},{5,3},{6,4},{7,5},{8,14},{9,15},{10,... | collective-permute-start | bytes 245768 | tf_op jit(solution)/shard_map/ppermute | solution.py:313
  122.7 9.6 %collective-permute-start.17 = (bf16[64,640]{1,0:T(8,128)(2,1)S(1)}, bf16[64,640]{1,0:T(8,128)(2,1)S(1)}, u32[]{:S(2)}, u32[]{:S(2)}) collective-permute-start(bf16[64,640]{1,0:T(8,128)(2,1)S(1)} %get-tuple-element.135), channel_id=1, source_target_pairs={{0,7},{1,0},{2,1},{3,2},{4,3},{5,4},{6,5},{7,6},{8,15},{9,8},{10,9... | collective-permute-start | bytes 245768 | tf_op jit(solution)/shard_map/ppermute | solution.py:313
  132.3 1.2 copy-start.1
  133.6 5.2 %collective-permute-start.18 = (bf16[1,32,128]{2,1,0:T(8,128)(2,1)S(1)}, bf16[1,32,128]{2,1,0:T(8,128)(2,1)S(1)}, u32[]{:S(2)}, u32[]{:S(2)}) collective-permute-start(bf16[1,32,128]{2,1,0:T(8,128)(2,1)S(1)} %bitcast.23), channel_id=1, source_target_pairs={{0,128},{8,136},{16,144},{24,152},{32,160},{40,168},{48,176},{56,1... | collective-permute-start | bytes 24584 | tf_op jit(solution)/shard_map/ppermute | solution.py:532
  136.7 4.9 %collective-permute-start.20 = (bf16[1,32,128]{2,1,0:T(8,128)(2,1)S(1)}, bf16[1,32,128]{2,1,0:T(8,128)(2,1)S(1)}, u32[]{:S(2)}, u32[]{:S(2)}) collective-permute-start(bf16[1,32,128]{2,1,0:T(8,128)(2,1)S(1)} %bitcast.24), channel_id=1, source_target_pairs={{0,192},{8,200},{16,208},{24,216},{32,224},{40,232},{48,240},{56,2... | collective-permute-start | bytes 24584 | tf_op jit(solution)/shard_map/ppermute | solution.py:532
  137.9 3.7 %collective-permute-start.19 = (bf16[1,32,128]{2,1,0:T(8,128)(2,1)S(1)}, bf16[1,32,128]{2,1,0:T(8,128)(2,1)S(1)}, u32[]{:S(2)}, u32[]{:S(2)}) collective-permute-start(bf16[1,32,128]{2,1,0:T(8,128)(2,1)S(1)} %bitcast.25), channel_id=1, source_target_pairs={{0,64},{8,72},{16,80},{24,88},{32,96},{40,104},{48,112},{56,120},{... | collective-permute-start | bytes 24584 | tf_op jit(solution)/shard_map/ppermute | solution.py:532
  141.6 3.8 %collective-permute-start.21 = (bf16[2,32,128]{2,1,0:T(8,128)(2,1)S(1)}, bf16[2,32,128]{2,1,0:T(8,128)(2,1)S(1)}, u32[]{:S(2)}, u32[]{:S(2)}) collective-permute-start(bf16[2,32,128]{2,1,0:T(8,128)(2,1)S(1)} %pad_maximum_fusion.2), channel_id=1, source_target_pairs={{0,16},{8,24},{16,0},{24,8},{32,48},{40,56},{48,32},{56,40},{64,80... | collective-permute-start | bytes 49160 | tf_op jit(solution)/shard_map/ppermute | solution.py:539
  145.4 2.2 %collective-permute-start.22 = (bf16[4,32,128]{2,1,0:T(8,128)(2,1)S(1)}, bf16[4,32,128]{2,1,0:T(8,128)(2,1)S(1)}, u32[]{:S(2)}, u32[]{:S(2)}) collective-permute-start(bf16[4,32,128]{2,1,0:T(8,128)(2,1)S(1)} %pad_maximum_fusion.1), channel_id=1, source_target_pairs={{0,8},{8,0},{16,24},{24,16},{32,40},{40,32},{48,56},{56,48},{64,72... | collective-permute-start | bytes 98312 | tf_op jit(solution)/shard_map/ppermute | solution.py:539

commit v5 on v4

--- a/solution.py
+++ b/solution.py
@@ -280,12 +280,13 @@
         target[row * rows : (row + 1) * rows, column * lanes : (column + 1) * lanes] = value
 
 
-def near_kernel(chans, me_ref, own_ref, *refs):
+def near_kernel(shifts, me_ref, own_ref, *refs):
+    chans = len(shifts)
     packed_refs = refs[:chans]
     (out_ref,) = refs[chans:]
     blocks, _, size = out_ref.shape
     rows = blocks // chans
-    for shift, packed_ref in enumerate(packed_refs):
+    for shift, packed_ref in zip(shifts, packed_refs):
         group = lax.rem(me_ref[0] + (chans - shift), chans)
         for row in range(rows):
             index = group * rows + row
@@ -309,10 +310,10 @@
 
 def exchange(chunks):
     count = len(chunks)
-    return [chunks[0]] + [
-        lax.ppermute(chunks[shift], "chan", [(i, (i + shift) % count) for i in range(count)])
-        for shift in range(1, count)
-    ]
+    received = list(chunks)
+    for shift in range(1, count):
+        received[shift] = lax.ppermute(chunks[shift], "chan", [(i, (i + shift) % count) for i in range(count)])
+    return received
 
 
 def sds(shape, dtype):
@@ -508,6 +509,8 @@
         name="pack_messages",
     )(me, total, *side[1:])
     packed = exchange(packed)
+    shifts = sorted(range(chans), key=lambda shift: -min(shift, chans - shift))
+    packed = [packed[shift] for shift in shifts]
     held = pl.pallas_call(
         unit_kernel,
         out_shape=sds((pieces * unit, lanes), BF),
@@ -518,7 +521,7 @@
         name="weight_sum",
     )(*packed).reshape(1, pieces * unit, lanes)
     near = pl.pallas_call(
-        functools.partial(near_kernel, chans),
+        functools.partial(near_kernel, shifts),
         out_shape=sds((block_rows, chan_width, size), F32),
         in_specs=[smem()] + [vmem()] * (1 + chans),
         out_specs=vmem(),
@@ -526,7 +529,6 @@
         cost_estimate=cost(0, 3 * MIB),
         name="sum_near",
     )(me, own_grad, *packed)
-    held, near = lax.optimization_barrier((held, near))
     whole, half = 1 << order[-1], 1 << halves[-1]
     across, beside, both = (
         lax.ppermute(held, "dom", [(i, i ^ flip) for i in range(parts)]) for flip in (whole, half, whole | half)
@@ -534,9 +536,21 @@
     mine = held.astype(F32) + across.astype(F32)
     other = beside.astype(F32) + both.astype(F32)
     held = jnp.concatenate([mine, other], axis=0).astype(BF)
-    held, back = lax.optimization_barrier((held, back))
+    held, back, near = lax.optimization_barrier((held, back, near))
+    grad_feats = pl.pallas_call(
+        final_kernel,
+        out_shape=sds((chan_width, node_count), BF),
+        in_specs=[smem()] + [vmem()] * 2,
+        out_specs=vmem(),
+        scratch_shapes=[pltpu.VMEM((block_rows, chan_width, size), F32)],
+        compiler_params=params(BIG),
+        cost_estimate=cost(0, 4 * MIB),
+        name="sum_returned",
+    )(send, near, back)
     for level in reversed(range(len(halves) - 1)):
         held = jnp.concatenate([held, lax.ppermute(held, "dom", flips[level])], axis=0)
+        if level == len(halves) - 2:
+            held, grad_feats = lax.optimization_barrier((held, grad_feats))
     address = jnp.int32(0)
     for level in range(len(halves)):
         address = address * 2 + bits[level][0]
@@ -550,16 +564,6 @@
         name="weight_spread",
     )(address.reshape(1), held)
 
-    grad_feats = pl.pallas_call(
-        final_kernel,
-        out_shape=sds((chan_width, node_count), BF),
-        in_specs=[smem()] + [vmem()] * 2,
-        out_specs=vmem(),
-        scratch_shapes=[pltpu.VMEM((block_rows, chan_width, size), F32)],
-        compiler_params=params(BIG),
-        cost_estimate=cost(0, 4 * MIB),
-        name="sum_returned",
-    )(send, near, back)
     return (out_h, grad_feats.T, grad_w_self, grad_w_neigh)
 
 

time: 150 us -> 145 us (0.967)
  waiting for transfers between devices: 50.4 us -> 45.1 us
    ppermute x14, waiting for transfers between devices: 13.9 us -> 10.2 us  [exchange(): lax.ppermute(chunks[shift], 'chan', [(i, (i + shift) % count) for i in ra...]
  transfers between devices with their start and end apart: 27 -> 27, of which waited for: 14 -> 17; matrix products, arithmetic and copies ran while one was open for 0% -> 0% of each run, Pallas kernels for 4% -> 4%
where the time goes in v5:
time: 145 us; the launch traced here: 143 us
  starting transfers between devices  70.2 us (48%)
  waiting for transfers between devices  45.1 us (31%)
  Pallas kernels  23.9 us (16%)
  local copies, waits for them, and re-layouts  2.63 us (2%)
    ppermute x14, starting transfers between devices, exchange(): lax.ppermute(chunks[shift], 'chan', [(i, (i + shift) % count) for i in ra...  35.5 us
    all_to_all x1, waiting for transfers between devices, per_device(): lax.all_to_all(mean, 'chan', split_axis=0, concat_axis=0, tiled=True)  15.5 us
    ppermute x14, waiting for transfers between devices, exchange(): lax.ppermute(chunks[shift], 'chan', [(i, (i + shift) % count) for i in ra...  10.2 us
    all_to_all x1, starting transfers between devices, per_device(): lax.all_to_all(mean, 'chan', split_axis=0, concat_axis=0, tiled=True)  8.48 us
    all_to_all x1, starting transfers between devices, per_device(): lax.all_to_all(outgoing, 'dom', split_axis=0, concat_axis=0, tiled=True)  7.76 us
    pallas_call x1, Pallas kernels, per_device(): pl.pallas_call(scatter_kernel, out_shape=[pltpu.HBM((block_rows, chan_wid...  6.44 us
    pallas_call x1, Pallas kernels, per_device(): pl.pallas_call(gather_kernel, out_shape=[pltpu.HBM((chans, chan_width, no...  6.18 us
    all_to_all x1, starting transfers between devices, per_device(): lax.all_to_all(far_grad.reshape(parts, slots, chan_width, size), 'dom', s...  6.16 us
  transfers between devices with their start and end apart: 27, of which 17 were waited for; matrix products, arithmetic and copies ran while one was open for 0% of the time, Pallas kernels for 4%

profile of v5, /device:TPU:2, one launch (start us, length us, event | category | flops | bytes accessed | tf_op | source)
XLA Modules:
  0.0 142.8 jit_solution(8751329012465558865)
XLA Ops:
  0.6 2.5 %pack_outgoing.1 = bf16[32,4,64,128]{3,2,1,0:T(8,128)(2,1)} custom-call(s32[4,32]{1,0:T(4,128)} %bitcast.29, bf16[64,4096]{1,0:T(8,128)(2,1)} %bitcast.21), custom_call_target="tpu_custom_call" | custom-call | bytes 5242880 | tf_op jit(solution)/shard_map/pack_outgoing/pallas_call | solution.py:363
  3.2 7.8 %all-to-all-start = ((bf16[32,4,64,128]{3,2,1,0:T(8,128)(2,1)}), bf16[32,4,64,128]{3,2,1,0:T(8,128)(2,1)S(1)}, u32[]{:S(2)}, u32[]{:S(2)}) async-start(bf16[32,4,64,128]{3,2,1,0:T(8,128)(2,1)} %pack_outgoing.1), calls=%async_computation | async-start | bytes 4194304 | tf_op jit(solution)/shard_map/all_to_all | solution.py:376
  11.0 0.9 split_feats.1
  11.9 2.0 %collective-permute-start = (bf16[64,512]{1,0:T(8,128)(2,1)}, bf16[64,512]{1,0:T(8,128)(2,1)S(1)}, u32[]{:S(2)}, u32[]{:S(2)}) collective-permute-start(bf16[64,512]{1,0:T(8,128)(2,1)} %get-tuple-element.76), channel_id=1, source_target_pairs={{0,1},{1,2},{2,3},{3,4},{4,5},{5,6},{6,7},{7,0},{8,9},{9,10},{10,1... | collective-permute-start | bytes 196616 | tf_op jit(solution)/shard_map/ppermute | solution.py:315
  13.9 3.3 %collective-permute-start.1 = (bf16[64,512]{1,0:T(8,128)(2,1)}, bf16[64,512]{1,0:T(8,128)(2,1)S(1)}, u32[]{:S(2)}, u32[]{:S(2)}) collective-permute-start(bf16[64,512]{1,0:T(8,128)(2,1)} %get-tuple-element.77), channel_id=1, source_target_pairs={{0,2},{1,3},{2,4},{3,5},{4,6},{5,7},{6,0},{7,1},{8,10},{9,11},{10,... | collective-permute-start | bytes 196616 | tf_op jit(solution)/shard_map/ppermute | solution.py:315
  17.1 4.0 %collective-permute-start.2 = (bf16[64,512]{1,0:T(8,128)(2,1)}, bf16[64,512]{1,0:T(8,128)(2,1)S(1)}, u32[]{:S(2)}, u32[]{:S(2)}) collective-permute-start(bf16[64,512]{1,0:T(8,128)(2,1)} %get-tuple-element.78), channel_id=1, source_target_pairs={{0,3},{1,4},{2,5},{3,6},{4,7},{5,0},{6,1},{7,2},{8,11},{9,12},{10,... | collective-permute-start | bytes 196616 | tf_op jit(solution)/shard_map/ppermute | solution.py:315
  21.7 4.9 %collective-permute-start.4 = (bf16[64,512]{1,0:T(8,128)(2,1)}, bf16[64,512]{1,0:T(8,128)(2,1)S(1)}, u32[]{:S(2)}, u32[]{:S(2)}) collective-permute-start(bf16[64,512]{1,0:T(8,128)(2,1)} %get-tuple-element.80), channel_id=1, source_target_pairs={{0,5},{1,6},{2,7},{3,0},{4,1},{5,2},{6,3},{7,4},{8,13},{9,14},{10,... | collective-permute-start | bytes 196616 | tf_op jit(solution)/shard_map/ppermute | solution.py:315
  26.7 2.7 %collective-permute-start.5 = (bf16[64,512]{1,0:T(8,128)(2,1)}, bf16[64,512]{1,0:T(8,128)(2,1)S(1)}, u32[]{:S(2)}, u32[]{:S(2)}) collective-permute-start(bf16[64,512]{1,0:T(8,128)(2,1)} %get-tuple-element.81), channel_id=1, source_target_pairs={{0,6},{1,7},{2,0},{3,1},{4,2},{5,3},{6,4},{7,5},{8,14},{9,15},{10,... | collective-permute-start | bytes 196616 | tf_op jit(solution)/shard_map/ppermute | solution.py:315
  29.3 1.0 collective-permute-start.6
  30.4 5.7 %collective-permute-done.4.refs_5_ = bf16[64,512]{1,0:T(8,128)(2,1)S(1)} collective-permute-done((bf16[64,512]{1,0:T(8,128)(2,1)}, bf16[64,512]{1,0:T(8,128)(2,1)S(1)}, u32[]{:S(2)}, u32[]{:S(2)}) %collective-permute-start.4) | collective-permute-done | bytes 65568 | tf_op jit(solution)/shard_map/ppermute | solution.py:315
  36.1 0.6 copy-done.12
  36.7 0.6 copy-done.13
  37.4 1.5 %all-to-all-done = bf16[32,4,64,128]{3,2,1,0:T(8,128)(2,1)S(1)} async-done(((bf16[32,4,64,128]{3,2,1,0:T(8,128)(2,1)}), bf16[32,4,64,128]{3,2,1,0:T(8,128)(2,1)S(1)}, u32[]{:S(2)}, u32[]{:S(2)}) %all-to-all-start) | async-done | bytes 2097184 | tf_op jit(solution)/shard_map/all_to_all | solution.py:376
  38.9 6.2 %neighbour_mean.1 = (bf16[8,64,512]{2,1,0:T(8,128)(2,1)}, f32[8,8,512]{2,1,0:T(8,128)S(1)}) custom-call(s32[8,32]{1,0:T(8,128)S(1)} %bitcast.27, s32[32]{0:T(128)S(1)} %copy-done.7, bf16[64,4096]{1,0:T(8,128)(2,1)S(1)} %bitcast.23, bf16[128,64,128]{2,1,0:T(8,128)(2,1)S(1)} %bitcast.18, bf16[32,8,128,128]{3,2,1,0:T(8,128)(2,1)} %vals_ref.3), custom_call_target="tpu_custom_call" | custom-call | flops 536870912 | bytes 11534336 | tf_op jit(solution)/shard_map/neighbour_mean/pallas_call | solution.py:400
  45.1 8.5 %all-to-all-start.1 = ((bf16[8,64,512]{2,1,0:T(8,128)(2,1)}), bf16[8,64,512]{2,1,0:T(8,128)(2,1)S(1)}, u32[]{:S(2)}, u32[]{:S(2)}) async-start(bf16[8,64,512]{2,1,0:T(8,128)(2,1)} %get-tuple-element.96), calls=%async_computation.1 | async-start | bytes 1048576 | tf_op jit(solution)/shard_map/all_to_all | solution.py:415
  53.7 1.4 %self_part.1 = (bf16[512,512]{1,0:T(8,128)(2,1)S(1)}, f32[256,512]{1,0:T(8,128)S(1)}, bf16[256,512]{1,0:T(8,128)(2,1)S(1)}, bf16[256,512]{1,0:T(8,128)(2,1)S(1)}) custom-call(s32[1]{0:T(128)} %bitcast.me_ref, bf16[512,256]{1,0:T(8,128)(2,1)S(1)} %copy-done.3, f32[256,1]{1,0:T(8,128)S(1)} %copy.13.bias_ref, bf16[512,256]{1,0:T(8,128)(2,1)S(1)} %copy-done.2, ...), custom_call_target="tpu_custom_call" | custom-call | flops 134217728 | bytes 2097152 | tf_op jit(solution)/shard_map/self_part/pallas_call | solution.py:390
  55.2 15.5 %all-to-all-done.1 = bf16[8,64,512]{2,1,0:T(8,128)(2,1)S(1)} async-done(((bf16[8,64,512]{2,1,0:T(8,128)(2,1)}), bf16[8,64,512]{2,1,0:T(8,128)(2,1)S(1)}, u32[]{:S(2)}, u32[]{:S(2)}) %all-to-all-start.1) | async-done | bytes 524320 | tf_op jit(solution)/shard_map/all_to_all | solution.py:415
  70.7 1.8 %layer_head.1 = (bf16[256,512]{1,0:T(8,128)(2,1)S(1)}, bf16[256,512]{1,0:T(8,128)(2,1)S(1)}, bf16[512,512]{1,0:T(8,128)(2,1)}) custom-call(s32[1]{0:T(128)} %bitcast.me_ref, f32[8,8,512]{2,1,0:T(8,128)S(1)} %get-tuple-element.84.degree_ref, f32[256,512]{1,0:T(8,128)S(1)} %get-tuple-element.93.pre_ref, bf16[256,512]{1,0:T(8,128)(2,1)S(1)} %get-tuple-element.94.turned_ref, ...), custom_call_target="tpu_custom_call" | custom-call | flops 268435456 | bytes 4194304 | tf_op jit(solution)/shard_map/layer_head/pallas_call | solution.py:417
  72.5 3.5 %all-to-all-start.2 = ((bf16[8,64,512]{2,1,0:T(8,128)(2,1)}), bf16[8,64,512]{2,1,0:T(8,128)(2,1)S(1)}, u32[]{:S(2)}, u32[]{:S(2)}) async-start(bf16[8,64,512]{2,1,0:T(8,128)(2,1)} %bitcast.8), calls=%async_computation.2 | async-start | bytes 1048576 | tf_op jit(solution)/shard_map/all_to_all | solution.py:426
  76.6 1.5 %collective-permute-done.7.recv_ref = bf16[16,8,8,128]{3,2,1,0:T(8,128)(2,1)S(1)} collective-permute-done((bf16[16,8,8,128]{3,2,1,0:T(8,128)(2,1)S(1)}, bf16[16,8,8,128]{3,2,1,0:T(8,128)(2,1)S(1)}, u32[]{:S(2)}, u32[]{:S(2)}) %collective-permute-start.7) | collective-permute-done | bytes 262176 | tf_op jit(solution)/shard_map/ppermute | solution.py:447
  78.2 1.1 collective-permute-start.8
  79.3 4.5 %collective-permute-done.8.recv_ref = bf16[8,8,8,128]{3,2,1,0:T(8,128)(2,1)S(1)} collective-permute-done((bf16[8,8,8,128]{3,2,1,0:T(8,128)(2,1)S(1)}, bf16[8,8,8,128]{3,2,1,0:T(8,128)(2,1)S(1)}, u32[]{:S(2)}, u32[]{:S(2)}) %collective-permute-start.8) | collective-permute-done | bytes 131104 | tf_op jit(solution)/shard_map/ppermute | solution.py:447
  83.9 1.0 collective-permute-start.9
  85.0 3.3 %collective-permute-done.9.recv_ref = bf16[4,8,8,128]{3,2,1,0:T(8,128)(2,1)S(1)} collective-permute-done((bf16[4,8,8,128]{3,2,1,0:T(8,128)(2,1)S(1)}, bf16[4,8,8,128]{3,2,1,0:T(8,128)(2,1)S(1)}, u32[]{:S(2)}, u32[]{:S(2)}) %collective-permute-start.9) | collective-permute-done | bytes 65568 | tf_op jit(solution)/shard_map/ppermute | solution.py:459
  88.3 1.8 %collective-permute-start.10 = (bf16[4,8,8,128]{3,2,1,0:T(8,128)(2,1)S(1)}, bf16[4,8,8,128]{3,2,1,0:T(8,128)(2,1)S(1)}, u32[]{:S(2)}, u32[]{:S(2)}) collective-permute-start(bf16[4,8,8,128]{3,2,1,0:T(8,128)(2,1)S(1)} %weight_add.2.held_ref), channel_id=1, source_target_pairs={{0,32},{8,40},{16,48},{24,56},{32,0},{40,8},{48,16},{56,24},{64,96... | collective-permute-start | bytes 196616 | tf_op jit(solution)/shard_map/ppermute | solution.py:473
  90.0 0.9 side_grads.1
  91.0 3.3 %collective-permute-done.10.recv_ref = bf16[4,8,8,128]{3,2,1,0:T(8,128)(2,1)S(1)} collective-permute-done((bf16[4,8,8,128]{3,2,1,0:T(8,128)(2,1)S(1)}, bf16[4,8,8,128]{3,2,1,0:T(8,128)(2,1)S(1)}, u32[]{:S(2)}, u32[]{:S(2)}) %collective-permute-start.10) | collective-permute-done | bytes 65568 | tf_op jit(solution)/shard_map/ppermute | solution.py:473
  94.3 6.4 %table_grad.1 = (f32[32,64,128]{2,1,0:T(8,128)}, bf16[128,64,128]{2,1,0:T(8,128)(2,1)}) custom-call(s32[8,32]{1,0:T(8,128)S(1)} %bitcast.28, s32[32]{0:T(128)S(1)} %copy-done.7, bf16[32,8,128,128]{3,2,1,0:T(8,128)(2,1)} %vals_ref.3, bf16[8,64,512]{2,1,0:T(8,128)(2,1)S(1)} %all-to-all-done.2.scaled_ref), custom_call_target="tpu_custom_call" | custom-call | flops 536870912 | bytes 12582912 | tf_op jit(solution)/shard_map/table_grad/pallas_call | solution.py:477
  100.8 6.2 %all-to-all-start.3 = ((bf16[32,4,64,128]{3,2,1,0:T(8,128)(2,1)}), bf16[32,4,64,128]{3,2,1,0:T(8,128)(2,1)S(1)}, u32[]{:S(2)}, u32[]{:S(2)}) async-start(bf16[32,4,64,128]{3,2,1,0:T(8,128)(2,1)} %bitcast.31), calls=%async_computation.3 | async-start | bytes 4194304 | tf_op jit(solution)/shard_map/all_to_all | solution.py:498
  107.0 5.9 %collective-permute-start.11 = (bf16[64,640]{1,0:T(8,128)(2,1)S(1)}, bf16[64,640]{1,0:T(8,128)(2,1)S(1)}, u32[]{:S(2)}, u32[]{:S(2)}) collective-permute-start(bf16[64,640]{1,0:T(8,128)(2,1)S(1)} %get-tuple-element.129), channel_id=1, source_target_pairs={{0,4},{1,5},{2,6},{3,7},{4,0},{5,1},{6,2},{7,3},{8,12},{9,13},{10,... | collective-permute-start | bytes 245768 | tf_op jit(solution)/shard_map/ppermute | solution.py:315
  113.5 4.5 %collective-permute-start.13 = (bf16[64,640]{1,0:T(8,128)(2,1)S(1)}, bf16[64,640]{1,0:T(8,128)(2,1)S(1)}, u32[]{:S(2)}, u32[]{:S(2)}) collective-permute-start(bf16[64,640]{1,0:T(8,128)(2,1)S(1)} %get-tuple-element.131), channel_id=1, source_target_pairs={{0,5},{1,6},{2,7},{3,0},{4,1},{5,2},{6,3},{7,4},{8,13},{9,14},{10,... | collective-permute-start | bytes 245768 | tf_op jit(solution)/shard_map/ppermute | solution.py:315
  118.0 0.6 collective-permute-start.14
  118.6 3.6 %collective-permute-start.15 = (bf16[64,640]{1,0:T(8,128)(2,1)S(1)}, bf16[64,640]{1,0:T(8,128)(2,1)S(1)}, u32[]{:S(2)}, u32[]{:S(2)}) collective-permute-start(bf16[64,640]{1,0:T(8,128)(2,1)S(1)} %get-tuple-element.133), channel_id=1, source_target_pairs={{0,6},{1,7},{2,0},{3,1},{4,2},{5,3},{6,4},{7,5},{8,14},{9,15},{10,... | collective-permute-start | bytes 245768 | tf_op jit(solution)/shard_map/ppermute | solution.py:315
  122.7 1.4 collective-permute-done.12.refs_1_
  124.1 1.3 collective-permute-start.17
  125.4 0.9 collective-permute-done.14.refs_3_
  126.3 1.0 collective-permute-done.15.refs_4_
  127.4 0.6 collective-permute-done.16.refs_5_
  128.5 3.1 %collective-permute-start.18 = (bf16[1,32,128]{2,1,0:T(8,128)(2,1)S(1)}, bf16[1,32,128]{2,1,0:T(8,128)(2,1)S(1)}, u32[]{:S(2)}, u32[]{:S(2)}) collective-permute-start(bf16[1,32,128]{2,1,0:T(8,128)(2,1)S(1)} %bitcast.24), channel_id=1, source_target_pairs={{0,128},{8,136},{16,144},{24,152},{32,160},{40,168},{48,176},{56,1... | collective-permute-start | bytes 24584 | tf_op jit(solution)/shard_map/ppermute | solution.py:534
  131.6 0.6 collective-permute-start.19
  132.8 1.2 copy-done.1
  134.1 0.6 collective-permute-done.18
  135.2 1.8 %collective-permute-done.20 = bf16[1,32,128]{2,1,0:T(8,128)(2,1)S(1)} collective-permute-done((bf16[1,32,128]{2,1,0:T(8,128)(2,1)S(1)}, bf16[1,32,128]{2,1,0:T(8,128)(2,1)S(1)}, u32[]{:S(2)}, u32[]{:S(2)}) %collective-permute-start.20) | collective-permute-done | bytes 8224 | tf_op jit(solution)/shard_map/ppermute | solution.py:534
  137.1 0.6 collective-permute-start.21
  137.7 2.2 %sum_returned.1 = bf16[64,4096]{1,0:T(8,128)(2,1)} custom-call(s32[4,32]{1,0:T(4,128)S(1)} %bitcast.30, f32[32,64,128]{2,1,0:T(8,128)S(1)} %sum_near.1.near_ref, bf16[32,4,64,128]{3,2,1,0:T(8,128)(2,1)S(1)} %all-to-all-done.3.back_ref), custom_call_target="tpu_custom_call" | custom-call | bytes 4194304 | tf_op jit(solution)/shard_map/sum_returned/pallas_call | solution.py:540
  139.9 1.0 collective-permute-done.21
  140.9 1.2 collective-permute-done.22
  142.1 0.7 weight_spread.1
  (59 shorter events, 4.4 us)
Async XLA Ops:
  3.2 7.8 %copy-start = (bf16[4096,64]{0,1:T(8,128)(2,1)S(1)}, bf16[4096,64]{0,1:T(8,128)(2,1)}, u32[]{:S(2)}) copy-start(bf16[4096,64]{0,1:T(8,128)(2,1)} %param.9) | copy-start | bytes 1572868
  3.2 35.7 %copy-start.5 = (s32[32,8]{0,1:T(8,128)S(1)}, s32[32,8]{0,1:T(8,128)}, u32[]{:S(2)}) copy-start(s32[32,8]{0,1:T(8,128)} %param.11) | copy-start | bytes 3076
  3.2 35.7 %copy-start.7 = (s32[32]{0:T(128)S(1)}, s32[32]{0:T(128)}, u32[]{:S(2)}) copy-start(s32[32]{0:T(128)} %counts_ref.3) | copy-start | bytes 388
  3.2 35.6 %all-to-all-start = ((bf16[32,4,64,128]{3,2,1,0:T(8,128)(2,1)}), bf16[32,4,64,128]{3,2,1,0:T(8,128)(2,1)S(1)}, u32[]{:S(2)}, u32[]{:S(2)}) async-start(bf16[32,4,64,128]{3,2,1,0:T(8,128)(2,1)} %pack_outgoing.1), calls=%async_computation | async-start | bytes 4194304 | tf_op jit(solution)/shard_map/all_to_all | solution.py:376
  11.9 14.8 %collective-permute-start = (bf16[64,512]{1,0:T(8,128)(2,1)}, bf16[64,512]{1,0:T(8,128)(2,1)S(1)}, u32[]{:S(2)}, u32[]{:S(2)}) collective-permute-start(bf16[64,512]{1,0:T(8,128)(2,1)} %get-tuple-element.76), channel_id=1, source_target_pairs={{0,1},{1,2},{2,3},{3,4},{4,5},{5,6},{6,7},{7,0},{8,9},{9,10},{10,1... | collective-permute-start | bytes 196616 | tf_op jit(solution)/shard_map/ppermute | solution.py:315
  13.9 15.5 %collective-permute-start.1 = (bf16[64,512]{1,0:T(8,128)(2,1)}, bf16[64,512]{1,0:T(8,128)(2,1)S(1)}, u32[]{:S(2)}, u32[]{:S(2)}) collective-permute-start(bf16[64,512]{1,0:T(8,128)(2,1)} %get-tuple-element.77), channel_id=1, source_target_pairs={{0,2},{1,3},{2,4},{3,5},{4,6},{5,7},{6,0},{7,1},{8,10},{9,11},{10,... | collective-permute-start | bytes 196616 | tf_op jit(solution)/shard_map/ppermute | solution.py:315
  17.1 13.2 %collective-permute-start.2 = (bf16[64,512]{1,0:T(8,128)(2,1)}, bf16[64,512]{1,0:T(8,128)(2,1)S(1)}, u32[]{:S(2)}, u32[]{:S(2)}) collective-permute-start(bf16[64,512]{1,0:T(8,128)(2,1)} %get-tuple-element.78), channel_id=1, source_target_pairs={{0,3},{1,4},{2,5},{3,6},{4,7},{5,0},{6,1},{7,2},{8,11},{9,12},{10,... | collective-permute-start | bytes 196616 | tf_op jit(solution)/shard_map/ppermute | solution.py:315
  21.2 9.2 %collective-permute-start.3 = (bf16[64,512]{1,0:T(8,128)(2,1)}, bf16[64,512]{1,0:T(8,128)(2,1)S(1)}, u32[]{:S(2)}, u32[]{:S(2)}) collective-permute-start(bf16[64,512]{1,0:T(8,128)(2,1)} %get-tuple-element.79), channel_id=1, source_target_pairs={{0,4},{1,5},{2,6},{3,7},{4,0},{5,1},{6,2},{7,3},{8,12},{9,13},{10,... | collective-permute-start | bytes 196616 | tf_op jit(solution)/shard_map/ppermute | solution.py:315
  21.7 14.4 %collective-permute-start.4 = (bf16[64,512]{1,0:T(8,128)(2,1)}, bf16[64,512]{1,0:T(8,128)(2,1)S(1)}, u32[]{:S(2)}, u32[]{:S(2)}) collective-permute-start(bf16[64,512]{1,0:T(8,128)(2,1)} %get-tuple-element.80), channel_id=1, source_target_pairs={{0,5},{1,6},{2,7},{3,0},{4,1},{5,2},{6,3},{7,4},{8,13},{9,14},{10,... | collective-permute-start | bytes 196616 | tf_op jit(solution)/shard_map/ppermute | solution.py:315
  26.7 9.4 %copy-start.8 = (bf16[64,512]{1,0:T(8,128)(2,1)}, bf16[64,512]{1,0:T(8,128)(2,1)S(1)}, u32[]{:S(2)}) copy-start(bf16[64,512]{1,0:T(8,128)(2,1)S(1)} %collective-permute-done.refs_1_) | copy-start | bytes 196612
  26.7 9.4 %collective-permute-start.5 = (bf16[64,512]{1,0:T(8,128)(2,1)}, bf16[64,512]{1,0:T(8,128)(2,1)S(1)}, u32[]{:S(2)}, u32[]{:S(2)}) collective-permute-start(bf16[64,512]{1,0:T(8,128)(2,1)} %get-tuple-element.81), channel_id=1, source_target_pairs={{0,6},{1,7},{2,0},{3,1},{4,2},{5,3},{6,4},{7,5},{8,14},{9,15},{10,... | collective-permute-start | bytes 196616 | tf_op jit(solution)/shard_map/ppermute | solution.py:315
  29.3 6.8 %copy-start.9 = (bf16[64,512]{1,0:T(8,128)(2,1)}, bf16[64,512]{1,0:T(8,128)(2,1)S(1)}, u32[]{:S(2)}) copy-start(bf16[64,512]{1,0:T(8,128)(2,1)S(1)} %collective-permute-done.1.refs_2_) | copy-start | bytes 196612
  29.3 8.0 %collective-permute-start.6 = (bf16[64,512]{1,0:T(8,128)(2,1)}, bf16[64,512]{1,0:T(8,128)(2,1)}, u32[]{:S(2)}, u32[]{:S(2)}) collective-permute-start(bf16[64,512]{1,0:T(8,128)(2,1)} %get-tuple-element.82), channel_id=1, source_target_pairs={{0,7},{1,0},{2,1},{3,2},{4,3},{5,4},{6,5},{7,6},{8,15},{9,8},{10,9... | collective-permute-start | bytes 196616 | tf_op jit(solution)/shard_map/ppermute | solution.py:315
  30.3 5.8 %copy-start.10 = (bf16[64,512]{1,0:T(8,128)(2,1)}, bf16[64,512]{1,0:T(8,128)(2,1)S(1)}, u32[]{:S(2)}) copy-start(bf16[64,512]{1,0:T(8,128)(2,1)S(1)} %collective-permute-done.2.refs_3_) | copy-start | bytes 196612
  30.4 5.8 %copy-start.11 = (bf16[64,512]{1,0:T(8,128)(2,1)}, bf16[64,512]{1,0:T(8,128)(2,1)S(1)}, u32[]{:S(2)}) copy-start(bf16[64,512]{1,0:T(8,128)(2,1)S(1)} %collective-permute-done.3.refs_4_) | copy-start | bytes 196612
  36.1 0.6 copy-start.12
  36.7 0.6 copy-start.13
  38.9 14.7 %copy-start.14 = (f32[256]{0:T(256)S(1)}, f32[256]{0:T(256)}, u32[]{:S(2)}) copy-start(f32[256]{0:T(256)} %param.16) | copy-start | bytes 3076
  38.9 14.8 %copy-start.2 = (bf16[512,256]{1,0:T(8,128)(2,1)S(1)}, bf16[512,256]{1,0:T(8,128)(2,1)}, u32[]{:S(2)}) copy-start(bf16[512,256]{1,0:T(8,128)(2,1)} %weight_ref.4) | copy-start | bytes 786436
  38.9 14.8 %copy-start.3 = (bf16[512,256]{1,0:T(8,128)(2,1)S(1)}, bf16[512,256]{1,0:T(8,128)(2,1)}, u32[]{:S(2)}) copy-start(bf16[512,256]{1,0:T(8,128)(2,1)} %weight_ref.5) | copy-start | bytes 786436
  38.9 14.8 %copy-start.4 = (bf16[512,256]{1,0:T(8,128)(2,1)S(1)}, bf16[512,256]{1,0:T(8,128)(2,1)}, u32[]{:S(2)}) copy-start(bf16[512,256]{1,0:T(8,128)(2,1)} %cot_ref.1) | copy-start | bytes 786436
  45.1 25.6 %all-to-all-start.1 = ((bf16[8,64,512]{2,1,0:T(8,128)(2,1)}), bf16[8,64,512]{2,1,0:T(8,128)(2,1)S(1)}, u32[]{:S(2)}, u32[]{:S(2)}) async-start(bf16[8,64,512]{2,1,0:T(8,128)(2,1)} %get-tuple-element.96), calls=%async_computation.1 | async-start | bytes 1048576 | tf_op jit(solution)/shard_map/all_to_all | solution.py:415
  72.5 21.9 %all-to-all-start.2 = ((bf16[8,64,512]{2,1,0:T(8,128)(2,1)}), bf16[8,64,512]{2,1,0:T(8,128)(2,1)S(1)}, u32[]{:S(2)}, u32[]{:S(2)}) async-start(bf16[8,64,512]{2,1,0:T(8,128)(2,1)} %bitcast.8), calls=%async_computation.2 | async-start | bytes 1048576 | tf_op jit(solution)/shard_map/all_to_all | solution.py:426
  76.5 1.6 %collective-permute-start.7 = (bf16[16,8,8,128]{3,2,1,0:T(8,128)(2,1)S(1)}, bf16[16,8,8,128]{3,2,1,0:T(8,128)(2,1)S(1)}, u32[]{:S(2)}, u32[]{:S(2)}) collective-permute-start(bf16[16,8,8,128]{3,2,1,0:T(8,128)(2,1)S(1)} %get-tuple-element.101), channel_id=1, source_target_pairs={{0,8},{8,0},{16,24},{24,16},{32,40},{40,32},{48,56},{56,48},{64,72... | collective-permute-start | bytes 786440 | tf_op jit(solution)/shard_map/ppermute | solution.py:447
  78.2 5.6 %collective-permute-start.8 = (bf16[8,8,8,128]{3,2,1,0:T(8,128)(2,1)S(1)}, bf16[8,8,8,128]{3,2,1,0:T(8,128)(2,1)S(1)}, u32[]{:S(2)}, u32[]{:S(2)}) collective-permute-start(bf16[8,8,8,128]{3,2,1,0:T(8,128)(2,1)S(1)} %get-tuple-element.103), channel_id=1, source_target_pairs={{0,16},{8,24},{16,0},{24,8},{32,48},{40,56},{48,32},{56,40},{64,80... | collective-permute-start | bytes 393224 | tf_op jit(solution)/shard_map/ppermute | solution.py:447
  83.9 4.4 %collective-permute-start.9 = (bf16[4,8,8,128]{3,2,1,0:T(8,128)(2,1)S(1)}, bf16[4,8,8,128]{3,2,1,0:T(8,128)(2,1)S(1)}, u32[]{:S(2)}, u32[]{:S(2)}) collective-permute-start(bf16[4,8,8,128]{3,2,1,0:T(8,128)(2,1)S(1)} %get-tuple-element.105), channel_id=1, source_target_pairs={{0,64},{8,72},{16,80},{24,88},{32,96},{40,104},{48,112},{56,120},{... | collective-permute-start | bytes 196616 | tf_op jit(solution)/shard_map/ppermute | solution.py:459
  88.3 6.0 %collective-permute-start.10 = (bf16[4,8,8,128]{3,2,1,0:T(8,128)(2,1)S(1)}, bf16[4,8,8,128]{3,2,1,0:T(8,128)(2,1)S(1)}, u32[]{:S(2)}, u32[]{:S(2)}) collective-permute-start(bf16[4,8,8,128]{3,2,1,0:T(8,128)(2,1)S(1)} %weight_add.2.held_ref), channel_id=1, source_target_pairs={{0,32},{8,40},{16,48},{24,56},{32,0},{40,8},{48,16},{56,24},{64,96... | collective-permute-start | bytes 196616 | tf_op jit(solution)/shard_map/ppermute | solution.py:473
  100.8 36.3 %all-to-all-start.3 = ((bf16[32,4,64,128]{3,2,1,0:T(8,128)(2,1)}), bf16[32,4,64,128]{3,2,1,0:T(8,128)(2,1)S(1)}, u32[]{:S(2)}, u32[]{:S(2)}) async-start(bf16[32,4,64,128]{3,2,1,0:T(8,128)(2,1)} %bitcast.31), calls=%async_computation.3 | async-start | bytes 4194304 | tf_op jit(solution)/shard_map/all_to_all | solution.py:498
  107.0 30.8 %copy-start.6 = (s32[1,32,4]{1,2,0:T(4,128)S(1)}, s32[1,32,4]{1,2,0:T(4,128)}, u32[]{:S(2)}) copy-start(s32[1,32,4]{1,2,0:T(4,128)} %param.13) | copy-start | bytes 1540
  107.0 15.1 %collective-permute-start.11 = (bf16[64,640]{1,0:T(8,128)(2,1)S(1)}, bf16[64,640]{1,0:T(8,128)(2,1)S(1)}, u32[]{:S(2)}, u32[]{:S(2)}) collective-permute-start(bf16[64,640]{1,0:T(8,128)(2,1)S(1)} %get-tuple-element.129), channel_id=1, source_target_pairs={{0,4},{1,5},{2,6},{3,7},{4,0},{5,1},{6,2},{7,3},{8,12},{9,13},{10,... | collective-permute-start | bytes 245768 | tf_op jit(solution)/shard_map/ppermute | solution.py:315
  113.0 11.1 %collective-permute-start.12 = (bf16[64,640]{1,0:T(8,128)(2,1)S(1)}, bf16[64,640]{1,0:T(8,128)(2,1)S(1)}, u32[]{:S(2)}, u32[]{:S(2)}) collective-permute-start(bf16[64,640]{1,0:T(8,128)(2,1)S(1)} %get-tuple-element.130), channel_id=1, source_target_pairs={{0,3},{1,4},{2,5},{3,6},{4,7},{5,0},{6,1},{7,2},{8,11},{9,12},{10,... | collective-permute-start | bytes 245768 | tf_op jit(solution)/shard_map/ppermute | solution.py:315
  113.5 11.9 %collective-permute-start.13 = (bf16[64,640]{1,0:T(8,128)(2,1)S(1)}, bf16[64,640]{1,0:T(8,128)(2,1)S(1)}, u32[]{:S(2)}, u32[]{:S(2)}) collective-permute-start(bf16[64,640]{1,0:T(8,128)(2,1)S(1)} %get-tuple-element.131), channel_id=1, source_target_pairs={{0,5},{1,6},{2,7},{3,0},{4,1},{5,2},{6,3},{7,4},{8,13},{9,14},{10,... | collective-permute-start | bytes 245768 | tf_op jit(solution)/shard_map/ppermute | solution.py:315
  118.0 8.3 %collective-permute-start.14 = (bf16[64,640]{1,0:T(8,128)(2,1)S(1)}, bf16[64,640]{1,0:T(8,128)(2,1)S(1)}, u32[]{:S(2)}, u32[]{:S(2)}) collective-permute-start(bf16[64,640]{1,0:T(8,128)(2,1)S(1)} %get-tuple-element.132), channel_id=1, source_target_pairs={{0,2},{1,3},{2,4},{3,5},{4,6},{5,7},{6,0},{7,1},{8,10},{9,11},{10,... | collective-permute-start | bytes 245768 | tf_op jit(solution)/shard_map/ppermute | solution.py:315
  118.6 8.8 %collective-permute-start.15 = (bf16[64,640]{1,0:T(8,128)(2,1)S(1)}, bf16[64,640]{1,0:T(8,128)(2,1)S(1)}, u32[]{:S(2)}, u32[]{:S(2)}) collective-permute-start(bf16[64,640]{1,0:T(8,128)(2,1)S(1)} %get-tuple-element.133), channel_id=1, source_target_pairs={{0,6},{1,7},{2,0},{3,1},{4,2},{5,3},{6,4},{7,5},{8,14},{9,15},{10,... | collective-permute-start | bytes 245768 | tf_op jit(solution)/shard_map/ppermute | solution.py:315
  122.1 5.9 %collective-permute-start.16 = (bf16[64,640]{1,0:T(8,128)(2,1)S(1)}, bf16[64,640]{1,0:T(8,128)(2,1)S(1)}, u32[]{:S(2)}, u32[]{:S(2)}) collective-permute-start(bf16[64,640]{1,0:T(8,128)(2,1)S(1)} %get-tuple-element.134), channel_id=1, source_target_pairs={{0,1},{1,2},{2,3},{3,4},{4,5},{5,6},{6,7},{7,0},{8,9},{9,10},{10,1... | collective-permute-start | bytes 245768 | tf_op jit(solution)/shard_map/ppermute | solution.py:315
  124.1 4.4 %collective-permute-start.17 = (bf16[64,640]{1,0:T(8,128)(2,1)S(1)}, bf16[64,640]{1,0:T(8,128)(2,1)S(1)}, u32[]{:S(2)}, u32[]{:S(2)}) collective-permute-start(bf16[64,640]{1,0:T(8,128)(2,1)S(1)} %get-tuple-element.135), channel_id=1, source_target_pairs={{0,7},{1,0},{2,1},{3,2},{4,3},{5,4},{6,5},{7,6},{8,15},{9,8},{10,9... | collective-permute-start | bytes 245768 | tf_op jit(solution)/shard_map/ppermute | solution.py:315
  128.5 6.2 %collective-permute-start.18 = (bf16[1,32,128]{2,1,0:T(8,128)(2,1)S(1)}, bf16[1,32,128]{2,1,0:T(8,128)(2,1)S(1)}, u32[]{:S(2)}, u32[]{:S(2)}) collective-permute-start(bf16[1,32,128]{2,1,0:T(8,128)(2,1)S(1)} %bitcast.24), channel_id=1, source_target_pairs={{0,128},{8,136},{16,144},{24,152},{32,160},{40,168},{48,176},{56,1... | collective-permute-start | bytes 24584 | tf_op jit(solution)/shard_map/ppermute | solution.py:534
  131.6 3.7 %collective-permute-start.19 = (bf16[1,32,128]{2,1,0:T(8,128)(2,1)S(1)}, bf16[1,32,128]{2,1,0:T(8,128)(2,1)S(1)}, u32[]{:S(2)}, u32[]{:S(2)}) collective-permute-start(bf16[1,32,128]{2,1,0:T(8,128)(2,1)S(1)} %bitcast.25), channel_id=1, source_target_pairs={{0,64},{8,72},{16,80},{24,88},{32,96},{40,104},{48,112},{56,120},{... | collective-permute-start | bytes 24584 | tf_op jit(solution)/shard_map/ppermute | solution.py:534
  132.2 4.9 %collective-permute-start.20 = (bf16[1,32,128]{2,1,0:T(8,128)(2,1)S(1)}, bf16[1,32,128]{2,1,0:T(8,128)(2,1)S(1)}, u32[]{:S(2)}, u32[]{:S(2)}) collective-permute-start(bf16[1,32,128]{2,1,0:T(8,128)(2,1)S(1)} %bitcast.26), channel_id=1, source_target_pairs={{0,192},{8,200},{16,208},{24,216},{32,224},{40,232},{48,240},{56,2... | collective-permute-start | bytes 24584 | tf_op jit(solution)/shard_map/ppermute | solution.py:534
  132.7 1.2 copy-start.1
  137.1 3.8 %collective-permute-start.21 = (bf16[2,32,128]{2,1,0:T(8,128)(2,1)S(1)}, bf16[2,32,128]{2,1,0:T(8,128)(2,1)S(1)}, u32[]{:S(2)}, u32[]{:S(2)}) collective-permute-start(bf16[2,32,128]{2,1,0:T(8,128)(2,1)S(1)} %pad_maximum_fusion.2), channel_id=1, source_target_pairs={{0,16},{8,24},{16,0},{24,8},{32,48},{40,56},{48,32},{56,40},{64,80... | collective-permute-start | bytes 49160 | tf_op jit(solution)/shard_map/ppermute | solution.py:551
  140.9 1.2 collective-permute-start.22

commit v6 on v5

--- a/solution.py
+++ b/solution.py
@@ -529,13 +529,16 @@
         cost_estimate=cost(0, 3 * MIB),
         name="sum_near",
     )(me, own_grad, *packed)
-    whole, half = 1 << order[-1], 1 << halves[-1]
-    across, beside, both = (
-        lax.ppermute(held, "dom", [(i, i ^ flip) for i in range(parts)]) for flip in (whole, half, whole | half)
-    )
-    mine = held.astype(F32) + across.astype(F32)
-    other = beside.astype(F32) + both.astype(F32)
-    held = jnp.concatenate([mine, other], axis=0).astype(BF)
+    whole = 1 << order[-1]
+    places = []
+    for place in range(1 << (len(halves) - 1)):
+        flip = sum(1 << bit for level, bit in enumerate(reversed(halves[1:])) if place >> level & 1)
+        pair = [
+            lax.ppermute(held, "dom", [(i, i ^ away) for i in range(parts)]) if away else held
+            for away in (flip, flip | whole)
+        ]
+        places.append(pair[0].astype(F32) + pair[1].astype(F32))
+    held = jnp.concatenate(places, axis=0).astype(BF)
     held, back, near = lax.optimization_barrier((held, back, near))
     grad_feats = pl.pallas_call(
         final_kernel,
@@ -547,10 +550,7 @@
         cost_estimate=cost(0, 4 * MIB),
         name="sum_returned",
     )(send, near, back)
-    for level in reversed(range(len(halves) - 1)):
-        held = jnp.concatenate([held, lax.ppermute(held, "dom", flips[level])], axis=0)
-        if level == len(halves) - 2:
-            held, grad_feats = lax.optimization_barrier((held, grad_feats))
+    held = jnp.concatenate([held, lax.ppermute(held, "dom", flips[0])], axis=0)
     address = jnp.int32(0)
     for level in range(len(halves)):
         address = address * 2 + bits[level][0]

time: 145 us -> 151 us (1.041)
  starting transfers between devices: 70.2 us -> 76.3 us
    ppermute x5 -> x8, starting transfers between devices: 4.87 us -> 10.9 us  [the longest x7 10.9 us: per_device(): lax.ppermute(held, 'dom', [(i, i ^ away) for i in range(parts)])]
    ppermute x5 -> x8, waiting for transfers between devices: 5.16 us -> 4.26 us  [the longest x7 4.26 us: per_device(): lax.ppermute(held, 'dom', [(i, i ^ away) for i in range(parts)])]
  transfers between devices with their start and end apart: 27 -> 30, of which waited for: 17 -> 14; matrix products, arithmetic and copies ran while one was open for 0% -> 0% of each run, Pallas kernels for 4% -> 4%
where the time goes in v6:
time: 151 us; the launch traced here: 148 us
  starting transfers between devices  76.3 us (51%)
  waiting for transfers between devices  44.2 us (29%)
  Pallas kernels  23.9 us (16%)
  local copies, waits for them, and re-layouts  2.61 us (2%)
    ppermute x14, starting transfers between devices, exchange(): lax.ppermute(chunks[shift], 'chan', [(i, (i + shift) % count) for i in ra...  35.4 us
    all_to_all x1, waiting for transfers between devices, per_device(): lax.all_to_all(mean, 'chan', split_axis=0, concat_axis=0, tiled=True)  15.5 us
    ppermute x7, starting transfers between devices, per_device(): lax.ppermute(held, 'dom', [(i, i ^ away) for i in range(parts)])  10.9 us
    ppermute x14, waiting for transfers between devices, exchange(): lax.ppermute(chunks[shift], 'chan', [(i, (i + shift) % count) for i in ra...  10.3 us
    all_to_all x1, starting transfers between devices, per_device(): lax.all_to_all(mean, 'chan', split_axis=0, concat_axis=0, tiled=True)  8.48 us
    all_to_all x1, starting transfers between devices, per_device(): lax.all_to_all(outgoing, 'dom', split_axis=0, concat_axis=0, tiled=True)  7.76 us
    pallas_call x1, Pallas kernels, per_device(): pl.pallas_call(scatter_kernel, out_shape=[pltpu.HBM((block_rows, chan_wid...  6.44 us
    pallas_call x1, Pallas kernels, per_device(): pl.pallas_call(gather_kernel, out_shape=[pltpu.HBM((chans, chan_width, no...  6.18 us
  transfers between devices with their start and end apart: 30, of which 14 were waited for; matrix products, arithmetic and copies ran while one was open for 0% of the time, Pallas kernels for 4%

profile of v6, /device:TPU:2, one launch (start us, length us, event | category | flops | bytes accessed | tf_op | source)
XLA Modules:
  0.0 148.1 jit_solution(17057244448028162444)
XLA Ops:
  0.6 2.6 %pack_outgoing.1 = bf16[32,4,64,128]{3,2,1,0:T(8,128)(2,1)} custom-call(s32[4,32]{1,0:T(4,128)} %bitcast.33, bf16[64,4096]{1,0:T(8,128)(2,1)} %bitcast.21), custom_call_target="tpu_custom_call" | custom-call | bytes 5242880 | tf_op jit(solution)/shard_map/pack_outgoing/pallas_call | solution.py:363
  3.2 7.8 %all-to-all-start = ((bf16[32,4,64,128]{3,2,1,0:T(8,128)(2,1)}), bf16[32,4,64,128]{3,2,1,0:T(8,128)(2,1)S(1)}, u32[]{:S(2)}, u32[]{:S(2)}) async-start(bf16[32,4,64,128]{3,2,1,0:T(8,128)(2,1)} %pack_outgoing.1), calls=%async_computation | async-start | bytes 4194304 | tf_op jit(solution)/shard_map/all_to_all | solution.py:376
  11.0 0.8 split_feats.1
  11.9 2.0 %collective-permute-start = (bf16[64,512]{1,0:T(8,128)(2,1)}, bf16[64,512]{1,0:T(8,128)(2,1)S(1)}, u32[]{:S(2)}, u32[]{:S(2)}) collective-permute-start(bf16[64,512]{1,0:T(8,128)(2,1)} %get-tuple-element.74), channel_id=1, source_target_pairs={{0,1},{1,2},{2,3},{3,4},{4,5},{5,6},{6,7},{7,0},{8,9},{9,10},{10,1... | collective-permute-start | bytes 196616 | tf_op jit(solution)/shard_map/ppermute | solution.py:315
  13.9 3.3 %collective-permute-start.1 = (bf16[64,512]{1,0:T(8,128)(2,1)}, bf16[64,512]{1,0:T(8,128)(2,1)S(1)}, u32[]{:S(2)}, u32[]{:S(2)}) collective-permute-start(bf16[64,512]{1,0:T(8,128)(2,1)} %get-tuple-element.75), channel_id=1, source_target_pairs={{0,2},{1,3},{2,4},{3,5},{4,6},{5,7},{6,0},{7,1},{8,10},{9,11},{10,... | collective-permute-start | bytes 196616 | tf_op jit(solution)/shard_map/ppermute | solution.py:315
  17.1 4.0 %collective-permute-start.2 = (bf16[64,512]{1,0:T(8,128)(2,1)}, bf16[64,512]{1,0:T(8,128)(2,1)S(1)}, u32[]{:S(2)}, u32[]{:S(2)}) collective-permute-start(bf16[64,512]{1,0:T(8,128)(2,1)} %get-tuple-element.76), channel_id=1, source_target_pairs={{0,3},{1,4},{2,5},{3,6},{4,7},{5,0},{6,1},{7,2},{8,11},{9,12},{10,... | collective-permute-start | bytes 196616 | tf_op jit(solution)/shard_map/ppermute | solution.py:315
  21.7 4.9 %collective-permute-start.4 = (bf16[64,512]{1,0:T(8,128)(2,1)}, bf16[64,512]{1,0:T(8,128)(2,1)S(1)}, u32[]{:S(2)}, u32[]{:S(2)}) collective-permute-start(bf16[64,512]{1,0:T(8,128)(2,1)} %get-tuple-element.78), channel_id=1, source_target_pairs={{0,5},{1,6},{2,7},{3,0},{4,1},{5,2},{6,3},{7,4},{8,13},{9,14},{10,... | collective-permute-start | bytes 196616 | tf_op jit(solution)/shard_map/ppermute | solution.py:315
  26.7 2.7 %collective-permute-start.5 = (bf16[64,512]{1,0:T(8,128)(2,1)}, bf16[64,512]{1,0:T(8,128)(2,1)S(1)}, u32[]{:S(2)}, u32[]{:S(2)}) collective-permute-start(bf16[64,512]{1,0:T(8,128)(2,1)} %get-tuple-element.79), channel_id=1, source_target_pairs={{0,6},{1,7},{2,0},{3,1},{4,2},{5,3},{6,4},{7,5},{8,14},{9,15},{10,... | collective-permute-start | bytes 196616 | tf_op jit(solution)/shard_map/ppermute | solution.py:315
  29.3 1.0 collective-permute-start.6
  30.4 5.7 %collective-permute-done.4.refs_5_ = bf16[64,512]{1,0:T(8,128)(2,1)S(1)} collective-permute-done((bf16[64,512]{1,0:T(8,128)(2,1)}, bf16[64,512]{1,0:T(8,128)(2,1)S(1)}, u32[]{:S(2)}, u32[]{:S(2)}) %collective-permute-start.4) | collective-permute-done | bytes 65568 | tf_op jit(solution)/shard_map/ppermute | solution.py:315
  36.7 0.6 copy-done.13
  37.3 1.5 %all-to-all-done = bf16[32,4,64,128]{3,2,1,0:T(8,128)(2,1)S(1)} async-done(((bf16[32,4,64,128]{3,2,1,0:T(8,128)(2,1)}), bf16[32,4,64,128]{3,2,1,0:T(8,128)(2,1)S(1)}, u32[]{:S(2)}, u32[]{:S(2)}) %all-to-all-start) | async-done | bytes 2097184 | tf_op jit(solution)/shard_map/all_to_all | solution.py:376
  38.9 6.2 %neighbour_mean.1 = (bf16[8,64,512]{2,1,0:T(8,128)(2,1)}, f32[8,8,512]{2,1,0:T(8,128)S(1)}) custom-call(s32[8,32]{1,0:T(8,128)S(1)} %bitcast.31, s32[32]{0:T(128)S(1)} %copy-done.7, bf16[64,4096]{1,0:T(8,128)(2,1)S(1)} %bitcast.23, bf16[128,64,128]{2,1,0:T(8,128)(2,1)S(1)} %bitcast.18, bf16[32,8,128,128]{3,2,1,0:T(8,128)(2,1)} %vals_ref.3), custom_call_target="tpu_custom_call" | custom-call | flops 536870912 | bytes 11534336 | tf_op jit(solution)/shard_map/neighbour_mean/pallas_call | solution.py:400
  45.1 8.5 %all-to-all-start.1 = ((bf16[8,64,512]{2,1,0:T(8,128)(2,1)}), bf16[8,64,512]{2,1,0:T(8,128)(2,1)S(1)}, u32[]{:S(2)}, u32[]{:S(2)}) async-start(bf16[8,64,512]{2,1,0:T(8,128)(2,1)} %get-tuple-element.94), calls=%async_computation.1 | async-start | bytes 1048576 | tf_op jit(solution)/shard_map/all_to_all | solution.py:415
  53.8 1.4 self_part.1
  55.2 15.5 %all-to-all-done.1 = bf16[8,64,512]{2,1,0:T(8,128)(2,1)S(1)} async-done(((bf16[8,64,512]{2,1,0:T(8,128)(2,1)}), bf16[8,64,512]{2,1,0:T(8,128)(2,1)S(1)}, u32[]{:S(2)}, u32[]{:S(2)}) %all-to-all-start.1) | async-done | bytes 524320 | tf_op jit(solution)/shard_map/all_to_all | solution.py:415
  70.7 1.8 %layer_head.1 = (bf16[256,512]{1,0:T(8,128)(2,1)S(1)}, bf16[256,512]{1,0:T(8,128)(2,1)S(1)}, bf16[512,512]{1,0:T(8,128)(2,1)}) custom-call(s32[1]{0:T(128)} %bitcast.me_ref, f32[8,8,512]{2,1,0:T(8,128)S(1)} %get-tuple-element.82.degree_ref, f32[256,512]{1,0:T(8,128)S(1)} %get-tuple-element.91.pre_ref, bf16[256,512]{1,0:T(8,128)(2,1)S(1)} %get-tuple-element.92.turned_ref, ...), custom_call_target="tpu_custom_call" | custom-call | flops 268435456 | bytes 4194304 | tf_op jit(solution)/shard_map/layer_head/pallas_call | solution.py:417
  72.5 3.5 %all-to-all-start.2 = ((bf16[8,64,512]{2,1,0:T(8,128)(2,1)}), bf16[8,64,512]{2,1,0:T(8,128)(2,1)S(1)}, u32[]{:S(2)}, u32[]{:S(2)}) async-start(bf16[8,64,512]{2,1,0:T(8,128)(2,1)} %bitcast.8), calls=%async_computation.2 | async-start | bytes 1048576 | tf_op jit(solution)/shard_map/all_to_all | solution.py:426
  76.6 1.5 %collective-permute-done.7.recv_ref = bf16[16,8,8,128]{3,2,1,0:T(8,128)(2,1)S(1)} collective-permute-done((bf16[16,8,8,128]{3,2,1,0:T(8,128)(2,1)S(1)}, bf16[16,8,8,128]{3,2,1,0:T(8,128)(2,1)S(1)}, u32[]{:S(2)}, u32[]{:S(2)}) %collective-permute-start.7) | collective-permute-done | bytes 262176 | tf_op jit(solution)/shard_map/ppermute | solution.py:447
  78.2 1.1 collective-permute-start.8
  79.4 4.5 %collective-permute-done.8.recv_ref = bf16[8,8,8,128]{3,2,1,0:T(8,128)(2,1)S(1)} collective-permute-done((bf16[8,8,8,128]{3,2,1,0:T(8,128)(2,1)S(1)}, bf16[8,8,8,128]{3,2,1,0:T(8,128)(2,1)S(1)}, u32[]{:S(2)}, u32[]{:S(2)}) %collective-permute-start.8) | collective-permute-done | bytes 131104 | tf_op jit(solution)/shard_map/ppermute | solution.py:447
  83.9 1.0 collective-permute-start.9
  85.0 3.3 %collective-permute-done.9.recv_ref = bf16[4,8,8,128]{3,2,1,0:T(8,128)(2,1)S(1)} collective-permute-done((bf16[4,8,8,128]{3,2,1,0:T(8,128)(2,1)S(1)}, bf16[4,8,8,128]{3,2,1,0:T(8,128)(2,1)S(1)}, u32[]{:S(2)}, u32[]{:S(2)}) %collective-permute-start.9) | collective-permute-done | bytes 65568 | tf_op jit(solution)/shard_map/ppermute | solution.py:459
  88.3 1.8 %collective-permute-start.10 = (bf16[4,8,8,128]{3,2,1,0:T(8,128)(2,1)S(1)}, bf16[4,8,8,128]{3,2,1,0:T(8,128)(2,1)S(1)}, u32[]{:S(2)}, u32[]{:S(2)}) collective-permute-start(bf16[4,8,8,128]{3,2,1,0:T(8,128)(2,1)S(1)} %weight_add.2.held_ref), channel_id=1, source_target_pairs={{0,32},{8,40},{16,48},{24,56},{32,0},{40,8},{48,16},{56,24},{64,96... | collective-permute-start | bytes 196616 | tf_op jit(solution)/shard_map/ppermute | solution.py:473
  90.1 0.9 side_grads.1
  91.0 3.3 %collective-permute-done.10.recv_ref = bf16[4,8,8,128]{3,2,1,0:T(8,128)(2,1)S(1)} collective-permute-done((bf16[4,8,8,128]{3,2,1,0:T(8,128)(2,1)S(1)}, bf16[4,8,8,128]{3,2,1,0:T(8,128)(2,1)S(1)}, u32[]{:S(2)}, u32[]{:S(2)}) %collective-permute-start.10) | collective-permute-done | bytes 65568 | tf_op jit(solution)/shard_map/ppermute | solution.py:473
  94.3 6.4 %table_grad.1 = (f32[32,64,128]{2,1,0:T(8,128)}, bf16[128,64,128]{2,1,0:T(8,128)(2,1)}) custom-call(s32[8,32]{1,0:T(8,128)S(1)} %bitcast.32, s32[32]{0:T(128)S(1)} %copy-done.7, bf16[32,8,128,128]{3,2,1,0:T(8,128)(2,1)} %vals_ref.3, bf16[8,64,512]{2,1,0:T(8,128)(2,1)S(1)} %all-to-all-done.2.scaled_ref), custom_call_target="tpu_custom_call" | custom-call | flops 536870912 | bytes 12582912 | tf_op jit(solution)/shard_map/table_grad/pallas_call | solution.py:477
  100.8 6.1 %all-to-all-start.3 = ((bf16[32,4,64,128]{3,2,1,0:T(8,128)(2,1)}), bf16[32,4,64,128]{3,2,1,0:T(8,128)(2,1)S(1)}, u32[]{:S(2)}, u32[]{:S(2)}) async-start(bf16[32,4,64,128]{3,2,1,0:T(8,128)(2,1)} %bitcast.35), calls=%async_computation.3 | async-start | bytes 4194304 | tf_op jit(solution)/shard_map/all_to_all | solution.py:498
  107.0 5.9 %collective-permute-start.11 = (bf16[64,640]{1,0:T(8,128)(2,1)S(1)}, bf16[64,640]{1,0:T(8,128)(2,1)S(1)}, u32[]{:S(2)}, u32[]{:S(2)}) collective-permute-start(bf16[64,640]{1,0:T(8,128)(2,1)S(1)} %get-tuple-element.127), channel_id=1, source_target_pairs={{0,4},{1,5},{2,6},{3,7},{4,0},{5,1},{6,2},{7,3},{8,12},{9,13},{10,... | collective-permute-start | bytes 245768 | tf_op jit(solution)/shard_map/ppermute | solution.py:315
  113.0 0.6 collective-permute-start.12
  113.5 4.4 %collective-permute-start.13 = (bf16[64,640]{1,0:T(8,128)(2,1)S(1)}, bf16[64,640]{1,0:T(8,128)(2,1)S(1)}, u32[]{:S(2)}, u32[]{:S(2)}) collective-permute-start(bf16[64,640]{1,0:T(8,128)(2,1)S(1)} %get-tuple-element.129), channel_id=1, source_target_pairs={{0,5},{1,6},{2,7},{3,0},{4,1},{5,2},{6,3},{7,4},{8,13},{9,14},{10,... | collective-permute-start | bytes 245768 | tf_op jit(solution)/shard_map/ppermute | solution.py:315
  118.0 0.6 collective-permute-start.14
  118.6 3.6 %collective-permute-start.15 = (bf16[64,640]{1,0:T(8,128)(2,1)S(1)}, bf16[64,640]{1,0:T(8,128)(2,1)S(1)}, u32[]{:S(2)}, u32[]{:S(2)}) collective-permute-start(bf16[64,640]{1,0:T(8,128)(2,1)S(1)} %get-tuple-element.131), channel_id=1, source_target_pairs={{0,6},{1,7},{2,0},{3,1},{4,2},{5,3},{6,4},{7,5},{8,14},{9,15},{10,... | collective-permute-start | bytes 245768 | tf_op jit(solution)/shard_map/ppermute | solution.py:315
  122.7 1.4 collective-permute-done.12.refs_1_
  124.1 1.3 collective-permute-start.17
  125.4 0.9 collective-permute-done.14.refs_3_
  126.3 1.1 collective-permute-done.15.refs_4_
  127.4 0.6 collective-permute-done.16.refs_5_
  128.5 3.1 %collective-permute-start.18 = (bf16[1,32,128]{2,1,0:T(8,128)(2,1)S(1)}, bf16[1,32,128]{2,1,0:T(8,128)(2,1)S(1)}, u32[]{:S(2)}, u32[]{:S(2)}) collective-permute-start(bf16[1,32,128]{2,1,0:T(8,128)(2,1)S(1)} %bitcast.24), channel_id=1, source_target_pairs={{0,128},{8,136},{16,144},{24,152},{32,160},{40,168},{48,176},{56,1... | collective-permute-start | bytes 24584 | tf_op jit(solution)/shard_map/ppermute | solution.py:537
  131.6 0.6 collective-permute-start.19
  133.3 3.8 %collective-permute-start.22 = (bf16[1,32,128]{2,1,0:T(8,128)(2,1)S(1)}, bf16[1,32,128]{2,1,0:T(8,128)(2,1)S(1)}, u32[]{:S(2)}, u32[]{:S(2)}) collective-permute-start(bf16[1,32,128]{2,1,0:T(8,128)(2,1)S(1)} %bitcast.28), channel_id=1, source_target_pairs={{0,144},{8,152},{16,128},{24,136},{32,176},{40,184},{48,160},{56,1... | collective-permute-start | bytes 24584 | tf_op jit(solution)/shard_map/ppermute | solution.py:537
  137.2 1.2 copy-done.1
  138.5 0.7 collective-permute-start.23
  139.2 1.6 %collective-permute-start.24 = (bf16[1,32,128]{2,1,0:T(8,128)(2,1)S(1)}, bf16[1,32,128]{2,1,0:T(8,128)(2,1)S(1)}, u32[]{:S(2)}, u32[]{:S(2)}) collective-permute-start(bf16[1,32,128]{2,1,0:T(8,128)(2,1)S(1)} %bitcast.30), channel_id=1, source_target_pairs={{0,208},{8,216},{16,192},{24,200},{32,240},{40,248},{48,224},{56,2... | collective-permute-start | bytes 24584 | tf_op jit(solution)/shard_map/ppermute | solution.py:537
  140.8 2.3 %collective-permute-done.23 = bf16[1,32,128]{2,1,0:T(8,128)(2,1)S(1)} collective-permute-done((bf16[1,32,128]{2,1,0:T(8,128)(2,1)S(1)}, bf16[1,32,128]{2,1,0:T(8,128)(2,1)S(1)}, u32[]{:S(2)}, u32[]{:S(2)}) %collective-permute-start.23) | collective-permute-done | bytes 8224 | tf_op jit(solution)/shard_map/ppermute | solution.py:537
  143.1 1.9 %collective-permute-done.24 = bf16[1,32,128]{2,1,0:T(8,128)(2,1)S(1)} collective-permute-done((bf16[1,32,128]{2,1,0:T(8,128)(2,1)S(1)}, bf16[1,32,128]{2,1,0:T(8,128)(2,1)S(1)}, u32[]{:S(2)}, u32[]{:S(2)}) %collective-permute-start.24) | collective-permute-done | bytes 8224 | tf_op jit(solution)/shard_map/ppermute | solution.py:537
  145.2 2.2 %sum_returned.1 = bf16[64,4096]{1,0:T(8,128)(2,1)} custom-call(s32[4,32]{1,0:T(4,128)S(1)} %bitcast.34, f32[32,64,128]{2,1,0:T(8,128)S(1)} %sum_near.1.near_ref, bf16[32,4,64,128]{3,2,1,0:T(8,128)(2,1)S(1)} %all-to-all-done.3.back_ref), custom_call_target="tpu_custom_call" | custom-call | bytes 4194304 | tf_op jit(solution)/shard_map/sum_returned/pallas_call | solution.py:543
  147.4 0.7 weight_spread.1
  (66 shorter events, 4.7 us)
Async XLA Ops:
  3.2 7.8 %copy-start = (bf16[4096,64]{0,1:T(8,128)(2,1)S(1)}, bf16[4096,64]{0,1:T(8,128)(2,1)}, u32[]{:S(2)}) copy-start(bf16[4096,64]{0,1:T(8,128)(2,1)} %param.9) | copy-start | bytes 1572868
  3.2 35.7 %copy-start.5 = (s32[32,8]{0,1:T(8,128)S(1)}, s32[32,8]{0,1:T(8,128)}, u32[]{:S(2)}) copy-start(s32[32,8]{0,1:T(8,128)} %param.11) | copy-start | bytes 3076
  3.2 35.7 %copy-start.7 = (s32[32]{0:T(128)S(1)}, s32[32]{0:T(128)}, u32[]{:S(2)}) copy-start(s32[32]{0:T(128)} %counts_ref.3) | copy-start | bytes 388
  3.2 35.6 %all-to-all-start = ((bf16[32,4,64,128]{3,2,1,0:T(8,128)(2,1)}), bf16[32,4,64,128]{3,2,1,0:T(8,128)(2,1)S(1)}, u32[]{:S(2)}, u32[]{:S(2)}) async-start(bf16[32,4,64,128]{3,2,1,0:T(8,128)(2,1)} %pack_outgoing.1), calls=%async_computation | async-start | bytes 4194304 | tf_op jit(solution)/shard_map/all_to_all | solution.py:376
  11.9 14.8 %collective-permute-start = (bf16[64,512]{1,0:T(8,128)(2,1)}, bf16[64,512]{1,0:T(8,128)(2,1)S(1)}, u32[]{:S(2)}, u32[]{:S(2)}) collective-permute-start(bf16[64,512]{1,0:T(8,128)(2,1)} %get-tuple-element.74), channel_id=1, source_target_pairs={{0,1},{1,2},{2,3},{3,4},{4,5},{5,6},{6,7},{7,0},{8,9},{9,10},{10,1... | collective-permute-start | bytes 196616 | tf_op jit(solution)/shard_map/ppermute | solution.py:315
  13.9 15.5 %collective-permute-start.1 = (bf16[64,512]{1,0:T(8,128)(2,1)}, bf16[64,512]{1,0:T(8,128)(2,1)S(1)}, u32[]{:S(2)}, u32[]{:S(2)}) collective-permute-start(bf16[64,512]{1,0:T(8,128)(2,1)} %get-tuple-element.75), channel_id=1, source_target_pairs={{0,2},{1,3},{2,4},{3,5},{4,6},{5,7},{6,0},{7,1},{8,10},{9,11},{10,... | collective-permute-start | bytes 196616 | tf_op jit(solution)/shard_map/ppermute | solution.py:315
  17.1 13.2 %collective-permute-start.2 = (bf16[64,512]{1,0:T(8,128)(2,1)}, bf16[64,512]{1,0:T(8,128)(2,1)S(1)}, u32[]{:S(2)}, u32[]{:S(2)}) collective-permute-start(bf16[64,512]{1,0:T(8,128)(2,1)} %get-tuple-element.76), channel_id=1, source_target_pairs={{0,3},{1,4},{2,5},{3,6},{4,7},{5,0},{6,1},{7,2},{8,11},{9,12},{10,... | collective-permute-start | bytes 196616 | tf_op jit(solution)/shard_map/ppermute | solution.py:315
  21.2 9.2 %collective-permute-start.3 = (bf16[64,512]{1,0:T(8,128)(2,1)}, bf16[64,512]{1,0:T(8,128)(2,1)S(1)}, u32[]{:S(2)}, u32[]{:S(2)}) collective-permute-start(bf16[64,512]{1,0:T(8,128)(2,1)} %get-tuple-element.77), channel_id=1, source_target_pairs={{0,4},{1,5},{2,6},{3,7},{4,0},{5,1},{6,2},{7,3},{8,12},{9,13},{10,... | collective-permute-start | bytes 196616 | tf_op jit(solution)/shard_map/ppermute | solution.py:315
  21.7 14.4 %collective-permute-start.4 = (bf16[64,512]{1,0:T(8,128)(2,1)}, bf16[64,512]{1,0:T(8,128)(2,1)S(1)}, u32[]{:S(2)}, u32[]{:S(2)}) collective-permute-start(bf16[64,512]{1,0:T(8,128)(2,1)} %get-tuple-element.78), channel_id=1, source_target_pairs={{0,5},{1,6},{2,7},{3,0},{4,1},{5,2},{6,3},{7,4},{8,13},{9,14},{10,... | collective-permute-start | bytes 196616 | tf_op jit(solution)/shard_map/ppermute | solution.py:315
  26.7 9.4 %copy-start.8 = (bf16[64,512]{1,0:T(8,128)(2,1)}, bf16[64,512]{1,0:T(8,128)(2,1)S(1)}, u32[]{:S(2)}) copy-start(bf16[64,512]{1,0:T(8,128)(2,1)S(1)} %collective-permute-done.refs_1_) | copy-start | bytes 196612
  26.7 9.4 %collective-permute-start.5 = (bf16[64,512]{1,0:T(8,128)(2,1)}, bf16[64,512]{1,0:T(8,128)(2,1)S(1)}, u32[]{:S(2)}, u32[]{:S(2)}) collective-permute-start(bf16[64,512]{1,0:T(8,128)(2,1)} %get-tuple-element.79), channel_id=1, source_target_pairs={{0,6},{1,7},{2,0},{3,1},{4,2},{5,3},{6,4},{7,5},{8,14},{9,15},{10,... | collective-permute-start | bytes 196616 | tf_op jit(solution)/shard_map/ppermute | solution.py:315
  29.3 6.8 %copy-start.9 = (bf16[64,512]{1,0:T(8,128)(2,1)}, bf16[64,512]{1,0:T(8,128)(2,1)S(1)}, u32[]{:S(2)}) copy-start(bf16[64,512]{1,0:T(8,128)(2,1)S(1)} %collective-permute-done.1.refs_2_) | copy-start | bytes 196612
  29.3 8.0 %collective-permute-start.6 = (bf16[64,512]{1,0:T(8,128)(2,1)}, bf16[64,512]{1,0:T(8,128)(2,1)}, u32[]{:S(2)}, u32[]{:S(2)}) collective-permute-start(bf16[64,512]{1,0:T(8,128)(2,1)} %get-tuple-element.80), channel_id=1, source_target_pairs={{0,7},{1,0},{2,1},{3,2},{4,3},{5,4},{6,5},{7,6},{8,15},{9,8},{10,9... | collective-permute-start | bytes 196616 | tf_op jit(solution)/shard_map/ppermute | solution.py:315
  30.3 5.8 %copy-start.10 = (bf16[64,512]{1,0:T(8,128)(2,1)}, bf16[64,512]{1,0:T(8,128)(2,1)S(1)}, u32[]{:S(2)}) copy-start(bf16[64,512]{1,0:T(8,128)(2,1)S(1)} %collective-permute-done.2.refs_3_) | copy-start | bytes 196612
  30.4 5.8 %copy-start.11 = (bf16[64,512]{1,0:T(8,128)(2,1)}, bf16[64,512]{1,0:T(8,128)(2,1)S(1)}, u32[]{:S(2)}) copy-start(bf16[64,512]{1,0:T(8,128)(2,1)S(1)} %collective-permute-done.3.refs_4_) | copy-start | bytes 196612
  36.1 0.6 copy-start.12
  36.7 0.6 copy-start.13
  38.9 14.7 %copy-start.14 = (f32[256]{0:T(256)S(1)}, f32[256]{0:T(256)}, u32[]{:S(2)}) copy-start(f32[256]{0:T(256)} %param.16) | copy-start | bytes 3076
  38.9 14.8 %copy-start.2 = (bf16[512,256]{1,0:T(8,128)(2,1)S(1)}, bf16[512,256]{1,0:T(8,128)(2,1)}, u32[]{:S(2)}) copy-start(bf16[512,256]{1,0:T(8,128)(2,1)} %weight_ref.4) | copy-start | bytes 786436
  38.9 14.8 %copy-start.3 = (bf16[512,256]{1,0:T(8,128)(2,1)S(1)}, bf16[512,256]{1,0:T(8,128)(2,1)}, u32[]{:S(2)}) copy-start(bf16[512,256]{1,0:T(8,128)(2,1)} %weight_ref.5) | copy-start | bytes 786436
  38.9 14.8 %copy-start.4 = (bf16[512,256]{1,0:T(8,128)(2,1)S(1)}, bf16[512,256]{1,0:T(8,128)(2,1)}, u32[]{:S(2)}) copy-start(bf16[512,256]{1,0:T(8,128)(2,1)} %cot_ref.1) | copy-start | bytes 786436
  45.1 25.6 %all-to-all-start.1 = ((bf16[8,64,512]{2,1,0:T(8,128)(2,1)}), bf16[8,64,512]{2,1,0:T(8,128)(2,1)S(1)}, u32[]{:S(2)}, u32[]{:S(2)}) async-start(bf16[8,64,512]{2,1,0:T(8,128)(2,1)} %get-tuple-element.94), calls=%async_computation.1 | async-start | bytes 1048576 | tf_op jit(solution)/shard_map/all_to_all | solution.py:415
  72.5 21.9 %all-to-all-start.2 = ((bf16[8,64,512]{2,1,0:T(8,128)(2,1)}), bf16[8,64,512]{2,1,0:T(8,128)(2,1)S(1)}, u32[]{:S(2)}, u32[]{:S(2)}) async-start(bf16[8,64,512]{2,1,0:T(8,128)(2,1)} %bitcast.8), calls=%async_computation.2 | async-start | bytes 1048576 | tf_op jit(solution)/shard_map/all_to_all | solution.py:426
  76.5 1.6 %collective-permute-start.7 = (bf16[16,8,8,128]{3,2,1,0:T(8,128)(2,1)S(1)}, bf16[16,8,8,128]{3,2,1,0:T(8,128)(2,1)S(1)}, u32[]{:S(2)}, u32[]{:S(2)}) collective-permute-start(bf16[16,8,8,128]{3,2,1,0:T(8,128)(2,1)S(1)} %get-tuple-element.99), channel_id=1, source_target_pairs={{0,8},{8,0},{16,24},{24,16},{32,40},{40,32},{48,56},{56,48},{64,72... | collective-permute-start | bytes 786440 | tf_op jit(solution)/shard_map/ppermute | solution.py:447
  78.2 5.6 %collective-permute-start.8 = (bf16[8,8,8,128]{3,2,1,0:T(8,128)(2,1)S(1)}, bf16[8,8,8,128]{3,2,1,0:T(8,128)(2,1)S(1)}, u32[]{:S(2)}, u32[]{:S(2)}) collective-permute-start(bf16[8,8,8,128]{3,2,1,0:T(8,128)(2,1)S(1)} %get-tuple-element.101), channel_id=1, source_target_pairs={{0,16},{8,24},{16,0},{24,8},{32,48},{40,56},{48,32},{56,40},{64,80... | collective-permute-start | bytes 393224 | tf_op jit(solution)/shard_map/ppermute | solution.py:447
  83.9 4.4 %collective-permute-start.9 = (bf16[4,8,8,128]{3,2,1,0:T(8,128)(2,1)S(1)}, bf16[4,8,8,128]{3,2,1,0:T(8,128)(2,1)S(1)}, u32[]{:S(2)}, u32[]{:S(2)}) collective-permute-start(bf16[4,8,8,128]{3,2,1,0:T(8,128)(2,1)S(1)} %get-tuple-element.103), channel_id=1, source_target_pairs={{0,64},{8,72},{16,80},{24,88},{32,96},{40,104},{48,112},{56,120},{... | collective-permute-start | bytes 196616 | tf_op jit(solution)/shard_map/ppermute | solution.py:459
  88.3 6.0 %collective-permute-start.10 = (bf16[4,8,8,128]{3,2,1,0:T(8,128)(2,1)S(1)}, bf16[4,8,8,128]{3,2,1,0:T(8,128)(2,1)S(1)}, u32[]{:S(2)}, u32[]{:S(2)}) collective-permute-start(bf16[4,8,8,128]{3,2,1,0:T(8,128)(2,1)S(1)} %weight_add.2.held_ref), channel_id=1, source_target_pairs={{0,32},{8,40},{16,48},{24,56},{32,0},{40,8},{48,16},{56,24},{64,96... | collective-permute-start | bytes 196616 | tf_op jit(solution)/shard_map/ppermute | solution.py:473
  100.8 44.3 %all-to-all-start.3 = ((bf16[32,4,64,128]{3,2,1,0:T(8,128)(2,1)}), bf16[32,4,64,128]{3,2,1,0:T(8,128)(2,1)S(1)}, u32[]{:S(2)}, u32[]{:S(2)}) async-start(bf16[32,4,64,128]{3,2,1,0:T(8,128)(2,1)} %bitcast.35), calls=%async_computation.3 | async-start | bytes 4194304 | tf_op jit(solution)/shard_map/all_to_all | solution.py:498
  106.9 38.2 %copy-start.6 = (s32[1,32,4]{1,2,0:T(4,128)S(1)}, s32[1,32,4]{1,2,0:T(4,128)}, u32[]{:S(2)}) copy-start(s32[1,32,4]{1,2,0:T(4,128)} %param.13) | copy-start | bytes 1540
  107.0 15.1 %collective-permute-start.11 = (bf16[64,640]{1,0:T(8,128)(2,1)S(1)}, bf16[64,640]{1,0:T(8,128)(2,1)S(1)}, u32[]{:S(2)}, u32[]{:S(2)}) collective-permute-start(bf16[64,640]{1,0:T(8,128)(2,1)S(1)} %get-tuple-element.127), channel_id=1, source_target_pairs={{0,4},{1,5},{2,6},{3,7},{4,0},{5,1},{6,2},{7,3},{8,12},{9,13},{10,... | collective-permute-start | bytes 245768 | tf_op jit(solution)/shard_map/ppermute | solution.py:315
  113.0 11.1 %collective-permute-start.12 = (bf16[64,640]{1,0:T(8,128)(2,1)S(1)}, bf16[64,640]{1,0:T(8,128)(2,1)S(1)}, u32[]{:S(2)}, u32[]{:S(2)}) collective-permute-start(bf16[64,640]{1,0:T(8,128)(2,1)S(1)} %get-tuple-element.128), channel_id=1, source_target_pairs={{0,3},{1,4},{2,5},{3,6},{4,7},{5,0},{6,1},{7,2},{8,11},{9,12},{10,... | collective-permute-start | bytes 245768 | tf_op jit(solution)/shard_map/ppermute | solution.py:315
  113.5 11.8 %collective-permute-start.13 = (bf16[64,640]{1,0:T(8,128)(2,1)S(1)}, bf16[64,640]{1,0:T(8,128)(2,1)S(1)}, u32[]{:S(2)}, u32[]{:S(2)}) collective-permute-start(bf16[64,640]{1,0:T(8,128)(2,1)S(1)} %get-tuple-element.129), channel_id=1, source_target_pairs={{0,5},{1,6},{2,7},{3,0},{4,1},{5,2},{6,3},{7,4},{8,13},{9,14},{10,... | collective-permute-start | bytes 245768 | tf_op jit(solution)/shard_map/ppermute | solution.py:315
  118.0 8.3 %collective-permute-start.14 = (bf16[64,640]{1,0:T(8,128)(2,1)S(1)}, bf16[64,640]{1,0:T(8,128)(2,1)S(1)}, u32[]{:S(2)}, u32[]{:S(2)}) collective-permute-start(bf16[64,640]{1,0:T(8,128)(2,1)S(1)} %get-tuple-element.130), channel_id=1, source_target_pairs={{0,2},{1,3},{2,4},{3,5},{4,6},{5,7},{6,0},{7,1},{8,10},{9,11},{10,... | collective-permute-start | bytes 245768 | tf_op jit(solution)/shard_map/ppermute | solution.py:315
  118.6 8.8 %collective-permute-start.15 = (bf16[64,640]{1,0:T(8,128)(2,1)S(1)}, bf16[64,640]{1,0:T(8,128)(2,1)S(1)}, u32[]{:S(2)}, u32[]{:S(2)}) collective-permute-start(bf16[64,640]{1,0:T(8,128)(2,1)S(1)} %get-tuple-element.131), channel_id=1, source_target_pairs={{0,6},{1,7},{2,0},{3,1},{4,2},{5,3},{6,4},{7,5},{8,14},{9,15},{10,... | collective-permute-start | bytes 245768 | tf_op jit(solution)/shard_map/ppermute | solution.py:315
  122.1 5.9 %collective-permute-start.16 = (bf16[64,640]{1,0:T(8,128)(2,1)S(1)}, bf16[64,640]{1,0:T(8,128)(2,1)S(1)}, u32[]{:S(2)}, u32[]{:S(2)}) collective-permute-start(bf16[64,640]{1,0:T(8,128)(2,1)S(1)} %get-tuple-element.132), channel_id=1, source_target_pairs={{0,1},{1,2},{2,3},{3,4},{4,5},{5,6},{6,7},{7,0},{8,9},{9,10},{10,1... | collective-permute-start | bytes 245768 | tf_op jit(solution)/shard_map/ppermute | solution.py:315
  124.1 4.4 %collective-permute-start.17 = (bf16[64,640]{1,0:T(8,128)(2,1)S(1)}, bf16[64,640]{1,0:T(8,128)(2,1)S(1)}, u32[]{:S(2)}, u32[]{:S(2)}) collective-permute-start(bf16[64,640]{1,0:T(8,128)(2,1)S(1)} %get-tuple-element.133), channel_id=1, source_target_pairs={{0,7},{1,0},{2,1},{3,2},{4,3},{5,4},{6,5},{7,6},{8,15},{9,8},{10,9... | collective-permute-start | bytes 245768 | tf_op jit(solution)/shard_map/ppermute | solution.py:315
  128.5 9.9 %collective-permute-start.18 = (bf16[1,32,128]{2,1,0:T(8,128)(2,1)S(1)}, bf16[1,32,128]{2,1,0:T(8,128)(2,1)S(1)}, u32[]{:S(2)}, u32[]{:S(2)}) collective-permute-start(bf16[1,32,128]{2,1,0:T(8,128)(2,1)S(1)} %bitcast.24), channel_id=1, source_target_pairs={{0,128},{8,136},{16,144},{24,152},{32,160},{40,168},{48,176},{56,1... | collective-permute-start | bytes 24584 | tf_op jit(solution)/shard_map/ppermute | solution.py:537
  131.6 7.6 %collective-permute-start.19 = (bf16[1,32,128]{2,1,0:T(8,128)(2,1)S(1)}, bf16[1,32,128]{2,1,0:T(8,128)(2,1)S(1)}, u32[]{:S(2)}, u32[]{:S(2)}) collective-permute-start(bf16[1,32,128]{2,1,0:T(8,128)(2,1)S(1)} %bitcast.25), channel_id=1, source_target_pairs={{0,64},{8,72},{16,80},{24,88},{32,96},{40,104},{48,112},{56,120},{... | collective-permute-start | bytes 24584 | tf_op jit(solution)/shard_map/ppermute | solution.py:537
  132.2 8.5 %collective-permute-start.20 = (bf16[1,32,128]{2,1,0:T(8,128)(2,1)S(1)}, bf16[1,32,128]{2,1,0:T(8,128)(2,1)S(1)}, u32[]{:S(2)}, u32[]{:S(2)}) collective-permute-start(bf16[1,32,128]{2,1,0:T(8,128)(2,1)S(1)} %bitcast.26), channel_id=1, source_target_pairs={{0,192},{8,200},{16,208},{24,216},{32,224},{40,232},{48,240},{56,2... | collective-permute-start | bytes 24584 | tf_op jit(solution)/shard_map/ppermute | solution.py:537
  132.8 8.0 %collective-permute-start.21 = (bf16[1,32,128]{2,1,0:T(8,128)(2,1)S(1)}, bf16[1,32,128]{2,1,0:T(8,128)(2,1)S(1)}, u32[]{:S(2)}, u32[]{:S(2)}) collective-permute-start(bf16[1,32,128]{2,1,0:T(8,128)(2,1)S(1)} %bitcast.27), channel_id=1, source_target_pairs={{0,16},{8,24},{16,0},{24,8},{32,48},{40,56},{48,32},{56,40},{64,80... | collective-permute-start | bytes 24584 | tf_op jit(solution)/shard_map/ppermute | solution.py:537
  133.3 7.4 %collective-permute-start.22 = (bf16[1,32,128]{2,1,0:T(8,128)(2,1)S(1)}, bf16[1,32,128]{2,1,0:T(8,128)(2,1)S(1)}, u32[]{:S(2)}, u32[]{:S(2)}) collective-permute-start(bf16[1,32,128]{2,1,0:T(8,128)(2,1)S(1)} %bitcast.28), channel_id=1, source_target_pairs={{0,144},{8,152},{16,128},{24,136},{32,176},{40,184},{48,160},{56,1... | collective-permute-start | bytes 24584 | tf_op jit(solution)/shard_map/ppermute | solution.py:537
  137.2 1.2 copy-start.1
  138.5 4.6 %collective-permute-start.23 = (bf16[1,32,128]{2,1,0:T(8,128)(2,1)S(1)}, bf16[1,32,128]{2,1,0:T(8,128)(2,1)S(1)}, u32[]{:S(2)}, u32[]{:S(2)}) collective-permute-start(bf16[1,32,128]{2,1,0:T(8,128)(2,1)S(1)} %bitcast.29), channel_id=1, source_target_pairs={{0,80},{8,88},{16,64},{24,72},{32,112},{40,120},{48,96},{56,104},{... | collective-permute-start | bytes 24584 | tf_op jit(solution)/shard_map/ppermute | solution.py:537
  139.2 5.8 %collective-permute-start.24 = (bf16[1,32,128]{2,1,0:T(8,128)(2,1)S(1)}, bf16[1,32,128]{2,1,0:T(8,128)(2,1)S(1)}, u32[]{:S(2)}, u32[]{:S(2)}) collective-permute-start(bf16[1,32,128]{2,1,0:T(8,128)(2,1)S(1)} %bitcast.30), channel_id=1, source_target_pairs={{0,208},{8,216},{16,192},{24,200},{32,240},{40,248},{48,224},{56,2... | collective-permute-start | bytes 24584 | tf_op jit(solution)/shard_map/ppermute | solution.py:537
  145.1 2.3 %collective-permute-start.25 = (bf16[4,32,128]{2,1,0:T(8,128)(2,1)S(1)}, bf16[4,32,128]{2,1,0:T(8,128)(2,1)S(1)}, u32[]{:S(2)}, u32[]{:S(2)}) collective-permute-start(bf16[4,32,128]{2,1,0:T(8,128)(2,1)S(1)} %pad_maximum_fusion.1), channel_id=1, source_target_pairs={{0,8},{8,0},{16,24},{24,16},{32,40},{40,32},{48,56},{56,48},{64,72... | collective-permute-start | bytes 98312 | tf_op jit(solution)/shard_map/ppermute | solution.py:553

commit v7 on v5

--- a/solution.py
+++ b/solution.py
@@ -185,16 +185,20 @@
     give_ref[...] = hold_ref[pl.ds((1 - bit) * half, half)].astype(BF)
 
 
-def halve_kernel(me_ref, held_ref, recv_ref, keep_ref, give_ref, hold_ref):
-    half = keep_ref.shape[0]
-    bit = me_ref[0]
+def quarter_kernel(me_ref, held_ref, recv_ref, keep_ref, *refs):
+    give_refs, hold_ref = refs[:-1], refs[-1]
+    span = keep_ref.shape[0]
     hold_ref[...] = held_ref[...] + recv_ref[...].astype(F32)
-    keep_ref[...] = hold_ref[pl.ds(bit * half, half)]
-    give_ref[...] = hold_ref[pl.ds((1 - bit) * half, half)].astype(BF)
-
-
-def add_round_kernel(held_ref, recv_ref, out_ref):
-    out_ref[...] = (held_ref[...] + recv_ref[...].astype(F32)).astype(BF)
+    keep_ref[...] = hold_ref[pl.ds(me_ref[0] * span, span)]
+    for flip, give_ref in enumerate(give_refs, 1):
+        give_ref[...] = hold_ref[pl.ds(lax.bitwise_xor(me_ref[0], flip) * span, span)].astype(BF)
+
+
+def add_round_kernel(held_ref, *refs):
+    total = held_ref[...]
+    for recv_ref in refs[:-1]:
+        total = total + recv_ref[...].astype(F32)
+    refs[-1][...] = total.astype(BF)
 
 
 def add_pair_kernel(held_ref, recv_ref, out_ref):
@@ -325,16 +329,16 @@
     return [bit for bit in (0, 1, 3, 2, 4) if bit < count] + list(range(5, count))
 
 
-def add_round(kernel, left, right):
+def add_round(kernel, left, *rights):
     return pl.pallas_call(
         kernel,
         out_shape=sds(left.shape, BF),
-        in_specs=[vmem()] * 2,
+        in_specs=[vmem()] * (1 + len(rights)),
         out_specs=vmem(),
         compiler_params=params(BIG),
         cost_estimate=cost(0, MIB),
         name="weight_add",
-    )(left, right)
+    )(left, *rights)
 
 
 def per_device(feats, block_vals, block_cols, block_counts, send_list, w_self, w_neigh, bias, cotangent):
@@ -443,22 +447,24 @@
         name="weight_partial",
     )(bits[0], feats_own, mean, grad_t)
     pieces //= 2
-    for level in range(1, len(halves)):
-        got = lax.ppermute(give, "dom", flips[level - 1])
-        keep, give = pl.pallas_call(
-            halve_kernel,
-            out_shape=[sds((pieces // 2, chans, unit, lanes), F32), sds((pieces // 2, chans, unit, lanes), BF)],
-            in_specs=[smem()] + [vmem()] * 2,
-            out_specs=[vmem()] * 2,
-            scratch_shapes=[pltpu.VMEM((pieces, chans, unit, lanes), F32)],
-            compiler_params=params(BIG),
-            cost_estimate=cost(0, MIB),
-            name="weight_halve",
-        )(bits[level], keep, got)
-        pieces //= 2
-    got = lax.ppermute(give, "dom", flips[len(halves) - 1])
-    total = add_round(add_round_kernel, keep, got)
-
+    got = lax.ppermute(give, "dom", flips[0])
+    quarter = (bits[1] << 1) | bits[2]
+    pieces //= 4
+    keep, *gives = pl.pallas_call(
+        quarter_kernel,
+        out_shape=[sds((pieces, chans, unit, lanes), F32)] + [sds((pieces, chans, unit, lanes), BF)] * 3,
+        in_specs=[smem()] + [vmem()] * 2,
+        out_specs=[vmem()] * 4,
+        scratch_shapes=[pltpu.VMEM((pieces * 4, chans, unit, lanes), F32)],
+        compiler_params=params(BIG),
+        cost_estimate=cost(0, MIB),
+        name="weight_quarter",
+    )(quarter, keep, got)
+    gots = []
+    for flip, give in enumerate(gives, 1):
+        away = (flip >> 1) << halves[1] | (flip & 1) << halves[2]
+        gots.append(lax.ppermute(give, "dom", [(i, i ^ away) for i in range(parts)]))
+    total = add_round(add_round_kernel, keep, *gots)
     side = pl.pallas_call(
         functools.partial(side_kernel, chans),
         out_shape=[sds((nodes, f_out), BF)] + [sds((chan_width, nodes), BF)] * chans,

time: 145 us -> 144 us (level)
    ppermute x3 -> x4, waiting for transfers between devices: 9.34 us -> 4.77 us  [the longest x3 3.26 us: per_device(): lax.ppermute(give, 'dom', [(i, i ^ away) for i in range(parts)])]
    ppermute x14, starting transfers between devices: 35.5 us -> 31.8 us  [exchange(): lax.ppermute(chunks[shift], 'chan', [(i, (i + shift) % count) for i in ra...]
    ppermute x14, waiting for transfers between devices: 10.2 us -> 13.6 us  [exchange(): lax.ppermute(chunks[shift], 'chan', [(i, (i + shift) % count) for i in ra...]
    ppermute x3 -> x4, starting transfers between devices: 2.25 us -> 3.67 us  [the longest x3 3.57 us: per_device(): lax.ppermute(give, 'dom', [(i, i ^ away) for i in range(parts)])]
  transfers between devices with their start and end apart: 27 -> 28, of which waited for: 17 -> 17; matrix products, arithmetic and copies ran while one was open for 0% -> 0% of each run, Pallas kernels for 4% -> 4%
where the time goes in v7:
time: 144 us; the launch traced here: 142 us
  starting transfers between devices  69 us (48%)
  waiting for transfers between devices  45.6 us (32%)
  Pallas kernels  23.9 us (17%)
  local copies, waits for them, and re-layouts  2.63 us (2%)
    ppermute x14, starting transfers between devices, exchange(): lax.ppermute(chunks[shift], 'chan', [(i, (i + shift) % count) for i in ra...  31.8 us
    all_to_all x1, waiting for transfers between devices, per_device(): lax.all_to_all(mean, 'chan', split_axis=0, concat_axis=0, tiled=True)  15.5 us
    ppermute x14, waiting for transfers between devices, exchange(): lax.ppermute(chunks[shift], 'chan', [(i, (i + shift) % count) for i in ra...  13.6 us
    all_to_all x1, starting transfers between devices, per_device(): lax.all_to_all(mean, 'chan', split_axis=0, concat_axis=0, tiled=True)  8.48 us
    all_to_all x1, starting transfers between devices, per_device(): lax.all_to_all(outgoing, 'dom', split_axis=0, concat_axis=0, tiled=True)  7.76 us
    all_to_all x1, starting transfers between devices, per_device(): lax.all_to_all(far_grad.reshape(parts, slots, chan_width, size), 'dom', s...  7.48 us
    pallas_call x1, Pallas kernels, per_device(): pl.pallas_call(scatter_kernel, out_shape=[pltpu.HBM((block_rows, chan_wid...  6.43 us
    pallas_call x1, Pallas kernels, per_device(): pl.pallas_call(gather_kernel, out_shape=[pltpu.HBM((chans, chan_width, no...  6.18 us
  transfers between devices with their start and end apart: 28, of which 17 were waited for; matrix products, arithmetic and copies ran while one was open for 0% of the time, Pallas kernels for 4%

profile of v7, /device:TPU:2, one launch (start us, length us, event | category | flops | bytes accessed | tf_op | source)
XLA Modules:
  0.0 142.1 jit_solution(9194446784259720787)
XLA Ops:
  0.6 2.5 %pack_outgoing.1 = bf16[32,4,64,128]{3,2,1,0:T(8,128)(2,1)} custom-call(s32[4,32]{1,0:T(4,128)} %bitcast.28, bf16[64,4096]{1,0:T(8,128)(2,1)} %bitcast.20), custom_call_target="tpu_custom_call" | custom-call | bytes 5242880 | tf_op jit(solution)/shard_map/pack_outgoing/pallas_call | solution.py:367
  3.2 7.8 %all-to-all-start = ((bf16[32,4,64,128]{3,2,1,0:T(8,128)(2,1)}), bf16[32,4,64,128]{3,2,1,0:T(8,128)(2,1)S(1)}, u32[]{:S(2)}, u32[]{:S(2)}) async-start(bf16[32,4,64,128]{3,2,1,0:T(8,128)(2,1)} %pack_outgoing.1), calls=%async_computation | async-start | bytes 4194304 | tf_op jit(solution)/shard_map/all_to_all | solution.py:380
  11.0 0.9 split_feats.1
  11.9 2.0 %collective-permute-start = (bf16[64,512]{1,0:T(8,128)(2,1)}, bf16[64,512]{1,0:T(8,128)(2,1)S(1)}, u32[]{:S(2)}, u32[]{:S(2)}) collective-permute-start(bf16[64,512]{1,0:T(8,128)(2,1)} %get-tuple-element.76), channel_id=1, source_target_pairs={{0,1},{1,2},{2,3},{3,4},{4,5},{5,6},{6,7},{7,0},{8,9},{9,10},{10,1... | collective-permute-start | bytes 196616 | tf_op jit(solution)/shard_map/ppermute | solution.py:319
  13.9 3.3 %collective-permute-start.1 = (bf16[64,512]{1,0:T(8,128)(2,1)}, bf16[64,512]{1,0:T(8,128)(2,1)S(1)}, u32[]{:S(2)}, u32[]{:S(2)}) collective-permute-start(bf16[64,512]{1,0:T(8,128)(2,1)} %get-tuple-element.77), channel_id=1, source_target_pairs={{0,2},{1,3},{2,4},{3,5},{4,6},{5,7},{6,0},{7,1},{8,10},{9,11},{10,... | collective-permute-start | bytes 196616 | tf_op jit(solution)/shard_map/ppermute | solution.py:319
  17.1 4.0 %collective-permute-start.2 = (bf16[64,512]{1,0:T(8,128)(2,1)}, bf16[64,512]{1,0:T(8,128)(2,1)S(1)}, u32[]{:S(2)}, u32[]{:S(2)}) collective-permute-start(bf16[64,512]{1,0:T(8,128)(2,1)} %get-tuple-element.78), channel_id=1, source_target_pairs={{0,3},{1,4},{2,5},{3,6},{4,7},{5,0},{6,1},{7,2},{8,11},{9,12},{10,... | collective-permute-start | bytes 196616 | tf_op jit(solution)/shard_map/ppermute | solution.py:319
  21.7 4.9 %collective-permute-start.4 = (bf16[64,512]{1,0:T(8,128)(2,1)}, bf16[64,512]{1,0:T(8,128)(2,1)S(1)}, u32[]{:S(2)}, u32[]{:S(2)}) collective-permute-start(bf16[64,512]{1,0:T(8,128)(2,1)} %get-tuple-element.80), channel_id=1, source_target_pairs={{0,5},{1,6},{2,7},{3,0},{4,1},{5,2},{6,3},{7,4},{8,13},{9,14},{10,... | collective-permute-start | bytes 196616 | tf_op jit(solution)/shard_map/ppermute | solution.py:319
  26.7 2.7 %collective-permute-start.5 = (bf16[64,512]{1,0:T(8,128)(2,1)}, bf16[64,512]{1,0:T(8,128)(2,1)S(1)}, u32[]{:S(2)}, u32[]{:S(2)}) collective-permute-start(bf16[64,512]{1,0:T(8,128)(2,1)} %get-tuple-element.81), channel_id=1, source_target_pairs={{0,6},{1,7},{2,0},{3,1},{4,2},{5,3},{6,4},{7,5},{8,14},{9,15},{10,... | collective-permute-start | bytes 196616 | tf_op jit(solution)/shard_map/ppermute | solution.py:319
  29.3 1.0 collective-permute-start.6
  30.4 5.7 %collective-permute-done.4.refs_5_ = bf16[64,512]{1,0:T(8,128)(2,1)S(1)} collective-permute-done((bf16[64,512]{1,0:T(8,128)(2,1)}, bf16[64,512]{1,0:T(8,128)(2,1)S(1)}, u32[]{:S(2)}, u32[]{:S(2)}) %collective-permute-start.4) | collective-permute-done | bytes 65568 | tf_op jit(solution)/shard_map/ppermute | solution.py:319
  36.1 0.6 copy-done.12
  36.7 0.6 copy-done.13
  37.4 1.5 %all-to-all-done = bf16[32,4,64,128]{3,2,1,0:T(8,128)(2,1)S(1)} async-done(((bf16[32,4,64,128]{3,2,1,0:T(8,128)(2,1)}), bf16[32,4,64,128]{3,2,1,0:T(8,128)(2,1)S(1)}, u32[]{:S(2)}, u32[]{:S(2)}) %all-to-all-start) | async-done | bytes 2097184 | tf_op jit(solution)/shard_map/all_to_all | solution.py:380
  38.9 6.2 %neighbour_mean.1 = (bf16[8,64,512]{2,1,0:T(8,128)(2,1)}, f32[8,8,512]{2,1,0:T(8,128)S(1)}) custom-call(s32[8,32]{1,0:T(8,128)S(1)} %bitcast.26, s32[32]{0:T(128)S(1)} %copy-done.7, bf16[64,4096]{1,0:T(8,128)(2,1)S(1)} %bitcast.22, bf16[128,64,128]{2,1,0:T(8,128)(2,1)S(1)} %bitcast.17, bf16[32,8,128,128]{3,2,1,0:T(8,128)(2,1)} %vals_ref.3), custom_call_target="tpu_custom_call" | custom-call | flops 536870912 | bytes 11534336 | tf_op jit(solution)/shard_map/neighbour_mean/pallas_call | solution.py:404
  45.1 8.5 %all-to-all-start.1 = ((bf16[8,64,512]{2,1,0:T(8,128)(2,1)}), bf16[8,64,512]{2,1,0:T(8,128)(2,1)S(1)}, u32[]{:S(2)}, u32[]{:S(2)}) async-start(bf16[8,64,512]{2,1,0:T(8,128)(2,1)} %get-tuple-element.96), calls=%async_computation.1 | async-start | bytes 1048576 | tf_op jit(solution)/shard_map/all_to_all | solution.py:419
  53.8 1.4 %self_part.1 = (bf16[512,512]{1,0:T(8,128)(2,1)S(1)}, f32[256,512]{1,0:T(8,128)S(1)}, bf16[256,512]{1,0:T(8,128)(2,1)S(1)}, bf16[256,512]{1,0:T(8,128)(2,1)S(1)}) custom-call(s32[1]{0:T(128)} %bitcast.me_ref, bf16[512,256]{1,0:T(8,128)(2,1)S(1)} %copy-done.3, f32[256,1]{1,0:T(8,128)S(1)} %copy.13.bias_ref, bf16[512,256]{1,0:T(8,128)(2,1)S(1)} %copy-done.2, ...), custom_call_target="tpu_custom_call" | custom-call | flops 134217728 | bytes 2097152 | tf_op jit(solution)/shard_map/self_part/pallas_call | solution.py:394
  55.2 15.5 %all-to-all-done.1 = bf16[8,64,512]{2,1,0:T(8,128)(2,1)S(1)} async-done(((bf16[8,64,512]{2,1,0:T(8,128)(2,1)}), bf16[8,64,512]{2,1,0:T(8,128)(2,1)S(1)}, u32[]{:S(2)}, u32[]{:S(2)}) %all-to-all-start.1) | async-done | bytes 524320 | tf_op jit(solution)/shard_map/all_to_all | solution.py:419
  70.7 1.8 %layer_head.1 = (bf16[256,512]{1,0:T(8,128)(2,1)S(1)}, bf16[256,512]{1,0:T(8,128)(2,1)S(1)}, bf16[512,512]{1,0:T(8,128)(2,1)}) custom-call(s32[1]{0:T(128)} %bitcast.me_ref, f32[8,8,512]{2,1,0:T(8,128)S(1)} %get-tuple-element.84.degree_ref, f32[256,512]{1,0:T(8,128)S(1)} %get-tuple-element.93.pre_ref, bf16[256,512]{1,0:T(8,128)(2,1)S(1)} %get-tuple-element.94.turned_ref, ...), custom_call_target="tpu_custom_call" | custom-call | flops 268435456 | bytes 4194304 | tf_op jit(solution)/shard_map/layer_head/pallas_call | solution.py:421
  72.5 3.5 %all-to-all-start.2 = ((bf16[8,64,512]{2,1,0:T(8,128)(2,1)}), bf16[8,64,512]{2,1,0:T(8,128)(2,1)S(1)}, u32[]{:S(2)}, u32[]{:S(2)}) async-start(bf16[8,64,512]{2,1,0:T(8,128)(2,1)} %bitcast.8), calls=%async_computation.2 | async-start | bytes 1048576 | tf_op jit(solution)/shard_map/all_to_all | solution.py:430
  76.6 1.5 %collective-permute-done.7.recv_ref = bf16[16,8,8,128]{3,2,1,0:T(8,128)(2,1)S(1)} collective-permute-done((bf16[16,8,8,128]{3,2,1,0:T(8,128)(2,1)S(1)}, bf16[16,8,8,128]{3,2,1,0:T(8,128)(2,1)S(1)}, u32[]{:S(2)}, u32[]{:S(2)}) %collective-permute-start.7) | collective-permute-done | bytes 262176 | tf_op jit(solution)/shard_map/ppermute | solution.py:450
  78.2 1.5 %collective-permute-start.10 = (bf16[4,8,8,128]{3,2,1,0:T(8,128)(2,1)S(1)}, bf16[4,8,8,128]{3,2,1,0:T(8,128)(2,1)S(1)}, u32[]{:S(2)}, u32[]{:S(2)}) collective-permute-start(bf16[4,8,8,128]{3,2,1,0:T(8,128)(2,1)S(1)} %get-tuple-element.105), channel_id=1, source_target_pairs={{0,80},{8,88},{16,64},{24,72},{32,112},{40,120},{48,96},{56,104},{... | collective-permute-start | bytes 196616 | tf_op jit(solution)/shard_map/ppermute | solution.py:466
  79.7 1.1 collective-permute-start.8
  80.8 1.0 collective-permute-start.9
  81.8 1.8 %collective-permute-done.10.refs_2_ = bf16[4,8,8,128]{3,2,1,0:T(8,128)(2,1)S(1)} collective-permute-done((bf16[4,8,8,128]{3,2,1,0:T(8,128)(2,1)S(1)}, bf16[4,8,8,128]{3,2,1,0:T(8,128)(2,1)S(1)}, u32[]{:S(2)}, u32[]{:S(2)}) %collective-permute-start.10) | collective-permute-done | bytes 65568 | tf_op jit(solution)/shard_map/ppermute | solution.py:466
  83.7 1.1 collective-permute-done.8.refs_0_
  85.1 1.5 %collective-permute-start.11 = (bf16[4,8,8,128]{3,2,1,0:T(8,128)(2,1)S(1)}, bf16[4,8,8,128]{3,2,1,0:T(8,128)(2,1)S(1)}, u32[]{:S(2)}, u32[]{:S(2)}) collective-permute-start(bf16[4,8,8,128]{3,2,1,0:T(8,128)(2,1)S(1)} %weight_add.2.held_ref), channel_id=1, source_target_pairs={{0,32},{8,40},{16,48},{24,56},{32,0},{40,8},{48,16},{56,24},{64,96... | collective-permute-start | bytes 196616 | tf_op jit(solution)/shard_map/ppermute | solution.py:479
  86.6 0.9 side_grads.1
  87.5 3.6 %collective-permute-done.11.recv_ref = bf16[4,8,8,128]{3,2,1,0:T(8,128)(2,1)S(1)} collective-permute-done((bf16[4,8,8,128]{3,2,1,0:T(8,128)(2,1)S(1)}, bf16[4,8,8,128]{3,2,1,0:T(8,128)(2,1)S(1)}, u32[]{:S(2)}, u32[]{:S(2)}) %collective-permute-start.11) | collective-permute-done | bytes 65568 | tf_op jit(solution)/shard_map/ppermute | solution.py:479
  91.2 1.4 %all-to-all-done.2.scaled_ref = bf16[8,64,512]{2,1,0:T(8,128)(2,1)S(1)} async-done(((bf16[8,64,512]{2,1,0:T(8,128)(2,1)}), bf16[8,64,512]{2,1,0:T(8,128)(2,1)S(1)}, u32[]{:S(2)}, u32[]{:S(2)}) %all-to-all-start.2) | async-done | bytes 524320 | tf_op jit(solution)/shard_map/all_to_all | solution.py:430
  92.6 6.4 %table_grad.1 = (f32[32,64,128]{2,1,0:T(8,128)}, bf16[128,64,128]{2,1,0:T(8,128)(2,1)}) custom-call(s32[8,32]{1,0:T(8,128)S(1)} %bitcast.27, s32[32]{0:T(128)S(1)} %copy-done.7, bf16[32,8,128,128]{3,2,1,0:T(8,128)(2,1)} %vals_ref.3, bf16[8,64,512]{2,1,0:T(8,128)(2,1)S(1)} %all-to-all-done.2.scaled_ref), custom_call_target="tpu_custom_call" | custom-call | flops 536870912 | bytes 12582912 | tf_op jit(solution)/shard_map/table_grad/pallas_call | solution.py:483
  99.0 7.5 %all-to-all-start.3 = ((bf16[32,4,64,128]{3,2,1,0:T(8,128)(2,1)}), bf16[32,4,64,128]{3,2,1,0:T(8,128)(2,1)S(1)}, u32[]{:S(2)}, u32[]{:S(2)}) async-start(bf16[32,4,64,128]{3,2,1,0:T(8,128)(2,1)} %bitcast.30), calls=%async_computation.3 | async-start | bytes 4194304 | tf_op jit(solution)/shard_map/all_to_all | solution.py:504
  106.6 3.6 %collective-permute-start.12 = (bf16[64,640]{1,0:T(8,128)(2,1)S(1)}, bf16[64,640]{1,0:T(8,128)(2,1)S(1)}, u32[]{:S(2)}, u32[]{:S(2)}) collective-permute-start(bf16[64,640]{1,0:T(8,128)(2,1)S(1)} %get-tuple-element.129), channel_id=1, source_target_pairs={{0,4},{1,5},{2,6},{3,7},{4,0},{5,1},{6,2},{7,3},{8,12},{9,13},{10,... | collective-permute-start | bytes 245768 | tf_op jit(solution)/shard_map/ppermute | solution.py:319
  110.8 4.5 %collective-permute-start.14 = (bf16[64,640]{1,0:T(8,128)(2,1)S(1)}, bf16[64,640]{1,0:T(8,128)(2,1)S(1)}, u32[]{:S(2)}, u32[]{:S(2)}) collective-permute-start(bf16[64,640]{1,0:T(8,128)(2,1)S(1)} %get-tuple-element.131), channel_id=1, source_target_pairs={{0,5},{1,6},{2,7},{3,0},{4,1},{5,2},{6,3},{7,4},{8,13},{9,14},{10,... | collective-permute-start | bytes 245768 | tf_op jit(solution)/shard_map/ppermute | solution.py:319
  115.8 3.6 %collective-permute-start.16 = (bf16[64,640]{1,0:T(8,128)(2,1)S(1)}, bf16[64,640]{1,0:T(8,128)(2,1)S(1)}, u32[]{:S(2)}, u32[]{:S(2)}) collective-permute-start(bf16[64,640]{1,0:T(8,128)(2,1)S(1)} %get-tuple-element.133), channel_id=1, source_target_pairs={{0,6},{1,7},{2,0},{3,1},{4,2},{5,3},{6,4},{7,5},{8,14},{9,15},{10,... | collective-permute-start | bytes 245768 | tf_op jit(solution)/shard_map/ppermute | solution.py:319
  120.0 3.4 %collective-permute-done.13.refs_1_ = bf16[64,640]{1,0:T(8,128)(2,1)S(1)} collective-permute-done((bf16[64,640]{1,0:T(8,128)(2,1)S(1)}, bf16[64,640]{1,0:T(8,128)(2,1)S(1)}, u32[]{:S(2)}, u32[]{:S(2)}) %collective-permute-start.13) | collective-permute-done | bytes 81952 | tf_op jit(solution)/shard_map/ppermute | solution.py:319
  123.4 1.4 collective-permute-done.16.refs_4_
  124.8 0.8 collective-permute-done.17.refs_5_
  125.6 2.2 %collective-permute-done.18.refs_6_ = bf16[64,640]{1,0:T(8,128)(2,1)S(1)} collective-permute-done((bf16[64,640]{1,0:T(8,128)(2,1)S(1)}, bf16[64,640]{1,0:T(8,128)(2,1)S(1)}, u32[]{:S(2)}, u32[]{:S(2)}) %collective-permute-start.18) | collective-permute-done | bytes 81952 | tf_op jit(solution)/shard_map/ppermute | solution.py:319
  127.8 3.1 %collective-permute-start.19 = (bf16[1,32,128]{2,1,0:T(8,128)(2,1)S(1)}, bf16[1,32,128]{2,1,0:T(8,128)(2,1)S(1)}, u32[]{:S(2)}, u32[]{:S(2)}) collective-permute-start(bf16[1,32,128]{2,1,0:T(8,128)(2,1)S(1)} %bitcast.23), channel_id=1, source_target_pairs={{0,128},{8,136},{16,144},{24,152},{32,160},{40,168},{48,176},{56,1... | collective-permute-start | bytes 24584 | tf_op jit(solution)/shard_map/ppermute | solution.py:540
  130.9 0.6 collective-permute-start.20
  132.1 1.2 copy-done.1
  133.4 1.1 collective-permute-done.20
  134.6 1.8 %collective-permute-done.21 = bf16[1,32,128]{2,1,0:T(8,128)(2,1)S(1)} collective-permute-done((bf16[1,32,128]{2,1,0:T(8,128)(2,1)S(1)}, bf16[1,32,128]{2,1,0:T(8,128)(2,1)S(1)}, u32[]{:S(2)}, u32[]{:S(2)}) %collective-permute-start.21) | collective-permute-done | bytes 8224 | tf_op jit(solution)/shard_map/ppermute | solution.py:540
  136.4 0.6 collective-permute-start.22
  137.0 2.2 %sum_returned.1 = bf16[64,4096]{1,0:T(8,128)(2,1)} custom-call(s32[4,32]{1,0:T(4,128)S(1)} %bitcast.29, f32[32,64,128]{2,1,0:T(8,128)S(1)} %sum_near.1.near_ref, bf16[32,4,64,128]{3,2,1,0:T(8,128)(2,1)S(1)} %all-to-all-done.3.back_ref), custom_call_target="tpu_custom_call" | custom-call | bytes 4194304 | tf_op jit(solution)/shard_map/sum_returned/pallas_call | solution.py:546
  139.2 1.0 collective-permute-done.22
  140.2 1.2 collective-permute-done.23
  141.5 0.7 weight_spread.1
  (60 shorter events, 4.3 us)
Async XLA Ops:
  3.2 7.8 %copy-start = (bf16[4096,64]{0,1:T(8,128)(2,1)S(1)}, bf16[4096,64]{0,1:T(8,128)(2,1)}, u32[]{:S(2)}) copy-start(bf16[4096,64]{0,1:T(8,128)(2,1)} %param.9) | copy-start | bytes 1572868
  3.2 35.7 %copy-start.5 = (s32[32,8]{0,1:T(8,128)S(1)}, s32[32,8]{0,1:T(8,128)}, u32[]{:S(2)}) copy-start(s32[32,8]{0,1:T(8,128)} %param.11) | copy-start | bytes 3076
  3.2 35.7 %copy-start.7 = (s32[32]{0:T(128)S(1)}, s32[32]{0:T(128)}, u32[]{:S(2)}) copy-start(s32[32]{0:T(128)} %counts_ref.3) | copy-start | bytes 388
  3.2 35.6 %all-to-all-start = ((bf16[32,4,64,128]{3,2,1,0:T(8,128)(2,1)}), bf16[32,4,64,128]{3,2,1,0:T(8,128)(2,1)S(1)}, u32[]{:S(2)}, u32[]{:S(2)}) async-start(bf16[32,4,64,128]{3,2,1,0:T(8,128)(2,1)} %pack_outgoing.1), calls=%async_computation | async-start | bytes 4194304 | tf_op jit(solution)/shard_map/all_to_all | solution.py:380
  11.9 14.8 %collective-permute-start = (bf16[64,512]{1,0:T(8,128)(2,1)}, bf16[64,512]{1,0:T(8,128)(2,1)S(1)}, u32[]{:S(2)}, u32[]{:S(2)}) collective-permute-start(bf16[64,512]{1,0:T(8,128)(2,1)} %get-tuple-element.76), channel_id=1, source_target_pairs={{0,1},{1,2},{2,3},{3,4},{4,5},{5,6},{6,7},{7,0},{8,9},{9,10},{10,1... | collective-permute-start | bytes 196616 | tf_op jit(solution)/shard_map/ppermute | solution.py:319
  13.9 15.5 %collective-permute-start.1 = (bf16[64,512]{1,0:T(8,128)(2,1)}, bf16[64,512]{1,0:T(8,128)(2,1)S(1)}, u32[]{:S(2)}, u32[]{:S(2)}) collective-permute-start(bf16[64,512]{1,0:T(8,128)(2,1)} %get-tuple-element.77), channel_id=1, source_target_pairs={{0,2},{1,3},{2,4},{3,5},{4,6},{5,7},{6,0},{7,1},{8,10},{9,11},{10,... | collective-permute-start | bytes 196616 | tf_op jit(solution)/shard_map/ppermute | solution.py:319
  17.1 13.2 %collective-permute-start.2 = (bf16[64,512]{1,0:T(8,128)(2,1)}, bf16[64,512]{1,0:T(8,128)(2,1)S(1)}, u32[]{:S(2)}, u32[]{:S(2)}) collective-permute-start(bf16[64,512]{1,0:T(8,128)(2,1)} %get-tuple-element.78), channel_id=1, source_target_pairs={{0,3},{1,4},{2,5},{3,6},{4,7},{5,0},{6,1},{7,2},{8,11},{9,12},{10,... | collective-permute-start | bytes 196616 | tf_op jit(solution)/shard_map/ppermute | solution.py:319
  21.2 9.2 %collective-permute-start.3 = (bf16[64,512]{1,0:T(8,128)(2,1)}, bf16[64,512]{1,0:T(8,128)(2,1)S(1)}, u32[]{:S(2)}, u32[]{:S(2)}) collective-permute-start(bf16[64,512]{1,0:T(8,128)(2,1)} %get-tuple-element.79), channel_id=1, source_target_pairs={{0,4},{1,5},{2,6},{3,7},{4,0},{5,1},{6,2},{7,3},{8,12},{9,13},{10,... | collective-permute-start | bytes 196616 | tf_op jit(solution)/shard_map/ppermute | solution.py:319
  21.7 14.4 %collective-permute-start.4 = (bf16[64,512]{1,0:T(8,128)(2,1)}, bf16[64,512]{1,0:T(8,128)(2,1)S(1)}, u32[]{:S(2)}, u32[]{:S(2)}) collective-permute-start(bf16[64,512]{1,0:T(8,128)(2,1)} %get-tuple-element.80), channel_id=1, source_target_pairs={{0,5},{1,6},{2,7},{3,0},{4,1},{5,2},{6,3},{7,4},{8,13},{9,14},{10,... | collective-permute-start | bytes 196616 | tf_op jit(solution)/shard_map/ppermute | solution.py:319
  26.7 9.4 %copy-start.8 = (bf16[64,512]{1,0:T(8,128)(2,1)}, bf16[64,512]{1,0:T(8,128)(2,1)S(1)}, u32[]{:S(2)}) copy-start(bf16[64,512]{1,0:T(8,128)(2,1)S(1)} %collective-permute-done.refs_1_) | copy-start | bytes 196612
  26.7 9.4 %collective-permute-start.5 = (bf16[64,512]{1,0:T(8,128)(2,1)}, bf16[64,512]{1,0:T(8,128)(2,1)S(1)}, u32[]{:S(2)}, u32[]{:S(2)}) collective-permute-start(bf16[64,512]{1,0:T(8,128)(2,1)} %get-tuple-element.81), channel_id=1, source_target_pairs={{0,6},{1,7},{2,0},{3,1},{4,2},{5,3},{6,4},{7,5},{8,14},{9,15},{10,... | collective-permute-start | bytes 196616 | tf_op jit(solution)/shard_map/ppermute | solution.py:319
  29.3 6.8 %copy-start.9 = (bf16[64,512]{1,0:T(8,128)(2,1)}, bf16[64,512]{1,0:T(8,128)(2,1)S(1)}, u32[]{:S(2)}) copy-start(bf16[64,512]{1,0:T(8,128)(2,1)S(1)} %collective-permute-done.1.refs_2_) | copy-start | bytes 196612
  29.3 8.0 %collective-permute-start.6 = (bf16[64,512]{1,0:T(8,128)(2,1)}, bf16[64,512]{1,0:T(8,128)(2,1)}, u32[]{:S(2)}, u32[]{:S(2)}) collective-permute-start(bf16[64,512]{1,0:T(8,128)(2,1)} %get-tuple-element.82), channel_id=1, source_target_pairs={{0,7},{1,0},{2,1},{3,2},{4,3},{5,4},{6,5},{7,6},{8,15},{9,8},{10,9... | collective-permute-start | bytes 196616 | tf_op jit(solution)/shard_map/ppermute | solution.py:319
  30.3 5.8 %copy-start.10 = (bf16[64,512]{1,0:T(8,128)(2,1)}, bf16[64,512]{1,0:T(8,128)(2,1)S(1)}, u32[]{:S(2)}) copy-start(bf16[64,512]{1,0:T(8,128)(2,1)S(1)} %collective-permute-done.2.refs_3_) | copy-start | bytes 196612
  30.4 5.8 %copy-start.11 = (bf16[64,512]{1,0:T(8,128)(2,1)}, bf16[64,512]{1,0:T(8,128)(2,1)S(1)}, u32[]{:S(2)}) copy-start(bf16[64,512]{1,0:T(8,128)(2,1)S(1)} %collective-permute-done.3.refs_4_) | copy-start | bytes 196612
  36.1 0.6 copy-start.12
  36.7 0.6 copy-start.13
  38.9 14.7 %copy-start.14 = (f32[256]{0:T(256)S(1)}, f32[256]{0:T(256)}, u32[]{:S(2)}) copy-start(f32[256]{0:T(256)} %param.16) | copy-start | bytes 3076
  38.9 14.8 %copy-start.2 = (bf16[512,256]{1,0:T(8,128)(2,1)S(1)}, bf16[512,256]{1,0:T(8,128)(2,1)}, u32[]{:S(2)}) copy-start(bf16[512,256]{1,0:T(8,128)(2,1)} %weight_ref.4) | copy-start | bytes 786436
  38.9 14.8 %copy-start.3 = (bf16[512,256]{1,0:T(8,128)(2,1)S(1)}, bf16[512,256]{1,0:T(8,128)(2,1)}, u32[]{:S(2)}) copy-start(bf16[512,256]{1,0:T(8,128)(2,1)} %weight_ref.5) | copy-start | bytes 786436
  38.9 14.8 %copy-start.4 = (bf16[512,256]{1,0:T(8,128)(2,1)S(1)}, bf16[512,256]{1,0:T(8,128)(2,1)}, u32[]{:S(2)}) copy-start(bf16[512,256]{1,0:T(8,128)(2,1)} %cot_ref.1) | copy-start | bytes 786436
  45.1 25.6 %all-to-all-start.1 = ((bf16[8,64,512]{2,1,0:T(8,128)(2,1)}), bf16[8,64,512]{2,1,0:T(8,128)(2,1)S(1)}, u32[]{:S(2)}, u32[]{:S(2)}) async-start(bf16[8,64,512]{2,1,0:T(8,128)(2,1)} %get-tuple-element.96), calls=%async_computation.1 | async-start | bytes 1048576 | tf_op jit(solution)/shard_map/all_to_all | solution.py:419
  72.5 20.1 %all-to-all-start.2 = ((bf16[8,64,512]{2,1,0:T(8,128)(2,1)}), bf16[8,64,512]{2,1,0:T(8,128)(2,1)S(1)}, u32[]{:S(2)}, u32[]{:S(2)}) async-start(bf16[8,64,512]{2,1,0:T(8,128)(2,1)} %bitcast.8), calls=%async_computation.2 | async-start | bytes 1048576 | tf_op jit(solution)/shard_map/all_to_all | solution.py:430
  76.5 1.6 %collective-permute-start.7 = (bf16[16,8,8,128]{3,2,1,0:T(8,128)(2,1)S(1)}, bf16[16,8,8,128]{3,2,1,0:T(8,128)(2,1)S(1)}, u32[]{:S(2)}, u32[]{:S(2)}) collective-permute-start(bf16[16,8,8,128]{3,2,1,0:T(8,128)(2,1)S(1)} %get-tuple-element.101), channel_id=1, source_target_pairs={{0,8},{8,0},{16,24},{24,16},{32,40},{40,32},{48,56},{56,48},{64,72... | collective-permute-start | bytes 786440 | tf_op jit(solution)/shard_map/ppermute | solution.py:450
  78.2 5.4 %collective-permute-start.10 = (bf16[4,8,8,128]{3,2,1,0:T(8,128)(2,1)S(1)}, bf16[4,8,8,128]{3,2,1,0:T(8,128)(2,1)S(1)}, u32[]{:S(2)}, u32[]{:S(2)}) collective-permute-start(bf16[4,8,8,128]{3,2,1,0:T(8,128)(2,1)S(1)} %get-tuple-element.105), channel_id=1, source_target_pairs={{0,80},{8,88},{16,64},{24,72},{32,112},{40,120},{48,96},{56,104},{... | collective-permute-start | bytes 196616 | tf_op jit(solution)/shard_map/ppermute | solution.py:466
  79.7 5.0 %collective-permute-start.8 = (bf16[4,8,8,128]{3,2,1,0:T(8,128)(2,1)S(1)}, bf16[4,8,8,128]{3,2,1,0:T(8,128)(2,1)S(1)}, u32[]{:S(2)}, u32[]{:S(2)}) collective-permute-start(bf16[4,8,8,128]{3,2,1,0:T(8,128)(2,1)S(1)} %get-tuple-element.103), channel_id=1, source_target_pairs={{0,64},{8,72},{16,80},{24,88},{32,96},{40,104},{48,112},{56,120},{... | collective-permute-start | bytes 196616 | tf_op jit(solution)/shard_map/ppermute | solution.py:466
  80.8 4.3 %collective-permute-start.9 = (bf16[4,8,8,128]{3,2,1,0:T(8,128)(2,1)S(1)}, bf16[4,8,8,128]{3,2,1,0:T(8,128)(2,1)S(1)}, u32[]{:S(2)}, u32[]{:S(2)}) collective-permute-start(bf16[4,8,8,128]{3,2,1,0:T(8,128)(2,1)S(1)} %get-tuple-element.104), channel_id=1, source_target_pairs={{0,16},{8,24},{16,0},{24,8},{32,48},{40,56},{48,32},{56,40},{64,80... | collective-permute-start | bytes 196616 | tf_op jit(solution)/shard_map/ppermute | solution.py:466
  85.1 6.0 %collective-permute-start.11 = (bf16[4,8,8,128]{3,2,1,0:T(8,128)(2,1)S(1)}, bf16[4,8,8,128]{3,2,1,0:T(8,128)(2,1)S(1)}, u32[]{:S(2)}, u32[]{:S(2)}) collective-permute-start(bf16[4,8,8,128]{3,2,1,0:T(8,128)(2,1)S(1)} %weight_add.2.held_ref), channel_id=1, source_target_pairs={{0,32},{8,40},{16,48},{24,56},{32,0},{40,8},{48,16},{56,24},{64,96... | collective-permute-start | bytes 196616 | tf_op jit(solution)/shard_map/ppermute | solution.py:479
  99.0 37.4 %all-to-all-start.3 = ((bf16[32,4,64,128]{3,2,1,0:T(8,128)(2,1)}), bf16[32,4,64,128]{3,2,1,0:T(8,128)(2,1)S(1)}, u32[]{:S(2)}, u32[]{:S(2)}) async-start(bf16[32,4,64,128]{3,2,1,0:T(8,128)(2,1)} %bitcast.30), calls=%async_computation.3 | async-start | bytes 4194304 | tf_op jit(solution)/shard_map/all_to_all | solution.py:504
  106.5 30.5 %copy-start.6 = (s32[1,32,4]{1,2,0:T(4,128)S(1)}, s32[1,32,4]{1,2,0:T(4,128)}, u32[]{:S(2)}) copy-start(s32[1,32,4]{1,2,0:T(4,128)} %param.13) | copy-start | bytes 1540
  106.6 12.8 %collective-permute-start.12 = (bf16[64,640]{1,0:T(8,128)(2,1)S(1)}, bf16[64,640]{1,0:T(8,128)(2,1)S(1)}, u32[]{:S(2)}, u32[]{:S(2)}) collective-permute-start(bf16[64,640]{1,0:T(8,128)(2,1)S(1)} %get-tuple-element.129), channel_id=1, source_target_pairs={{0,4},{1,5},{2,6},{3,7},{4,0},{5,1},{6,2},{7,3},{8,12},{9,13},{10,... | collective-permute-start | bytes 245768 | tf_op jit(solution)/shard_map/ppermute | solution.py:319
  110.2 13.1 %collective-permute-start.13 = (bf16[64,640]{1,0:T(8,128)(2,1)S(1)}, bf16[64,640]{1,0:T(8,128)(2,1)S(1)}, u32[]{:S(2)}, u32[]{:S(2)}) collective-permute-start(bf16[64,640]{1,0:T(8,128)(2,1)S(1)} %get-tuple-element.130), channel_id=1, source_target_pairs={{0,3},{1,4},{2,5},{3,6},{4,7},{5,0},{6,1},{7,2},{8,11},{9,12},{10,... | collective-permute-start | bytes 245768 | tf_op jit(solution)/shard_map/ppermute | solution.py:319
  110.8 12.6 %collective-permute-start.14 = (bf16[64,640]{1,0:T(8,128)(2,1)S(1)}, bf16[64,640]{1,0:T(8,128)(2,1)S(1)}, u32[]{:S(2)}, u32[]{:S(2)}) collective-permute-start(bf16[64,640]{1,0:T(8,128)(2,1)S(1)} %get-tuple-element.131), channel_id=1, source_target_pairs={{0,5},{1,6},{2,7},{3,0},{4,1},{5,2},{6,3},{7,4},{8,13},{9,14},{10,... | collective-permute-start | bytes 245768 | tf_op jit(solution)/shard_map/ppermute | solution.py:319
  115.3 8.1 %collective-permute-start.15 = (bf16[64,640]{1,0:T(8,128)(2,1)S(1)}, bf16[64,640]{1,0:T(8,128)(2,1)S(1)}, u32[]{:S(2)}, u32[]{:S(2)}) collective-permute-start(bf16[64,640]{1,0:T(8,128)(2,1)S(1)} %get-tuple-element.132), channel_id=1, source_target_pairs={{0,2},{1,3},{2,4},{3,5},{4,6},{5,7},{6,0},{7,1},{8,10},{9,11},{10,... | collective-permute-start | bytes 245768 | tf_op jit(solution)/shard_map/ppermute | solution.py:319
  115.8 9.0 %collective-permute-start.16 = (bf16[64,640]{1,0:T(8,128)(2,1)S(1)}, bf16[64,640]{1,0:T(8,128)(2,1)S(1)}, u32[]{:S(2)}, u32[]{:S(2)}) collective-permute-start(bf16[64,640]{1,0:T(8,128)(2,1)S(1)} %get-tuple-element.133), channel_id=1, source_target_pairs={{0,6},{1,7},{2,0},{3,1},{4,2},{5,3},{6,4},{7,5},{8,14},{9,15},{10,... | collective-permute-start | bytes 245768 | tf_op jit(solution)/shard_map/ppermute | solution.py:319
  119.4 6.2 %collective-permute-start.17 = (bf16[64,640]{1,0:T(8,128)(2,1)S(1)}, bf16[64,640]{1,0:T(8,128)(2,1)S(1)}, u32[]{:S(2)}, u32[]{:S(2)}) collective-permute-start(bf16[64,640]{1,0:T(8,128)(2,1)S(1)} %get-tuple-element.134), channel_id=1, source_target_pairs={{0,1},{1,2},{2,3},{3,4},{4,5},{5,6},{6,7},{7,0},{8,9},{9,10},{10,1... | collective-permute-start | bytes 245768 | tf_op jit(solution)/shard_map/ppermute | solution.py:319
  123.4 4.4 %collective-permute-start.18 = (bf16[64,640]{1,0:T(8,128)(2,1)S(1)}, bf16[64,640]{1,0:T(8,128)(2,1)S(1)}, u32[]{:S(2)}, u32[]{:S(2)}) collective-permute-start(bf16[64,640]{1,0:T(8,128)(2,1)S(1)} %get-tuple-element.135), channel_id=1, source_target_pairs={{0,7},{1,0},{2,1},{3,2},{4,3},{5,4},{6,5},{7,6},{8,15},{9,8},{10,9... | collective-permute-start | bytes 245768 | tf_op jit(solution)/shard_map/ppermute | solution.py:319
  127.8 5.6 %collective-permute-start.19 = (bf16[1,32,128]{2,1,0:T(8,128)(2,1)S(1)}, bf16[1,32,128]{2,1,0:T(8,128)(2,1)S(1)}, u32[]{:S(2)}, u32[]{:S(2)}) collective-permute-start(bf16[1,32,128]{2,1,0:T(8,128)(2,1)S(1)} %bitcast.23), channel_id=1, source_target_pairs={{0,128},{8,136},{16,144},{24,152},{32,160},{40,168},{48,176},{56,1... | collective-permute-start | bytes 24584 | tf_op jit(solution)/shard_map/ppermute | solution.py:540
  130.9 3.7 %collective-permute-start.20 = (bf16[1,32,128]{2,1,0:T(8,128)(2,1)S(1)}, bf16[1,32,128]{2,1,0:T(8,128)(2,1)S(1)}, u32[]{:S(2)}, u32[]{:S(2)}) collective-permute-start(bf16[1,32,128]{2,1,0:T(8,128)(2,1)S(1)} %bitcast.24), channel_id=1, source_target_pairs={{0,64},{8,72},{16,80},{24,88},{32,96},{40,104},{48,112},{56,120},{... | collective-permute-start | bytes 24584 | tf_op jit(solution)/shard_map/ppermute | solution.py:540
  131.5 4.9 %collective-permute-start.21 = (bf16[1,32,128]{2,1,0:T(8,128)(2,1)S(1)}, bf16[1,32,128]{2,1,0:T(8,128)(2,1)S(1)}, u32[]{:S(2)}, u32[]{:S(2)}) collective-permute-start(bf16[1,32,128]{2,1,0:T(8,128)(2,1)S(1)} %bitcast.25), channel_id=1, source_target_pairs={{0,192},{8,200},{16,208},{24,216},{32,224},{40,232},{48,240},{56,2... | collective-permute-start | bytes 24584 | tf_op jit(solution)/shard_map/ppermute | solution.py:540
  132.1 1.2 copy-start.1
  136.4 3.8 %collective-permute-start.22 = (bf16[2,32,128]{2,1,0:T(8,128)(2,1)S(1)}, bf16[2,32,128]{2,1,0:T(8,128)(2,1)S(1)}, u32[]{:S(2)}, u32[]{:S(2)}) collective-permute-start(bf16[2,32,128]{2,1,0:T(8,128)(2,1)S(1)} %pad_maximum_fusion.2), channel_id=1, source_target_pairs={{0,16},{8,24},{16,0},{24,8},{32,48},{40,56},{48,32},{56,40},{64,80... | collective-permute-start | bytes 49160 | tf_op jit(solution)/shard_map/ppermute | solution.py:557
  140.2 1.2 collective-permute-start.23

commit v8 on v7

--- a/solution.py
+++ b/solution.py
@@ -77,27 +77,38 @@
 
 
 def stream_rows(vals_ref, held_ref, sems, body, before=None, after=None):
-    copies = sems.shape[0]
-    span = held_ref.shape[0] // copies
-
-    def copy(place):
-        rows = pl.ds(place * span, span)
+    total = held_ref.shape[0]
+    small = total // 8
+    large = 2 * small
+
+    def copy(start, span, place):
+        rows = pl.ds(start, span)
         return pltpu.make_async_copy(vals_ref.at[rows], held_ref.at[rows], sems.at[place])
 
-    for place in range(copies):
-        copy(place).start()
+    heads = [(place * small, small, place) for place in range(2)]
+    tails = total // large - 1
+    for start, span, place in heads:
+        copy(start, span, place).start()
+    for place in range(tails):
+        copy((place + 1) * large, large, place + 2).start()
     if before is not None:
         before()
 
+    def work(start, span, place):
+        copy(start, span, place).wait()
+        for row in range(span):
+            body(start + row)
+        if after is not None:
+            after(start, span, place)
+
+    for start, span, place in heads:
+        work(jnp.int32(start), span, place)
+
     def one(place, carry):
-        copy(place).wait()
-        for row in range(span):
-            body(place * span + row)
-        if after is not None:
-            after(place)
+        work((place + 1) * large, large, place + 2)
         return carry
 
-    lax.fori_loop(0, copies, one, 0)
+    lax.fori_loop(0, tails, one, 0)
 
 
 def gather_kernel(
@@ -125,16 +136,16 @@
         degree_ref[group, :, place] = total[width : width + 8]
         mean_ref[group, :, place] = (total[:width] / total[width : width + 1]).astype(BF)
 
-    copies = out_sems.shape[0]
-    span = mean_ref.shape[0] // copies
-
-    def copy(place):
-        groups = pl.ds(place * span, span)
+    def copy(start, span, place):
+        groups = pl.ds(start // rows, span // rows)
         return pltpu.make_async_copy(mean_ref.at[groups], out_ref.at[groups], out_sems.at[place])
 
-    stream_rows(vals_ref, held_ref, sems, body, after=lambda place: copy(place).start())
-    for place in range(copies):
-        copy(place).wait()
+    stream_rows(vals_ref, held_ref, sems, body, after=lambda *which: copy(*which).start())
+    small = held_ref.shape[0] // 8
+    copy(0, small, 0).wait()
+    copy(small, small, 1).wait()
+    for place in range(2, out_sems.shape[0]):
+        copy((place - 1) * 2 * small, 2 * small, place).wait()
 
 
 def self_kernel(chans, me_ref, weight_ref, bias_ref, neigh_ref, cot_ref, *refs):
@@ -277,7 +288,9 @@
     unit_rows = self_ref.shape[0]
     per = unit_rows // rows
     for place in range(pieces):
-        value = held_ref[lax.bitwise_xor(me_ref[0], place)].astype(F32) * scale
+        away = lax.bitwise_xor(me_ref[0], place)
+        first, second, third = away // 4, lax.rem(away // 2, 2), lax.rem(away, 2)
+        value = held_ref[second * 4 + third * 2 + first].astype(F32) * scale
         target = self_ref if place < half else neigh_ref
         inside = place % half
         column, row = inside // per, inside % per
@@ -362,7 +375,7 @@
     block_flops = 2 * block_rows * depth * size * size * chan_width
     layer_flops = 2 * f_in * f_out * nodes
     unit, lanes = 8, 128
-    copies, streams = 8, 4
+    copies, streams = 8, 5
 
     outgoing = pl.pallas_call(
         pack_kernel,
@@ -535,6 +548,7 @@
         cost_estimate=cost(0, 3 * MIB),
         name="sum_near",
     )(me, own_grad, *packed)
+    held = jnp.concatenate([held, lax.ppermute(held, "dom", flips[0])], axis=0)
     whole, half = 1 << order[-1], 1 << halves[-1]
     across, beside, both = (
         lax.ppermute(held, "dom", [(i, i ^ flip) for i in range(parts)]) for flip in (whole, half, whole | half)
@@ -542,7 +556,7 @@
     mine = held.astype(F32) + across.astype(F32)
     other = beside.astype(F32) + both.astype(F32)
     held = jnp.concatenate([mine, other], axis=0).astype(BF)
-    held, back, near = lax.optimization_barrier((held, back, near))
+    held, back, near = lax.optimization_barrier((held.reshape(4, pieces * unit, lanes), back, near))
     grad_feats = pl.pallas_call(
         final_kernel,
         out_shape=sds((chan_width, node_count), BF),
@@ -553,10 +567,7 @@
         cost_estimate=cost(0, 4 * MIB),
         name="sum_returned",
     )(send, near, back)
-    for level in reversed(range(len(halves) - 1)):
-        held = jnp.concatenate([held, lax.ppermute(held, "dom", flips[level])], axis=0)
-        if level == len(halves) - 2:
-            held, grad_feats = lax.optimization_barrier((held, grad_feats))
+    held = jnp.concatenate([held, lax.ppermute(held, "dom", flips[1])], axis=0)
     address = jnp.int32(0)
     for level in range(len(halves)):
         address = address * 2 + bits[level][0]

time: 144 us -> 144 us (level)
  waiting for transfers between devices: 45.6 us -> 47.5 us
  transfers between devices with their start and end apart: 28 -> 28, of which waited for: 17 -> 20; matrix products, arithmetic and copies ran while one was open for 0% -> 0% of each run, Pallas kernels for 4% -> 4%
where the time goes in v8:
time: 144 us; the launch traced here: 143 us
  starting transfers between devices  68.3 us (47%)
  waiting for transfers between devices  47.5 us (33%)
  Pallas kernels  23.9 us (17%)
  local copies, waits for them, and re-layouts  2.63 us (2%)
    ppermute x14, starting transfers between devices, exchange(): lax.ppermute(chunks[shift], 'chan', [(i, (i + shift) % count) for i in ra...  31.2 us
    all_to_all x1, waiting for transfers between devices, per_device(): lax.all_to_all(mean, 'chan', split_axis=0, concat_axis=0, tiled=True)  15.5 us
    ppermute x14, waiting for transfers between devices, exchange(): lax.ppermute(chunks[shift], 'chan', [(i, (i + shift) % count) for i in ra...  13.8 us
    all_to_all x1, starting transfers between devices, per_device(): lax.all_to_all(mean, 'chan', split_axis=0, concat_axis=0, tiled=True)  8.48 us
    all_to_all x1, starting transfers between devices, per_device(): lax.all_to_all(outgoing, 'dom', split_axis=0, concat_axis=0, tiled=True)  7.76 us
    all_to_all x1, starting transfers between devices, per_device(): lax.all_to_all(far_grad.reshape(parts, slots, chan_width, size), 'dom', s...  7.46 us
    pallas_call x1, Pallas kernels, per_device(): pl.pallas_call(scatter_kernel, out_shape=[pltpu.HBM((block_rows, chan_wid...  6.47 us
    pallas_call x1, Pallas kernels, per_device(): pl.pallas_call(gather_kernel, out_shape=[pltpu.HBM((chans, chan_width, no...  6.08 us
  transfers between devices with their start and end apart: 28, of which 20 were waited for; matrix products, arithmetic and copies ran while one was open for 0% of the time, Pallas kernels for 4%

profile of v8, /device:TPU:2, one launch (start us, length us, event | category | flops | bytes accessed | tf_op | source)
XLA Modules:
  0.0 143.3 jit_solution(15884147488381760136)
XLA Ops:
  0.6 2.5 %pack_outgoing.1 = bf16[32,4,64,128]{3,2,1,0:T(8,128)(2,1)} custom-call(s32[4,32]{1,0:T(4,128)} %bitcast.27, bf16[64,4096]{1,0:T(8,128)(2,1)} %bitcast.19), custom_call_target="tpu_custom_call" | custom-call | bytes 5242880 | tf_op jit(solution)/shard_map/pack_outgoing/pallas_call | solution.py:380
  3.2 7.8 %all-to-all-start = ((bf16[32,4,64,128]{3,2,1,0:T(8,128)(2,1)}), bf16[32,4,64,128]{3,2,1,0:T(8,128)(2,1)S(1)}, u32[]{:S(2)}, u32[]{:S(2)}) async-start(bf16[32,4,64,128]{3,2,1,0:T(8,128)(2,1)} %pack_outgoing.1), calls=%async_computation | async-start | bytes 4194304 | tf_op jit(solution)/shard_map/all_to_all | solution.py:393
  11.0 0.9 split_feats.1
  11.9 2.0 %collective-permute-start = (bf16[64,512]{1,0:T(8,128)(2,1)}, bf16[64,512]{1,0:T(8,128)(2,1)S(1)}, u32[]{:S(2)}, u32[]{:S(2)}) collective-permute-start(bf16[64,512]{1,0:T(8,128)(2,1)} %get-tuple-element.74), channel_id=1, source_target_pairs={{0,1},{1,2},{2,3},{3,4},{4,5},{5,6},{6,7},{7,0},{8,9},{9,10},{10,1... | collective-permute-start | bytes 196616 | tf_op jit(solution)/shard_map/ppermute | solution.py:332
  13.9 3.3 %collective-permute-start.1 = (bf16[64,512]{1,0:T(8,128)(2,1)}, bf16[64,512]{1,0:T(8,128)(2,1)S(1)}, u32[]{:S(2)}, u32[]{:S(2)}) collective-permute-start(bf16[64,512]{1,0:T(8,128)(2,1)} %get-tuple-element.75), channel_id=1, source_target_pairs={{0,2},{1,3},{2,4},{3,5},{4,6},{5,7},{6,0},{7,1},{8,10},{9,11},{10,... | collective-permute-start | bytes 196616 | tf_op jit(solution)/shard_map/ppermute | solution.py:332
  17.1 4.0 %collective-permute-start.2 = (bf16[64,512]{1,0:T(8,128)(2,1)}, bf16[64,512]{1,0:T(8,128)(2,1)S(1)}, u32[]{:S(2)}, u32[]{:S(2)}) collective-permute-start(bf16[64,512]{1,0:T(8,128)(2,1)} %get-tuple-element.76), channel_id=1, source_target_pairs={{0,3},{1,4},{2,5},{3,6},{4,7},{5,0},{6,1},{7,2},{8,11},{9,12},{10,... | collective-permute-start | bytes 196616 | tf_op jit(solution)/shard_map/ppermute | solution.py:332
  21.7 4.9 %collective-permute-start.4 = (bf16[64,512]{1,0:T(8,128)(2,1)}, bf16[64,512]{1,0:T(8,128)(2,1)S(1)}, u32[]{:S(2)}, u32[]{:S(2)}) collective-permute-start(bf16[64,512]{1,0:T(8,128)(2,1)} %get-tuple-element.78), channel_id=1, source_target_pairs={{0,5},{1,6},{2,7},{3,0},{4,1},{5,2},{6,3},{7,4},{8,13},{9,14},{10,... | collective-permute-start | bytes 196616 | tf_op jit(solution)/shard_map/ppermute | solution.py:332
  26.7 2.7 %collective-permute-start.5 = (bf16[64,512]{1,0:T(8,128)(2,1)}, bf16[64,512]{1,0:T(8,128)(2,1)S(1)}, u32[]{:S(2)}, u32[]{:S(2)}) collective-permute-start(bf16[64,512]{1,0:T(8,128)(2,1)} %get-tuple-element.79), channel_id=1, source_target_pairs={{0,6},{1,7},{2,0},{3,1},{4,2},{5,3},{6,4},{7,5},{8,14},{9,15},{10,... | collective-permute-start | bytes 196616 | tf_op jit(solution)/shard_map/ppermute | solution.py:332
  29.3 1.0 collective-permute-start.6
  30.4 5.7 %collective-permute-done.4.refs_5_ = bf16[64,512]{1,0:T(8,128)(2,1)S(1)} collective-permute-done((bf16[64,512]{1,0:T(8,128)(2,1)}, bf16[64,512]{1,0:T(8,128)(2,1)S(1)}, u32[]{:S(2)}, u32[]{:S(2)}) %collective-permute-start.4) | collective-permute-done | bytes 65568 | tf_op jit(solution)/shard_map/ppermute | solution.py:332
  36.7 0.6 copy-done.13
  37.4 1.5 %all-to-all-done = bf16[32,4,64,128]{3,2,1,0:T(8,128)(2,1)S(1)} async-done(((bf16[32,4,64,128]{3,2,1,0:T(8,128)(2,1)}), bf16[32,4,64,128]{3,2,1,0:T(8,128)(2,1)S(1)}, u32[]{:S(2)}, u32[]{:S(2)}) %all-to-all-start) | async-done | bytes 2097184 | tf_op jit(solution)/shard_map/all_to_all | solution.py:393
  38.9 6.1 %neighbour_mean.1 = (bf16[8,64,512]{2,1,0:T(8,128)(2,1)}, f32[8,8,512]{2,1,0:T(8,128)S(1)}) custom-call(s32[8,32]{1,0:T(8,128)S(1)} %bitcast.25, s32[32]{0:T(128)S(1)} %copy-done.7, bf16[64,4096]{1,0:T(8,128)(2,1)S(1)} %bitcast.21, bf16[128,64,128]{2,1,0:T(8,128)(2,1)S(1)} %bitcast.16, bf16[32,8,128,128]{3,2,1,0:T(8,128)(2,1)} %vals_ref.3), custom_call_target="tpu_custom_call" | custom-call | flops 536870912 | bytes 11534336 | tf_op jit(solution)/shard_map/neighbour_mean/pallas_call | solution.py:417
  45.0 8.5 %all-to-all-start.1 = ((bf16[8,64,512]{2,1,0:T(8,128)(2,1)}), bf16[8,64,512]{2,1,0:T(8,128)(2,1)S(1)}, u32[]{:S(2)}, u32[]{:S(2)}) async-start(bf16[8,64,512]{2,1,0:T(8,128)(2,1)} %get-tuple-element.94), calls=%async_computation.1 | async-start | bytes 1048576 | tf_op jit(solution)/shard_map/all_to_all | solution.py:432
  53.7 1.4 %self_part.1 = (bf16[512,512]{1,0:T(8,128)(2,1)S(1)}, f32[256,512]{1,0:T(8,128)S(1)}, bf16[256,512]{1,0:T(8,128)(2,1)S(1)}, bf16[256,512]{1,0:T(8,128)(2,1)S(1)}) custom-call(s32[1]{0:T(128)} %bitcast.me_ref, bf16[512,256]{1,0:T(8,128)(2,1)S(1)} %copy-done.3, f32[256,1]{1,0:T(8,128)S(1)} %copy.13.bias_ref, bf16[512,256]{1,0:T(8,128)(2,1)S(1)} %copy-done.2, ...), custom_call_target="tpu_custom_call" | custom-call | flops 134217728 | bytes 2097152 | tf_op jit(solution)/shard_map/self_part/pallas_call | solution.py:407
  55.1 15.5 %all-to-all-done.1 = bf16[8,64,512]{2,1,0:T(8,128)(2,1)S(1)} async-done(((bf16[8,64,512]{2,1,0:T(8,128)(2,1)}), bf16[8,64,512]{2,1,0:T(8,128)(2,1)S(1)}, u32[]{:S(2)}, u32[]{:S(2)}) %all-to-all-start.1) | async-done | bytes 524320 | tf_op jit(solution)/shard_map/all_to_all | solution.py:432
  70.6 1.8 %layer_head.1 = (bf16[256,512]{1,0:T(8,128)(2,1)S(1)}, bf16[256,512]{1,0:T(8,128)(2,1)S(1)}, bf16[512,512]{1,0:T(8,128)(2,1)}) custom-call(s32[1]{0:T(128)} %bitcast.me_ref, f32[8,8,512]{2,1,0:T(8,128)S(1)} %get-tuple-element.82.degree_ref, f32[256,512]{1,0:T(8,128)S(1)} %get-tuple-element.91.pre_ref, bf16[256,512]{1,0:T(8,128)(2,1)S(1)} %get-tuple-element.92.turned_ref, ...), custom_call_target="tpu_custom_call" | custom-call | flops 268435456 | bytes 4194304 | tf_op jit(solution)/shard_map/layer_head/pallas_call | solution.py:434
  72.4 3.5 %all-to-all-start.2 = ((bf16[8,64,512]{2,1,0:T(8,128)(2,1)}), bf16[8,64,512]{2,1,0:T(8,128)(2,1)S(1)}, u32[]{:S(2)}, u32[]{:S(2)}) async-start(bf16[8,64,512]{2,1,0:T(8,128)(2,1)} %bitcast.8), calls=%async_computation.2 | async-start | bytes 1048576 | tf_op jit(solution)/shard_map/all_to_all | solution.py:443
  76.5 1.5 %collective-permute-done.7.recv_ref = bf16[16,8,8,128]{3,2,1,0:T(8,128)(2,1)S(1)} collective-permute-done((bf16[16,8,8,128]{3,2,1,0:T(8,128)(2,1)S(1)}, bf16[16,8,8,128]{3,2,1,0:T(8,128)(2,1)S(1)}, u32[]{:S(2)}, u32[]{:S(2)}) %collective-permute-start.7) | collective-permute-done | bytes 262176 | tf_op jit(solution)/shard_map/ppermute | solution.py:463
  78.1 1.5 %collective-permute-start.10 = (bf16[4,8,8,128]{3,2,1,0:T(8,128)(2,1)S(1)}, bf16[4,8,8,128]{3,2,1,0:T(8,128)(2,1)S(1)}, u32[]{:S(2)}, u32[]{:S(2)}) collective-permute-start(bf16[4,8,8,128]{3,2,1,0:T(8,128)(2,1)S(1)} %get-tuple-element.103), channel_id=1, source_target_pairs={{0,80},{8,88},{16,64},{24,72},{32,112},{40,120},{48,96},{56,104},{... | collective-permute-start | bytes 196616 | tf_op jit(solution)/shard_map/ppermute | solution.py:479
  79.7 1.1 collective-permute-start.8
  80.7 1.0 collective-permute-start.9
  81.7 1.8 %collective-permute-done.10.refs_2_ = bf16[4,8,8,128]{3,2,1,0:T(8,128)(2,1)S(1)} collective-permute-done((bf16[4,8,8,128]{3,2,1,0:T(8,128)(2,1)S(1)}, bf16[4,8,8,128]{3,2,1,0:T(8,128)(2,1)S(1)}, u32[]{:S(2)}, u32[]{:S(2)}) %collective-permute-start.10) | collective-permute-done | bytes 65568 | tf_op jit(solution)/shard_map/ppermute | solution.py:479
  83.5 1.1 collective-permute-done.8.refs_0_
  85.0 1.3 collective-permute-start.11
  86.3 0.9 side_grads.1
  87.2 3.7 %collective-permute-done.11.recv_ref = bf16[4,8,8,128]{3,2,1,0:T(8,128)(2,1)S(1)} collective-permute-done((bf16[4,8,8,128]{3,2,1,0:T(8,128)(2,1)S(1)}, bf16[4,8,8,128]{3,2,1,0:T(8,128)(2,1)S(1)}, u32[]{:S(2)}, u32[]{:S(2)}) %collective-permute-start.11) | collective-permute-done | bytes 65568 | tf_op jit(solution)/shard_map/ppermute | solution.py:492
  90.9 1.6 %all-to-all-done.2.scaled_ref = bf16[8,64,512]{2,1,0:T(8,128)(2,1)S(1)} async-done(((bf16[8,64,512]{2,1,0:T(8,128)(2,1)}), bf16[8,64,512]{2,1,0:T(8,128)(2,1)S(1)}, u32[]{:S(2)}, u32[]{:S(2)}) %all-to-all-start.2) | async-done | bytes 524320 | tf_op jit(solution)/shard_map/all_to_all | solution.py:443
  92.5 6.5 %table_grad.1 = (f32[32,64,128]{2,1,0:T(8,128)}, bf16[128,64,128]{2,1,0:T(8,128)(2,1)}) custom-call(s32[8,32]{1,0:T(8,128)S(1)} %bitcast.26, s32[32]{0:T(128)S(1)} %copy-done.7, bf16[32,8,128,128]{3,2,1,0:T(8,128)(2,1)} %vals_ref.3, bf16[8,64,512]{2,1,0:T(8,128)(2,1)S(1)} %all-to-all-done.2.scaled_ref), custom_call_target="tpu_custom_call" | custom-call | flops 536870912 | bytes 12582912 | tf_op jit(solution)/shard_map/table_grad/pallas_call | solution.py:496
  99.0 7.5 %all-to-all-start.3 = ((bf16[32,4,64,128]{3,2,1,0:T(8,128)(2,1)}), bf16[32,4,64,128]{3,2,1,0:T(8,128)(2,1)S(1)}, u32[]{:S(2)}, u32[]{:S(2)}) async-start(bf16[32,4,64,128]{3,2,1,0:T(8,128)(2,1)} %bitcast.29), calls=%async_computation.3 | async-start | bytes 4194304 | tf_op jit(solution)/shard_map/all_to_all | solution.py:517
  106.5 3.4 %collective-permute-start.12 = (bf16[64,640]{1,0:T(8,128)(2,1)S(1)}, bf16[64,640]{1,0:T(8,128)(2,1)S(1)}, u32[]{:S(2)}, u32[]{:S(2)}) collective-permute-start(bf16[64,640]{1,0:T(8,128)(2,1)S(1)} %get-tuple-element.127), channel_id=1, source_target_pairs={{0,4},{1,5},{2,6},{3,7},{4,0},{5,1},{6,2},{7,3},{8,12},{9,13},{10,... | collective-permute-start | bytes 245768 | tf_op jit(solution)/shard_map/ppermute | solution.py:332
  110.5 4.5 %collective-permute-start.14 = (bf16[64,640]{1,0:T(8,128)(2,1)S(1)}, bf16[64,640]{1,0:T(8,128)(2,1)S(1)}, u32[]{:S(2)}, u32[]{:S(2)}) collective-permute-start(bf16[64,640]{1,0:T(8,128)(2,1)S(1)} %get-tuple-element.129), channel_id=1, source_target_pairs={{0,5},{1,6},{2,7},{3,0},{4,1},{5,2},{6,3},{7,4},{8,13},{9,14},{10,... | collective-permute-start | bytes 245768 | tf_op jit(solution)/shard_map/ppermute | solution.py:332
  115.6 3.6 %collective-permute-start.16 = (bf16[64,640]{1,0:T(8,128)(2,1)S(1)}, bf16[64,640]{1,0:T(8,128)(2,1)S(1)}, u32[]{:S(2)}, u32[]{:S(2)}) collective-permute-start(bf16[64,640]{1,0:T(8,128)(2,1)S(1)} %get-tuple-element.131), channel_id=1, source_target_pairs={{0,6},{1,7},{2,0},{3,1},{4,2},{5,3},{6,4},{7,5},{8,14},{9,15},{10,... | collective-permute-start | bytes 245768 | tf_op jit(solution)/shard_map/ppermute | solution.py:332
  119.7 3.2 %collective-permute-done.13.refs_1_ = bf16[64,640]{1,0:T(8,128)(2,1)S(1)} collective-permute-done((bf16[64,640]{1,0:T(8,128)(2,1)S(1)}, bf16[64,640]{1,0:T(8,128)(2,1)S(1)}, u32[]{:S(2)}, u32[]{:S(2)}) %collective-permute-start.13) | collective-permute-done | bytes 81952 | tf_op jit(solution)/shard_map/ppermute | solution.py:332
  123.3 1.3 collective-permute-done.16.refs_4_
  124.7 0.9 collective-permute-done.17.refs_5_
  125.6 1.8 %collective-permute-done.18.refs_6_ = bf16[64,640]{1,0:T(8,128)(2,1)S(1)} collective-permute-done((bf16[64,640]{1,0:T(8,128)(2,1)S(1)}, bf16[64,640]{1,0:T(8,128)(2,1)S(1)}, u32[]{:S(2)}, u32[]{:S(2)}) %collective-permute-start.18) | collective-permute-done | bytes 81952 | tf_op jit(solution)/shard_map/ppermute | solution.py:332
  127.4 1.2 collective-permute-done.19
  128.6 3.0 %collective-permute-start.20 = (bf16[2,32,128]{2,1,0:T(8,128)(2,1)S(1)}, bf16[2,32,128]{2,1,0:T(8,128)(2,1)S(1)}, u32[]{:S(2)}, u32[]{:S(2)}) collective-permute-start(bf16[2,32,128]{2,1,0:T(8,128)(2,1)S(1)} %pad_maximum_fusion.2), channel_id=1, source_target_pairs={{0,128},{8,136},{16,144},{24,152},{32,160},{40,168},{48,176},{56,1... | collective-permute-start | bytes 49160 | tf_op jit(solution)/shard_map/ppermute | solution.py:554
  131.6 1.2 copy-done.1
  132.9 0.7 collective-permute-start.21
  133.6 0.7 collective-permute-start.22
  134.4 2.3 %collective-permute-done.21 = bf16[2,32,128]{2,1,0:T(8,128)(2,1)S(1)} collective-permute-done((bf16[2,32,128]{2,1,0:T(8,128)(2,1)S(1)}, bf16[2,32,128]{2,1,0:T(8,128)(2,1)S(1)}, u32[]{:S(2)}, u32[]{:S(2)}) %collective-permute-start.21) | collective-permute-done | bytes 16416 | tf_op jit(solution)/shard_map/ppermute | solution.py:554
  136.7 1.8 %collective-permute-done.22 = bf16[2,32,128]{2,1,0:T(8,128)(2,1)S(1)} collective-permute-done((bf16[2,32,128]{2,1,0:T(8,128)(2,1)S(1)}, bf16[2,32,128]{2,1,0:T(8,128)(2,1)S(1)}, u32[]{:S(2)}, u32[]{:S(2)}) %collective-permute-start.22) | collective-permute-done | bytes 16416 | tf_op jit(solution)/shard_map/ppermute | solution.py:554
  138.6 0.6 collective-permute-start.23
  139.2 2.2 %sum_returned.1 = bf16[64,4096]{1,0:T(8,128)(2,1)} custom-call(s32[4,32]{1,0:T(4,128)S(1)} %bitcast.28, f32[32,64,128]{2,1,0:T(8,128)S(1)} %sum_near.1.near_ref, bf16[32,4,64,128]{3,2,1,0:T(8,128)(2,1)S(1)} %all-to-all-done.3.back_ref), custom_call_target="tpu_custom_call" | custom-call | bytes 4194304 | tf_op jit(solution)/shard_map/sum_returned/pallas_call | solution.py:560
  141.4 1.2 collective-permute-done.23
  142.6 0.7 weight_spread.1
  (60 shorter events, 5.1 us)
Async XLA Ops:
  3.2 7.8 %copy-start = (bf16[4096,64]{0,1:T(8,128)(2,1)S(1)}, bf16[4096,64]{0,1:T(8,128)(2,1)}, u32[]{:S(2)}) copy-start(bf16[4096,64]{0,1:T(8,128)(2,1)} %param.9) | copy-start | bytes 1572868
  3.2 35.7 %copy-start.5 = (s32[32,8]{0,1:T(8,128)S(1)}, s32[32,8]{0,1:T(8,128)}, u32[]{:S(2)}) copy-start(s32[32,8]{0,1:T(8,128)} %param.11) | copy-start | bytes 3076
  3.2 35.7 %copy-start.7 = (s32[32]{0:T(128)S(1)}, s32[32]{0:T(128)}, u32[]{:S(2)}) copy-start(s32[32]{0:T(128)} %counts_ref.3) | copy-start | bytes 388
  3.2 35.6 %all-to-all-start = ((bf16[32,4,64,128]{3,2,1,0:T(8,128)(2,1)}), bf16[32,4,64,128]{3,2,1,0:T(8,128)(2,1)S(1)}, u32[]{:S(2)}, u32[]{:S(2)}) async-start(bf16[32,4,64,128]{3,2,1,0:T(8,128)(2,1)} %pack_outgoing.1), calls=%async_computation | async-start | bytes 4194304 | tf_op jit(solution)/shard_map/all_to_all | solution.py:393
  11.9 14.8 %collective-permute-start = (bf16[64,512]{1,0:T(8,128)(2,1)}, bf16[64,512]{1,0:T(8,128)(2,1)S(1)}, u32[]{:S(2)}, u32[]{:S(2)}) collective-permute-start(bf16[64,512]{1,0:T(8,128)(2,1)} %get-tuple-element.74), channel_id=1, source_target_pairs={{0,1},{1,2},{2,3},{3,4},{4,5},{5,6},{6,7},{7,0},{8,9},{9,10},{10,1... | collective-permute-start | bytes 196616 | tf_op jit(solution)/shard_map/ppermute | solution.py:332
  13.9 15.5 %collective-permute-start.1 = (bf16[64,512]{1,0:T(8,128)(2,1)}, bf16[64,512]{1,0:T(8,128)(2,1)S(1)}, u32[]{:S(2)}, u32[]{:S(2)}) collective-permute-start(bf16[64,512]{1,0:T(8,128)(2,1)} %get-tuple-element.75), channel_id=1, source_target_pairs={{0,2},{1,3},{2,4},{3,5},{4,6},{5,7},{6,0},{7,1},{8,10},{9,11},{10,... | collective-permute-start | bytes 196616 | tf_op jit(solution)/shard_map/ppermute | solution.py:332
  17.1 13.2 %collective-permute-start.2 = (bf16[64,512]{1,0:T(8,128)(2,1)}, bf16[64,512]{1,0:T(8,128)(2,1)S(1)}, u32[]{:S(2)}, u32[]{:S(2)}) collective-permute-start(bf16[64,512]{1,0:T(8,128)(2,1)} %get-tuple-element.76), channel_id=1, source_target_pairs={{0,3},{1,4},{2,5},{3,6},{4,7},{5,0},{6,1},{7,2},{8,11},{9,12},{10,... | collective-permute-start | bytes 196616 | tf_op jit(solution)/shard_map/ppermute | solution.py:332
  21.2 9.2 %collective-permute-start.3 = (bf16[64,512]{1,0:T(8,128)(2,1)}, bf16[64,512]{1,0:T(8,128)(2,1)S(1)}, u32[]{:S(2)}, u32[]{:S(2)}) collective-permute-start(bf16[64,512]{1,0:T(8,128)(2,1)} %get-tuple-element.77), channel_id=1, source_target_pairs={{0,4},{1,5},{2,6},{3,7},{4,0},{5,1},{6,2},{7,3},{8,12},{9,13},{10,... | collective-permute-start | bytes 196616 | tf_op jit(solution)/shard_map/ppermute | solution.py:332
  21.7 14.4 %collective-permute-start.4 = (bf16[64,512]{1,0:T(8,128)(2,1)}, bf16[64,512]{1,0:T(8,128)(2,1)S(1)}, u32[]{:S(2)}, u32[]{:S(2)}) collective-permute-start(bf16[64,512]{1,0:T(8,128)(2,1)} %get-tuple-element.78), channel_id=1, source_target_pairs={{0,5},{1,6},{2,7},{3,0},{4,1},{5,2},{6,3},{7,4},{8,13},{9,14},{10,... | collective-permute-start | bytes 196616 | tf_op jit(solution)/shard_map/ppermute | solution.py:332
  26.7 9.4 %copy-start.8 = (bf16[64,512]{1,0:T(8,128)(2,1)}, bf16[64,512]{1,0:T(8,128)(2,1)S(1)}, u32[]{:S(2)}) copy-start(bf16[64,512]{1,0:T(8,128)(2,1)S(1)} %collective-permute-done.refs_1_) | copy-start | bytes 196612
  26.7 9.4 %collective-permute-start.5 = (bf16[64,512]{1,0:T(8,128)(2,1)}, bf16[64,512]{1,0:T(8,128)(2,1)S(1)}, u32[]{:S(2)}, u32[]{:S(2)}) collective-permute-start(bf16[64,512]{1,0:T(8,128)(2,1)} %get-tuple-element.79), channel_id=1, source_target_pairs={{0,6},{1,7},{2,0},{3,1},{4,2},{5,3},{6,4},{7,5},{8,14},{9,15},{10,... | collective-permute-start | bytes 196616 | tf_op jit(solution)/shard_map/ppermute | solution.py:332
  29.3 6.8 %copy-start.9 = (bf16[64,512]{1,0:T(8,128)(2,1)}, bf16[64,512]{1,0:T(8,128)(2,1)S(1)}, u32[]{:S(2)}) copy-start(bf16[64,512]{1,0:T(8,128)(2,1)S(1)} %collective-permute-done.1.refs_2_) | copy-start | bytes 196612
  29.3 8.0 %collective-permute-start.6 = (bf16[64,512]{1,0:T(8,128)(2,1)}, bf16[64,512]{1,0:T(8,128)(2,1)}, u32[]{:S(2)}, u32[]{:S(2)}) collective-permute-start(bf16[64,512]{1,0:T(8,128)(2,1)} %get-tuple-element.80), channel_id=1, source_target_pairs={{0,7},{1,0},{2,1},{3,2},{4,3},{5,4},{6,5},{7,6},{8,15},{9,8},{10,9... | collective-permute-start | bytes 196616 | tf_op jit(solution)/shard_map/ppermute | solution.py:332
  30.3 5.8 %copy-start.10 = (bf16[64,512]{1,0:T(8,128)(2,1)}, bf16[64,512]{1,0:T(8,128)(2,1)S(1)}, u32[]{:S(2)}) copy-start(bf16[64,512]{1,0:T(8,128)(2,1)S(1)} %collective-permute-done.2.refs_3_) | copy-start | bytes 196612
  30.4 5.8 %copy-start.11 = (bf16[64,512]{1,0:T(8,128)(2,1)}, bf16[64,512]{1,0:T(8,128)(2,1)S(1)}, u32[]{:S(2)}) copy-start(bf16[64,512]{1,0:T(8,128)(2,1)S(1)} %collective-permute-done.3.refs_4_) | copy-start | bytes 196612
  36.1 0.6 copy-start.12
  36.7 0.6 copy-start.13
  38.9 14.6 %copy-start.14 = (f32[256]{0:T(256)S(1)}, f32[256]{0:T(256)}, u32[]{:S(2)}) copy-start(f32[256]{0:T(256)} %param.16) | copy-start | bytes 3076
  38.9 14.7 %copy-start.2 = (bf16[512,256]{1,0:T(8,128)(2,1)S(1)}, bf16[512,256]{1,0:T(8,128)(2,1)}, u32[]{:S(2)}) copy-start(bf16[512,256]{1,0:T(8,128)(2,1)} %weight_ref.4) | copy-start | bytes 786436
  38.9 14.8 %copy-start.3 = (bf16[512,256]{1,0:T(8,128)(2,1)S(1)}, bf16[512,256]{1,0:T(8,128)(2,1)}, u32[]{:S(2)}) copy-start(bf16[512,256]{1,0:T(8,128)(2,1)} %weight_ref.5) | copy-start | bytes 786436
  38.9 14.7 %copy-start.4 = (bf16[512,256]{1,0:T(8,128)(2,1)S(1)}, bf16[512,256]{1,0:T(8,128)(2,1)}, u32[]{:S(2)}) copy-start(bf16[512,256]{1,0:T(8,128)(2,1)} %cot_ref.1) | copy-start | bytes 786436
  45.0 25.6 %all-to-all-start.1 = ((bf16[8,64,512]{2,1,0:T(8,128)(2,1)}), bf16[8,64,512]{2,1,0:T(8,128)(2,1)S(1)}, u32[]{:S(2)}, u32[]{:S(2)}) async-start(bf16[8,64,512]{2,1,0:T(8,128)(2,1)} %get-tuple-element.94), calls=%async_computation.1 | async-start | bytes 1048576 | tf_op jit(solution)/shard_map/all_to_all | solution.py:432
  72.4 20.1 %all-to-all-start.2 = ((bf16[8,64,512]{2,1,0:T(8,128)(2,1)}), bf16[8,64,512]{2,1,0:T(8,128)(2,1)S(1)}, u32[]{:S(2)}, u32[]{:S(2)}) async-start(bf16[8,64,512]{2,1,0:T(8,128)(2,1)} %bitcast.8), calls=%async_computation.2 | async-start | bytes 1048576 | tf_op jit(solution)/shard_map/all_to_all | solution.py:443
  76.4 1.6 %collective-permute-start.7 = (bf16[16,8,8,128]{3,2,1,0:T(8,128)(2,1)S(1)}, bf16[16,8,8,128]{3,2,1,0:T(8,128)(2,1)S(1)}, u32[]{:S(2)}, u32[]{:S(2)}) collective-permute-start(bf16[16,8,8,128]{3,2,1,0:T(8,128)(2,1)S(1)} %get-tuple-element.99), channel_id=1, source_target_pairs={{0,8},{8,0},{16,24},{24,16},{32,40},{40,32},{48,56},{56,48},{64,72... | collective-permute-start | bytes 786440 | tf_op jit(solution)/shard_map/ppermute | solution.py:463
  78.1 5.4 %collective-permute-start.10 = (bf16[4,8,8,128]{3,2,1,0:T(8,128)(2,1)S(1)}, bf16[4,8,8,128]{3,2,1,0:T(8,128)(2,1)S(1)}, u32[]{:S(2)}, u32[]{:S(2)}) collective-permute-start(bf16[4,8,8,128]{3,2,1,0:T(8,128)(2,1)S(1)} %get-tuple-element.103), channel_id=1, source_target_pairs={{0,80},{8,88},{16,64},{24,72},{32,112},{40,120},{48,96},{56,104},{... | collective-permute-start | bytes 196616 | tf_op jit(solution)/shard_map/ppermute | solution.py:479
  79.7 5.0 %collective-permute-start.8 = (bf16[4,8,8,128]{3,2,1,0:T(8,128)(2,1)S(1)}, bf16[4,8,8,128]{3,2,1,0:T(8,128)(2,1)S(1)}, u32[]{:S(2)}, u32[]{:S(2)}) collective-permute-start(bf16[4,8,8,128]{3,2,1,0:T(8,128)(2,1)S(1)} %get-tuple-element.101), channel_id=1, source_target_pairs={{0,64},{8,72},{16,80},{24,88},{32,96},{40,104},{48,112},{56,120},{... | collective-permute-start | bytes 196616 | tf_op jit(solution)/shard_map/ppermute | solution.py:479
  80.7 4.3 %collective-permute-start.9 = (bf16[4,8,8,128]{3,2,1,0:T(8,128)(2,1)S(1)}, bf16[4,8,8,128]{3,2,1,0:T(8,128)(2,1)S(1)}, u32[]{:S(2)}, u32[]{:S(2)}) collective-permute-start(bf16[4,8,8,128]{3,2,1,0:T(8,128)(2,1)S(1)} %get-tuple-element.102), channel_id=1, source_target_pairs={{0,16},{8,24},{16,0},{24,8},{32,48},{40,56},{48,32},{56,40},{64,80... | collective-permute-start | bytes 196616 | tf_op jit(solution)/shard_map/ppermute | solution.py:479
  85.0 5.9 %collective-permute-start.11 = (bf16[4,8,8,128]{3,2,1,0:T(8,128)(2,1)S(1)}, bf16[4,8,8,128]{3,2,1,0:T(8,128)(2,1)S(1)}, u32[]{:S(2)}, u32[]{:S(2)}) collective-permute-start(bf16[4,8,8,128]{3,2,1,0:T(8,128)(2,1)S(1)} %weight_add.2.held_ref), channel_id=1, source_target_pairs={{0,32},{8,40},{16,48},{24,56},{32,0},{40,8},{48,16},{56,24},{64,96... | collective-permute-start | bytes 196616 | tf_op jit(solution)/shard_map/ppermute | solution.py:492
  99.0 39.6 %all-to-all-start.3 = ((bf16[32,4,64,128]{3,2,1,0:T(8,128)(2,1)}), bf16[32,4,64,128]{3,2,1,0:T(8,128)(2,1)S(1)}, u32[]{:S(2)}, u32[]{:S(2)}) async-start(bf16[32,4,64,128]{3,2,1,0:T(8,128)(2,1)} %bitcast.29), calls=%async_computation.3 | async-start | bytes 4194304 | tf_op jit(solution)/shard_map/all_to_all | solution.py:517
  106.5 32.8 %copy-start.6 = (s32[1,32,4]{1,2,0:T(4,128)S(1)}, s32[1,32,4]{1,2,0:T(4,128)}, u32[]{:S(2)}) copy-start(s32[1,32,4]{1,2,0:T(4,128)} %param.13) | copy-start | bytes 1540
  106.5 13.1 %collective-permute-start.12 = (bf16[64,640]{1,0:T(8,128)(2,1)S(1)}, bf16[64,640]{1,0:T(8,128)(2,1)S(1)}, u32[]{:S(2)}, u32[]{:S(2)}) collective-permute-start(bf16[64,640]{1,0:T(8,128)(2,1)S(1)} %get-tuple-element.127), channel_id=1, source_target_pairs={{0,4},{1,5},{2,6},{3,7},{4,0},{5,1},{6,2},{7,3},{8,12},{9,13},{10,... | collective-permute-start | bytes 245768 | tf_op jit(solution)/shard_map/ppermute | solution.py:332
  110.0 12.9 %collective-permute-start.13 = (bf16[64,640]{1,0:T(8,128)(2,1)S(1)}, bf16[64,640]{1,0:T(8,128)(2,1)S(1)}, u32[]{:S(2)}, u32[]{:S(2)}) collective-permute-start(bf16[64,640]{1,0:T(8,128)(2,1)S(1)} %get-tuple-element.128), channel_id=1, source_target_pairs={{0,3},{1,4},{2,5},{3,6},{4,7},{5,0},{6,1},{7,2},{8,11},{9,12},{10,... | collective-permute-start | bytes 245768 | tf_op jit(solution)/shard_map/ppermute | solution.py:332
  110.5 12.3 %collective-permute-start.14 = (bf16[64,640]{1,0:T(8,128)(2,1)S(1)}, bf16[64,640]{1,0:T(8,128)(2,1)S(1)}, u32[]{:S(2)}, u32[]{:S(2)}) collective-permute-start(bf16[64,640]{1,0:T(8,128)(2,1)S(1)} %get-tuple-element.129), channel_id=1, source_target_pairs={{0,5},{1,6},{2,7},{3,0},{4,1},{5,2},{6,3},{7,4},{8,13},{9,14},{10,... | collective-permute-start | bytes 245768 | tf_op jit(solution)/shard_map/ppermute | solution.py:332
  115.0 8.3 %collective-permute-start.15 = (bf16[64,640]{1,0:T(8,128)(2,1)S(1)}, bf16[64,640]{1,0:T(8,128)(2,1)S(1)}, u32[]{:S(2)}, u32[]{:S(2)}) collective-permute-start(bf16[64,640]{1,0:T(8,128)(2,1)S(1)} %get-tuple-element.130), channel_id=1, source_target_pairs={{0,2},{1,3},{2,4},{3,5},{4,6},{5,7},{6,0},{7,1},{8,10},{9,11},{10,... | collective-permute-start | bytes 245768 | tf_op jit(solution)/shard_map/ppermute | solution.py:332
  115.6 9.1 %collective-permute-start.16 = (bf16[64,640]{1,0:T(8,128)(2,1)S(1)}, bf16[64,640]{1,0:T(8,128)(2,1)S(1)}, u32[]{:S(2)}, u32[]{:S(2)}) collective-permute-start(bf16[64,640]{1,0:T(8,128)(2,1)S(1)} %get-tuple-element.131), channel_id=1, source_target_pairs={{0,6},{1,7},{2,0},{3,1},{4,2},{5,3},{6,4},{7,5},{8,14},{9,15},{10,... | collective-permute-start | bytes 245768 | tf_op jit(solution)/shard_map/ppermute | solution.py:332
  119.7 5.9 %collective-permute-start.17 = (bf16[64,640]{1,0:T(8,128)(2,1)S(1)}, bf16[64,640]{1,0:T(8,128)(2,1)S(1)}, u32[]{:S(2)}, u32[]{:S(2)}) collective-permute-start(bf16[64,640]{1,0:T(8,128)(2,1)S(1)} %get-tuple-element.132), channel_id=1, source_target_pairs={{0,1},{1,2},{2,3},{3,4},{4,5},{5,6},{6,7},{7,0},{8,9},{9,10},{10,1... | collective-permute-start | bytes 245768 | tf_op jit(solution)/shard_map/ppermute | solution.py:332
  122.9 4.4 %collective-permute-start.18 = (bf16[64,640]{1,0:T(8,128)(2,1)S(1)}, bf16[64,640]{1,0:T(8,128)(2,1)S(1)}, u32[]{:S(2)}, u32[]{:S(2)}) collective-permute-start(bf16[64,640]{1,0:T(8,128)(2,1)S(1)} %get-tuple-element.133), channel_id=1, source_target_pairs={{0,7},{1,0},{2,1},{3,2},{4,3},{5,4},{6,5},{7,6},{8,15},{9,8},{10,9... | collective-permute-start | bytes 245768 | tf_op jit(solution)/shard_map/ppermute | solution.py:332
  127.3 1.3 collective-permute-start.19
  128.6 5.8 %collective-permute-start.20 = (bf16[2,32,128]{2,1,0:T(8,128)(2,1)S(1)}, bf16[2,32,128]{2,1,0:T(8,128)(2,1)S(1)}, u32[]{:S(2)}, u32[]{:S(2)}) collective-permute-start(bf16[2,32,128]{2,1,0:T(8,128)(2,1)S(1)} %pad_maximum_fusion.2), channel_id=1, source_target_pairs={{0,128},{8,136},{16,144},{24,152},{32,160},{40,168},{48,176},{56,1... | collective-permute-start | bytes 49160 | tf_op jit(solution)/shard_map/ppermute | solution.py:554
  131.6 1.2 copy-start.1
  132.9 3.8 %collective-permute-start.21 = (bf16[2,32,128]{2,1,0:T(8,128)(2,1)S(1)}, bf16[2,32,128]{2,1,0:T(8,128)(2,1)S(1)}, u32[]{:S(2)}, u32[]{:S(2)}) collective-permute-start(bf16[2,32,128]{2,1,0:T(8,128)(2,1)S(1)} %pad_maximum_fusion.2), channel_id=1, source_target_pairs={{0,64},{8,72},{16,80},{24,88},{32,96},{40,104},{48,112},{56,120},{... | collective-permute-start | bytes 49160 | tf_op jit(solution)/shard_map/ppermute | solution.py:554
  133.6 4.9 %collective-permute-start.22 = (bf16[2,32,128]{2,1,0:T(8,128)(2,1)S(1)}, bf16[2,32,128]{2,1,0:T(8,128)(2,1)S(1)}, u32[]{:S(2)}, u32[]{:S(2)}) collective-permute-start(bf16[2,32,128]{2,1,0:T(8,128)(2,1)S(1)} %pad_maximum_fusion.2), channel_id=1, source_target_pairs={{0,192},{8,200},{16,208},{24,216},{32,224},{40,232},{48,240},{56,2... | collective-permute-start | bytes 49160 | tf_op jit(solution)/shard_map/ppermute | solution.py:554
  138.6 4.0 %collective-permute-start.23 = (bf16[4,32,128]{2,1,0:T(8,128)(2,1)S(1)}, bf16[4,32,128]{2,1,0:T(8,128)(2,1)S(1)}, u32[]{:S(2)}, u32[]{:S(2)}) collective-permute-start(bf16[4,32,128]{2,1,0:T(8,128)(2,1)S(1)} %pad_maximum_fusion.1), channel_id=1, source_target_pairs={{0,16},{8,24},{16,0},{24,8},{32,48},{40,56},{48,32},{56,40},{64,80... | collective-permute-start | bytes 98312 | tf_op jit(solution)/shard_map/ppermute | solution.py:570

commit v9 on v8

--- a/solution.py
+++ b/solution.py
@@ -111,41 +111,46 @@
     lax.fori_loop(0, tails, one, 0)
 
 
-def gather_kernel(
-    cols_ref, counts_ref, feats_ref, recv_ref, vals_ref, out_ref, degree_ref, held_ref, mean_ref, sems, out_sems
-):
-    _, depth, size, _ = vals_ref.shape
+def gather_kernel(shifts, chans, me_ref, cols_ref, counts_ref, feats_ref, recv_ref, vals_ref, *refs):
+    out_refs = refs[: len(shifts)]
+    degree_ref, held_ref, mean_ref, sems, out_sems = refs[len(shifts) :]
+    _, rows, depth, size, _ = held_ref.shape
     width = feats_ref.shape[0]
-    rows = out_ref.shape[2] // size
     own = feats_ref.shape[1] // size
     ones = jnp.ones((16, size), BF)
-
-    def body(index):
-        count = counts_ref[index]
-        picked = []
-        for k in range(depth):
-            col = cols_ref[k, index]
-            lane = pl.multiple_of(jnp.minimum(col, own - 1) * size, size)
-            near = feats_ref[:, pl.ds(lane, size)]
-            far = recv_ref[jnp.maximum(col - own, 0)]
-            block = jnp.concatenate([jnp.where(col < own, near, far), ones], axis=0)
-            picked.append(jnp.where(k < count, block, jnp.zeros_like(block)))
-        total = nt_dot(join_slots(held_ref, index), jnp.concatenate(picked, axis=1)).T
-        group = index // rows
-        place = pl.ds(pl.multiple_of(lax.rem(index, rows) * size, size), size)
-        degree_ref[group, :, place] = total[width : width + 8]
-        mean_ref[group, :, place] = (total[:width] / total[width : width + 1]).astype(BF)
-
-    def copy(start, span, place):
-        groups = pl.ds(start // rows, span // rows)
-        return pltpu.make_async_copy(mean_ref.at[groups], out_ref.at[groups], out_sems.at[place])
-
-    stream_rows(vals_ref, held_ref, sems, body, after=lambda *which: copy(*which).start())
-    small = held_ref.shape[0] // 8
-    copy(0, small, 0).wait()
-    copy(small, small, 1).wait()
-    for place in range(2, out_sems.shape[0]):
-        copy((place - 1) * 2 * small, 2 * small, place).wait()
+    groups = [lax.rem(me_ref[0] + shift, chans) for shift in shifts]
+
+    def load(place):
+        return pltpu.make_async_copy(
+            vals_ref.at[pl.ds(groups[place] * rows, rows)], held_ref.at[place], sems.at[place]
+        )
+
+    def store(place):
+        return pltpu.make_async_copy(mean_ref.at[place], out_refs[place], out_sems.at[place])
+
+    for place in range(len(shifts)):
+        load(place).start()
+    for place in range(len(shifts)):
+        load(place).wait()
+        for row in range(rows):
+            index = groups[place] * rows + row
+            count = counts_ref[index]
+            picked = []
+            for k in range(depth):
+                col = cols_ref[k, index]
+                lane = pl.multiple_of(jnp.minimum(col, own - 1) * size, size)
+                near = feats_ref[:, pl.ds(lane, size)]
+                far = recv_ref[jnp.maximum(col - own, 0)]
+                block = jnp.concatenate([jnp.where(col < own, near, far), ones], axis=0)
+                picked.append(jnp.where(k < count, block, jnp.zeros_like(block)))
+            total = nt_dot(join_slots(held_ref.at[place], row), jnp.concatenate(picked, axis=1)).T
+            lanes = slice(row * size, (row + 1) * size)
+            mean_ref[place, :, lanes] = (total[:width] / total[width : width + 1]).astype(BF)
+            if place == len(shifts) - 1:
+                degree_ref[:, lanes] = total[width : width + 8]
+        store(place).start()
+    for place in range(len(shifts)):
+        store(place).wait()
 
 
 def self_kernel(chans, me_ref, weight_ref, bias_ref, neigh_ref, cot_ref, *refs):
@@ -160,7 +165,14 @@
     pre_ref[...] = nn_dot(weight_ref[...].T, full_ref[...]) + bias_ref[...]
 
 
-def head_kernel(me_ref, degree_ref, pre_ref, turned_ref, weight_ref, cot_ref, mean_ref, out_ref, grad_ref, scaled_ref):
+def head_kernel(shifts, me_ref, degree_ref, pre_ref, turned_ref, weight_ref, cot_ref, *refs):
+    chans = len(shifts)
+    chunk_refs = refs[:chans]
+    mean_ref, out_ref, grad_ref, scaled_ref = refs[chans:]
+    height = chunk_refs[0].shape[0]
+    for shift, chunk_ref in zip(shifts, chunk_refs):
+        start = pl.multiple_of(lax.rem(me_ref[0] + (chans - shift), chans) * height, height)
+        mean_ref[pl.ds(start, height), :] = chunk_ref[...]
     preact = pre_ref[...] + nn_dot(turned_ref[...], mean_ref[...])
     logistic = jax.nn.sigmoid(preact)
     activated = preact * logistic
@@ -173,7 +185,7 @@
     out_ref[...] = unit.astype(BF)
     grad_ref[...] = grad
     mean_grad = nn_dot(weight_ref[...], grad).astype(BF).astype(F32)
-    degree = degree_ref[me_ref[0], 0:1, :]
+    degree = degree_ref[0:1, :]
     scaled_ref[...] = (mean_grad / degree).astype(BF)
 
 
@@ -325,11 +337,12 @@
         out_ref[:, block * size : (block + 1) * size] = hold_ref[block].astype(BF)
 
 
-def exchange(chunks):
+def exchange(chunks, shifts=None):
     count = len(chunks)
     received = list(chunks)
-    for shift in range(1, count):
-        received[shift] = lax.ppermute(chunks[shift], "chan", [(i, (i + shift) % count) for i in range(count)])
+    for shift in shifts or range(count):
+        if shift:
+            received[shift] = lax.ppermute(chunks[shift], "chan", [(i, (i + shift) % count) for i in range(count)])
     return received
 
 
@@ -414,32 +427,38 @@
         name="self_part",
     )(me, w_self, bias.reshape(f_out, 1), w_neigh, cotangent, *feat_chunks)
 
-    mean, degree = pl.pallas_call(
-        gather_kernel,
-        out_shape=[pltpu.HBM((chans, chan_width, nodes), BF), sds((chans, 8, nodes), F32)],
-        in_specs=[smem(), smem()] + [vmem()] * 2 + [hbm()],
-        out_specs=[hbm(), vmem()],
-        scratch_shapes=[
-            pltpu.VMEM(block_vals.shape, BF),
-            pltpu.VMEM((chans, chan_width, nodes), BF),
-            pltpu.SemaphoreType.DMA((streams,)),
-            pltpu.SemaphoreType.DMA((streams,)),
-        ],
+    shifts = sorted(range(chans), key=lambda shift: -min(shift, chans - shift))
+    mean_chunks = [None] * chans
+    for part_shifts in (shifts[: chans // 2], shifts[chans // 2 :]):
+        count = len(part_shifts)
+        *chunks, degree = pl.pallas_call(
+            functools.partial(gather_kernel, part_shifts, chans),
+            out_shape=[pltpu.HBM((chan_width, nodes), BF)] * count + [sds((8, nodes), F32)],
+            in_specs=[smem()] * 3 + [vmem()] * 2 + [hbm()],
+            out_specs=[hbm()] * count + [vmem()],
+            scratch_shapes=[
+                pltpu.VMEM((count, rows, depth, size, size), BF),
+                pltpu.VMEM((count, chan_width, nodes), BF),
+                pltpu.SemaphoreType.DMA((count,)),
+                pltpu.SemaphoreType.DMA((count,)),
+            ],
+            compiler_params=params(16),
+            cost_estimate=cost(block_flops // 2, val_bytes // 2 + 3 * MIB),
+            name="neighbour_mean",
+        )(me, cols, block_counts, feats_t, incoming.reshape(parts * slots, chan_width, size), vals)
+        for shift, chunk in zip(part_shifts, chunks):
+            mean_chunks[shift] = chunk
+    mean_chunks = exchange(mean_chunks, shifts)
+
+    mean, out_t, grad_t, scaled = pl.pallas_call(
+        functools.partial(head_kernel, shifts),
+        out_shape=[sds((f_in, nodes), BF), sds((f_out, nodes), BF), sds((f_out, nodes), BF), sds((f_in, nodes), BF)],
+        in_specs=[smem()] + [vmem()] * (5 + chans),
+        out_specs=[vmem()] * 4,
         compiler_params=params(16),
-        cost_estimate=cost(block_flops, val_bytes + 3 * MIB),
-        name="neighbour_mean",
-    )(cols, block_counts, feats_t, incoming.reshape(parts * slots, chan_width, size), vals)
-    mean = lax.all_to_all(mean, "chan", split_axis=0, concat_axis=0, tiled=True).reshape(f_in, nodes)
-
-    out_t, grad_t, scaled = pl.pallas_call(
-        head_kernel,
-        out_shape=[sds((f_out, nodes), BF), sds((f_out, nodes), BF), sds((f_in, nodes), BF)],
-        in_specs=[smem()] + [vmem()] * 6,
-        out_specs=[vmem()] * 3,
-        compiler_params=params(BIG),
         cost_estimate=cost(2 * layer_flops, 4 * MIB),
         name="layer_head",
-    )(me, degree, pre_self, neigh_turned, w_neigh, cot_turned, mean)
+    )(me, degree, pre_self, neigh_turned, w_neigh, cot_turned, *[mean_chunks[shift] for shift in shifts])
     scaled = lax.all_to_all(
         scaled.reshape(chans, chan_width, nodes), "chan", split_axis=0, concat_axis=0, tiled=True
     )
@@ -548,6 +567,7 @@
         cost_estimate=cost(0, 3 * MIB),
         name="sum_near",
     )(me, own_grad, *packed)
+    held, near = lax.optimization_barrier((held, near))
     held = jnp.concatenate([held, lax.ppermute(held, "dom", flips[0])], axis=0)
     whole, half = 1 << order[-1], 1 << halves[-1]
     across, beside, both = (

time: 144 us -> 146 us (1.014)
  waiting for transfers between devices: 47.5 us -> 30.6 us
  starting transfers between devices: 68.3 us -> 81.6 us
  Pallas kernels: 23.9 us -> 28.6 us
    ppermute x14 -> x21, starting transfers between devices: 31.2 us -> 55.2 us  [exchange(): lax.ppermute(chunks[shift], 'chan', [(i, (i + shift) % count) for i in ra...]
    all_to_all x1 -> x0, waiting for transfers between devices: 15.5 us -> none  [per_device(): lax.all_to_all(mean, 'chan', split_axis=0, concat_axis=0, tiled=True)]
    all_to_all x1 -> x0, starting transfers between devices: 8.48 us -> none  [per_device(): lax.all_to_all(mean, 'chan', split_axis=0, concat_axis=0, tiled=True)]
    pallas_call x2 -> x3, Pallas kernels: 7.86 us -> 12.6 us  [the longest x2 9.9 us: per_device(): pl.pallas_call(functools.partial(gather_kernel, part_shifts, chans), out_...]
    all_to_all x1, starting transfers between devices: 7.46 us -> 5.15 us  [per_device(): lax.all_to_all(far_grad.reshape(parts, slots, chan_width, size), 'dom', s...]
    ppermute x14 -> x21, waiting for transfers between devices: 13.8 us -> 12 us  [exchange(): lax.ppermute(chunks[shift], 'chan', [(i, (i + shift) % count) for i in ra...]
    all_to_all x1, waiting for transfers between devices: 1.61 us -> 0.01 us  [per_device(): lax.all_to_all(scaled.reshape(chans, chan_width, nodes), 'chan', split_ax...]
    unnamed x30 -> x39, local copies, waits for them, and re-layouts: 2.5 us -> 3.44 us
  transfers between devices with their start and end apart: 28 -> 34, of which waited for: 20 -> 18; matrix products, arithmetic and copies ran while one was open for 0% -> 0% of each run, Pallas kernels for 4% -> 8%
where the time goes in v9:
time: 146 us; the launch traced here: 145 us
  starting transfers between devices  81.6 us (56%)
  waiting for transfers between devices  30.6 us (21%)
  Pallas kernels  28.6 us (20%)
  local copies, waits for them, and re-layouts  3.58 us (2%)
    ppermute x21, starting transfers between devices, exchange(): lax.ppermute(chunks[shift], 'chan', [(i, (i + shift) % count) for i in ra...  55.2 us
    ppermute x21, waiting for transfers between devices, exchange(): lax.ppermute(chunks[shift], 'chan', [(i, (i + shift) % count) for i in ra...  12 us
    pallas_call x2, Pallas kernels, per_device(): pl.pallas_call(functools.partial(gather_kernel, part_shifts, chans), out_...  9.9 us
    all_to_all x1, starting transfers between devices, per_device(): lax.all_to_all(outgoing, 'dom', split_axis=0, concat_axis=0, tiled=True)  7.76 us
    pallas_call x1, Pallas kernels, per_device(): pl.pallas_call(scatter_kernel, out_shape=[pltpu.HBM((block_rows, chan_wid...  6.45 us
    all_to_all x1, starting transfers between devices, per_device(): lax.all_to_all(far_grad.reshape(parts, slots, chan_width, size), 'dom', s...  5.15 us
    ppermute x1, waiting for transfers between devices, per_device(): got = lax.ppermute(total, 'dom', flips[level])  4.81 us
    all_to_all x1, starting transfers between devices, per_device(): lax.all_to_all(scaled.reshape(chans, chan_width, nodes), 'chan', split_ax...  4.51 us
  transfers between devices with their start and end apart: 34, of which 18 were waited for; matrix products, arithmetic and copies ran while one was open for 0% of the time, Pallas kernels for 8%

profile of v9, /device:TPU:2, one launch (start us, length us, event | category | flops | bytes accessed | tf_op | source)
XLA Modules:
  0.0 145.4 jit_solution(6805701810368732108)
XLA Ops:
  0.6 2.5 %pack_outgoing.1 = bf16[32,4,64,128]{3,2,1,0:T(8,128)(2,1)} custom-call(s32[4,32]{1,0:T(4,128)} %bitcast.26, bf16[64,4096]{1,0:T(8,128)(2,1)} %bitcast.17), custom_call_target="tpu_custom_call" | custom-call | bytes 5242880 | tf_op jit(solution)/shard_map/pack_outgoing/pallas_call | solution.py:393
  3.2 7.8 %all-to-all-start = ((bf16[32,4,64,128]{3,2,1,0:T(8,128)(2,1)}), bf16[32,4,64,128]{3,2,1,0:T(8,128)(2,1)S(1)}, u32[]{:S(2)}, u32[]{:S(2)}) async-start(bf16[32,4,64,128]{3,2,1,0:T(8,128)(2,1)} %pack_outgoing.1), calls=%async_computation | async-start | bytes 4194304 | tf_op jit(solution)/shard_map/all_to_all | solution.py:406
  11.0 0.9 split_feats.1
  11.9 2.0 %collective-permute-start = (bf16[64,512]{1,0:T(8,128)(2,1)}, bf16[64,512]{1,0:T(8,128)(2,1)S(1)}, u32[]{:S(2)}, u32[]{:S(2)}) collective-permute-start(bf16[64,512]{1,0:T(8,128)(2,1)} %get-tuple-element.84), channel_id=1, source_target_pairs={{0,1},{1,2},{2,3},{3,4},{4,5},{5,6},{6,7},{7,0},{8,9},{9,10},{10,1... | collective-permute-start | bytes 196616 | tf_op jit(solution)/shard_map/ppermute | solution.py:345
  13.9 3.3 %collective-permute-start.1 = (bf16[64,512]{1,0:T(8,128)(2,1)}, bf16[64,512]{1,0:T(8,128)(2,1)S(1)}, u32[]{:S(2)}, u32[]{:S(2)}) collective-permute-start(bf16[64,512]{1,0:T(8,128)(2,1)} %get-tuple-element.85), channel_id=1, source_target_pairs={{0,2},{1,3},{2,4},{3,5},{4,6},{5,7},{6,0},{7,1},{8,10},{9,11},{10,... | collective-permute-start | bytes 196616 | tf_op jit(solution)/shard_map/ppermute | solution.py:345
  17.1 4.0 %collective-permute-start.2 = (bf16[64,512]{1,0:T(8,128)(2,1)}, bf16[64,512]{1,0:T(8,128)(2,1)S(1)}, u32[]{:S(2)}, u32[]{:S(2)}) collective-permute-start(bf16[64,512]{1,0:T(8,128)(2,1)} %get-tuple-element.86), channel_id=1, source_target_pairs={{0,3},{1,4},{2,5},{3,6},{4,7},{5,0},{6,1},{7,2},{8,11},{9,12},{10,... | collective-permute-start | bytes 196616 | tf_op jit(solution)/shard_map/ppermute | solution.py:345
  21.7 4.9 %collective-permute-start.4 = (bf16[64,512]{1,0:T(8,128)(2,1)}, bf16[64,512]{1,0:T(8,128)(2,1)S(1)}, u32[]{:S(2)}, u32[]{:S(2)}) collective-permute-start(bf16[64,512]{1,0:T(8,128)(2,1)} %get-tuple-element.88), channel_id=1, source_target_pairs={{0,5},{1,6},{2,7},{3,0},{4,1},{5,2},{6,3},{7,4},{8,13},{9,14},{10,... | collective-permute-start | bytes 196616 | tf_op jit(solution)/shard_map/ppermute | solution.py:345
  26.7 2.7 %collective-permute-start.5 = (bf16[64,512]{1,0:T(8,128)(2,1)}, bf16[64,512]{1,0:T(8,128)(2,1)S(1)}, u32[]{:S(2)}, u32[]{:S(2)}) collective-permute-start(bf16[64,512]{1,0:T(8,128)(2,1)} %get-tuple-element.89), channel_id=1, source_target_pairs={{0,6},{1,7},{2,0},{3,1},{4,2},{5,3},{6,4},{7,5},{8,14},{9,15},{10,... | collective-permute-start | bytes 196616 | tf_op jit(solution)/shard_map/ppermute | solution.py:345
  29.3 1.0 collective-permute-start.6
  30.4 5.7 %collective-permute-done.4.refs_5_ = bf16[64,512]{1,0:T(8,128)(2,1)S(1)} collective-permute-done((bf16[64,512]{1,0:T(8,128)(2,1)}, bf16[64,512]{1,0:T(8,128)(2,1)S(1)}, u32[]{:S(2)}, u32[]{:S(2)}) %collective-permute-start.4) | collective-permute-done | bytes 65568 | tf_op jit(solution)/shard_map/ppermute | solution.py:345
  36.6 2.3 %all-to-all-done = bf16[32,4,64,128]{3,2,1,0:T(8,128)(2,1)S(1)} async-done(((bf16[32,4,64,128]{3,2,1,0:T(8,128)(2,1)}), bf16[32,4,64,128]{3,2,1,0:T(8,128)(2,1)S(1)}, u32[]{:S(2)}, u32[]{:S(2)}) %all-to-all-start) | async-done | bytes 2097184 | tf_op jit(solution)/shard_map/all_to_all | solution.py:406
  38.9 5.2 %neighbour_mean.3 = (bf16[64,512]{1,0:T(8,128)(2,1)}, bf16[64,512]{1,0:T(8,128)(2,1)}, bf16[64,512]{1,0:T(8,128)(2,1)}, bf16[64,512]{1,0:T(8,128)(2,1)}, f32[8,512]{1,0:T(8,128)}) custom-call(s32[1]{0:T(128)} %bitcast.me_ref, s32[8,32]{1,0:T(8,128)S(1)} %bitcast.21, s32[32]{0:T(128)S(1)} %copy-done.10, bf16[64,4096]{1,0:T(8,128)(2,1)S(1)} %bitcast.19, ...), custom_call_target="tpu_custom_call" | custom-call | flops 268435456 | bytes 7340032 | tf_op jit(solution)/shard_map/neighbour_mean/pallas_call | solution.py:434
  44.2 7.3 %collective-permute-start.7 = (bf16[64,512]{1,0:T(8,128)(2,1)}, bf16[64,512]{1,0:T(8,128)(2,1)S(1)}, u32[]{:S(2)}, u32[]{:S(2)}) collective-permute-start(bf16[64,512]{1,0:T(8,128)(2,1)} %get-tuple-element.104), channel_id=1, source_target_pairs={{0,4},{1,5},{2,6},{3,7},{4,0},{5,1},{6,2},{7,3},{8,12},{9,13},{10,... | collective-permute-start | bytes 196616 | tf_op jit(solution)/shard_map/ppermute | solution.py:345
  51.5 1.9 %collective-permute-start.8 = (bf16[64,512]{1,0:T(8,128)(2,1)}, bf16[64,512]{1,0:T(8,128)(2,1)S(1)}, u32[]{:S(2)}, u32[]{:S(2)}) collective-permute-start(bf16[64,512]{1,0:T(8,128)(2,1)} %get-tuple-element.105), channel_id=1, source_target_pairs={{0,3},{1,4},{2,5},{3,6},{4,7},{5,0},{6,1},{7,2},{8,11},{9,12},{10,... | collective-permute-start | bytes 196616 | tf_op jit(solution)/shard_map/ppermute | solution.py:345
  53.4 3.1 %collective-permute-start.9 = (bf16[64,512]{1,0:T(8,128)(2,1)}, bf16[64,512]{1,0:T(8,128)(2,1)}, u32[]{:S(2)}, u32[]{:S(2)}) collective-permute-start(bf16[64,512]{1,0:T(8,128)(2,1)} %get-tuple-element.106), channel_id=1, source_target_pairs={{0,5},{1,6},{2,7},{3,0},{4,1},{5,2},{6,3},{7,4},{8,13},{9,14},{10,... | collective-permute-start | bytes 196616 | tf_op jit(solution)/shard_map/ppermute | solution.py:345
  56.5 1.7 %collective-permute-start.10 = (bf16[64,512]{1,0:T(8,128)(2,1)}, bf16[64,512]{1,0:T(8,128)(2,1)}, u32[]{:S(2)}, u32[]{:S(2)}) collective-permute-start(bf16[64,512]{1,0:T(8,128)(2,1)} %get-tuple-element.107), channel_id=1, source_target_pairs={{0,2},{1,3},{2,4},{3,5},{4,6},{5,7},{6,0},{7,1},{8,10},{9,11},{10,... | collective-permute-start | bytes 196616 | tf_op jit(solution)/shard_map/ppermute | solution.py:345
  58.2 4.7 %neighbour_mean.2 = (bf16[64,512]{1,0:T(8,128)(2,1)}, bf16[64,512]{1,0:T(8,128)(2,1)}, bf16[64,512]{1,0:T(8,128)(2,1)}, bf16[64,512]{1,0:T(8,128)(2,1)}, f32[8,512]{1,0:T(8,128)S(1)}) custom-call(s32[1]{0:T(128)} %bitcast.me_ref, s32[8,32]{1,0:T(8,128)S(1)} %bitcast.22, s32[32]{0:T(128)S(1)} %copy-done.10, bf16[64,4096]{1,0:T(8,128)(2,1)S(1)} %bitcast.20, ...), custom_call_target="tpu_custom_call" | custom-call | flops 268435456 | bytes 7340032 | tf_op jit(solution)/shard_map/neighbour_mean/pallas_call | solution.py:434
  63.5 2.7 %collective-permute-start.11 = (bf16[64,512]{1,0:T(8,128)(2,1)}, bf16[64,512]{1,0:T(8,128)(2,1)S(1)}, u32[]{:S(2)}, u32[]{:S(2)}) collective-permute-start(bf16[64,512]{1,0:T(8,128)(2,1)} %get-tuple-element.108), channel_id=1, source_target_pairs={{0,6},{1,7},{2,0},{3,1},{4,2},{5,3},{6,4},{7,5},{8,14},{9,15},{10,... | collective-permute-start | bytes 196616 | tf_op jit(solution)/shard_map/ppermute | solution.py:345
  66.2 1.0 collective-permute-start.12
  67.2 2.2 %collective-permute-start.13 = (bf16[64,512]{1,0:T(8,128)(2,1)}, bf16[64,512]{1,0:T(8,128)(2,1)S(1)}, u32[]{:S(2)}, u32[]{:S(2)}) collective-permute-start(bf16[64,512]{1,0:T(8,128)(2,1)} %get-tuple-element.110), channel_id=1, source_target_pairs={{0,7},{1,0},{2,1},{3,2},{4,3},{5,4},{6,5},{7,6},{8,15},{9,8},{10,9... | collective-permute-start | bytes 196616 | tf_op jit(solution)/shard_map/ppermute | solution.py:345
  69.6 1.4 self_part.1
  71.1 0.8 collective-permute-done.12.refs_5_
  71.9 0.8 copy-done.5
  73.4 2.7 %layer_head.1 = (bf16[512,512]{1,0:T(8,128)(2,1)S(1)}, bf16[256,512]{1,0:T(8,128)(2,1)S(1)}, bf16[256,512]{1,0:T(8,128)(2,1)S(1)}, bf16[512,512]{1,0:T(8,128)(2,1)}) custom-call(s32[1]{0:T(128)} %bitcast.me_ref, f32[8,512]{1,0:T(8,128)S(1)} %copy-done.8, f32[256,512]{1,0:T(8,128)S(1)} %get-tuple-element.101.pre_ref, ...), custom_call_target="tpu_custom_call" | custom-call | flops 268435456 | bytes 4194304 | tf_op jit(solution)/shard_map/layer_head/pallas_call | solution.py:453
  76.1 4.5 %all-to-all-start.1 = ((bf16[8,64,512]{2,1,0:T(8,128)(2,1)}), bf16[8,64,512]{2,1,0:T(8,128)(2,1)S(1)}, u32[]{:S(2)}, u32[]{:S(2)}) async-start(bf16[8,64,512]{2,1,0:T(8,128)(2,1)} %bitcast.7), calls=%async_computation.1 | async-start | bytes 1048576 | tf_op jit(solution)/shard_map/all_to_all | solution.py:462
  81.3 1.5 %collective-permute-done.14.recv_ref = bf16[16,8,8,128]{3,2,1,0:T(8,128)(2,1)S(1)} collective-permute-done((bf16[16,8,8,128]{3,2,1,0:T(8,128)(2,1)S(1)}, bf16[16,8,8,128]{3,2,1,0:T(8,128)(2,1)S(1)}, u32[]{:S(2)}, u32[]{:S(2)}) %collective-permute-start.14) | collective-permute-done | bytes 262176 | tf_op jit(solution)/shard_map/ppermute | solution.py:482
  83.0 2.4 %collective-permute-start.16 = (bf16[4,8,8,128]{3,2,1,0:T(8,128)(2,1)S(1)}, bf16[4,8,8,128]{3,2,1,0:T(8,128)(2,1)S(1)}, u32[]{:S(2)}, u32[]{:S(2)}) collective-permute-start(bf16[4,8,8,128]{3,2,1,0:T(8,128)(2,1)S(1)} %get-tuple-element.120), channel_id=1, source_target_pairs={{0,16},{8,24},{16,0},{24,8},{32,48},{40,56},{48,32},{56,40},{64,80... | collective-permute-start | bytes 196616 | tf_op jit(solution)/shard_map/ppermute | solution.py:498
  85.4 1.4 collective-permute-start.17
  87.8 2.8 %collective-permute-done.17.refs_2_ = bf16[4,8,8,128]{3,2,1,0:T(8,128)(2,1)S(1)} collective-permute-done((bf16[4,8,8,128]{3,2,1,0:T(8,128)(2,1)S(1)}, bf16[4,8,8,128]{3,2,1,0:T(8,128)(2,1)S(1)}, u32[]{:S(2)}, u32[]{:S(2)}) %collective-permute-start.17) | collective-permute-done | bytes 65568 | tf_op jit(solution)/shard_map/ppermute | solution.py:498
  90.7 0.9 side_grads.1
  91.7 4.8 %collective-permute-done.18.recv_ref = bf16[4,8,8,128]{3,2,1,0:T(8,128)(2,1)S(1)} collective-permute-done((bf16[4,8,8,128]{3,2,1,0:T(8,128)(2,1)S(1)}, bf16[4,8,8,128]{3,2,1,0:T(8,128)(2,1)S(1)}, u32[]{:S(2)}, u32[]{:S(2)}) %collective-permute-start.18) | collective-permute-done | bytes 65568 | tf_op jit(solution)/shard_map/ppermute | solution.py:511
  96.5 6.4 %table_grad.1 = (f32[32,64,128]{2,1,0:T(8,128)}, bf16[128,64,128]{2,1,0:T(8,128)(2,1)}) custom-call(s32[8,32]{1,0:T(8,128)S(1)} %bitcast.23, s32[32]{0:T(128)S(1)} %copy-done.10, bf16[32,8,128,128]{3,2,1,0:T(8,128)(2,1)} %vals_ref.5, bf16[8,64,512]{2,1,0:T(8,128)(2,1)S(1)} %all-to-all-done.1.scaled_ref), custom_call_target="tpu_custom_call" | custom-call | flops 536870912 | bytes 12582912 | tf_op jit(solution)/shard_map/table_grad/pallas_call | solution.py:515
  103.0 5.1 %all-to-all-start.2 = ((bf16[32,4,64,128]{3,2,1,0:T(8,128)(2,1)}), bf16[32,4,64,128]{3,2,1,0:T(8,128)(2,1)S(1)}, u32[]{:S(2)}, u32[]{:S(2)}) async-start(bf16[32,4,64,128]{3,2,1,0:T(8,128)(2,1)} %bitcast.28), calls=%async_computation.2 | async-start | bytes 4194304 | tf_op jit(solution)/shard_map/all_to_all | solution.py:536
  108.2 6.0 %collective-permute-start.19 = (bf16[64,640]{1,0:T(8,128)(2,1)S(1)}, bf16[64,640]{1,0:T(8,128)(2,1)S(1)}, u32[]{:S(2)}, u32[]{:S(2)}) collective-permute-start(bf16[64,640]{1,0:T(8,128)(2,1)S(1)} %get-tuple-element.145), channel_id=1, source_target_pairs={{0,4},{1,5},{2,6},{3,7},{4,0},{5,1},{6,2},{7,3},{8,12},{9,13},{10,... | collective-permute-start | bytes 245768 | tf_op jit(solution)/shard_map/ppermute | solution.py:345
  114.8 4.5 %collective-permute-start.21 = (bf16[64,640]{1,0:T(8,128)(2,1)S(1)}, bf16[64,640]{1,0:T(8,128)(2,1)S(1)}, u32[]{:S(2)}, u32[]{:S(2)}) collective-permute-start(bf16[64,640]{1,0:T(8,128)(2,1)S(1)} %get-tuple-element.147), channel_id=1, source_target_pairs={{0,5},{1,6},{2,7},{3,0},{4,1},{5,2},{6,3},{7,4},{8,13},{9,14},{10,... | collective-permute-start | bytes 245768 | tf_op jit(solution)/shard_map/ppermute | solution.py:345
  119.8 3.6 %collective-permute-start.23 = (bf16[64,640]{1,0:T(8,128)(2,1)S(1)}, bf16[64,640]{1,0:T(8,128)(2,1)S(1)}, u32[]{:S(2)}, u32[]{:S(2)}) collective-permute-start(bf16[64,640]{1,0:T(8,128)(2,1)S(1)} %get-tuple-element.149), channel_id=1, source_target_pairs={{0,6},{1,7},{2,0},{3,1},{4,2},{5,3},{6,4},{7,5},{8,14},{9,15},{10,... | collective-permute-start | bytes 245768 | tf_op jit(solution)/shard_map/ppermute | solution.py:345
  123.9 1.6 %collective-permute-done.20.refs_1_ = bf16[64,640]{1,0:T(8,128)(2,1)S(1)} collective-permute-done((bf16[64,640]{1,0:T(8,128)(2,1)S(1)}, bf16[64,640]{1,0:T(8,128)(2,1)S(1)}, u32[]{:S(2)}, u32[]{:S(2)}) %collective-permute-start.20) | collective-permute-done | bytes 81952 | tf_op jit(solution)/shard_map/ppermute | solution.py:345
  125.5 1.1 collective-permute-start.25
  126.6 1.2 collective-permute-done.22.refs_3_
  128.6 0.8 collective-permute-done.24.refs_5_
  130.0 1.2 copy-done.1
  131.4 1.1 collective-permute-done.26
  132.6 3.1 %collective-permute-start.27 = (bf16[2,32,128]{2,1,0:T(8,128)(2,1)S(1)}, bf16[2,32,128]{2,1,0:T(8,128)(2,1)S(1)}, u32[]{:S(2)}, u32[]{:S(2)}) collective-permute-start(bf16[2,32,128]{2,1,0:T(8,128)(2,1)S(1)} %constant_dynamic-update-slice_fusion), channel_id=1, source_target_pairs={{0,128},{8,136},{16,144},{24,152},{32,160},{40,168},{48,176},{56,1... | collective-permute-start | bytes 49160 | tf_op jit(solution)/shard_map/ppermute | solution.py:574
  135.7 1.1 collective-permute-start.29
  136.8 1.0 collective-permute-done.27
  137.9 2.8 %collective-permute-done.29 = bf16[2,32,128]{2,1,0:T(8,128)(2,1)S(1)} collective-permute-done((bf16[2,32,128]{2,1,0:T(8,128)(2,1)S(1)}, bf16[2,32,128]{2,1,0:T(8,128)(2,1)S(1)}, u32[]{:S(2)}, u32[]{:S(2)}) %collective-permute-start.29) | collective-permute-done | bytes 16416 | tf_op jit(solution)/shard_map/ppermute | solution.py:574
  141.3 2.2 %sum_returned.1 = bf16[64,4096]{1,0:T(8,128)(2,1)} custom-call(s32[4,32]{1,0:T(4,128)S(1)} %bitcast.27, f32[32,64,128]{2,1,0:T(8,128)S(1)} %sum_near.1.near_ref, bf16[32,4,64,128]{3,2,1,0:T(8,128)(2,1)S(1)} %all-to-all-done.2.back_ref), custom_call_target="tpu_custom_call" | custom-call | bytes 4194304 | tf_op jit(solution)/shard_map/sum_returned/pallas_call | solution.py:580
  143.5 1.2 collective-permute-done.30
  (82 shorter events, 9.3 us)
Async XLA Ops:
  3.2 7.8 %copy-start = (bf16[4096,64]{0,1:T(8,128)(2,1)S(1)}, bf16[4096,64]{0,1:T(8,128)(2,1)}, u32[]{:S(2)}) copy-start(bf16[4096,64]{0,1:T(8,128)(2,1)} %param.9) | copy-start | bytes 1572868
  3.2 35.7 %copy-start.6 = (s32[32,8]{0,1:T(8,128)S(1)}, s32[32,8]{0,1:T(8,128)}, u32[]{:S(2)}) copy-start(s32[32,8]{0,1:T(8,128)} %param.11) | copy-start | bytes 3076
  3.2 35.7 %copy-start.10 = (s32[32]{0:T(128)S(1)}, s32[32]{0:T(128)}, u32[]{:S(2)}) copy-start(s32[32]{0:T(128)} %counts_ref.5) | copy-start | bytes 388
  3.2 35.6 %all-to-all-start = ((bf16[32,4,64,128]{3,2,1,0:T(8,128)(2,1)}), bf16[32,4,64,128]{3,2,1,0:T(8,128)(2,1)S(1)}, u32[]{:S(2)}, u32[]{:S(2)}) async-start(bf16[32,4,64,128]{3,2,1,0:T(8,128)(2,1)} %pack_outgoing.1), calls=%async_computation | async-start | bytes 4194304 | tf_op jit(solution)/shard_map/all_to_all | solution.py:406
  11.9 14.8 %collective-permute-start = (bf16[64,512]{1,0:T(8,128)(2,1)}, bf16[64,512]{1,0:T(8,128)(2,1)S(1)}, u32[]{:S(2)}, u32[]{:S(2)}) collective-permute-start(bf16[64,512]{1,0:T(8,128)(2,1)} %get-tuple-element.84), channel_id=1, source_target_pairs={{0,1},{1,2},{2,3},{3,4},{4,5},{5,6},{6,7},{7,0},{8,9},{9,10},{10,1... | collective-permute-start | bytes 196616 | tf_op jit(solution)/shard_map/ppermute | solution.py:345
  13.9 15.5 %collective-permute-start.1 = (bf16[64,512]{1,0:T(8,128)(2,1)}, bf16[64,512]{1,0:T(8,128)(2,1)S(1)}, u32[]{:S(2)}, u32[]{:S(2)}) collective-permute-start(bf16[64,512]{1,0:T(8,128)(2,1)} %get-tuple-element.85), channel_id=1, source_target_pairs={{0,2},{1,3},{2,4},{3,5},{4,6},{5,7},{6,0},{7,1},{8,10},{9,11},{10,... | collective-permute-start | bytes 196616 | tf_op jit(solution)/shard_map/ppermute | solution.py:345
  17.1 13.2 %collective-permute-start.2 = (bf16[64,512]{1,0:T(8,128)(2,1)}, bf16[64,512]{1,0:T(8,128)(2,1)S(1)}, u32[]{:S(2)}, u32[]{:S(2)}) collective-permute-start(bf16[64,512]{1,0:T(8,128)(2,1)} %get-tuple-element.86), channel_id=1, source_target_pairs={{0,3},{1,4},{2,5},{3,6},{4,7},{5,0},{6,1},{7,2},{8,11},{9,12},{10,... | collective-permute-start | bytes 196616 | tf_op jit(solution)/shard_map/ppermute | solution.py:345
  21.2 9.2 %collective-permute-start.3 = (bf16[64,512]{1,0:T(8,128)(2,1)}, bf16[64,512]{1,0:T(8,128)(2,1)S(1)}, u32[]{:S(2)}, u32[]{:S(2)}) collective-permute-start(bf16[64,512]{1,0:T(8,128)(2,1)} %get-tuple-element.87), channel_id=1, source_target_pairs={{0,4},{1,5},{2,6},{3,7},{4,0},{5,1},{6,2},{7,3},{8,12},{9,13},{10,... | collective-permute-start | bytes 196616 | tf_op jit(solution)/shard_map/ppermute | solution.py:345
  21.7 14.4 %collective-permute-start.4 = (bf16[64,512]{1,0:T(8,128)(2,1)}, bf16[64,512]{1,0:T(8,128)(2,1)S(1)}, u32[]{:S(2)}, u32[]{:S(2)}) collective-permute-start(bf16[64,512]{1,0:T(8,128)(2,1)} %get-tuple-element.88), channel_id=1, source_target_pairs={{0,5},{1,6},{2,7},{3,0},{4,1},{5,2},{6,3},{7,4},{8,13},{9,14},{10,... | collective-permute-start | bytes 196616 | tf_op jit(solution)/shard_map/ppermute | solution.py:345
  26.7 17.5 %copy-start.11 = (bf16[64,512]{1,0:T(8,128)(2,1)}, bf16[64,512]{1,0:T(8,128)(2,1)S(1)}, u32[]{:S(2)}) copy-start(bf16[64,512]{1,0:T(8,128)(2,1)S(1)} %collective-permute-done.refs_1_) | copy-start | bytes 196612
  26.7 9.4 %collective-permute-start.5 = (bf16[64,512]{1,0:T(8,128)(2,1)}, bf16[64,512]{1,0:T(8,128)(2,1)S(1)}, u32[]{:S(2)}, u32[]{:S(2)}) collective-permute-start(bf16[64,512]{1,0:T(8,128)(2,1)} %get-tuple-element.89), channel_id=1, source_target_pairs={{0,6},{1,7},{2,0},{3,1},{4,2},{5,3},{6,4},{7,5},{8,14},{9,15},{10,... | collective-permute-start | bytes 196616 | tf_op jit(solution)/shard_map/ppermute | solution.py:345
  29.3 14.8 %copy-start.12 = (bf16[64,512]{1,0:T(8,128)(2,1)}, bf16[64,512]{1,0:T(8,128)(2,1)S(1)}, u32[]{:S(2)}) copy-start(bf16[64,512]{1,0:T(8,128)(2,1)S(1)} %collective-permute-done.1.refs_2_) | copy-start | bytes 196612
  29.3 7.2 %collective-permute-start.6 = (bf16[64,512]{1,0:T(8,128)(2,1)}, bf16[64,512]{1,0:T(8,128)(2,1)S(1)}, u32[]{:S(2)}, u32[]{:S(2)}) collective-permute-start(bf16[64,512]{1,0:T(8,128)(2,1)} %get-tuple-element.90), channel_id=1, source_target_pairs={{0,7},{1,0},{2,1},{3,2},{4,3},{5,4},{6,5},{7,6},{8,15},{9,8},{10,9... | collective-permute-start | bytes 196616 | tf_op jit(solution)/shard_map/ppermute | solution.py:345
  30.3 13.8 %copy-start.13 = (bf16[64,512]{1,0:T(8,128)(2,1)}, bf16[64,512]{1,0:T(8,128)(2,1)S(1)}, u32[]{:S(2)}) copy-start(bf16[64,512]{1,0:T(8,128)(2,1)S(1)} %collective-permute-done.2.refs_3_) | copy-start | bytes 196612
  30.3 13.8 %copy-start.14 = (bf16[64,512]{1,0:T(8,128)(2,1)}, bf16[64,512]{1,0:T(8,128)(2,1)S(1)}, u32[]{:S(2)}) copy-start(bf16[64,512]{1,0:T(8,128)(2,1)S(1)} %collective-permute-done.3.refs_4_) | copy-start | bytes 196612
  36.1 8.1 %copy-start.15 = (bf16[64,512]{1,0:T(8,128)(2,1)}, bf16[64,512]{1,0:T(8,128)(2,1)S(1)}, u32[]{:S(2)}) copy-start(bf16[64,512]{1,0:T(8,128)(2,1)S(1)} %collective-permute-done.4.refs_5_) | copy-start | bytes 196612
  36.1 8.1 %copy-start.16 = (bf16[64,512]{1,0:T(8,128)(2,1)}, bf16[64,512]{1,0:T(8,128)(2,1)S(1)}, u32[]{:S(2)}) copy-start(bf16[64,512]{1,0:T(8,128)(2,1)S(1)} %collective-permute-done.5.refs_6_) | copy-start | bytes 196612
  44.2 22.0 %collective-permute-start.7 = (bf16[64,512]{1,0:T(8,128)(2,1)}, bf16[64,512]{1,0:T(8,128)(2,1)S(1)}, u32[]{:S(2)}, u32[]{:S(2)}) collective-permute-start(bf16[64,512]{1,0:T(8,128)(2,1)} %get-tuple-element.104), channel_id=1, source_target_pairs={{0,4},{1,5},{2,6},{3,7},{4,0},{5,1},{6,2},{7,3},{8,12},{9,13},{10,... | collective-permute-start | bytes 196616 | tf_op jit(solution)/shard_map/ppermute | solution.py:345
  51.5 15.7 %collective-permute-start.8 = (bf16[64,512]{1,0:T(8,128)(2,1)}, bf16[64,512]{1,0:T(8,128)(2,1)S(1)}, u32[]{:S(2)}, u32[]{:S(2)}) collective-permute-start(bf16[64,512]{1,0:T(8,128)(2,1)} %get-tuple-element.105), channel_id=1, source_target_pairs={{0,3},{1,4},{2,5},{3,6},{4,7},{5,0},{6,1},{7,2},{8,11},{9,12},{10,... | collective-permute-start | bytes 196616 | tf_op jit(solution)/shard_map/ppermute | solution.py:345
  53.4 17.6 %collective-permute-start.9 = (bf16[64,512]{1,0:T(8,128)(2,1)}, bf16[64,512]{1,0:T(8,128)(2,1)}, u32[]{:S(2)}, u32[]{:S(2)}) collective-permute-start(bf16[64,512]{1,0:T(8,128)(2,1)} %get-tuple-element.106), channel_id=1, source_target_pairs={{0,5},{1,6},{2,7},{3,0},{4,1},{5,2},{6,3},{7,4},{8,13},{9,14},{10,... | collective-permute-start | bytes 196616 | tf_op jit(solution)/shard_map/ppermute | solution.py:345
  56.5 12.9 %copy-start.18 = (f32[256]{0:T(256)S(1)}, f32[256]{0:T(256)}, u32[]{:S(2)}) copy-start(f32[256]{0:T(256)} %param.16) | copy-start | bytes 3076
  56.5 13.1 %copy-start.2 = (bf16[512,256]{1,0:T(8,128)(2,1)S(1)}, bf16[512,256]{1,0:T(8,128)(2,1)}, u32[]{:S(2)}) copy-start(bf16[512,256]{1,0:T(8,128)(2,1)} %weight_ref.4) | copy-start | bytes 786436
  56.5 13.1 %copy-start.3 = (bf16[512,256]{1,0:T(8,128)(2,1)S(1)}, bf16[512,256]{1,0:T(8,128)(2,1)}, u32[]{:S(2)}) copy-start(bf16[512,256]{1,0:T(8,128)(2,1)} %weight_ref.5) | copy-start | bytes 786436
  56.5 13.1 %copy-start.4 = (bf16[512,256]{1,0:T(8,128)(2,1)S(1)}, bf16[512,256]{1,0:T(8,128)(2,1)}, u32[]{:S(2)}) copy-start(bf16[512,256]{1,0:T(8,128)(2,1)} %cot_ref.1) | copy-start | bytes 786436
  56.5 14.5 %collective-permute-start.10 = (bf16[64,512]{1,0:T(8,128)(2,1)}, bf16[64,512]{1,0:T(8,128)(2,1)}, u32[]{:S(2)}, u32[]{:S(2)}) collective-permute-start(bf16[64,512]{1,0:T(8,128)(2,1)} %get-tuple-element.107), channel_id=1, source_target_pairs={{0,2},{1,3},{2,4},{3,5},{4,6},{5,7},{6,0},{7,1},{8,10},{9,11},{10,... | collective-permute-start | bytes 196616 | tf_op jit(solution)/shard_map/ppermute | solution.py:345
  63.5 7.5 %collective-permute-start.11 = (bf16[64,512]{1,0:T(8,128)(2,1)}, bf16[64,512]{1,0:T(8,128)(2,1)S(1)}, u32[]{:S(2)}, u32[]{:S(2)}) collective-permute-start(bf16[64,512]{1,0:T(8,128)(2,1)} %get-tuple-element.108), channel_id=1, source_target_pairs={{0,6},{1,7},{2,0},{3,1},{4,2},{5,3},{6,4},{7,5},{8,14},{9,15},{10,... | collective-permute-start | bytes 196616 | tf_op jit(solution)/shard_map/ppermute | solution.py:345
  66.2 5.7 %collective-permute-start.12 = (bf16[64,512]{1,0:T(8,128)(2,1)}, bf16[64,512]{1,0:T(8,128)(2,1)S(1)}, u32[]{:S(2)}, u32[]{:S(2)}) collective-permute-start(bf16[64,512]{1,0:T(8,128)(2,1)} %get-tuple-element.109), channel_id=1, source_target_pairs={{0,1},{1,2},{2,3},{3,4},{4,5},{5,6},{6,7},{7,0},{8,9},{9,10},{10,1... | collective-permute-start | bytes 196616 | tf_op jit(solution)/shard_map/ppermute | solution.py:345
  67.2 4.7 %collective-permute-start.13 = (bf16[64,512]{1,0:T(8,128)(2,1)}, bf16[64,512]{1,0:T(8,128)(2,1)S(1)}, u32[]{:S(2)}, u32[]{:S(2)}) collective-permute-start(bf16[64,512]{1,0:T(8,128)(2,1)} %get-tuple-element.110), channel_id=1, source_target_pairs={{0,7},{1,0},{2,1},{3,2},{4,3},{5,4},{6,5},{7,6},{8,15},{9,8},{10,9... | collective-permute-start | bytes 196616 | tf_op jit(solution)/shard_map/ppermute | solution.py:345
  76.1 20.4 %all-to-all-start.1 = ((bf16[8,64,512]{2,1,0:T(8,128)(2,1)}), bf16[8,64,512]{2,1,0:T(8,128)(2,1)S(1)}, u32[]{:S(2)}, u32[]{:S(2)}) async-start(bf16[8,64,512]{2,1,0:T(8,128)(2,1)} %bitcast.7), calls=%async_computation.1 | async-start | bytes 1048576 | tf_op jit(solution)/shard_map/all_to_all | solution.py:462
  81.2 1.6 %collective-permute-start.14 = (bf16[16,8,8,128]{3,2,1,0:T(8,128)(2,1)S(1)}, bf16[16,8,8,128]{3,2,1,0:T(8,128)(2,1)S(1)}, u32[]{:S(2)}, u32[]{:S(2)}) collective-permute-start(bf16[16,8,8,128]{3,2,1,0:T(8,128)(2,1)S(1)} %get-tuple-element.117), channel_id=1, source_target_pairs={{0,8},{8,0},{16,24},{24,16},{32,40},{40,32},{48,56},{56,48},{64,72... | collective-permute-start | bytes 786440 | tf_op jit(solution)/shard_map/ppermute | solution.py:482
  82.9 4.4 %collective-permute-start.15 = (bf16[4,8,8,128]{3,2,1,0:T(8,128)(2,1)S(1)}, bf16[4,8,8,128]{3,2,1,0:T(8,128)(2,1)S(1)}, u32[]{:S(2)}, u32[]{:S(2)}) collective-permute-start(bf16[4,8,8,128]{3,2,1,0:T(8,128)(2,1)S(1)} %get-tuple-element.119), channel_id=1, source_target_pairs={{0,64},{8,72},{16,80},{24,88},{32,96},{40,104},{48,112},{56,120},{... | collective-permute-start | bytes 196616 | tf_op jit(solution)/shard_map/ppermute | solution.py:498
  83.0 4.8 %collective-permute-start.16 = (bf16[4,8,8,128]{3,2,1,0:T(8,128)(2,1)S(1)}, bf16[4,8,8,128]{3,2,1,0:T(8,128)(2,1)S(1)}, u32[]{:S(2)}, u32[]{:S(2)}) collective-permute-start(bf16[4,8,8,128]{3,2,1,0:T(8,128)(2,1)S(1)} %get-tuple-element.120), channel_id=1, source_target_pairs={{0,16},{8,24},{16,0},{24,8},{32,48},{40,56},{48,32},{56,40},{64,80... | collective-permute-start | bytes 196616 | tf_op jit(solution)/shard_map/ppermute | solution.py:498
  85.4 5.2 %collective-permute-start.17 = (bf16[4,8,8,128]{3,2,1,0:T(8,128)(2,1)S(1)}, bf16[4,8,8,128]{3,2,1,0:T(8,128)(2,1)S(1)}, u32[]{:S(2)}, u32[]{:S(2)}) collective-permute-start(bf16[4,8,8,128]{3,2,1,0:T(8,128)(2,1)S(1)} %get-tuple-element.121), channel_id=1, source_target_pairs={{0,80},{8,88},{16,64},{24,72},{32,112},{40,120},{48,96},{56,104},{... | collective-permute-start | bytes 196616 | tf_op jit(solution)/shard_map/ppermute | solution.py:498
  90.6 5.9 %collective-permute-start.18 = (bf16[4,8,8,128]{3,2,1,0:T(8,128)(2,1)S(1)}, bf16[4,8,8,128]{3,2,1,0:T(8,128)(2,1)S(1)}, u32[]{:S(2)}, u32[]{:S(2)}) collective-permute-start(bf16[4,8,8,128]{3,2,1,0:T(8,128)(2,1)S(1)} %weight_add.2.held_ref), channel_id=1, source_target_pairs={{0,32},{8,40},{16,48},{24,56},{32,0},{40,8},{48,16},{56,24},{64,96... | collective-permute-start | bytes 196616 | tf_op jit(solution)/shard_map/ppermute | solution.py:511
  103.0 37.7 %all-to-all-start.2 = ((bf16[32,4,64,128]{3,2,1,0:T(8,128)(2,1)}), bf16[32,4,64,128]{3,2,1,0:T(8,128)(2,1)S(1)}, u32[]{:S(2)}, u32[]{:S(2)}) async-start(bf16[32,4,64,128]{3,2,1,0:T(8,128)(2,1)} %bitcast.28), calls=%async_computation.2 | async-start | bytes 4194304 | tf_op jit(solution)/shard_map/all_to_all | solution.py:536
  108.1 33.2 %copy-start.9 = (s32[1,32,4]{1,2,0:T(4,128)S(1)}, s32[1,32,4]{1,2,0:T(4,128)}, u32[]{:S(2)}) copy-start(s32[1,32,4]{1,2,0:T(4,128)} %param.13) | copy-start | bytes 1540
  108.2 15.2 %collective-permute-start.19 = (bf16[64,640]{1,0:T(8,128)(2,1)S(1)}, bf16[64,640]{1,0:T(8,128)(2,1)S(1)}, u32[]{:S(2)}, u32[]{:S(2)}) collective-permute-start(bf16[64,640]{1,0:T(8,128)(2,1)S(1)} %get-tuple-element.145), channel_id=1, source_target_pairs={{0,4},{1,5},{2,6},{3,7},{4,0},{5,1},{6,2},{7,3},{8,12},{9,13},{10,... | collective-permute-start | bytes 245768 | tf_op jit(solution)/shard_map/ppermute | solution.py:345
  114.2 11.4 %collective-permute-start.20 = (bf16[64,640]{1,0:T(8,128)(2,1)S(1)}, bf16[64,640]{1,0:T(8,128)(2,1)S(1)}, u32[]{:S(2)}, u32[]{:S(2)}) collective-permute-start(bf16[64,640]{1,0:T(8,128)(2,1)S(1)} %get-tuple-element.146), channel_id=1, source_target_pairs={{0,3},{1,4},{2,5},{3,6},{4,7},{5,0},{6,1},{7,2},{8,11},{9,12},{10,... | collective-permute-start | bytes 245768 | tf_op jit(solution)/shard_map/ppermute | solution.py:345
  114.8 11.9 %collective-permute-start.21 = (bf16[64,640]{1,0:T(8,128)(2,1)S(1)}, bf16[64,640]{1,0:T(8,128)(2,1)S(1)}, u32[]{:S(2)}, u32[]{:S(2)}) collective-permute-start(bf16[64,640]{1,0:T(8,128)(2,1)S(1)} %get-tuple-element.147), channel_id=1, source_target_pairs={{0,5},{1,6},{2,7},{3,0},{4,1},{5,2},{6,3},{7,4},{8,13},{9,14},{10,... | collective-permute-start | bytes 245768 | tf_op jit(solution)/shard_map/ppermute | solution.py:345
  119.2 8.6 %collective-permute-start.22 = (bf16[64,640]{1,0:T(8,128)(2,1)S(1)}, bf16[64,640]{1,0:T(8,128)(2,1)S(1)}, u32[]{:S(2)}, u32[]{:S(2)}) collective-permute-start(bf16[64,640]{1,0:T(8,128)(2,1)S(1)} %get-tuple-element.148), channel_id=1, source_target_pairs={{0,2},{1,3},{2,4},{3,5},{4,6},{5,7},{6,0},{7,1},{8,10},{9,11},{10,... | collective-permute-start | bytes 245768 | tf_op jit(solution)/shard_map/ppermute | solution.py:345
  119.8 8.8 %collective-permute-start.23 = (bf16[64,640]{1,0:T(8,128)(2,1)S(1)}, bf16[64,640]{1,0:T(8,128)(2,1)S(1)}, u32[]{:S(2)}, u32[]{:S(2)}) collective-permute-start(bf16[64,640]{1,0:T(8,128)(2,1)S(1)} %get-tuple-element.149), channel_id=1, source_target_pairs={{0,6},{1,7},{2,0},{3,1},{4,2},{5,3},{6,4},{7,5},{8,14},{9,15},{10,... | collective-permute-start | bytes 245768 | tf_op jit(solution)/shard_map/ppermute | solution.py:345
  123.4 6.0 %collective-permute-start.24 = (bf16[64,640]{1,0:T(8,128)(2,1)S(1)}, bf16[64,640]{1,0:T(8,128)(2,1)S(1)}, u32[]{:S(2)}, u32[]{:S(2)}) collective-permute-start(bf16[64,640]{1,0:T(8,128)(2,1)S(1)} %get-tuple-element.150), channel_id=1, source_target_pairs={{0,1},{1,2},{2,3},{3,4},{4,5},{5,6},{6,7},{7,0},{8,9},{9,10},{10,1... | collective-permute-start | bytes 245768 | tf_op jit(solution)/shard_map/ppermute | solution.py:345
  125.5 4.4 %collective-permute-start.25 = (bf16[64,640]{1,0:T(8,128)(2,1)S(1)}, bf16[64,640]{1,0:T(8,128)(2,1)S(1)}, u32[]{:S(2)}, u32[]{:S(2)}) collective-permute-start(bf16[64,640]{1,0:T(8,128)(2,1)S(1)} %get-tuple-element.151), channel_id=1, source_target_pairs={{0,7},{1,0},{2,1},{3,2},{4,3},{5,4},{6,5},{7,6},{8,15},{9,8},{10,9... | collective-permute-start | bytes 245768 | tf_op jit(solution)/shard_map/ppermute | solution.py:345
  131.3 1.3 collective-permute-start.26
  132.6 5.2 %collective-permute-start.27 = (bf16[2,32,128]{2,1,0:T(8,128)(2,1)S(1)}, bf16[2,32,128]{2,1,0:T(8,128)(2,1)S(1)}, u32[]{:S(2)}, u32[]{:S(2)}) collective-permute-start(bf16[2,32,128]{2,1,0:T(8,128)(2,1)S(1)} %constant_dynamic-update-slice_fusion), channel_id=1, source_target_pairs={{0,128},{8,136},{16,144},{24,152},{32,160},{40,168},{48,176},{56,1... | collective-permute-start | bytes 49160 | tf_op jit(solution)/shard_map/ppermute | solution.py:574
  135.7 4.9 %collective-permute-start.29 = (bf16[2,32,128]{2,1,0:T(8,128)(2,1)S(1)}, bf16[2,32,128]{2,1,0:T(8,128)(2,1)S(1)}, u32[]{:S(2)}, u32[]{:S(2)}) collective-permute-start(bf16[2,32,128]{2,1,0:T(8,128)(2,1)S(1)} %constant_dynamic-update-slice_fusion), channel_id=1, source_target_pairs={{0,192},{8,200},{16,208},{24,216},{32,224},{40,232},{48,240},{56,2... | collective-permute-start | bytes 49160 | tf_op jit(solution)/shard_map/ppermute | solution.py:574
  136.8 3.8 %collective-permute-start.28 = (bf16[2,32,128]{2,1,0:T(8,128)(2,1)S(1)}, bf16[2,32,128]{2,1,0:T(8,128)(2,1)S(1)}, u32[]{:S(2)}, u32[]{:S(2)}) collective-permute-start(bf16[2,32,128]{2,1,0:T(8,128)(2,1)S(1)} %constant_dynamic-update-slice_fusion), channel_id=1, source_target_pairs={{0,64},{8,72},{16,80},{24,88},{32,96},{40,104},{48,112},{56,120},{... | collective-permute-start | bytes 49160 | tf_op jit(solution)/shard_map/ppermute | solution.py:574
  140.7 4.0 %collective-permute-start.30 = (bf16[4,32,128]{2,1,0:T(8,128)(2,1)S(1)}, bf16[4,32,128]{2,1,0:T(8,128)(2,1)S(1)}, u32[]{:S(2)}, u32[]{:S(2)}) collective-permute-start(bf16[4,32,128]{2,1,0:T(8,128)(2,1)S(1)} %pad_maximum_fusion.1), channel_id=1, source_target_pairs={{0,16},{8,24},{16,0},{24,8},{32,48},{40,56},{48,32},{56,40},{64,80... | collective-permute-start | bytes 98312 | tf_op jit(solution)/shard_map/ppermute | solution.py:590
  (5 other events, 11.0 us)

commit v10 on v8

--- a/solution.py
+++ b/solution.py
@@ -548,6 +548,7 @@
         cost_estimate=cost(0, 3 * MIB),
         name="sum_near",
     )(me, own_grad, *packed)
+    held, near = lax.optimization_barrier((held, near))
     held = jnp.concatenate([held, lax.ppermute(held, "dom", flips[0])], axis=0)
     whole, half = 1 << order[-1], 1 << halves[-1]
     across, beside, both = (

time: 144 us -> 144 us (level)
  transfers between devices with their start and end apart: 28 -> 28, of which waited for: 20 -> 17; matrix products, arithmetic and copies ran while one was open for 0% -> 0% of each run, Pallas kernels for 4% -> 4%
where the time goes in v10:
time: 144 us
  starting transfers between devices  69.6 us (48%)
  waiting for transfers between devices  46.6 us (32%)
  Pallas kernels  23.9 us (17%)
  local copies, waits for them, and re-layouts  2.68 us (2%)
    ppermute x14, starting transfers between devices, exchange(): lax.ppermute(chunks[shift], 'chan', [(i, (i + shift) % count) for i in ra...  32.5 us
    all_to_all x1, waiting for transfers between devices, per_device(): lax.all_to_all(mean, 'chan', split_axis=0, concat_axis=0, tiled=True)  15.5 us
    ppermute x14, waiting for transfers between devices, exchange(): lax.ppermute(chunks[shift], 'chan', [(i, (i + shift) % count) for i in ra...  13.5 us
    all_to_all x1, starting transfers between devices, per_device(): lax.all_to_all(mean, 'chan', split_axis=0, concat_axis=0, tiled=True)  8.48 us
    all_to_all x1, starting transfers between devices, per_device(): lax.all_to_all(outgoing, 'dom', split_axis=0, concat_axis=0, tiled=True)  7.76 us
    all_to_all x1, starting transfers between devices, per_device(): lax.all_to_all(far_grad.reshape(parts, slots, chan_width, size), 'dom', s...  7.49 us
    pallas_call x1, Pallas kernels, per_device(): pl.pallas_call(scatter_kernel, out_shape=[pltpu.HBM((block_rows, chan_wid...  6.46 us
    pallas_call x1, Pallas kernels, per_device(): pl.pallas_call(gather_kernel, out_shape=[pltpu.HBM((chans, chan_width, no...  6.13 us
  transfers between devices with their start and end apart: 28, of which 17 were waited for; matrix products, arithmetic and copies ran while one was open for 0% of the time, Pallas kernels for 4%

profile of v10, /device:TPU:2, one launch (start us, length us, event | category | flops | bytes accessed | tf_op | source)
XLA Modules:
  0.0 143.8 jit_solution(6240908958643186748)
XLA Ops:
  0.6 2.5 %pack_outgoing.1 = bf16[32,4,64,128]{3,2,1,0:T(8,128)(2,1)} custom-call(s32[4,32]{1,0:T(4,128)} %bitcast.26, bf16[64,4096]{1,0:T(8,128)(2,1)} %bitcast.19), custom_call_target="tpu_custom_call" | custom-call | bytes 5242880 | tf_op jit(solution)/shard_map/pack_outgoing/pallas_call | solution.py:380
  3.2 7.8 %all-to-all-start = ((bf16[32,4,64,128]{3,2,1,0:T(8,128)(2,1)}), bf16[32,4,64,128]{3,2,1,0:T(8,128)(2,1)S(1)}, u32[]{:S(2)}, u32[]{:S(2)}) async-start(bf16[32,4,64,128]{3,2,1,0:T(8,128)(2,1)} %pack_outgoing.1), calls=%async_computation | async-start | bytes 4194304 | tf_op jit(solution)/shard_map/all_to_all | solution.py:393
  11.0 0.9 split_feats.1
  11.9 2.0 %collective-permute-start = (bf16[64,512]{1,0:T(8,128)(2,1)}, bf16[64,512]{1,0:T(8,128)(2,1)S(1)}, u32[]{:S(2)}, u32[]{:S(2)}) collective-permute-start(bf16[64,512]{1,0:T(8,128)(2,1)} %get-tuple-element.76), channel_id=1, source_target_pairs={{0,1},{1,2},{2,3},{3,4},{4,5},{5,6},{6,7},{7,0},{8,9},{9,10},{10,1... | collective-permute-start | bytes 196616 | tf_op jit(solution)/shard_map/ppermute | solution.py:332
  13.9 3.3 %collective-permute-start.1 = (bf16[64,512]{1,0:T(8,128)(2,1)}, bf16[64,512]{1,0:T(8,128)(2,1)S(1)}, u32[]{:S(2)}, u32[]{:S(2)}) collective-permute-start(bf16[64,512]{1,0:T(8,128)(2,1)} %get-tuple-element.77), channel_id=1, source_target_pairs={{0,2},{1,3},{2,4},{3,5},{4,6},{5,7},{6,0},{7,1},{8,10},{9,11},{10,... | collective-permute-start | bytes 196616 | tf_op jit(solution)/shard_map/ppermute | solution.py:332
  17.1 4.0 %collective-permute-start.2 = (bf16[64,512]{1,0:T(8,128)(2,1)}, bf16[64,512]{1,0:T(8,128)(2,1)S(1)}, u32[]{:S(2)}, u32[]{:S(2)}) collective-permute-start(bf16[64,512]{1,0:T(8,128)(2,1)} %get-tuple-element.78), channel_id=1, source_target_pairs={{0,3},{1,4},{2,5},{3,6},{4,7},{5,0},{6,1},{7,2},{8,11},{9,12},{10,... | collective-permute-start | bytes 196616 | tf_op jit(solution)/shard_map/ppermute | solution.py:332
  21.7 4.9 %collective-permute-start.4 = (bf16[64,512]{1,0:T(8,128)(2,1)}, bf16[64,512]{1,0:T(8,128)(2,1)S(1)}, u32[]{:S(2)}, u32[]{:S(2)}) collective-permute-start(bf16[64,512]{1,0:T(8,128)(2,1)} %get-tuple-element.80), channel_id=1, source_target_pairs={{0,5},{1,6},{2,7},{3,0},{4,1},{5,2},{6,3},{7,4},{8,13},{9,14},{10,... | collective-permute-start | bytes 196616 | tf_op jit(solution)/shard_map/ppermute | solution.py:332
  26.7 2.7 %collective-permute-start.5 = (bf16[64,512]{1,0:T(8,128)(2,1)}, bf16[64,512]{1,0:T(8,128)(2,1)S(1)}, u32[]{:S(2)}, u32[]{:S(2)}) collective-permute-start(bf16[64,512]{1,0:T(8,128)(2,1)} %get-tuple-element.81), channel_id=1, source_target_pairs={{0,6},{1,7},{2,0},{3,1},{4,2},{5,3},{6,4},{7,5},{8,14},{9,15},{10,... | collective-permute-start | bytes 196616 | tf_op jit(solution)/shard_map/ppermute | solution.py:332
  29.3 1.0 collective-permute-start.6
  30.4 5.7 %collective-permute-done.4.refs_5_ = bf16[64,512]{1,0:T(8,128)(2,1)S(1)} collective-permute-done((bf16[64,512]{1,0:T(8,128)(2,1)}, bf16[64,512]{1,0:T(8,128)(2,1)S(1)}, u32[]{:S(2)}, u32[]{:S(2)}) %collective-permute-start.4) | collective-permute-done | bytes 65568 | tf_op jit(solution)/shard_map/ppermute | solution.py:332
  36.7 0.6 copy-done.13
  37.4 1.5 %all-to-all-done = bf16[32,4,64,128]{3,2,1,0:T(8,128)(2,1)S(1)} async-done(((bf16[32,4,64,128]{3,2,1,0:T(8,128)(2,1)}), bf16[32,4,64,128]{3,2,1,0:T(8,128)(2,1)S(1)}, u32[]{:S(2)}, u32[]{:S(2)}) %all-to-all-start) | async-done | bytes 2097184 | tf_op jit(solution)/shard_map/all_to_all | solution.py:393
  39.0 6.1 %neighbour_mean.1 = (bf16[8,64,512]{2,1,0:T(8,128)(2,1)}, f32[8,8,512]{2,1,0:T(8,128)S(1)}) custom-call(s32[8,32]{1,0:T(8,128)S(1)} %bitcast.24, s32[32]{0:T(128)S(1)} %copy-done.7, bf16[64,4096]{1,0:T(8,128)(2,1)S(1)} %bitcast.21, bf16[128,64,128]{2,1,0:T(8,128)(2,1)S(1)} %bitcast.16, bf16[32,8,128,128]{3,2,1,0:T(8,128)(2,1)} %vals_ref.3), custom_call_target="tpu_custom_call" | custom-call | flops 536870912 | bytes 11534336 | tf_op jit(solution)/shard_map/neighbour_mean/pallas_call | solution.py:417
  45.1 8.5 %all-to-all-start.1 = ((bf16[8,64,512]{2,1,0:T(8,128)(2,1)}), bf16[8,64,512]{2,1,0:T(8,128)(2,1)S(1)}, u32[]{:S(2)}, u32[]{:S(2)}) async-start(bf16[8,64,512]{2,1,0:T(8,128)(2,1)} %get-tuple-element.96), calls=%async_computation.1 | async-start | bytes 1048576 | tf_op jit(solution)/shard_map/all_to_all | solution.py:432
  53.7 1.4 self_part.1
  55.2 15.5 %all-to-all-done.1 = bf16[8,64,512]{2,1,0:T(8,128)(2,1)S(1)} async-done(((bf16[8,64,512]{2,1,0:T(8,128)(2,1)}), bf16[8,64,512]{2,1,0:T(8,128)(2,1)S(1)}, u32[]{:S(2)}, u32[]{:S(2)}) %all-to-all-start.1) | async-done | bytes 524320 | tf_op jit(solution)/shard_map/all_to_all | solution.py:432
  70.7 1.8 %layer_head.1 = (bf16[256,512]{1,0:T(8,128)(2,1)S(1)}, bf16[256,512]{1,0:T(8,128)(2,1)S(1)}, bf16[512,512]{1,0:T(8,128)(2,1)}) custom-call(s32[1]{0:T(128)} %bitcast.me_ref, f32[8,8,512]{2,1,0:T(8,128)S(1)} %get-tuple-element.84.degree_ref, f32[256,512]{1,0:T(8,128)S(1)} %get-tuple-element.93.pre_ref, bf16[256,512]{1,0:T(8,128)(2,1)S(1)} %get-tuple-element.94.turned_ref, ...), custom_call_target="tpu_custom_call" | custom-call | flops 268435456 | bytes 4194304 | tf_op jit(solution)/shard_map/layer_head/pallas_call | solution.py:434
  72.5 3.5 %all-to-all-start.2 = ((bf16[8,64,512]{2,1,0:T(8,128)(2,1)}), bf16[8,64,512]{2,1,0:T(8,128)(2,1)S(1)}, u32[]{:S(2)}, u32[]{:S(2)}) async-start(bf16[8,64,512]{2,1,0:T(8,128)(2,1)} %bitcast.8), calls=%async_computation.2 | async-start | bytes 1048576 | tf_op jit(solution)/shard_map/all_to_all | solution.py:443
  76.6 1.5 %collective-permute-done.7.recv_ref = bf16[16,8,8,128]{3,2,1,0:T(8,128)(2,1)S(1)} collective-permute-done((bf16[16,8,8,128]{3,2,1,0:T(8,128)(2,1)S(1)}, bf16[16,8,8,128]{3,2,1,0:T(8,128)(2,1)S(1)}, u32[]{:S(2)}, u32[]{:S(2)}) %collective-permute-start.7) | collective-permute-done | bytes 262176 | tf_op jit(solution)/shard_map/ppermute | solution.py:463
  78.2 1.1 collective-permute-start.8
  79.3 1.0 collective-permute-start.9
  80.3 1.5 %collective-permute-start.10 = (bf16[4,8,8,128]{3,2,1,0:T(8,128)(2,1)S(1)}, bf16[4,8,8,128]{3,2,1,0:T(8,128)(2,1)S(1)}, u32[]{:S(2)}, u32[]{:S(2)}) collective-permute-start(bf16[4,8,8,128]{3,2,1,0:T(8,128)(2,1)S(1)} %get-tuple-element.105), channel_id=1, source_target_pairs={{0,80},{8,88},{16,64},{24,72},{32,112},{40,120},{48,96},{56,104},{... | collective-permute-start | bytes 196616 | tf_op jit(solution)/shard_map/ppermute | solution.py:479
  81.8 0.8 collective-permute-done.8.refs_0_
  82.6 1.6 %collective-permute-done.9.refs_1_ = bf16[4,8,8,128]{3,2,1,0:T(8,128)(2,1)S(1)} collective-permute-done((bf16[4,8,8,128]{3,2,1,0:T(8,128)(2,1)S(1)}, bf16[4,8,8,128]{3,2,1,0:T(8,128)(2,1)S(1)}, u32[]{:S(2)}, u32[]{:S(2)}) %collective-permute-start.9) | collective-permute-done | bytes 65568 | tf_op jit(solution)/shard_map/ppermute | solution.py:479
  84.1 1.3 collective-permute-done.10.refs_2_
  85.5 1.3 collective-permute-start.11
  86.8 0.9 side_grads.1
  87.7 3.6 %collective-permute-done.11.recv_ref = bf16[4,8,8,128]{3,2,1,0:T(8,128)(2,1)S(1)} collective-permute-done((bf16[4,8,8,128]{3,2,1,0:T(8,128)(2,1)S(1)}, bf16[4,8,8,128]{3,2,1,0:T(8,128)(2,1)S(1)}, u32[]{:S(2)}, u32[]{:S(2)}) %collective-permute-start.11) | collective-permute-done | bytes 65568 | tf_op jit(solution)/shard_map/ppermute | solution.py:492
  91.4 1.2 all-to-all-done.2.scaled_ref
  92.6 6.5 %table_grad.1 = (f32[32,64,128]{2,1,0:T(8,128)}, bf16[128,64,128]{2,1,0:T(8,128)(2,1)}) custom-call(s32[8,32]{1,0:T(8,128)S(1)} %bitcast.25, s32[32]{0:T(128)S(1)} %copy-done.7, bf16[32,8,128,128]{3,2,1,0:T(8,128)(2,1)} %vals_ref.3, bf16[8,64,512]{2,1,0:T(8,128)(2,1)S(1)} %all-to-all-done.2.scaled_ref), custom_call_target="tpu_custom_call" | custom-call | flops 536870912 | bytes 12582912 | tf_op jit(solution)/shard_map/table_grad/pallas_call | solution.py:496
  99.0 7.5 %all-to-all-start.3 = ((bf16[32,4,64,128]{3,2,1,0:T(8,128)(2,1)}), bf16[32,4,64,128]{3,2,1,0:T(8,128)(2,1)S(1)}, u32[]{:S(2)}, u32[]{:S(2)}) async-start(bf16[32,4,64,128]{3,2,1,0:T(8,128)(2,1)} %bitcast.28), calls=%async_computation.3 | async-start | bytes 4194304 | tf_op jit(solution)/shard_map/all_to_all | solution.py:517
  106.6 4.3 %collective-permute-start.12 = (bf16[64,640]{1,0:T(8,128)(2,1)S(1)}, bf16[64,640]{1,0:T(8,128)(2,1)S(1)}, u32[]{:S(2)}, u32[]{:S(2)}) collective-permute-start(bf16[64,640]{1,0:T(8,128)(2,1)S(1)} %get-tuple-element.129), channel_id=1, source_target_pairs={{0,4},{1,5},{2,6},{3,7},{4,0},{5,1},{6,2},{7,3},{8,12},{9,13},{10,... | collective-permute-start | bytes 245768 | tf_op jit(solution)/shard_map/ppermute | solution.py:332
  111.5 4.5 %collective-permute-start.14 = (bf16[64,640]{1,0:T(8,128)(2,1)S(1)}, bf16[64,640]{1,0:T(8,128)(2,1)S(1)}, u32[]{:S(2)}, u32[]{:S(2)}) collective-permute-start(bf16[64,640]{1,0:T(8,128)(2,1)S(1)} %get-tuple-element.131), channel_id=1, source_target_pairs={{0,5},{1,6},{2,7},{3,0},{4,1},{5,2},{6,3},{7,4},{8,13},{9,14},{10,... | collective-permute-start | bytes 245768 | tf_op jit(solution)/shard_map/ppermute | solution.py:332
  116.6 3.6 %collective-permute-start.16 = (bf16[64,640]{1,0:T(8,128)(2,1)S(1)}, bf16[64,640]{1,0:T(8,128)(2,1)S(1)}, u32[]{:S(2)}, u32[]{:S(2)}) collective-permute-start(bf16[64,640]{1,0:T(8,128)(2,1)S(1)} %get-tuple-element.133), channel_id=1, source_target_pairs={{0,6},{1,7},{2,0},{3,1},{4,2},{5,3},{6,4},{7,5},{8,14},{9,15},{10,... | collective-permute-start | bytes 245768 | tf_op jit(solution)/shard_map/ppermute | solution.py:332
  120.7 3.3 %collective-permute-done.13.refs_1_ = bf16[64,640]{1,0:T(8,128)(2,1)S(1)} collective-permute-done((bf16[64,640]{1,0:T(8,128)(2,1)S(1)}, bf16[64,640]{1,0:T(8,128)(2,1)S(1)}, u32[]{:S(2)}, u32[]{:S(2)}) %collective-permute-start.13) | collective-permute-done | bytes 81952 | tf_op jit(solution)/shard_map/ppermute | solution.py:332
  124.0 1.0 collective-permute-done.16.refs_4_
  125.0 1.3 collective-permute-done.17.refs_5_
  126.3 2.2 %collective-permute-done.18.refs_6_ = bf16[64,640]{1,0:T(8,128)(2,1)S(1)} collective-permute-done((bf16[64,640]{1,0:T(8,128)(2,1)S(1)}, bf16[64,640]{1,0:T(8,128)(2,1)S(1)}, u32[]{:S(2)}, u32[]{:S(2)}) %collective-permute-start.18) | collective-permute-done | bytes 81952 | tf_op jit(solution)/shard_map/ppermute | solution.py:332
  128.5 1.2 copy-done.1
  129.9 1.1 collective-permute-done.19
  131.1 3.0 %collective-permute-start.20 = (bf16[2,32,128]{2,1,0:T(8,128)(2,1)S(1)}, bf16[2,32,128]{2,1,0:T(8,128)(2,1)S(1)}, u32[]{:S(2)}, u32[]{:S(2)}) collective-permute-start(bf16[2,32,128]{2,1,0:T(8,128)(2,1)S(1)} %constant_dynamic-update-slice_fusion), channel_id=1, source_target_pairs={{0,128},{8,136},{16,144},{24,152},{32,160},{40,168},{48,176},{56,1... | collective-permute-start | bytes 49160 | tf_op jit(solution)/shard_map/ppermute | solution.py:555
  134.1 1.2 collective-permute-start.22
  135.2 1.1 collective-permute-done.20
  136.3 2.7 %collective-permute-done.22 = bf16[2,32,128]{2,1,0:T(8,128)(2,1)S(1)} collective-permute-done((bf16[2,32,128]{2,1,0:T(8,128)(2,1)S(1)}, bf16[2,32,128]{2,1,0:T(8,128)(2,1)S(1)}, u32[]{:S(2)}, u32[]{:S(2)}) %collective-permute-start.22) | collective-permute-done | bytes 16416 | tf_op jit(solution)/shard_map/ppermute | solution.py:555
  139.0 0.6 collective-permute-start.23
  139.7 2.2 %sum_returned.1 = bf16[64,4096]{1,0:T(8,128)(2,1)} custom-call(s32[4,32]{1,0:T(4,128)S(1)} %bitcast.27, f32[32,64,128]{2,1,0:T(8,128)S(1)} %sum_near.1.near_ref, bf16[32,4,64,128]{3,2,1,0:T(8,128)(2,1)S(1)} %all-to-all-done.3.back_ref), custom_call_target="tpu_custom_call" | custom-call | bytes 4194304 | tf_op jit(solution)/shard_map/sum_returned/pallas_call | solution.py:561
  141.9 1.2 collective-permute-done.23
  143.1 0.7 weight_spread.1
  (61 shorter events, 4.2 us)
Async XLA Ops:
  3.2 7.8 %copy-start = (bf16[4096,64]{0,1:T(8,128)(2,1)S(1)}, bf16[4096,64]{0,1:T(8,128)(2,1)}, u32[]{:S(2)}) copy-start(bf16[4096,64]{0,1:T(8,128)(2,1)} %param.9) | copy-start | bytes 1572868
  3.2 35.7 %copy-start.5 = (s32[32,8]{0,1:T(8,128)S(1)}, s32[32,8]{0,1:T(8,128)}, u32[]{:S(2)}) copy-start(s32[32,8]{0,1:T(8,128)} %param.11) | copy-start | bytes 3076
  3.2 35.7 %copy-start.7 = (s32[32]{0:T(128)S(1)}, s32[32]{0:T(128)}, u32[]{:S(2)}) copy-start(s32[32]{0:T(128)} %counts_ref.3) | copy-start | bytes 388
  3.2 35.6 %all-to-all-start = ((bf16[32,4,64,128]{3,2,1,0:T(8,128)(2,1)}), bf16[32,4,64,128]{3,2,1,0:T(8,128)(2,1)S(1)}, u32[]{:S(2)}, u32[]{:S(2)}) async-start(bf16[32,4,64,128]{3,2,1,0:T(8,128)(2,1)} %pack_outgoing.1), calls=%async_computation | async-start | bytes 4194304 | tf_op jit(solution)/shard_map/all_to_all | solution.py:393
  11.9 14.8 %collective-permute-start = (bf16[64,512]{1,0:T(8,128)(2,1)}, bf16[64,512]{1,0:T(8,128)(2,1)S(1)}, u32[]{:S(2)}, u32[]{:S(2)}) collective-permute-start(bf16[64,512]{1,0:T(8,128)(2,1)} %get-tuple-element.76), channel_id=1, source_target_pairs={{0,1},{1,2},{2,3},{3,4},{4,5},{5,6},{6,7},{7,0},{8,9},{9,10},{10,1... | collective-permute-start | bytes 196616 | tf_op jit(solution)/shard_map/ppermute | solution.py:332
  13.9 15.5 %collective-permute-start.1 = (bf16[64,512]{1,0:T(8,128)(2,1)}, bf16[64,512]{1,0:T(8,128)(2,1)S(1)}, u32[]{:S(2)}, u32[]{:S(2)}) collective-permute-start(bf16[64,512]{1,0:T(8,128)(2,1)} %get-tuple-element.77), channel_id=1, source_target_pairs={{0,2},{1,3},{2,4},{3,5},{4,6},{5,7},{6,0},{7,1},{8,10},{9,11},{10,... | collective-permute-start | bytes 196616 | tf_op jit(solution)/shard_map/ppermute | solution.py:332
  17.1 13.2 %collective-permute-start.2 = (bf16[64,512]{1,0:T(8,128)(2,1)}, bf16[64,512]{1,0:T(8,128)(2,1)S(1)}, u32[]{:S(2)}, u32[]{:S(2)}) collective-permute-start(bf16[64,512]{1,0:T(8,128)(2,1)} %get-tuple-element.78), channel_id=1, source_target_pairs={{0,3},{1,4},{2,5},{3,6},{4,7},{5,0},{6,1},{7,2},{8,11},{9,12},{10,... | collective-permute-start | bytes 196616 | tf_op jit(solution)/shard_map/ppermute | solution.py:332
  21.2 9.2 %collective-permute-start.3 = (bf16[64,512]{1,0:T(8,128)(2,1)}, bf16[64,512]{1,0:T(8,128)(2,1)S(1)}, u32[]{:S(2)}, u32[]{:S(2)}) collective-permute-start(bf16[64,512]{1,0:T(8,128)(2,1)} %get-tuple-element.79), channel_id=1, source_target_pairs={{0,4},{1,5},{2,6},{3,7},{4,0},{5,1},{6,2},{7,3},{8,12},{9,13},{10,... | collective-permute-start | bytes 196616 | tf_op jit(solution)/shard_map/ppermute | solution.py:332
  21.7 14.4 %collective-permute-start.4 = (bf16[64,512]{1,0:T(8,128)(2,1)}, bf16[64,512]{1,0:T(8,128)(2,1)S(1)}, u32[]{:S(2)}, u32[]{:S(2)}) collective-permute-start(bf16[64,512]{1,0:T(8,128)(2,1)} %get-tuple-element.80), channel_id=1, source_target_pairs={{0,5},{1,6},{2,7},{3,0},{4,1},{5,2},{6,3},{7,4},{8,13},{9,14},{10,... | collective-permute-start | bytes 196616 | tf_op jit(solution)/shard_map/ppermute | solution.py:332
  26.7 12.2 %copy-start.8 = (bf16[64,512]{1,0:T(8,128)(2,1)}, bf16[64,512]{1,0:T(8,128)(2,1)S(1)}, u32[]{:S(2)}) copy-start(bf16[64,512]{1,0:T(8,128)(2,1)S(1)} %collective-permute-done.refs_1_) | copy-start | bytes 196612
  26.7 9.4 %collective-permute-start.5 = (bf16[64,512]{1,0:T(8,128)(2,1)}, bf16[64,512]{1,0:T(8,128)(2,1)S(1)}, u32[]{:S(2)}, u32[]{:S(2)}) collective-permute-start(bf16[64,512]{1,0:T(8,128)(2,1)} %get-tuple-element.81), channel_id=1, source_target_pairs={{0,6},{1,7},{2,0},{3,1},{4,2},{5,3},{6,4},{7,5},{8,14},{9,15},{10,... | collective-permute-start | bytes 196616 | tf_op jit(solution)/shard_map/ppermute | solution.py:332
  29.3 9.5 %copy-start.9 = (bf16[64,512]{1,0:T(8,128)(2,1)}, bf16[64,512]{1,0:T(8,128)(2,1)S(1)}, u32[]{:S(2)}) copy-start(bf16[64,512]{1,0:T(8,128)(2,1)S(1)} %collective-permute-done.1.refs_2_) | copy-start | bytes 196612
  29.3 8.0 %collective-permute-start.6 = (bf16[64,512]{1,0:T(8,128)(2,1)}, bf16[64,512]{1,0:T(8,128)(2,1)}, u32[]{:S(2)}, u32[]{:S(2)}) collective-permute-start(bf16[64,512]{1,0:T(8,128)(2,1)} %get-tuple-element.82), channel_id=1, source_target_pairs={{0,7},{1,0},{2,1},{3,2},{4,3},{5,4},{6,5},{7,6},{8,15},{9,8},{10,9... | collective-permute-start | bytes 196616 | tf_op jit(solution)/shard_map/ppermute | solution.py:332
  30.3 8.5 %copy-start.10 = (bf16[64,512]{1,0:T(8,128)(2,1)}, bf16[64,512]{1,0:T(8,128)(2,1)S(1)}, u32[]{:S(2)}) copy-start(bf16[64,512]{1,0:T(8,128)(2,1)S(1)} %collective-permute-done.2.refs_3_) | copy-start | bytes 196612
  30.4 8.5 %copy-start.11 = (bf16[64,512]{1,0:T(8,128)(2,1)}, bf16[64,512]{1,0:T(8,128)(2,1)S(1)}, u32[]{:S(2)}) copy-start(bf16[64,512]{1,0:T(8,128)(2,1)S(1)} %collective-permute-done.3.refs_4_) | copy-start | bytes 196612
  36.1 0.6 copy-start.12
  36.7 0.6 copy-start.13
  38.9 14.7 %copy-start.14 = (f32[256]{0:T(256)S(1)}, f32[256]{0:T(256)}, u32[]{:S(2)}) copy-start(f32[256]{0:T(256)} %param.16) | copy-start | bytes 3076
  38.9 14.8 %copy-start.2 = (bf16[512,256]{1,0:T(8,128)(2,1)S(1)}, bf16[512,256]{1,0:T(8,128)(2,1)}, u32[]{:S(2)}) copy-start(bf16[512,256]{1,0:T(8,128)(2,1)} %weight_ref.4) | copy-start | bytes 786436
  38.9 14.8 %copy-start.3 = (bf16[512,256]{1,0:T(8,128)(2,1)S(1)}, bf16[512,256]{1,0:T(8,128)(2,1)}, u32[]{:S(2)}) copy-start(bf16[512,256]{1,0:T(8,128)(2,1)} %weight_ref.5) | copy-start | bytes 786436
  38.9 14.8 %copy-start.4 = (bf16[512,256]{1,0:T(8,128)(2,1)S(1)}, bf16[512,256]{1,0:T(8,128)(2,1)}, u32[]{:S(2)}) copy-start(bf16[512,256]{1,0:T(8,128)(2,1)} %cot_ref.1) | copy-start | bytes 786436
  45.1 25.6 %all-to-all-start.1 = ((bf16[8,64,512]{2,1,0:T(8,128)(2,1)}), bf16[8,64,512]{2,1,0:T(8,128)(2,1)S(1)}, u32[]{:S(2)}, u32[]{:S(2)}) async-start(bf16[8,64,512]{2,1,0:T(8,128)(2,1)} %get-tuple-element.96), calls=%async_computation.1 | async-start | bytes 1048576 | tf_op jit(solution)/shard_map/all_to_all | solution.py:432
  72.5 20.1 %all-to-all-start.2 = ((bf16[8,64,512]{2,1,0:T(8,128)(2,1)}), bf16[8,64,512]{2,1,0:T(8,128)(2,1)S(1)}, u32[]{:S(2)}, u32[]{:S(2)}) async-start(bf16[8,64,512]{2,1,0:T(8,128)(2,1)} %bitcast.8), calls=%async_computation.2 | async-start | bytes 1048576 | tf_op jit(solution)/shard_map/all_to_all | solution.py:443
  76.5 1.6 %collective-permute-start.7 = (bf16[16,8,8,128]{3,2,1,0:T(8,128)(2,1)S(1)}, bf16[16,8,8,128]{3,2,1,0:T(8,128)(2,1)S(1)}, u32[]{:S(2)}, u32[]{:S(2)}) collective-permute-start(bf16[16,8,8,128]{3,2,1,0:T(8,128)(2,1)S(1)} %get-tuple-element.101), channel_id=1, source_target_pairs={{0,8},{8,0},{16,24},{24,16},{32,40},{40,32},{48,56},{56,48},{64,72... | collective-permute-start | bytes 786440 | tf_op jit(solution)/shard_map/ppermute | solution.py:463
  78.2 4.4 %collective-permute-start.8 = (bf16[4,8,8,128]{3,2,1,0:T(8,128)(2,1)S(1)}, bf16[4,8,8,128]{3,2,1,0:T(8,128)(2,1)S(1)}, u32[]{:S(2)}, u32[]{:S(2)}) collective-permute-start(bf16[4,8,8,128]{3,2,1,0:T(8,128)(2,1)S(1)} %get-tuple-element.103), channel_id=1, source_target_pairs={{0,64},{8,72},{16,80},{24,88},{32,96},{40,104},{48,112},{56,120},{... | collective-permute-start | bytes 196616 | tf_op jit(solution)/shard_map/ppermute | solution.py:479
  79.3 4.9 %collective-permute-start.9 = (bf16[4,8,8,128]{3,2,1,0:T(8,128)(2,1)S(1)}, bf16[4,8,8,128]{3,2,1,0:T(8,128)(2,1)S(1)}, u32[]{:S(2)}, u32[]{:S(2)}) collective-permute-start(bf16[4,8,8,128]{3,2,1,0:T(8,128)(2,1)S(1)} %get-tuple-element.104), channel_id=1, source_target_pairs={{0,16},{8,24},{16,0},{24,8},{32,48},{40,56},{48,32},{56,40},{64,80... | collective-permute-start | bytes 196616 | tf_op jit(solution)/shard_map/ppermute | solution.py:479
  80.3 5.2 %collective-permute-start.10 = (bf16[4,8,8,128]{3,2,1,0:T(8,128)(2,1)S(1)}, bf16[4,8,8,128]{3,2,1,0:T(8,128)(2,1)S(1)}, u32[]{:S(2)}, u32[]{:S(2)}) collective-permute-start(bf16[4,8,8,128]{3,2,1,0:T(8,128)(2,1)S(1)} %get-tuple-element.105), channel_id=1, source_target_pairs={{0,80},{8,88},{16,64},{24,72},{32,112},{40,120},{48,96},{56,104},{... | collective-permute-start | bytes 196616 | tf_op jit(solution)/shard_map/ppermute | solution.py:479
  85.5 5.9 %collective-permute-start.11 = (bf16[4,8,8,128]{3,2,1,0:T(8,128)(2,1)S(1)}, bf16[4,8,8,128]{3,2,1,0:T(8,128)(2,1)S(1)}, u32[]{:S(2)}, u32[]{:S(2)}) collective-permute-start(bf16[4,8,8,128]{3,2,1,0:T(8,128)(2,1)S(1)} %weight_add.2.held_ref), channel_id=1, source_target_pairs={{0,32},{8,40},{16,48},{24,56},{32,0},{40,8},{48,16},{56,24},{64,96... | collective-permute-start | bytes 196616 | tf_op jit(solution)/shard_map/ppermute | solution.py:492
  99.0 40.0 %all-to-all-start.3 = ((bf16[32,4,64,128]{3,2,1,0:T(8,128)(2,1)}), bf16[32,4,64,128]{3,2,1,0:T(8,128)(2,1)S(1)}, u32[]{:S(2)}, u32[]{:S(2)}) async-start(bf16[32,4,64,128]{3,2,1,0:T(8,128)(2,1)} %bitcast.28), calls=%async_computation.3 | async-start | bytes 4194304 | tf_op jit(solution)/shard_map/all_to_all | solution.py:517
  106.5 33.2 %copy-start.6 = (s32[1,32,4]{1,2,0:T(4,128)S(1)}, s32[1,32,4]{1,2,0:T(4,128)}, u32[]{:S(2)}) copy-start(s32[1,32,4]{1,2,0:T(4,128)} %param.13) | copy-start | bytes 1540
  106.6 13.5 %collective-permute-start.12 = (bf16[64,640]{1,0:T(8,128)(2,1)S(1)}, bf16[64,640]{1,0:T(8,128)(2,1)S(1)}, u32[]{:S(2)}, u32[]{:S(2)}) collective-permute-start(bf16[64,640]{1,0:T(8,128)(2,1)S(1)} %get-tuple-element.129), channel_id=1, source_target_pairs={{0,4},{1,5},{2,6},{3,7},{4,0},{5,1},{6,2},{7,3},{8,12},{9,13},{10,... | collective-permute-start | bytes 245768 | tf_op jit(solution)/shard_map/ppermute | solution.py:332
  111.0 13.1 %collective-permute-start.13 = (bf16[64,640]{1,0:T(8,128)(2,1)S(1)}, bf16[64,640]{1,0:T(8,128)(2,1)S(1)}, u32[]{:S(2)}, u32[]{:S(2)}) collective-permute-start(bf16[64,640]{1,0:T(8,128)(2,1)S(1)} %get-tuple-element.130), channel_id=1, source_target_pairs={{0,3},{1,4},{2,5},{3,6},{4,7},{5,0},{6,1},{7,2},{8,11},{9,12},{10,... | collective-permute-start | bytes 245768 | tf_op jit(solution)/shard_map/ppermute | solution.py:332
  111.5 12.5 %collective-permute-start.14 = (bf16[64,640]{1,0:T(8,128)(2,1)S(1)}, bf16[64,640]{1,0:T(8,128)(2,1)S(1)}, u32[]{:S(2)}, u32[]{:S(2)}) collective-permute-start(bf16[64,640]{1,0:T(8,128)(2,1)S(1)} %get-tuple-element.131), channel_id=1, source_target_pairs={{0,5},{1,6},{2,7},{3,0},{4,1},{5,2},{6,3},{7,4},{8,13},{9,14},{10,... | collective-permute-start | bytes 245768 | tf_op jit(solution)/shard_map/ppermute | solution.py:332
  116.0 8.0 %collective-permute-start.15 = (bf16[64,640]{1,0:T(8,128)(2,1)S(1)}, bf16[64,640]{1,0:T(8,128)(2,1)S(1)}, u32[]{:S(2)}, u32[]{:S(2)}) collective-permute-start(bf16[64,640]{1,0:T(8,128)(2,1)S(1)} %get-tuple-element.132), channel_id=1, source_target_pairs={{0,2},{1,3},{2,4},{3,5},{4,6},{5,7},{6,0},{7,1},{8,10},{9,11},{10,... | collective-permute-start | bytes 245768 | tf_op jit(solution)/shard_map/ppermute | solution.py:332
  116.6 8.4 %collective-permute-start.16 = (bf16[64,640]{1,0:T(8,128)(2,1)S(1)}, bf16[64,640]{1,0:T(8,128)(2,1)S(1)}, u32[]{:S(2)}, u32[]{:S(2)}) collective-permute-start(bf16[64,640]{1,0:T(8,128)(2,1)S(1)} %get-tuple-element.133), channel_id=1, source_target_pairs={{0,6},{1,7},{2,0},{3,1},{4,2},{5,3},{6,4},{7,5},{8,14},{9,15},{10,... | collective-permute-start | bytes 245768 | tf_op jit(solution)/shard_map/ppermute | solution.py:332
  120.1 6.1 %collective-permute-start.17 = (bf16[64,640]{1,0:T(8,128)(2,1)S(1)}, bf16[64,640]{1,0:T(8,128)(2,1)S(1)}, u32[]{:S(2)}, u32[]{:S(2)}) collective-permute-start(bf16[64,640]{1,0:T(8,128)(2,1)S(1)} %get-tuple-element.134), channel_id=1, source_target_pairs={{0,1},{1,2},{2,3},{3,4},{4,5},{5,6},{6,7},{7,0},{8,9},{9,10},{10,1... | collective-permute-start | bytes 245768 | tf_op jit(solution)/shard_map/ppermute | solution.py:332
  124.0 4.4 %collective-permute-start.18 = (bf16[64,640]{1,0:T(8,128)(2,1)S(1)}, bf16[64,640]{1,0:T(8,128)(2,1)S(1)}, u32[]{:S(2)}, u32[]{:S(2)}) collective-permute-start(bf16[64,640]{1,0:T(8,128)(2,1)S(1)} %get-tuple-element.135), channel_id=1, source_target_pairs={{0,7},{1,0},{2,1},{3,2},{4,3},{5,4},{6,5},{7,6},{8,15},{9,8},{10,9... | collective-permute-start | bytes 245768 | tf_op jit(solution)/shard_map/ppermute | solution.py:332
  128.5 1.2 copy-start.1
  129.8 1.3 collective-permute-start.19
  131.1 5.2 %collective-permute-start.20 = (bf16[2,32,128]{2,1,0:T(8,128)(2,1)S(1)}, bf16[2,32,128]{2,1,0:T(8,128)(2,1)S(1)}, u32[]{:S(2)}, u32[]{:S(2)}) collective-permute-start(bf16[2,32,128]{2,1,0:T(8,128)(2,1)S(1)} %constant_dynamic-update-slice_fusion), channel_id=1, source_target_pairs={{0,128},{8,136},{16,144},{24,152},{32,160},{40,168},{48,176},{56,1... | collective-permute-start | bytes 49160 | tf_op jit(solution)/shard_map/ppermute | solution.py:555
  134.1 4.9 %collective-permute-start.22 = (bf16[2,32,128]{2,1,0:T(8,128)(2,1)S(1)}, bf16[2,32,128]{2,1,0:T(8,128)(2,1)S(1)}, u32[]{:S(2)}, u32[]{:S(2)}) collective-permute-start(bf16[2,32,128]{2,1,0:T(8,128)(2,1)S(1)} %constant_dynamic-update-slice_fusion), channel_id=1, source_target_pairs={{0,192},{8,200},{16,208},{24,216},{32,224},{40,232},{48,240},{56,2... | collective-permute-start | bytes 49160 | tf_op jit(solution)/shard_map/ppermute | solution.py:555
  135.2 3.8 %collective-permute-start.21 = (bf16[2,32,128]{2,1,0:T(8,128)(2,1)S(1)}, bf16[2,32,128]{2,1,0:T(8,128)(2,1)S(1)}, u32[]{:S(2)}, u32[]{:S(2)}) collective-permute-start(bf16[2,32,128]{2,1,0:T(8,128)(2,1)S(1)} %constant_dynamic-update-slice_fusion), channel_id=1, source_target_pairs={{0,64},{8,72},{16,80},{24,88},{32,96},{40,104},{48,112},{56,120},{... | collective-permute-start | bytes 49160 | tf_op jit(solution)/shard_map/ppermute | solution.py:555
  139.0 4.0 %collective-permute-start.23 = (bf16[4,32,128]{2,1,0:T(8,128)(2,1)S(1)}, bf16[4,32,128]{2,1,0:T(8,128)(2,1)S(1)}, u32[]{:S(2)}, u32[]{:S(2)}) collective-permute-start(bf16[4,32,128]{2,1,0:T(8,128)(2,1)S(1)} %pad_maximum_fusion.1), channel_id=1, source_target_pairs={{0,16},{8,24},{16,0},{24,8},{32,48},{40,56},{48,32},{56,40},{64,80... | collective-permute-start | bytes 98312 | tf_op jit(solution)/shard_map/ppermute | solution.py:571
